TPU v7x, 32 devices: a whole 2x2x4 slice. The times are simulated.
32 devices in a mesh: depth: 16 (over z, y, core), freq: 2 (over x).
Axes of the slice: x: 2, y: 2, z: 4, core: 2. Of those that a mesh axis runs over, the one named last changes fastest.
Arguments:
- extrapolation_operator: float32 [2, 16, 2, 512, 512], P('freq', 'depth'), may hold values from -0.1875 to 0.1875
- impedance_contrast: float32 [16, 512], P('depth'), may hold values from -3 to 3
- ascending_residual: float32 [2, 16, 5, 2, 96, 512], P('freq', 'depth'), may hold values from -6 to 6
- arriving_downward_matrices: float32 [2, 16, 2, 96, 512], P('freq', 'depth'), may hold values from -6 to 6
- shot_node_indices: int32 [4, 96], replicated, may hold values from 0 to 511
- emitted_pulse: float32 [2, 4, 2], P('freq'), may hold values from -4 to 4
Outputs:
- departing_downward_matrices: float32 [2, 16, 2, 96, 512], P('freq', 'depth')
- gradient: float32 [16, 512], P('depth', 'freq')
All inputs are finite; a program needn't handle non-finite values.
Results may differ from a plain program's by a relative error of at most 0.00013.
Values sent between devices are 32-bit elements; how exact they have to be, the bound alone decides.
No kernel may reach another device: no remote copies, remote signals or barrier semaphores. Data moves between devices by JAX's collectives and lax.ppermute only.
A program may use at most 64 MiB of HBM per device.

v0:
```python
import math

import jax
import jax.numpy as jnp
from jax import lax
from jax.sharding import PartitionSpec as P

TICKS = 5


def from_behind(block, axis, distance):
    devices = range(lax.axis_size(axis))
    route = [(i - distance, i) for i in devices if i - distance in devices]
    return lax.ppermute(block, axis, route)


def matmul_high(left, right):
    return jnp.dot(left, right, precision=lax.Precision.HIGHEST, preferred_element_type=jnp.float32)


def local(
    extrapolation_operator,
    impedance_contrast,
    ascending_residual,
    arriving_downward_matrices,
    shot_node_indices,
    emitted_pulse,
):
    prop_real = extrapolation_operator[0, 0, 0]
    prop_imag = extrapolation_operator[0, 0, 1]
    prop_both = prop_real + prop_imag
    reflect = impedance_contrast[0]
    shot_matrix = arriving_downward_matrices.shape[3]
    shot_matrix_breadth = arriving_downward_matrices.shape[4]
    at_surface = lax.axis_index("depth") == 0
    columns = jnp.arange(shot_matrix_breadth, dtype=jnp.int32)
    grad_scale = 1.0 / math.sqrt(shot_matrix * TICKS)
    present_shot_matrix = arriving_downward_matrices[0, 0]
    gradient_sum = jnp.zeros((shot_matrix_breadth,), jnp.float32)
    outgoing = present_shot_matrix
    for moment in range(TICKS):
        wave_now = ascending_residual[0, 0, moment]
        grad_term = jnp.sum(present_shot_matrix * wave_now, axis=(0, 1)) * grad_scale
        gradient_sum = gradient_sum + grad_term
        sending = moment < TICKS - 1
        mixed = present_shot_matrix + reflect[None, None, :] * wave_now
        first_term = matmul_high(mixed[0], prop_real)
        second_term = matmul_high(mixed[1], prop_imag)
        third_term = matmul_high(mixed[0] + mixed[1], prop_both)
        real_out = first_term - second_term
        imag_out = third_term - first_term - second_term
        outgoing = jnp.stack([real_out, imag_out], 0)
        if sending:
            shifted = from_behind(outgoing, "depth", 1)
        if sending:
            hits = (columns[None, :] == shot_node_indices[moment][:, None]).astype(jnp.float32)
            top_panel = emitted_pulse[0, moment][:, None, None] * hits[None]
            present_shot_matrix = jnp.where(at_surface, top_panel, shifted)
    gradient_out = lax.psum_scatter(gradient_sum[None, :], "freq", scatter_dimension=1, tiled=True)
    return (outgoing[None, None], gradient_out)


def solution(mesh):
    placed = (
        P("freq", "depth", None, None, None),
        P("depth", None),
        P("freq", "depth", None, None, None, None),
        P("freq", "depth", None, None, None),
        P(),
        P("freq", None, None),
    )
    return jax.shard_map(
        local,
        mesh=mesh,
        in_specs=placed,
        out_specs=(P("freq", "depth", None, None, None), P("depth", "freq")),
        check_vma=False,
    )
```

profile of v0, /device:TPU:0, one launch (start us, length us, event | category | flops | bytes accessed | tf_op | source)
XLA Modules:
  0.0 87.5 jit_solution(9363959600656597422)
XLA Ops:
  7.2 0.0 copy-start
  7.2 0.0 reduce-scatter.4.cloned.1.call-start
  7.2 1.3 %fusion.53 = f32[2,96,512]{2,1,0:T(8,128)S(1)} fusion(f32[1,1,2,96,512]{4,3,2,1,0:T(8,128)} %param.9, f32[1,1,5,2,96,512]{5,4,3,2,1,0:T(8,128)} %param.8, f32[512]{0:T(512)} %bitcast.152), kind=kLoop, calls=%fused_computation.74 | loop fusion | flops 196608 | bytes 1181696 | tf_op jit(solution)/shard_map/add | solution.py:46
  8.5 2.0 %fusion.23 = f32[96,512]{1,0:T(8,128)S(1)} fusion(f32[1,1,2,512,512]{4,3,2,1,0:T(8,128)} %param.6, f32[2,96,512]{2,1,0:T(8,128)S(1)} %fusion.53), kind=kOutput, calls=%fused_computation.28 | convolution fusion | flops 301989888 | bytes 1441792 | tf_op jit(solution)/shard_map/dot_general | solution.py:18
  10.5 0.0 copy-done
  10.5 0.7 fusion.33
  11.3 0.2 slice_add_fusion
  11.5 0.0 copy-start.6
  11.5 0.0 copy-start.4
  11.5 0.0 copy-start.3
  11.5 0.7 fusion.9
  12.3 0.8 pad_maximum_fusion
  13.1 2.4 %collective-permute-start = (f32[2,96,512]{2,1,0:T(8,128)}, f32[2,96,512]{2,1,0:T(8,128)S(1)}, u32[]{:S(2)}, u32[]{:S(2)}) collective-permute-start(f32[2,96,512]{2,1,0:T(8,128)} %pad_maximum_fusion), channel_id=1, source_target_pairs={{0,2},{2,4},{4,6},{6,8},{8,10},{10,12},{12,14},{14,16},{16,18},{18... | collective-permute-start | bytes 1179656 | tf_op jit(solution)/shard_map/ppermute | solution.py:14
  15.4 0.0 copy-done.6
  15.5 0.6 slice_bitcast_fusion.3
  16.1 0.0 copy-done.4
  16.1 0.2 slice_reduce_fusion.3
  16.3 0.7 fusion.78
  17.0 0.0 collective-permute-done
  17.0 0.0 copy-done.3
  17.0 1.1 %fusion.51 = f32[2,96,512]{2,1,0:T(8,128)S(1)} fusion(f32[1,1,5,2,96,512]{5,4,3,2,1,0:T(8,128)} %param.8, f32[2,96,512]{2,1,0:T(8,128)S(1)} %collective-permute-done, f32[512]{0:T(512)S(1)} %bitcast.153, f32[96,512]{1,0:T(8,128)S(1)} %fusion.78, f32[2]{0:T(128)S(1)} %get-tuple-element.9, pred[]{:T(512)S(6)} %eq.79), kind=kLoop, calls=%fused_computation.70 | loop fusion | flops 393216 | bytes 1378313 | tf_op jit(solution)/shard_map/add | solution.py:46
  18.2 0.7 fusion.21
  18.9 0.0 copy-start.5
  18.9 0.0 copy-start.1
  18.9 0.7 fusion.31
  19.7 0.8 fusion.7
  20.5 8.0 %collective-permute-start.1 = (f32[2,96,512]{2,1,0:T(8,128)S(1)}, f32[2,96,512]{2,1,0:T(8,128)S(1)}, u32[]{:S(2)}, u32[]{:S(2)}) collective-permute-start(f32[2,96,512]{2,1,0:T(8,128)S(1)} %pad_maximum_fusion.1), channel_id=1, source_target_pairs={{0,2},{2,4},{4,6},{6,8},{8,10},{10,12},{12,14},{14,16},{16,18},{18... | collective-permute-start | bytes 1179656 | tf_op jit(solution)/shard_map/ppermute | solution.py:14
  28.5 0.0 copy-done.5
  28.5 0.1 fusion.77
  28.6 1.2 %collective-permute-done.1 = f32[2,96,512]{2,1,0:T(8,128)S(1)} collective-permute-done((f32[2,96,512]{2,1,0:T(8,128)S(1)}, f32[2,96,512]{2,1,0:T(8,128)S(1)}, u32[]{:S(2)}, u32[]{:S(2)}) %collective-permute-start.1) | collective-permute-done | bytes 393248 | tf_op jit(solution)/shard_map/ppermute | solution.py:14
  29.8 0.0 copy-done.1
  29.8 0.1 fusion.49
  29.9 0.7 fusion.19
  30.7 0.7 fusion.29
  31.4 0.8 fusion.5
  32.2 7.7 %collective-permute-start.2 = (f32[2,96,512]{2,1,0:T(8,128)S(1)}, f32[2,96,512]{2,1,0:T(8,128)S(1)}, u32[]{:S(2)}, u32[]{:S(2)}) collective-permute-start(f32[2,96,512]{2,1,0:T(8,128)S(1)} %pad_maximum_fusion.2), channel_id=1, source_target_pairs={{0,2},{2,4},{4,6},{6,8},{8,10},{10,12},{12,14},{14,16},{16,18},{18... | collective-permute-start | bytes 1179656 | tf_op jit(solution)/shard_map/ppermute | solution.py:14
  39.9 0.1 fusion.76
  40.0 1.2 %collective-permute-done.2 = f32[2,96,512]{2,1,0:T(8,128)S(1)} collective-permute-done((f32[2,96,512]{2,1,0:T(8,128)S(1)}, f32[2,96,512]{2,1,0:T(8,128)S(1)}, u32[]{:S(2)}, u32[]{:S(2)}) %collective-permute-start.2) | collective-permute-done | bytes 393248 | tf_op jit(solution)/shard_map/ppermute | solution.py:14
  41.2 0.1 fusion.47
  41.4 0.7 fusion.17
  42.1 0.7 fusion.27
  42.9 0.8 fusion.3
  43.7 8.0 %collective-permute-start.3 = (f32[2,96,512]{2,1,0:T(8,128)S(1)}, f32[2,96,512]{2,1,0:T(8,128)S(1)}, u32[]{:S(2)}, u32[]{:S(2)}) collective-permute-start(f32[2,96,512]{2,1,0:T(8,128)S(1)} %pad_maximum_fusion.3), channel_id=1, source_target_pairs={{0,2},{2,4},{4,6},{6,8},{8,10},{10,12},{12,14},{14,16},{16,18},{18... | collective-permute-start | bytes 1179656 | tf_op jit(solution)/shard_map/ppermute | solution.py:14
  51.6 0.1 fusion.75
  51.7 1.0 %collective-permute-done.3 = f32[2,96,512]{2,1,0:T(8,128)S(1)} collective-permute-done((f32[2,96,512]{2,1,0:T(8,128)S(1)}, f32[2,96,512]{2,1,0:T(8,128)S(1)}, u32[]{:S(2)}, u32[]{:S(2)}) %collective-permute-start.3) | collective-permute-done | bytes 393248 | tf_op jit(solution)/shard_map/ppermute | solution.py:14
  52.8 0.1 fusion.45
  52.9 0.7 fusion.15
  53.6 0.0 copy-start.2
  53.7 0.7 fusion.25
  54.4 0.8 fusion.1
  55.2 0.0 copy-done.2
  55.2 0.6 fusion.52
  55.8 0.8 copy.8
  56.7 0.0 reduce-scatter.4.cloned.1.call-update
  56.7 0.8 maximum_bitcast_fusion
  57.5 21.7 %reduce-scatter.4.cloned.1.call-done = f32[256,1]{1,0:T(8,128)} async-done(((f32[512,1]{1,0:T(8,128)}), f32[256,1]{1,0:T(8,128)}) %reduce-scatter.4.cloned.1.call-update) | async-done | bytes 1040
  79.1 1.5 %copy.9 = f32[1,256]{1,0:T(1,128)} copy(f32[1,256]{0,1:T(8,128)} %bitcast.151) | data formatting | bytes 2048
  (9 shorter events, 0.2 us)
Async XLA Ops:
  7.2 3.4 %copy-start = (f32[1,1,2,512,512]{4,3,2,1,0:T(8,128)S(1)}, f32[1,1,2,512,512]{4,3,2,1,0:T(8,128)}, u32[]{:S(2)}) copy-start(f32[1,1,2,512,512]{4,3,2,1,0:T(8,128)} %param.6) | copy-start | bytes 6291460
  7.2 72.0 %reduce-scatter.4.cloned.1.call-start = ((), (), s32[]{:S(2)}) async-start(), calls=%async_computation.1 | async-start | bytes 393216
  11.5 4.0 %copy-start.6 = (s32[4,96]{1,0:T(4,128)S(1)}, s32[4,96]{1,0:T(4,128)}, u32[]{:S(2)}) copy-start(s32[4,96]{1,0:T(4,128)} %param.10) | copy-start | bytes 4612
  11.5 4.6 %copy-start.4 = (f32[1,4,2]{1,2,0:T(2,128)S(1)}, f32[1,4,2]{1,2,0:T(2,128)}, u32[]{:S(2)}) copy-start(f32[1,4,2]{1,2,0:T(2,128)} %param.11) | copy-start | bytes 100
  11.5 5.5 %copy-start.3 = (f32[1,512]{1,0:T(1,128)S(1)}, f32[1,512]{1,0:T(1,128)}, u32[]{:S(2)}) copy-start(f32[1,512]{1,0:T(1,128)} %param.7) | copy-start | bytes 6148
  13.1 4.0 %collective-permute-start = (f32[2,96,512]{2,1,0:T(8,128)}, f32[2,96,512]{2,1,0:T(8,128)S(1)}, u32[]{:S(2)}, u32[]{:S(2)}) collective-permute-start(f32[2,96,512]{2,1,0:T(8,128)} %pad_maximum_fusion), channel_id=1, source_target_pairs={{0,2},{2,4},{4,6},{6,8},{8,10},{10,12},{12,14},{14,16},{16,18},{18... | collective-permute-start | bytes 1179656 | tf_op jit(solution)/shard_map/ppermute | solution.py:14
  18.9 9.6 %copy-start.5 = (s32[96]{0:T(128)S(1)}, s32[96]{0:T(128)}, u32[]{:S(2)}) copy-start(s32[96]{0:T(128)} %get-tuple-element.14) | copy-start | bytes 1156
  18.9 10.9 %copy-start.1 = (f32[1,1,5,2,96,512]{5,4,3,2,1,0:T(8,128)S(1)}, f32[1,1,5,2,96,512]{5,4,3,2,1,0:T(8,128)}, u32[]{:S(2)}) copy-start(f32[1,1,5,2,96,512]{5,4,3,2,1,0:T(8,128)} %param.8) | copy-start | bytes 5898244
  20.5 9.3 %collective-permute-start.1 = (f32[2,96,512]{2,1,0:T(8,128)S(1)}, f32[2,96,512]{2,1,0:T(8,128)S(1)}, u32[]{:S(2)}, u32[]{:S(2)}) collective-permute-start(f32[2,96,512]{2,1,0:T(8,128)S(1)} %pad_maximum_fusion.1), channel_id=1, source_target_pairs={{0,2},{2,4},{4,6},{6,8},{8,10},{10,12},{12,14},{14,16},{16,18},{18... | collective-permute-start | bytes 1179656 | tf_op jit(solution)/shard_map/ppermute | solution.py:14
  32.2 9.0 %collective-permute-start.2 = (f32[2,96,512]{2,1,0:T(8,128)S(1)}, f32[2,96,512]{2,1,0:T(8,128)S(1)}, u32[]{:S(2)}, u32[]{:S(2)}) collective-permute-start(f32[2,96,512]{2,1,0:T(8,128)S(1)} %pad_maximum_fusion.2), channel_id=1, source_target_pairs={{0,2},{2,4},{4,6},{6,8},{8,10},{10,12},{12,14},{14,16},{16,18},{18... | collective-permute-start | bytes 1179656 | tf_op jit(solution)/shard_map/ppermute | solution.py:14
  43.7 9.1 %collective-permute-start.3 = (f32[2,96,512]{2,1,0:T(8,128)S(1)}, f32[2,96,512]{2,1,0:T(8,128)S(1)}, u32[]{:S(2)}, u32[]{:S(2)}) collective-permute-start(f32[2,96,512]{2,1,0:T(8,128)S(1)} %pad_maximum_fusion.3), channel_id=1, source_target_pairs={{0,2},{2,4},{4,6},{6,8},{8,10},{10,12},{12,14},{14,16},{16,18},{18... | collective-permute-start | bytes 1179656 | tf_op jit(solution)/shard_map/ppermute | solution.py:14
  53.6 1.5 %copy-start.2 = (f32[1,1,2,96,512]{4,3,2,1,0:T(8,128)S(1)}, f32[1,1,2,96,512]{4,3,2,1,0:T(8,128)}, u32[]{:S(2)}) copy-start(f32[1,1,2,96,512]{4,3,2,1,0:T(8,128)} %param.9) | copy-start | bytes 1179652
Sparse Core Ops, SparseCore 0:
  56.8 22.2 reduce-scatter.3
where the time goes:
time: 87.8 us; the launch traced here: 87.5 us
  starting transfers between devices  26 us (30%)
  waiting for transfers between devices  25.1 us (29%)
  between operations  14.3 us (16%)
  matrix products  12.4 us (14%)
  other arithmetic  6.46 us (7%)
  local copies, waits for them, and re-layouts  3.25 us (4%)
    ppermute x4, starting transfers between devices, from_behind(): return lax.ppermute(block, axis, route)  26 us
    unnamed x2, waiting for transfers between devices  21.7 us
    dot_general x15, matrix products, matmul_high(): jnp.dot(left, right, precision=lax.Precision.HIGHEST, preferred_element_t...  12.4 us
    ppermute x4, waiting for transfers between devices, from_behind(): return lax.ppermute(block, axis, route)  3.47 us
    add x5, other arithmetic, local(): mixed = present_shot_matrix + reflect[None, None, :] * wave_now  2.85 us
    unnamed x16, local copies, waits for them, and re-layouts  2.44 us
  transfers between devices with their start and end apart: 5, of which 4 were waited for; matrix products, arithmetic and copies ran while one was open for 3% of the time, Pallas kernels for 0%

commit v1 on v0

v1 whole, which is shorter than its diff:
```python
import math

import jax
import jax.numpy as jnp
from jax import lax
from jax.sharding import PartitionSpec as P

TICKS = 5


def product(left, right):
    return jnp.dot(left, right, precision=lax.Precision.HIGH, preferred_element_type=jnp.float32)


def after(value, *earlier):
    return lax.optimization_barrier((value,) + earlier)[0]


def sum_over(vector, axis):
    count = lax.axis_size(axis)
    me = lax.axis_index(axis)
    chunks = vector.reshape(count, -1)
    total = lax.dynamic_index_in_dim(chunks, me, 0, keepdims=True)
    for distance in range(1, count):
        chunk = lax.dynamic_index_in_dim(chunks, (me + distance) % count, 0, keepdims=True)
        route = [(i, (i + distance) % count) for i in range(count)]
        total = total + lax.ppermute(chunk, axis, route)
    return total


def local(
    extrapolation_operator,
    impedance_contrast,
    ascending_residual,
    arriving_downward_matrices,
    shot_node_indices,
    emitted_pulse,
):
    prop_real = extrapolation_operator[0, 0, 0]
    prop_imag = extrapolation_operator[0, 0, 1]
    prop_both = prop_real + prop_imag
    reflect = impedance_contrast[0]
    shots, breadth = arriving_downward_matrices.shape[3:]
    residual = ascending_residual[0, 0]
    levels = lax.axis_size("depth")
    at_surface = lax.axis_index("depth") == 0
    columns = jnp.arange(breadth, dtype=jnp.int32)
    fast_route = [(i, i + 1) for i in range(0, levels - 1, 2)]
    slow_route = [(i, i + 1) for i in range(1, levels - 1, 2)]
    terms = []

    def injected(tick):
        hits = (columns[None, :] == shot_node_indices[tick - 1][:, None]).astype(jnp.float32)
        return emitted_pulse[0, tick - 1][:, None, None] * hits[None]

    def work(arriving, tick):
        wave = residual[tick]
        terms.append(jnp.sum(arriving * wave, axis=(0, 1)))
        mixed = arriving + reflect[None, None, :] * wave
        first = product(mixed[0], prop_real)
        second = product(mixed[1], prop_imag)
        third = product(mixed[0] + mixed[1], prop_both)
        return jnp.stack([first - second, third - first - second], 0)

    def fast(panel):
        return lax.ppermute(panel, "depth", fast_route)

    def slow(panel, tick):
        got = lax.ppermute(panel, "depth", slow_route)
        return jnp.where(at_surface, injected(tick), got)

    out0 = work(arriving_downward_matrices[0, 0], 0)
    f0 = fast(out0)
    s0 = slow(out0, 1)
    odd1 = work(f0, 1)
    s1 = slow(odd1, 2)
    even1 = work(after(s0, odd1), 1)
    f1 = fast(even1)
    odd2 = work(f1, 2)
    s2 = slow(odd2, 3)
    even2 = work(after(s1, odd2), 2)
    f2 = fast(even2)
    odd3 = work(f2, 3)
    s3 = slow(odd3, 4)
    even3 = work(after(s2, odd3), 3)
    f3 = fast(even3)
    out4 = work(s3 + f3, 4)

    scale = 1.0 / math.sqrt(shots * TICKS)
    gradient = sum(terms[1:], terms[0]) * scale
    return (out4[None, None], sum_over(gradient, "freq"))


def solution(mesh):
    placed = (
        P("freq", "depth", None, None, None),
        P("depth", None),
        P("freq", "depth", None, None, None, None),
        P("freq", "depth", None, None, None),
        P(),
        P("freq", None, None),
    )
    return jax.shard_map(
        local,
        mesh=mesh,
        in_specs=placed,
        out_specs=(P("freq", "depth", None, None, None), P("depth", "freq")),
        check_vma=False,
    )
```

time: 87.8 us -> 65.6 us (0.75)
  the two profiles are of different devices: /device:TPU:0 before, /device:TPU:24 now
where the time goes in v1:
time: 65.6 us; the launch traced here: 65.2 us
  waiting for transfers between devices  25.3 us (39%)
  starting transfers between devices  14.1 us (21%)
  other arithmetic  11.7 us (18%)
  matrix products  11.7 us (18%)
  local copies, waits for them, and re-layouts  1.38 us (2%)
  between operations  1.09 us (2%)
    ppermute x4, waiting for transfers between devices, slow(): got = lax.ppermute(panel, 'depth', slow_route)  22.7 us
    dot_general x24, matrix products, product(): jnp.dot(left, right, precision=lax.Precision.HIGH, preferred_element_type...  11.7 us
    ppermute x4, starting transfers between devices, fast(): return lax.ppermute(panel, 'depth', fast_route)  7.41 us
    ppermute x4, starting transfers between devices, slow(): got = lax.ppermute(panel, 'depth', slow_route)  5.16 us
    add x6, other arithmetic, work(): mixed = arriving + reflect[None, None, :] * wave  2.69 us
    reduce_sum x2, other arithmetic, work(): terms.append(jnp.sum(arriving * wave, axis=(0, 1)))  2.58 us
    another operation x15, other arithmetic, work(): return jnp.stack([first - second, third - first - second], 0)  1.92 us
    convert_element_type x4, other arithmetic, injected(): (columns[None, :] == shot_node_indices[tick - 1][:, None]).astype(jnp.flo...  1.64 us
  transfers between devices with their start and end apart: 9, of which 6 were waited for; matrix products, arithmetic and copies ran while one was open for 12% of the time, Pallas kernels for 0%

profile of v1, /device:TPU:24, one launch (start us, length us, event | category | flops | bytes accessed | tf_op | source)
XLA Modules:
  0.0 65.2 jit_solution(10072616176353030803)
XLA Ops:
  0.6 1.3 %fusion.80 = f32[2,96,512]{2,1,0:T(8,128)S(1)} fusion(f32[1,1,2,96,512]{4,3,2,1,0:T(8,128)} %param.9, f32[1,1,5,2,96,512]{5,4,3,2,1,0:T(8,128)} %param.8, f32[512]{0:T(512)} %bitcast.219), kind=kLoop, calls=%fused_computation.110 | loop fusion | flops 196608 | bytes 1181696 | tf_op jit(solution)/shard_map/add | solution.py:59
  2.0 1.7 %fusion.38 = f32[96,512]{1,0:T(8,128)S(1)} fusion(f32[1,1,2,512,512]{4,3,2,1,0:T(8,128)} %param.6, f32[2,96,512]{2,1,0:T(8,128)S(1)} %fusion.80), kind=kOutput, calls=%fused_computation.46 | convolution fusion | flops 150994944 | bytes 1441792 | tf_op jit(solution)/shard_map/dot_general | solution.py:12
  3.6 0.4 fusion.54
  4.1 0.2 slice_add_fusion
  4.3 0.0 copy-start.4
  4.3 0.0 copy-start.3
  4.4 0.4 fusion.15
  4.8 0.8 %pad_maximum_fusion = f32[2,96,512]{2,1,0:T(8,128)} fusion(f32[1,96,512]{2,1,0:T(8,128)S(1)} %fusion.15, f32[1,96,512]{2,1,0:T(8,128)S(1)} %subtract_bitcast_fusion.7), kind=kLoop, calls=%fused_computation.81 | loop fusion | flops 98304 | bytes 786432 | tf_op jit(solution)/shard_map/stack | solution.py:63
  5.6 1.8 %collective-permute-start = (f32[2,96,512]{2,1,0:T(8,128)}, f32[2,96,512]{2,1,0:T(8,128)S(1)}, u32[]{:S(2)}, u32[]{:S(2)}) collective-permute-start(f32[2,96,512]{2,1,0:T(8,128)} %pad_maximum_fusion), channel_id=1, source_target_pairs={{0,2},{4,6},{8,10},{12,14},{16,18},{20,22},{24,26},{28,30},{1,3},{... | collective-permute-start | bytes 1179656 | tf_op jit(solution)/shard_map/ppermute | solution.py:66
  7.3 1.3 %collective-permute-start.2 = (f32[2,96,512]{2,1,0:T(8,128)}, f32[2,96,512]{2,1,0:T(8,128)}, u32[]{:S(2)}, u32[]{:S(2)}) collective-permute-start(f32[2,96,512]{2,1,0:T(8,128)} %pad_maximum_fusion), channel_id=1, source_target_pairs={{2,4},{6,8},{10,12},{14,16},{18,20},{22,24},{26,28},{3,5},{7,9},{1... | collective-permute-start | bytes 1179656 | tf_op jit(solution)/shard_map/ppermute | solution.py:69
  8.7 0.6 slice_bitcast_fusion.3
  9.2 0.7 %slice_reduce_fusion.3 = (f32[2]{0:T(128)}, f32[2]{0:T(128)S(1)}, f32[2]{0:T(128)S(1)}, f32[2]{0:T(128)S(1)}) fusion(f32[1,4,2]{1,2,0:T(2,128)S(1)} %copy-done.4), kind=kLoop, calls=%fused_computation.207 | loop fusion | bytes 64 | tf_op jit(solution)/shard_map/slice | solution.py:54
  10.0 0.7 %fusion.122 = f32[96,512]{1,0:T(8,128)S(1)} fusion(s32[96]{0:T(128)} %get-tuple-element.25), kind=kLoop, calls=%fused_computation.168 | loop fusion | flops 98304 | bytes 196992 | tf_op jit(solution)/shard_map/convert_element_type | solution.py:53
  10.7 1.1 %fusion.83 = f32[2,96,512]{2,1,0:T(8,128)S(1)} fusion(f32[2,96,512]{2,1,0:T(8,128)S(1)} %collective-permute-done, f32[1,1,5,2,96,512]{5,4,3,2,1,0:T(8,128)} %param.8, f32[512]{0:T(512)S(1)} %bitcast.220), kind=kLoop, calls=%fused_computation.117 | loop fusion | flops 196608 | bytes 1181696 | tf_op jit(solution)/shard_map/add | solution.py:59
  11.8 0.4 fusion.36
  12.2 0.4 fusion.52
  12.7 0.0 copy-start.1
  12.7 0.4 fusion.13
  13.2 4.4 %collective-permute-done.2 = f32[2,96,512]{2,1,0:T(8,128)} collective-permute-done((f32[2,96,512]{2,1,0:T(8,128)}, f32[2,96,512]{2,1,0:T(8,128)}, u32[]{:S(2)}, u32[]{:S(2)}) %collective-permute-start.2) | collective-permute-done | bytes 393248 | tf_op jit(solution)/shard_map/ppermute | solution.py:69
  17.7 1.1 %multiply_select_fusion.1 = f32[2,96,512]{2,1,0:T(8,128)S(1)} fusion(f32[2,96,512]{2,1,0:T(8,128)} %collective-permute-done.2, f32[96,512]{1,0:T(8,128)S(1)} %fusion.122, f32[2]{0:T(128)S(1)} %get-tuple-element.18, pred[]{:T(512)S(6)} %eq.81), kind=kLoop, calls=%fused_computation.114 | loop fusion | flops 196608 | bytes 983049 | tf_op jit(solution)/shard_map/jit(_where)/select_n | solution.py:70
  18.8 0.1 fusion.82
  18.9 0.4 fusion.34
  19.3 0.4 fusion.50
  19.8 0.4 fusion.11
  20.2 1.3 %collective-permute-start.3 = (f32[2,96,512]{2,1,0:T(8,128)S(1)}, f32[2,96,512]{2,1,0:T(8,128)S(1)}, u32[]{:S(2)}, u32[]{:S(2)}) collective-permute-start(f32[2,96,512]{2,1,0:T(8,128)S(1)} %pad_maximum_fusion.2), channel_id=1, source_target_pairs={{0,2},{4,6},{8,10},{12,14},{16,18},{20,22},{24,26},{28,30},{1,3},{... | collective-permute-start | bytes 1179656 | tf_op jit(solution)/shard_map/ppermute | solution.py:66
  21.6 1.3 %collective-permute-start.1 = (f32[2,96,512]{2,1,0:T(8,128)S(1)}, f32[2,96,512]{2,1,0:T(8,128)S(1)}, u32[]{:S(2)}, u32[]{:S(2)}) collective-permute-start(f32[2,96,512]{2,1,0:T(8,128)S(1)} %pad_maximum_fusion.1), channel_id=1, source_target_pairs={{2,4},{6,8},{10,12},{14,16},{18,20},{22,24},{26,28},{3,5},{7,9},{1... | collective-permute-start | bytes 1179656 | tf_op jit(solution)/shard_map/ppermute | solution.py:69
  22.9 0.0 collective-permute-done.3
  22.9 0.1 fusion.85
  23.0 0.4 fusion.32
  23.4 0.4 fusion.48
  23.9 0.4 fusion.9
  24.3 1.3 %collective-permute-start.6 = (f32[2,96,512]{2,1,0:T(8,128)S(1)}, f32[2,96,512]{2,1,0:T(8,128)S(1)}, u32[]{:S(2)}, u32[]{:S(2)}) collective-permute-start(f32[2,96,512]{2,1,0:T(8,128)S(1)} %pad_maximum_fusion.3), channel_id=1, source_target_pairs={{2,4},{6,8},{10,12},{14,16},{18,20},{22,24},{26,28},{3,5},{7,9},{1... | collective-permute-start | bytes 1179656 | tf_op jit(solution)/shard_map/ppermute | solution.py:69
  25.6 0.1 fusion.121
  25.7 0.1 fusion.123
  25.8 5.8 %collective-permute-done.1 = f32[2,96,512]{2,1,0:T(8,128)S(1)} collective-permute-done((f32[2,96,512]{2,1,0:T(8,128)S(1)}, f32[2,96,512]{2,1,0:T(8,128)S(1)}, u32[]{:S(2)}, u32[]{:S(2)}) %collective-permute-start.1) | collective-permute-done | bytes 393248 | tf_op jit(solution)/shard_map/ppermute | solution.py:69
  31.6 4.2 %collective-permute-done.6 = f32[2,96,512]{2,1,0:T(8,128)S(1)} collective-permute-done((f32[2,96,512]{2,1,0:T(8,128)S(1)}, f32[2,96,512]{2,1,0:T(8,128)S(1)}, u32[]{:S(2)}, u32[]{:S(2)}) %collective-permute-start.6) | collective-permute-done | bytes 393248 | tf_op jit(solution)/shard_map/ppermute | solution.py:69
  35.8 0.2 multiply_select_fusion
  36.0 0.1 fusion.84
  36.0 0.4 fusion.30
  36.5 0.4 fusion.46
  36.9 0.4 fusion.7
  37.4 1.3 %collective-permute-start.4 = (f32[2,96,512]{2,1,0:T(8,128)S(1)}, f32[2,96,512]{2,1,0:T(8,128)S(1)}, u32[]{:S(2)}, u32[]{:S(2)}) collective-permute-start(f32[2,96,512]{2,1,0:T(8,128)S(1)} %pad_maximum_fusion.4), channel_id=1, source_target_pairs={{0,2},{4,6},{8,10},{12,14},{16,18},{20,22},{24,26},{28,30},{1,3},{... | collective-permute-start | bytes 1179656 | tf_op jit(solution)/shard_map/ppermute | solution.py:66
  38.7 1.3 %collective-permute-done.4 = f32[2,96,512]{2,1,0:T(8,128)S(1)} collective-permute-done((f32[2,96,512]{2,1,0:T(8,128)S(1)}, f32[2,96,512]{2,1,0:T(8,128)S(1)}, u32[]{:S(2)}, u32[]{:S(2)}) %collective-permute-start.4) | collective-permute-done | bytes 393248 | tf_op jit(solution)/shard_map/ppermute | solution.py:66
  40.0 0.1 fusion.87
  40.1 0.4 fusion.28
  40.6 0.4 fusion.44
  41.0 0.4 fusion.5
  41.5 0.8 %pad_maximum_fusion.5 = f32[2,96,512]{2,1,0:T(8,128)} fusion(f32[1,96,512]{2,1,0:T(8,128)S(1)} %fusion.5, f32[1,96,512]{2,1,0:T(8,128)S(1)} %subtract_bitcast_fusion.2), kind=kLoop, calls=%fused_computation.86 | loop fusion | flops 98304 | bytes 786432 | tf_op jit(solution)/shard_map/stack | solution.py:63
  42.3 1.1 %fusion.78 = (f32[512]{0:T(512)S(1)}, f32[512]{0:T(512)S(1)}, f32[512]{0:T(512)S(1)}, f32[512]{0:T(512)}, f32[512]{0:T(512)}, /*index=5*/f32[512]{0:T(512)}, f32[512]{0:T(512)}, f32[2,96,512]{2,1,0:T(8,128)S(1)}) fusion(f32[2,96,512]{2,1,0:T(8,128)S(1)} %collective-permute-done, f32[1,1,5,2,96,512]{5,4,3,2,1,0:T(8,128)S(1)} %copy-done.1, ...), kind=kLoop, calls=%fused_computation.106 | loop fusion | flops 1569280 | bytes 4734976 | tf_op jit(solution)/shard_map/reduce_sum | solution.py:58
  43.4 0.4 fusion.26
  43.8 0.4 fusion.42
  44.3 0.4 fusion.3
  44.8 3.0 %collective-permute-start.7 = (f32[2,96,512]{2,1,0:T(8,128)S(1)}, f32[2,96,512]{2,1,0:T(8,128)}, u32[]{:S(2)}, u32[]{:S(2)}) collective-permute-start(f32[2,96,512]{2,1,0:T(8,128)S(1)} %pad_maximum_fusion.6), channel_id=1, source_target_pairs={{0,2},{4,6},{8,10},{12,14},{16,18},{20,22},{24,26},{28,30},{1,3},{... | collective-permute-start | bytes 1179656 | tf_op jit(solution)/shard_map/ppermute | solution.py:66
  47.8 1.3 %collective-permute-start.5 = (f32[2,96,512]{2,1,0:T(8,128)}, f32[2,96,512]{2,1,0:T(8,128)}, u32[]{:S(2)}, u32[]{:S(2)}) collective-permute-start(f32[2,96,512]{2,1,0:T(8,128)} %pad_maximum_fusion.5), channel_id=1, source_target_pairs={{2,4},{6,8},{10,12},{14,16},{18,20},{22,24},{26,28},{3,5},{7,9},{1... | collective-permute-start | bytes 1179656 | tf_op jit(solution)/shard_map/ppermute | solution.py:69
  49.1 0.7 %fusion.120 = f32[96,512]{1,0:T(8,128)S(1)} fusion(s32[96]{0:T(128)} %get-tuple-element.22), kind=kLoop, calls=%fused_computation.166 | loop fusion | flops 98304 | bytes 196992 | tf_op jit(solution)/shard_map/convert_element_type | solution.py:53
  49.9 8.2 %collective-permute-done.5 = f32[2,96,512]{2,1,0:T(8,128)} collective-permute-done((f32[2,96,512]{2,1,0:T(8,128)}, f32[2,96,512]{2,1,0:T(8,128)}, u32[]{:S(2)}, u32[]{:S(2)}) %collective-permute-start.5) | collective-permute-done | bytes 393248 | tf_op jit(solution)/shard_map/ppermute | solution.py:69
  58.1 1.4 %fusion.73 = (f32[512]{0:T(512)S(1)}, f32[2,96,512]{2,1,0:T(8,128)S(1)}) fusion(f32[1,1,5,2,96,512]{5,4,3,2,1,0:T(8,128)} %param.8, f32[2,96,512]{2,1,0:T(8,128)} %collective-permute-done.7, f32[2,96,512]{2,1,0:T(8,128)} %collective-permute-done.5, f32[96,512]{1,0:T(8,128)S(1)} %fusion.120, f32[2]{0:T(128)} %get-tuple-element.15, pred[]{:T(512)S(6)} %eq.81, ...), kind=kLoop, calls=%fused_computation.92 | loop fusion | flops 687616 | bytes 1773577 | tf_op jit(solution)/shard_map/reduce_sum | solution.py:58
  59.5 0.4 fusion.24
  60.0 0.4 fusion.40
  60.5 0.4 fusion.1
  61.0 1.6 %collective-permute-start.8 = (f32[1,256]{1,0:T(1,128)S(1)}, f32[1,256]{1,0:T(1,128)S(1)}, u32[]{:S(2)}, u32[]{:S(2)}) collective-permute-start(f32[1,256]{1,0:T(1,128)S(1)} %constant_dynamic-slice_fusion), channel_id=1, source_target_pairs={{0,1},{1,0},{2,3},{3,2},{4,5},{5,4},{6,7},{7,6},{8,9},{9,8},{10,11... | collective-permute-start | bytes 3080 | tf_op jit(solution)/shard_map/ppermute | solution.py:27
  62.6 0.8 %maximum_bitcast_fusion = f32[1,1,2,96,512]{4,3,2,1,0:T(8,128)} fusion(f32[1,96,512]{2,1,0:T(8,128)S(1)} %fusion.1, f32[1,96,512]{2,1,0:T(8,128)S(1)} %subtract_bitcast_fusion), kind=kLoop, calls=%fused_computation.88 | loop fusion | flops 98304 | bytes 786432 | tf_op jit(solution)/shard_map/broadcast_in_dim | solution.py:91
  63.3 1.3 %collective-permute-done.8 = f32[1,256]{1,0:T(1,128)S(1)} collective-permute-done((f32[1,256]{1,0:T(1,128)S(1)}, f32[1,256]{1,0:T(1,128)S(1)}, u32[]{:S(2)}, u32[]{:S(2)}) %collective-permute-start.8) | collective-permute-done | bytes 1056 | tf_op jit(solution)/shard_map/ppermute | solution.py:27
  64.7 0.6 dynamic-slice_add_fusion
  (35 shorter events, 0.5 us)
Async XLA Ops:
  0.6 3.0 %copy-start = (f32[1,1,2,512,512]{4,3,2,1,0:T(8,128)S(1)}, f32[1,1,2,512,512]{4,3,2,1,0:T(8,128)}, u32[]{:S(2)}) copy-start(f32[1,1,2,512,512]{4,3,2,1,0:T(8,128)} %param.6) | copy-start | bytes 6291460
  4.3 4.4 %copy-start.9 = (s32[4,96]{1,0:T(4,128)S(1)}, s32[4,96]{1,0:T(4,128)}, u32[]{:S(2)}) copy-start(s32[4,96]{1,0:T(4,128)} %param.10) | copy-start | bytes 4612
  4.3 4.9 %copy-start.4 = (f32[1,4,2]{1,2,0:T(2,128)S(1)}, f32[1,4,2]{1,2,0:T(2,128)}, u32[]{:S(2)}) copy-start(f32[1,4,2]{1,2,0:T(2,128)} %param.11) | copy-start | bytes 100
  4.3 6.4 %copy-start.3 = (f32[1,512]{1,0:T(1,128)S(1)}, f32[1,512]{1,0:T(1,128)}, u32[]{:S(2)}) copy-start(f32[1,512]{1,0:T(1,128)} %param.7) | copy-start | bytes 6148
  5.6 5.1 %collective-permute-start = (f32[2,96,512]{2,1,0:T(8,128)}, f32[2,96,512]{2,1,0:T(8,128)S(1)}, u32[]{:S(2)}, u32[]{:S(2)}) collective-permute-start(f32[2,96,512]{2,1,0:T(8,128)} %pad_maximum_fusion), channel_id=1, source_target_pairs={{0,2},{4,6},{8,10},{12,14},{16,18},{20,22},{24,26},{28,30},{1,3},{... | collective-permute-start | bytes 1179656 | tf_op jit(solution)/shard_map/ppermute | solution.py:66
  7.3 10.3 %collective-permute-start.2 = (f32[2,96,512]{2,1,0:T(8,128)}, f32[2,96,512]{2,1,0:T(8,128)}, u32[]{:S(2)}, u32[]{:S(2)}) collective-permute-start(f32[2,96,512]{2,1,0:T(8,128)} %pad_maximum_fusion), channel_id=1, source_target_pairs={{2,4},{6,8},{10,12},{14,16},{18,20},{22,24},{26,28},{3,5},{7,9},{1... | collective-permute-start | bytes 1179656 | tf_op jit(solution)/shard_map/ppermute | solution.py:69
  12.7 6.1 %copy-start.1 = (f32[1,1,5,2,96,512]{5,4,3,2,1,0:T(8,128)S(1)}, f32[1,1,5,2,96,512]{5,4,3,2,1,0:T(8,128)}, u32[]{:S(2)}) copy-start(f32[1,1,5,2,96,512]{5,4,3,2,1,0:T(8,128)} %param.8) | copy-start | bytes 5898244
  20.2 2.6 %collective-permute-start.3 = (f32[2,96,512]{2,1,0:T(8,128)S(1)}, f32[2,96,512]{2,1,0:T(8,128)S(1)}, u32[]{:S(2)}, u32[]{:S(2)}) collective-permute-start(f32[2,96,512]{2,1,0:T(8,128)S(1)} %pad_maximum_fusion.2), channel_id=1, source_target_pairs={{0,2},{4,6},{8,10},{12,14},{16,18},{20,22},{24,26},{28,30},{1,3},{... | collective-permute-start | bytes 1179656 | tf_op jit(solution)/shard_map/ppermute | solution.py:66
  21.6 10.0 %collective-permute-start.1 = (f32[2,96,512]{2,1,0:T(8,128)S(1)}, f32[2,96,512]{2,1,0:T(8,128)S(1)}, u32[]{:S(2)}, u32[]{:S(2)}) collective-permute-start(f32[2,96,512]{2,1,0:T(8,128)S(1)} %pad_maximum_fusion.1), channel_id=1, source_target_pairs={{2,4},{6,8},{10,12},{14,16},{18,20},{22,24},{26,28},{3,5},{7,9},{1... | collective-permute-start | bytes 1179656 | tf_op jit(solution)/shard_map/ppermute | solution.py:69
  24.3 11.4 %collective-permute-start.6 = (f32[2,96,512]{2,1,0:T(8,128)S(1)}, f32[2,96,512]{2,1,0:T(8,128)S(1)}, u32[]{:S(2)}, u32[]{:S(2)}) collective-permute-start(f32[2,96,512]{2,1,0:T(8,128)S(1)} %pad_maximum_fusion.3), channel_id=1, source_target_pairs={{2,4},{6,8},{10,12},{14,16},{18,20},{22,24},{26,28},{3,5},{7,9},{1... | collective-permute-start | bytes 1179656 | tf_op jit(solution)/shard_map/ppermute | solution.py:69
  37.4 2.6 %collective-permute-start.4 = (f32[2,96,512]{2,1,0:T(8,128)S(1)}, f32[2,96,512]{2,1,0:T(8,128)S(1)}, u32[]{:S(2)}, u32[]{:S(2)}) collective-permute-start(f32[2,96,512]{2,1,0:T(8,128)S(1)} %pad_maximum_fusion.4), channel_id=1, source_target_pairs={{0,2},{4,6},{8,10},{12,14},{16,18},{20,22},{24,26},{28,30},{1,3},{... | collective-permute-start | bytes 1179656 | tf_op jit(solution)/shard_map/ppermute | solution.py:66
  40.5 1.7 %copy-start.2 = (f32[1,1,2,96,512]{4,3,2,1,0:T(8,128)S(1)}, f32[1,1,2,96,512]{4,3,2,1,0:T(8,128)}, u32[]{:S(2)}) copy-start(f32[1,1,2,96,512]{4,3,2,1,0:T(8,128)} %param.9) | copy-start | bytes 1179652
  44.8 5.1 %collective-permute-start.7 = (f32[2,96,512]{2,1,0:T(8,128)S(1)}, f32[2,96,512]{2,1,0:T(8,128)}, u32[]{:S(2)}, u32[]{:S(2)}) collective-permute-start(f32[2,96,512]{2,1,0:T(8,128)S(1)} %pad_maximum_fusion.6), channel_id=1, source_target_pairs={{0,2},{4,6},{8,10},{12,14},{16,18},{20,22},{24,26},{28,30},{1,3},{... | collective-permute-start | bytes 1179656 | tf_op jit(solution)/shard_map/ppermute | solution.py:66
  47.8 10.3 %collective-permute-start.5 = (f32[2,96,512]{2,1,0:T(8,128)}, f32[2,96,512]{2,1,0:T(8,128)}, u32[]{:S(2)}, u32[]{:S(2)}) collective-permute-start(f32[2,96,512]{2,1,0:T(8,128)} %pad_maximum_fusion.5), channel_id=1, source_target_pairs={{2,4},{6,8},{10,12},{14,16},{18,20},{22,24},{26,28},{3,5},{7,9},{1... | collective-permute-start | bytes 1179656 | tf_op jit(solution)/shard_map/ppermute | solution.py:69
  60.0 1.0 %copy-start.5 = (f32[512]{0:T(512)S(1)}, f32[512]{0:T(512)}, u32[]{:S(2)}) copy-start(f32[512]{0:T(512)} %get-tuple-element.11) | copy-start | bytes 6148
  60.0 1.0 %copy-start.6 = (f32[512]{0:T(512)S(1)}, f32[512]{0:T(512)}, u32[]{:S(2)}) copy-start(f32[512]{0:T(512)} %get-tuple-element.12) | copy-start | bytes 6148
  60.0 1.0 %copy-start.7 = (f32[512]{0:T(512)S(1)}, f32[512]{0:T(512)}, u32[]{:S(2)}) copy-start(f32[512]{0:T(512)} %get-tuple-element.13) | copy-start | bytes 6148
  60.0 1.0 %copy-start.8 = (f32[512]{0:T(512)S(1)}, f32[512]{0:T(512)}, u32[]{:S(2)}) copy-start(f32[512]{0:T(512)} %get-tuple-element.14) | copy-start | bytes 6148
  61.0 3.6 %collective-permute-start.8 = (f32[1,256]{1,0:T(1,128)S(1)}, f32[1,256]{1,0:T(1,128)S(1)}, u32[]{:S(2)}, u32[]{:S(2)}) collective-permute-start(f32[1,256]{1,0:T(1,128)S(1)} %constant_dynamic-slice_fusion), channel_id=1, source_target_pairs={{0,1},{1,0},{2,3},{3,2},{4,5},{5,4},{6,7},{7,6},{8,9},{9,8},{10,11... | collective-permute-start | bytes 3080 | tf_op jit(solution)/shard_map/ppermute | solution.py:27

commit v2 on v1

--- a/solution.py
+++ b/solution.py
@@ -45,8 +45,9 @@
     levels = lax.axis_size("depth")
     at_surface = lax.axis_index("depth") == 0
     columns = jnp.arange(breadth, dtype=jnp.int32)
-    fast_route = [(i, i + 1) for i in range(0, levels - 1, 2)]
-    slow_route = [(i, i + 1) for i in range(1, levels - 1, 2)]
+    odd = lax.axis_index("depth") % 2 == 1
+    fast_route = [(i, i ^ 1) for i in range(levels)]
+    slow_route = [(i, (i + 1) % levels) for i in range(levels)]
     terms = []
 
     def injected(tick):
@@ -63,11 +64,12 @@
         return jnp.stack([first - second, third - first - second], 0)
 
     def fast(panel):
-        return lax.ppermute(panel, "depth", fast_route)
+        got = lax.ppermute(panel, "depth", fast_route)
+        return jnp.where(odd, got, 0.0)
 
     def slow(panel, tick):
         got = lax.ppermute(panel, "depth", slow_route)
-        return jnp.where(at_surface, injected(tick), got)
+        return jnp.where(odd, 0.0, jnp.where(at_surface, injected(tick), got))
 
     out0 = work(arriving_downward_matrices[0, 0], 0)
     f0 = fast(out0)

time: 65.6 us -> 59.7 us (0.910)
  the two profiles are of different devices: /device:TPU:24 before, /device:TPU:0 now
where the time goes in v2:
time: 59.7 us; the launch traced here: 59.5 us
  waiting for transfers between devices  30.8 us (52%)
  matrix products  11.7 us (20%)
  other arithmetic  11.2 us (19%)
  starting transfers between devices  3.41 us (6%)
  local copies, waits for them, and re-layouts  1.37 us (2%)
  between operations  1.02 us (2%)
    ppermute x4, waiting for transfers between devices, slow(): got = lax.ppermute(panel, 'depth', slow_route)  25.9 us
    dot_general x24, matrix products, product(): jnp.dot(left, right, precision=lax.Precision.HIGH, preferred_element_type...  11.7 us
    ppermute x4, waiting for transfers between devices, fast(): got = lax.ppermute(panel, 'depth', fast_route)  3.61 us
    add x6, other arithmetic, work(): mixed = arriving + reflect[None, None, :] * wave  2.7 us
    another operation x15, other arithmetic, work(): return jnp.stack([first - second, third - first - second], 0)  2.66 us
    reduce_sum x2, other arithmetic, work(): terms.append(jnp.sum(arriving * wave, axis=(0, 1)))  2.34 us
    convert_element_type x4, other arithmetic, injected(): (columns[None, :] == shot_node_indices[tick - 1][:, None]).astype(jnp.flo...  1.63 us
    ppermute x1, starting transfers between devices, sum_over(): total = total + lax.ppermute(chunk, axis, route)  1.56 us
  transfers between devices with their start and end apart: 9, of which 8 were waited for; matrix products, arithmetic and copies ran while one was open for 13% of the time, Pallas kernels for 0%

profile of v2, /device:TPU:0, one launch (start us, length us, event | category | flops | bytes accessed | tf_op | source)
XLA Modules:
  0.0 59.5 jit_solution(1379149065200932282)
XLA Ops:
  0.6 0.0 copy-start
  0.6 1.3 %fusion.80 = f32[2,96,512]{2,1,0:T(8,128)S(1)} fusion(f32[1,1,2,96,512]{4,3,2,1,0:T(8,128)} %param.9, f32[1,1,5,2,96,512]{5,4,3,2,1,0:T(8,128)} %param.8, f32[512]{0:T(512)} %bitcast.219), kind=kLoop, calls=%fused_computation.110 | loop fusion | flops 196608 | bytes 1181696 | tf_op jit(solution)/shard_map/add | solution.py:60
  2.0 1.7 %fusion.38 = f32[96,512]{1,0:T(8,128)S(1)} fusion(f32[1,1,2,512,512]{4,3,2,1,0:T(8,128)} %param.6, f32[2,96,512]{2,1,0:T(8,128)S(1)} %fusion.80), kind=kOutput, calls=%fused_computation.46 | convolution fusion | flops 150994944 | bytes 1441792 | tf_op jit(solution)/shard_map/dot_general | solution.py:12
  3.6 0.4 fusion.54
  4.1 0.2 slice_add_fusion
  4.4 0.4 fusion.15
  4.8 0.8 %pad_maximum_fusion = f32[2,96,512]{2,1,0:T(8,128)} fusion(f32[1,96,512]{2,1,0:T(8,128)S(1)} %fusion.15, f32[1,96,512]{2,1,0:T(8,128)S(1)} %subtract_bitcast_fusion.7), kind=kLoop, calls=%fused_computation.81 | loop fusion | flops 98304 | bytes 786432 | tf_op jit(solution)/shard_map/stack | solution.py:64
  5.6 0.5 collective-permute-start
  6.0 0.1 collective-permute-start.2
  6.1 0.6 slice_bitcast_fusion.3
  6.7 0.7 %slice_reduce_fusion.3 = (f32[2]{0:T(128)}, f32[2]{0:T(128)S(1)}, f32[2]{0:T(128)S(1)}, f32[2]{0:T(128)S(1)}) fusion(f32[1,4,2]{1,2,0:T(2,128)S(1)} %copy-done.4), kind=kLoop, calls=%fused_computation.207 | loop fusion | bytes 64 | tf_op jit(solution)/shard_map/slice | solution.py:55
  7.4 0.7 %fusion.122 = f32[96,512]{1,0:T(8,128)S(1)} fusion(s32[96]{0:T(128)} %get-tuple-element.25), kind=kLoop, calls=%fused_computation.168 | loop fusion | flops 98304 | bytes 196992 | tf_op jit(solution)/shard_map/convert_element_type | solution.py:54
  8.2 1.1 %fusion.83 = f32[2,96,512]{2,1,0:T(8,128)S(1)} fusion(f32[2,96,512]{2,1,0:T(8,128)S(1)} %collective-permute-done, f32[1,1,5,2,96,512]{5,4,3,2,1,0:T(8,128)} %param.8, f32[512]{0:T(512)S(1)} %bitcast.220, pred[]{:T(512)S(6)} %eq.85), kind=kLoop, calls=%fused_computation.117 | loop fusion | flops 294912 | bytes 1181697 | tf_op jit(solution)/shard_map/add | solution.py:60
  9.3 0.4 fusion.36
  9.7 0.4 fusion.52
  10.1 0.4 fusion.13
  10.7 6.8 %collective-permute-done.2 = f32[2,96,512]{2,1,0:T(8,128)} collective-permute-done((f32[2,96,512]{2,1,0:T(8,128)}, f32[2,96,512]{2,1,0:T(8,128)}, u32[]{:S(2)}, u32[]{:S(2)}) %collective-permute-start.2) | collective-permute-done | bytes 393248 | tf_op jit(solution)/shard_map/ppermute | solution.py:71
  17.5 0.1 select_select_fusion.1
  17.6 0.1 fusion.82
  17.7 0.4 fusion.34
  18.1 0.4 fusion.50
  18.6 0.4 fusion.11
  19.1 0.1 collective-permute-start.3
  19.2 0.5 collective-permute-start.1
  19.6 1.2 %collective-permute-done.3 = f32[2,96,512]{2,1,0:T(8,128)S(1)} collective-permute-done((f32[2,96,512]{2,1,0:T(8,128)S(1)}, f32[2,96,512]{2,1,0:T(8,128)S(1)}, u32[]{:S(2)}, u32[]{:S(2)}) %collective-permute-start.3) | collective-permute-done | bytes 393248 | tf_op jit(solution)/shard_map/ppermute | solution.py:67
  20.9 0.1 fusion.85
  20.9 0.4 fusion.32
  21.4 0.4 fusion.48
  21.8 0.4 fusion.9
  22.3 0.2 collective-permute-start.6
  22.5 0.1 fusion.121
  22.6 0.1 fusion.123
  22.7 6.4 %collective-permute-done.1 = f32[2,96,512]{2,1,0:T(8,128)S(1)} collective-permute-done((f32[2,96,512]{2,1,0:T(8,128)S(1)}, f32[2,96,512]{2,1,0:T(8,128)S(1)}, u32[]{:S(2)}, u32[]{:S(2)}) %collective-permute-start.1) | collective-permute-done | bytes 393248 | tf_op jit(solution)/shard_map/ppermute | solution.py:71
  29.1 4.2 %collective-permute-done.6 = f32[2,96,512]{2,1,0:T(8,128)S(1)} collective-permute-done((f32[2,96,512]{2,1,0:T(8,128)S(1)}, f32[2,96,512]{2,1,0:T(8,128)S(1)}, u32[]{:S(2)}, u32[]{:S(2)}) %collective-permute-start.6) | collective-permute-done | bytes 393248 | tf_op jit(solution)/shard_map/ppermute | solution.py:71
  33.3 0.2 select_select_fusion
  33.5 0.1 fusion.84
  33.6 0.4 fusion.30
  34.0 0.4 fusion.46
  34.5 0.4 fusion.7
  35.0 0.1 collective-permute-start.4
  35.1 1.7 %collective-permute-done.4 = f32[2,96,512]{2,1,0:T(8,128)S(1)} collective-permute-done((f32[2,96,512]{2,1,0:T(8,128)S(1)}, f32[2,96,512]{2,1,0:T(8,128)S(1)}, u32[]{:S(2)}, u32[]{:S(2)}) %collective-permute-start.4) | collective-permute-done | bytes 393248 | tf_op jit(solution)/shard_map/ppermute | solution.py:67
  36.8 0.1 fusion.87
  36.9 0.4 fusion.28
  37.3 0.4 fusion.44
  37.8 0.4 fusion.5
  38.2 0.8 %pad_maximum_fusion.5 = f32[2,96,512]{2,1,0:T(8,128)} fusion(f32[1,96,512]{2,1,0:T(8,128)S(1)} %fusion.5, f32[1,96,512]{2,1,0:T(8,128)S(1)} %subtract_bitcast_fusion.2), kind=kLoop, calls=%fused_computation.86 | loop fusion | flops 98304 | bytes 786432 | tf_op jit(solution)/shard_map/stack | solution.py:64
  39.0 1.1 %fusion.78 = (f32[512]{0:T(512)S(1)}, f32[512]{0:T(512)S(1)}, f32[512]{0:T(512)S(1)}, f32[512]{0:T(512)}, f32[512]{0:T(512)}, /*index=5*/f32[512]{0:T(512)}, f32[512]{0:T(512)}, f32[2,96,512]{2,1,0:T(8,128)S(1)}) fusion(f32[2,96,512]{2,1,0:T(8,128)S(1)} %collective-permute-done, f32[1,1,5,2,96,512]{5,4,3,2,1,0:T(8,128)S(1)} %copy-done.1, pred[]{:T(512)S(6)} %eq.85, ...), kind=kLoop, calls=%fused_computation.106 | loop fusion | flops 1864192 | bytes 4734977 | tf_op jit(solution)/shard_map/reduce_sum | solution.py:59
  40.1 0.4 fusion.26
  40.6 0.4 fusion.42
  41.0 0.4 fusion.3
  41.5 0.8 %pad_maximum_fusion.6 = f32[2,96,512]{2,1,0:T(8,128)} fusion(f32[1,96,512]{2,1,0:T(8,128)S(1)} %fusion.3, f32[1,96,512]{2,1,0:T(8,128)S(1)} %subtract_bitcast_fusion.1), kind=kLoop, calls=%fused_computation.87 | loop fusion | flops 98304 | bytes 786432 | tf_op jit(solution)/shard_map/stack | solution.py:64
  42.2 0.1 collective-permute-start.7
  42.4 0.4 collective-permute-start.5
  42.8 0.7 %fusion.120 = f32[96,512]{1,0:T(8,128)S(1)} fusion(s32[96]{0:T(128)} %get-tuple-element.22), kind=kLoop, calls=%fused_computation.166 | loop fusion | flops 98304 | bytes 196992 | tf_op jit(solution)/shard_map/convert_element_type | solution.py:54
  43.5 0.7 %collective-permute-done.7 = f32[2,96,512]{2,1,0:T(8,128)S(1)} collective-permute-done((f32[2,96,512]{2,1,0:T(8,128)}, f32[2,96,512]{2,1,0:T(8,128)S(1)}, u32[]{:S(2)}, u32[]{:S(2)}) %collective-permute-start.7) | collective-permute-done | bytes 393248 | tf_op jit(solution)/shard_map/ppermute | solution.py:67
  44.2 8.4 %collective-permute-done.5 = f32[2,96,512]{2,1,0:T(8,128)} collective-permute-done((f32[2,96,512]{2,1,0:T(8,128)}, f32[2,96,512]{2,1,0:T(8,128)}, u32[]{:S(2)}, u32[]{:S(2)}) %collective-permute-start.5) | collective-permute-done | bytes 393248 | tf_op jit(solution)/shard_map/ppermute | solution.py:71
  52.6 1.2 %fusion.73 = (f32[512]{0:T(512)S(1)}, f32[2,96,512]{2,1,0:T(8,128)S(1)}) fusion(f32[1,1,5,2,96,512]{5,4,3,2,1,0:T(8,128)} %param.8, f32[2,96,512]{2,1,0:T(8,128)S(1)} %collective-permute-done.7, f32[2,96,512]{2,1,0:T(8,128)} %collective-permute-done.5, f32[96,512]{1,0:T(8,128)S(1)} %fusion.120, f32[2]{0:T(128)} %get-tuple-element.15, pred[]{:T(512)S(6)} %eq.86, ...), kind=kLoop, calls=%fused_computation.92 | loop fusion | flops 884224 | bytes 1773578 | tf_op jit(solution)/shard_map/reduce_sum | solution.py:59
  53.8 0.4 fusion.24
  54.3 0.4 fusion.40
  54.7 0.4 fusion.1
  55.3 1.6 %collective-permute-start.8 = (f32[1,256]{1,0:T(1,128)S(1)}, f32[1,256]{1,0:T(1,128)S(1)}, u32[]{:S(2)}, u32[]{:S(2)}) collective-permute-start(f32[1,256]{1,0:T(1,128)S(1)} %constant_dynamic-slice_fusion), channel_id=1, source_target_pairs={{0,1},{1,0},{2,3},{3,2},{4,5},{5,4},{6,7},{7,6},{8,9},{9,8},{10,11... | collective-permute-start | bytes 3080 | tf_op jit(solution)/shard_map/ppermute | solution.py:27
  56.8 0.8 %maximum_bitcast_fusion = f32[1,1,2,96,512]{4,3,2,1,0:T(8,128)} fusion(f32[1,96,512]{2,1,0:T(8,128)S(1)} %fusion.1, f32[1,96,512]{2,1,0:T(8,128)S(1)} %subtract_bitcast_fusion), kind=kLoop, calls=%fused_computation.88 | loop fusion | flops 98304 | bytes 786432 | tf_op jit(solution)/shard_map/broadcast_in_dim | solution.py:93
  57.6 1.3 %collective-permute-done.8 = f32[1,256]{1,0:T(1,128)S(1)} collective-permute-done((f32[1,256]{1,0:T(1,128)S(1)}, f32[1,256]{1,0:T(1,128)S(1)}, u32[]{:S(2)}, u32[]{:S(2)}) %collective-permute-start.8) | collective-permute-done | bytes 1056 | tf_op jit(solution)/shard_map/ppermute | solution.py:27
  58.9 0.6 dynamic-slice_add_fusion
  (35 shorter events, 0.4 us)
Async XLA Ops:
  0.6 3.0 %copy-start = (f32[1,1,2,512,512]{4,3,2,1,0:T(8,128)S(1)}, f32[1,1,2,512,512]{4,3,2,1,0:T(8,128)}, u32[]{:S(2)}) copy-start(f32[1,1,2,512,512]{4,3,2,1,0:T(8,128)} %param.6) | copy-start | bytes 6291460
  4.3 1.8 %copy-start.9 = (s32[4,96]{1,0:T(4,128)S(1)}, s32[4,96]{1,0:T(4,128)}, u32[]{:S(2)}) copy-start(s32[4,96]{1,0:T(4,128)} %param.10) | copy-start | bytes 4612
  4.3 2.4 %copy-start.4 = (f32[1,4,2]{1,2,0:T(2,128)S(1)}, f32[1,4,2]{1,2,0:T(2,128)}, u32[]{:S(2)}) copy-start(f32[1,4,2]{1,2,0:T(2,128)} %param.11) | copy-start | bytes 100
  4.3 3.8 %copy-start.3 = (f32[1,512]{1,0:T(1,128)S(1)}, f32[1,512]{1,0:T(1,128)}, u32[]{:S(2)}) copy-start(f32[1,512]{1,0:T(1,128)} %param.7) | copy-start | bytes 6148
  5.6 2.6 %collective-permute-start = (f32[2,96,512]{2,1,0:T(8,128)}, f32[2,96,512]{2,1,0:T(8,128)S(1)}, u32[]{:S(2)}, u32[]{:S(2)}) collective-permute-start(f32[2,96,512]{2,1,0:T(8,128)} %pad_maximum_fusion), channel_id=1, source_target_pairs={{0,2},{2,0},{4,6},{6,4},{8,10},{10,8},{12,14},{14,12},{16,18},{18,... | collective-permute-start | bytes 1179656 | tf_op jit(solution)/shard_map/ppermute | solution.py:67
  6.0 11.4 %collective-permute-start.2 = (f32[2,96,512]{2,1,0:T(8,128)}, f32[2,96,512]{2,1,0:T(8,128)}, u32[]{:S(2)}, u32[]{:S(2)}) collective-permute-start(f32[2,96,512]{2,1,0:T(8,128)} %pad_maximum_fusion), channel_id=1, source_target_pairs={{0,2},{2,4},{4,6},{6,8},{8,10},{10,12},{12,14},{14,16},{16,18},{18... | collective-permute-start | bytes 1179656 | tf_op jit(solution)/shard_map/ppermute | solution.py:71
  10.1 7.5 %copy-start.1 = (f32[1,1,5,2,96,512]{5,4,3,2,1,0:T(8,128)S(1)}, f32[1,1,5,2,96,512]{5,4,3,2,1,0:T(8,128)}, u32[]{:S(2)}) copy-start(f32[1,1,5,2,96,512]{5,4,3,2,1,0:T(8,128)} %param.8) | copy-start | bytes 5898244
  19.1 1.8 %collective-permute-start.3 = (f32[2,96,512]{2,1,0:T(8,128)S(1)}, f32[2,96,512]{2,1,0:T(8,128)S(1)}, u32[]{:S(2)}, u32[]{:S(2)}) collective-permute-start(f32[2,96,512]{2,1,0:T(8,128)S(1)} %pad_maximum_fusion.2), channel_id=1, source_target_pairs={{0,2},{2,0},{4,6},{6,4},{8,10},{10,8},{12,14},{14,12},{16,18},{18,... | collective-permute-start | bytes 1179656 | tf_op jit(solution)/shard_map/ppermute | solution.py:67
  19.2 10.0 %collective-permute-start.1 = (f32[2,96,512]{2,1,0:T(8,128)S(1)}, f32[2,96,512]{2,1,0:T(8,128)S(1)}, u32[]{:S(2)}, u32[]{:S(2)}) collective-permute-start(f32[2,96,512]{2,1,0:T(8,128)S(1)} %pad_maximum_fusion.1), channel_id=1, source_target_pairs={{0,2},{2,4},{4,6},{6,8},{8,10},{10,12},{12,14},{14,16},{16,18},{18... | collective-permute-start | bytes 1179656 | tf_op jit(solution)/shard_map/ppermute | solution.py:71
  22.3 11.0 %collective-permute-start.6 = (f32[2,96,512]{2,1,0:T(8,128)S(1)}, f32[2,96,512]{2,1,0:T(8,128)S(1)}, u32[]{:S(2)}, u32[]{:S(2)}) collective-permute-start(f32[2,96,512]{2,1,0:T(8,128)S(1)} %pad_maximum_fusion.3), channel_id=1, source_target_pairs={{0,2},{2,4},{4,6},{6,8},{8,10},{10,12},{12,14},{14,16},{16,18},{18... | collective-permute-start | bytes 1179656 | tf_op jit(solution)/shard_map/ppermute | solution.py:71
  35.0 1.8 %collective-permute-start.4 = (f32[2,96,512]{2,1,0:T(8,128)S(1)}, f32[2,96,512]{2,1,0:T(8,128)S(1)}, u32[]{:S(2)}, u32[]{:S(2)}) collective-permute-start(f32[2,96,512]{2,1,0:T(8,128)S(1)} %pad_maximum_fusion.4), channel_id=1, source_target_pairs={{0,2},{2,0},{4,6},{6,4},{8,10},{10,8},{12,14},{14,12},{16,18},{18,... | collective-permute-start | bytes 1179656 | tf_op jit(solution)/shard_map/ppermute | solution.py:67
  37.3 1.7 %copy-start.2 = (f32[1,1,2,96,512]{4,3,2,1,0:T(8,128)S(1)}, f32[1,1,2,96,512]{4,3,2,1,0:T(8,128)}, u32[]{:S(2)}) copy-start(f32[1,1,2,96,512]{4,3,2,1,0:T(8,128)} %param.9) | copy-start | bytes 1179652
  42.2 1.9 %collective-permute-start.7 = (f32[2,96,512]{2,1,0:T(8,128)}, f32[2,96,512]{2,1,0:T(8,128)S(1)}, u32[]{:S(2)}, u32[]{:S(2)}) collective-permute-start(f32[2,96,512]{2,1,0:T(8,128)} %pad_maximum_fusion.6), channel_id=1, source_target_pairs={{0,2},{2,0},{4,6},{6,4},{8,10},{10,8},{12,14},{14,12},{16,18},{18,... | collective-permute-start | bytes 1179656 | tf_op jit(solution)/shard_map/ppermute | solution.py:67
  42.4 10.2 %collective-permute-start.5 = (f32[2,96,512]{2,1,0:T(8,128)}, f32[2,96,512]{2,1,0:T(8,128)}, u32[]{:S(2)}, u32[]{:S(2)}) collective-permute-start(f32[2,96,512]{2,1,0:T(8,128)} %pad_maximum_fusion.5), channel_id=1, source_target_pairs={{0,2},{2,4},{4,6},{6,8},{8,10},{10,12},{12,14},{14,16},{16,18},{18... | collective-permute-start | bytes 1179656 | tf_op jit(solution)/shard_map/ppermute | solution.py:71
  54.2 1.0 %copy-start.5 = (f32[512]{0:T(512)S(1)}, f32[512]{0:T(512)}, u32[]{:S(2)}) copy-start(f32[512]{0:T(512)} %get-tuple-element.11) | copy-start | bytes 6148
  54.2 1.0 %copy-start.6 = (f32[512]{0:T(512)S(1)}, f32[512]{0:T(512)}, u32[]{:S(2)}) copy-start(f32[512]{0:T(512)} %get-tuple-element.12) | copy-start | bytes 6148
  54.2 1.0 %copy-start.7 = (f32[512]{0:T(512)S(1)}, f32[512]{0:T(512)}, u32[]{:S(2)}) copy-start(f32[512]{0:T(512)} %get-tuple-element.13) | copy-start | bytes 6148
  54.3 1.0 %copy-start.8 = (f32[512]{0:T(512)S(1)}, f32[512]{0:T(512)}, u32[]{:S(2)}) copy-start(f32[512]{0:T(512)} %get-tuple-element.14) | copy-start | bytes 6148
  55.3 3.6 %collective-permute-start.8 = (f32[1,256]{1,0:T(1,128)S(1)}, f32[1,256]{1,0:T(1,128)S(1)}, u32[]{:S(2)}, u32[]{:S(2)}) collective-permute-start(f32[1,256]{1,0:T(1,128)S(1)} %constant_dynamic-slice_fusion), channel_id=1, source_target_pairs={{0,1},{1,0},{2,3},{3,2},{4,5},{5,4},{6,7},{7,6},{8,9},{9,8},{10,11... | collective-permute-start | bytes 3080 | tf_op jit(solution)/shard_map/ppermute | solution.py:27

commit v3 on v0

v3 whole, which is shorter than its diff:
```python
import functools
import math

import jax
import jax.numpy as jnp
from jax import lax
from jax.experimental import pallas as pl
from jax.experimental.pallas import tpu as pltpu
from jax.sharding import PartitionSpec as P

TICKS = 5
VMEM_LIMIT = 24 * 1024 * 1024
QUICK = pl.CostEstimate(flops=1, bytes_accessed=1, transcendentals=0)


def pinned(value):
    return pltpu.with_memory_space_constraint(value, pltpu.VMEM)


def in_vmem():
    return pl.BlockSpec(memory_space=pltpu.VMEM)


def is_odd():
    return lax.axis_index("depth") % 2 == 1


def split(value):
    high = value.astype(jnp.bfloat16)
    low = (value - high.astype(jnp.float32)).astype(jnp.bfloat16)
    return high, low


def fold(product):
    rows = product.shape[0] * product.shape[1]
    return jnp.sum(product.reshape(rows // 8, 8, product.shape[2]), axis=0)


def load_left(mixed, left):
    shots = mixed.shape[1]
    for part in range(2):
        high, low = split(mixed[part])
        left[pl.ds(part * shots, shots), :] = high
        left[pl.ds((2 + part) * shots, shots), :] = low


def multiply(left, high, low, out):
    shots = out.shape[1]
    dot = functools.partial(jnp.dot, preferred_element_type=jnp.float32)

    def by(part):
        big = dot(left[...], high[part])
        small = dot(left[pl.ds(0, 2 * shots), :], low[part])
        real = big[:shots] + (big[2 * shots : 3 * shots] + small[:shots])
        imag = big[shots : 2 * shots] + (big[3 * shots :] + small[shots:])
        return real, imag

    real_real, imag_real = by(0)
    real_imag, imag_imag = by(1)
    out[0] = real_real - imag_imag
    out[1] = real_imag + imag_real


def injected(tick, sites, pulse, shape):
    shots, breadth = shape
    row = lax.broadcasted_iota(jnp.int32, (shots, shots), 0)
    column = lax.broadcasted_iota(jnp.int32, (shots, shots), 1)
    spread = jnp.broadcast_to(sites[pl.ds(tick - 1, 1), :], (shots, shots)).astype(jnp.float32)
    site = jnp.sum(jnp.where(row == column, spread, 0.0), axis=1, keepdims=True)
    lanes = lax.broadcasted_iota(jnp.int32, (shots, breadth), 1).astype(jnp.float32)
    hit = lanes == site
    return [jnp.where(hit, pulse[part, tick - 1], 0.0) for part in range(2)]


def first_kernel(parity, chained, *refs):
    if chained:
        refs = refs[:4] + refs[8:]
    operator, contrast, residual, panel = refs[:4]
    out, high, low, grad = refs[4:8]
    whole, wave, arrived, left, sems = refs[8:]

    @pl.when(is_odd() if parity else jnp.logical_not(is_odd()))
    def _():
        copies = [
            pltpu.make_async_copy(residual.at[0, 0, 0], wave, sems.at[0]),
            pltpu.make_async_copy(panel.at[0, 0], arrived, sems.at[1]),
            pltpu.make_async_copy(operator.at[0, 0, 0], whole.at[0], sems.at[2]),
            pltpu.make_async_copy(operator.at[0, 0, 1], whole.at[1], sems.at[3]),
        ]
        for copy in copies:
            copy.start()
        copies[0].wait()
        copies[1].wait()
        grad[...] = fold(arrived[...] * wave[...])
        load_left(arrived[...] + contrast[...][None] * wave[...], left)
        for part in range(2):
            copies[2 + part].wait()
            high[part], low[part] = split(whole[part])
        multiply(left, high, low, out)


def first(parity, operator, contrast, residual, panel, carried):
    shots, breadth = panel.shape[3:]
    any_ref = pl.BlockSpec(memory_space=pl.ANY)
    half = pltpu.VMEM((2, breadth, breadth), jnp.bfloat16)
    carried = [pinned(value) for value in carried]
    out = pl.pallas_call(
        functools.partial(first_kernel, parity, bool(carried)),
        out_shape=(
            pltpu.VMEM((2, shots, breadth), jnp.float32),
            half,
            half,
            pltpu.VMEM((8, breadth), jnp.float32),
        ),
        in_specs=[any_ref, in_vmem(), any_ref, any_ref] + [in_vmem()] * len(carried),
        out_specs=(in_vmem(),) * 4,
        scratch_shapes=[
            pltpu.VMEM((2, breadth, breadth), jnp.float32),
            pltpu.VMEM((2, shots, breadth), jnp.float32),
            pltpu.VMEM((2, shots, breadth), jnp.float32),
            pltpu.VMEM((4 * shots, breadth), jnp.bfloat16),
            pltpu.SemaphoreType.DMA((4,)),
        ],
        input_output_aliases={4 + i: i for i in range(len(carried))},
        compiler_params=pltpu.CompilerParams(vmem_limit_bytes=VMEM_LIMIT),
        cost_estimate=QUICK,
    )(operator, contrast, residual, panel, *carried)
    return out


def arrive(tick, arrived, residual, contrast, sites, pulse, grad_in, grad, left, odd_side):
    def take(panel):
        wave = residual[0, 0, tick]
        if grad is not None:
            grad[...] = grad_in[...] + fold(panel * wave)
        if left is not None:
            load_left(panel + contrast[...][None] * wave, left)

    if odd_side:
        take(arrived[...])
        return
    surface = lax.axis_index("depth") == 0

    @pl.when(surface)
    def _():
        take(jnp.stack(injected(tick, sites, pulse, arrived.shape[1:]), 0))

    @pl.when(jnp.logical_not(surface))
    def _():
        take(arrived[...])


def step_kernel(tick, parity, arrived, residual, contrast, sites, pulse, high, low, grad_in, out, grad, left):
    @pl.when(is_odd() if parity else jnp.logical_not(is_odd()))
    def _():
        arrive(tick, arrived, residual, contrast, sites, pulse, grad_in, grad, left, parity)
        multiply(left, high, low, out)


def step(tick, parity, arrived, shared, high, low, grad):
    shots, breadth = arrived.shape[1:]
    residual, contrast, sites, pulse = shared
    return pl.pallas_call(
        functools.partial(step_kernel, tick, parity),
        out_shape=(
            pltpu.VMEM((2, shots, breadth), jnp.float32),
            pltpu.VMEM(grad.shape, jnp.float32),
        ),
        in_specs=[in_vmem()] * 4 + [pl.BlockSpec(memory_space=pltpu.SMEM)] + [in_vmem()] * 3,
        out_specs=(in_vmem(),) * 2,
        scratch_shapes=[pltpu.VMEM((4 * shots, breadth), jnp.bfloat16)],
        input_output_aliases={7: 1},
        compiler_params=pltpu.CompilerParams(vmem_limit_bytes=VMEM_LIMIT),
        cost_estimate=QUICK,
    )(pinned(arrived), residual, contrast, sites, pulse, pinned(high), pinned(low), pinned(grad))


def gradient_kernel(count, scale, from_above, from_mate, residual, contrast, sites, pulse, grad_in, chunks, total):
    tick = TICKS - 1
    rest = (residual, contrast, sites, pulse, grad_in, total, None)

    @pl.when(is_odd())
    def _():
        arrive(tick, from_mate, *rest, True)

    @pl.when(jnp.logical_not(is_odd()))
    def _():
        arrive(tick, from_above, *rest, False)

    gradient = jnp.sum(total[...], axis=0, keepdims=True) * scale
    width = gradient.shape[1] // count
    me = lax.axis_index("freq")
    for distance in range(count):
        owner = lax.rem(me + distance, count)
        chunk = jnp.zeros((1, width), jnp.float32)
        for place in range(count):
            piece = gradient[:, place * width : (place + 1) * width]
            chunk = jnp.where(owner == place, piece, chunk)
        chunks[distance][...] = chunk


def gradient_chunks(from_above, from_mate, shared, grad):
    shots, breadth = from_above.shape[1:]
    residual, contrast, sites, pulse = shared
    count = lax.axis_size("freq")

    def body(*refs):
        gradient_kernel(count, 1.0 / math.sqrt(shots * TICKS), *refs[:7], refs[7 : 7 + count], refs[7 + count])

    return pl.pallas_call(
        body,
        out_shape=(pltpu.VMEM((1, breadth // count), jnp.float32),) * count,
        in_specs=[in_vmem()] * 5 + [pl.BlockSpec(memory_space=pltpu.SMEM)] + [in_vmem()],
        out_specs=(in_vmem(),) * count,
        scratch_shapes=[pltpu.VMEM(grad.shape, jnp.float32)],
        compiler_params=pltpu.CompilerParams(vmem_limit_bytes=VMEM_LIMIT),
        cost_estimate=QUICK,
    )(pinned(from_above), pinned(from_mate), residual, contrast, sites, pulse, pinned(grad))


def last_kernel(from_above, from_mate, residual, contrast, sites, pulse, high, low, out, left):
    tick = TICKS - 1
    rest = (residual, contrast, sites, pulse, None, None, left)

    @pl.when(is_odd())
    def _():
        arrive(tick, from_mate, *rest, True)

    @pl.when(jnp.logical_not(is_odd()))
    def _():
        arrive(tick, from_above, *rest, False)

    multiply(left, high, low, out)


def last(from_above, from_mate, shared, high, low):
    shots, breadth = from_above.shape[1:]
    residual, contrast, sites, pulse = shared
    return pl.pallas_call(
        last_kernel,
        out_shape=jax.ShapeDtypeStruct((2, shots, breadth), jnp.float32),
        in_specs=[in_vmem()] * 5 + [pl.BlockSpec(memory_space=pltpu.SMEM)] + [in_vmem()] * 2,
        out_specs=in_vmem(),
        scratch_shapes=[pltpu.VMEM((4 * shots, breadth), jnp.bfloat16)],
        compiler_params=pltpu.CompilerParams(vmem_limit_bytes=VMEM_LIMIT),
        cost_estimate=QUICK,
    )(pinned(from_above), pinned(from_mate), residual, contrast, sites, pulse, pinned(high), pinned(low))


def cross_route(levels):
    route = {level: level + 1 for level in range(levels - 1)}
    chips = levels // 2
    route[levels - 1] = 0
    if chips % 2 == 0 and chips > 2:
        route[levels - 1] = levels - 3
        for chip in range(chips - 2, 2, -2):
            route[2 * chip] = 2 * (chip - 2) + 1
        route[4] = 0
    return sorted(route.items())


def local(
    extrapolation_operator,
    impedance_contrast,
    ascending_residual,
    arriving_downward_matrices,
    shot_node_indices,
    emitted_pulse,
):
    levels = lax.axis_size("depth")
    mate_route = [(level, level ^ 1) for level in range(levels)]
    down_route = cross_route(levels)
    freqs = lax.axis_size("freq")
    shared = (
        pinned(ascending_residual),
        impedance_contrast,
        shot_node_indices,
        emitted_pulse[0].T,
    )

    def mate(panel):
        return lax.ppermute(panel, "depth", mate_route)

    def down(panel):
        return lax.ppermute(panel, "depth", down_route)

    start = (extrapolation_operator, impedance_contrast, ascending_residual, arriving_downward_matrices)
    odd, *carried = first(1, *start, ())
    from_above = down(odd)
    even, high, low, grad = first(0, *start, (odd, *carried))
    from_mate = mate(even)
    for tick in range(1, TICKS):
        if tick == TICKS - 1:
            chunks = gradient_chunks(from_above, from_mate, shared, grad)
            out = last(from_above, from_mate, shared, high, low)
            break
        odd, grad = step(tick, 1, from_mate, shared, high, low, grad)
        later = down(odd)
        even, grad = step(tick, 0, from_above, shared, high, low, grad)
        from_mate = mate(even)
        from_above = later

    gradient = chunks[0]
    for distance in range(1, freqs):
        route = [(i, (i + distance) % freqs) for i in range(freqs)]
        gradient = gradient + lax.ppermute(chunks[distance], "freq", route)
    return (out[None, None], gradient)


def solution(mesh):
    placed = (
        P("freq", "depth", None, None, None),
        P("depth", None),
        P("freq", "depth", None, None, None, None),
        P("freq", "depth", None, None, None),
        P(),
        P("freq", None, None),
    )
    return jax.shard_map(
        local,
        mesh=mesh,
        in_specs=placed,
        out_specs=(P("freq", "depth", None, None, None), P("depth", "freq")),
        check_vma=False,
    )
```

time: 87.8 us -> 60.8 us (0.69)
  the two profiles are of different devices: /device:TPU:0 before, /device:TPU:25 now
where the time goes in v3:
time: 60.8 us; the launch traced here: 60.6 us
  waiting for transfers between devices  42 us (69%)
  Pallas kernels  10.3 us (17%)
  local copies, waits for them, and re-layouts  4.82 us (8%)
  starting transfers between devices  2.17 us (4%)
  between operations  0.76 us (1%)
    ppermute x4, waiting for transfers between devices, down(): return lax.ppermute(panel, 'depth', down_route)  35.5 us
    ppermute x4, waiting for transfers between devices, mate(): return lax.ppermute(panel, 'depth', mate_route)  6.43 us
    pallas_call x6, Pallas kernels, step(): pl.pallas_call(functools.partial(step_kernel, tick, parity), out_shape=(p...  5.78 us
    unnamed x14, local copies, waits for them, and re-layouts  4.82 us
    pallas_call x1, Pallas kernels, last(): pl.pallas_call(last_kernel, out_shape=jax.ShapeDtypeStruct((2, shots, bre...  2.18 us
    pallas_call x2, Pallas kernels, first(): pl.pallas_call(functools.partial(first_kernel, parity, bool(carried)), ou...  1.71 us
    ppermute x1, starting transfers between devices, local(): gradient = gradient + lax.ppermute(chunks[distance], 'freq', route)  1.27 us
  transfers between devices with their start and end apart: 9, of which 8 were waited for; matrix products, arithmetic and copies ran while one was open for 0% of the time, Pallas kernels for 8%

profile of v3, /device:TPU:25, one launch (start us, length us, event | category | flops | bytes accessed | tf_op | source)
XLA Modules:
  0.0 60.6 jit_solution(12935676415538623230)
XLA Ops:
  0.6 0.0 copy-start
  0.6 1.5 %copy-done = f32[1,1,5,2,96,512]{5,4,3,2,1,0:T(8,128)S(1)} copy-done((f32[1,1,5,2,96,512]{5,4,3,2,1,0:T(8,128)S(1)}, f32[1,1,5,2,96,512]{5,4,3,2,1,0:T(8,128)}, u32[]{:S(2)}) %copy-start) | copy-done | bytes 1966104
  2.2 0.0 copy-start.2
  2.2 1.6 %copy-done.2 = f32[1,1,2,512,512]{4,3,2,1,0:T(8,128)S(1)} copy-done((f32[1,1,2,512,512]{4,3,2,1,0:T(8,128)S(1)}, f32[1,1,2,512,512]{4,3,2,1,0:T(8,128)}, u32[]{:S(2)}) %copy-start.2) | copy-done | bytes 2097176
  3.8 0.0 copy-start.3
  3.8 1.0 %copy-done.3 = f32[1,1,2,96,512]{4,3,2,1,0:T(8,128)S(1)} copy-done((f32[1,1,2,96,512]{4,3,2,1,0:T(8,128)S(1)}, f32[1,1,2,96,512]{4,3,2,1,0:T(8,128)}, u32[]{:S(2)}) %copy-start.3) | copy-done | bytes 393240
  4.8 0.0 copy-start.4
  4.8 0.7 %copy-done.4 = f32[1,512]{1,0:T(1,128)S(1)} copy-done((f32[1,512]{1,0:T(1,128)S(1)}, f32[1,512]{1,0:T(1,128)}, u32[]{:S(2)}) %copy-start.4) | copy-done | bytes 2072
  5.4 1.7 %shard_map.77 = (f32[2,96,512]{2,1,0:T(8,128)S(1)}, bf16[2,512,512]{2,1,0:T(8,128)(2,1)S(1)}, bf16[2,512,512]{2,1,0:T(8,128)(2,1)S(1)}, f32[8,512]{1,0:T(8,128)S(1)}) custom-call(f32[1,1,2,512,512]{4,3,2,1,0:T(8,128)S(1)} %copy-done.2, f32[1,512]{1,0:T(1,128)S(1)} %copy-done.4, f32[1,1,5,2,96,512]{5,4,3,2,1,0:T(8,128)S(1)} %copy-done, ...), custom_call_target="tpu_custom_call" | custom-call | flops 1 | bytes 1 | tf_op jit(solution)/shard_map/pallas_call | solution.py:107
  7.1 0.2 collective-permute-start.2
  7.3 10.5 %collective-permute-done.2.arrived = f32[2,96,512]{2,1,0:T(8,128)S(1)} collective-permute-done((f32[2,96,512]{2,1,0:T(8,128)S(1)}, f32[2,96,512]{2,1,0:T(8,128)S(1)}, u32[]{:S(2)}, u32[]{:S(2)}) %collective-permute-start.2) | collective-permute-done | bytes 393248 | tf_op jit(solution)/shard_map/ppermute | solution.py:285
  17.9 0.0 copy-start.1
  17.9 0.0 copy-start.5
  17.9 0.0 copy-start.6
  17.9 0.1 collective-permute-start
  18.0 1.7 %collective-permute-done.arrived = f32[2,96,512]{2,1,0:T(8,128)S(1)} collective-permute-done((f32[2,96,512]{2,1,0:T(8,128)S(1)}, f32[2,96,512]{2,1,0:T(8,128)S(1)}, u32[]{:S(2)}, u32[]{:S(2)}) %collective-permute-start) | collective-permute-done | bytes 393248 | tf_op jit(solution)/shard_map/ppermute | solution.py:282
  19.7 0.0 copy-done.1
  19.7 0.0 copy-done.5
  19.7 0.0 copy-done.6
  19.7 1.4 %shard_map.79 = (f32[2,96,512]{2,1,0:T(8,128)S(1)}, f32[8,512]{1,0:T(8,128)S(1)}) custom-call(f32[2,96,512]{2,1,0:T(8,128)S(1)} %collective-permute-done.arrived, f32[1,1,5,2,96,512]{5,4,3,2,1,0:T(8,128)S(1)} %copy-done.1, f32[1,512]{1,0:T(1,128)S(1)} %copy-done.4, s32[4,96]{1,0:T(4,128)S(1)} %copy-done.5, ...), custom_call_target="tpu_custom_call", output_to_operand_aliasing={{1}: (7, {})} | custom-call | flops 1 | bytes 1 | tf_op jit(solution)/shard_map/pallas_call | solution.py:163
  21.1 0.6 shard_map.80
  21.6 0.3 collective-permute-start.3
  22.0 0.0 collective-permute-start.1
  22.0 1.4 %collective-permute-done.3.arrived = f32[2,96,512]{2,1,0:T(8,128)S(1)} collective-permute-done((f32[2,96,512]{2,1,0:T(8,128)S(1)}, f32[2,96,512]{2,1,0:T(8,128)S(1)}, u32[]{:S(2)}, u32[]{:S(2)}) %collective-permute-start.3) | collective-permute-done | bytes 393248 | tf_op jit(solution)/shard_map/ppermute | solution.py:282
  23.4 1.4 %shard_map.81 = (f32[2,96,512]{2,1,0:T(8,128)S(1)}, f32[8,512]{1,0:T(8,128)S(1)}) custom-call(f32[2,96,512]{2,1,0:T(8,128)S(1)} %collective-permute-done.3.arrived, f32[1,1,5,2,96,512]{5,4,3,2,1,0:T(8,128)S(1)} %copy-done.1, f32[1,512]{1,0:T(1,128)S(1)} %copy-done.4, s32[4,96]{1,0:T(4,128)S(1)} %copy-done.5, ...), custom_call_target="tpu_custom_call", output_to_operand_aliasing={{1}: (7, {})} | custom-call | flops 1 | bytes 1 | tf_op jit(solution)/shard_map/pallas_call | solution.py:163
  24.8 8.0 %collective-permute-done.1.arrived = f32[2,96,512]{2,1,0:T(8,128)S(1)} collective-permute-done((f32[2,96,512]{2,1,0:T(8,128)S(1)}, f32[2,96,512]{2,1,0:T(8,128)S(1)}, u32[]{:S(2)}, u32[]{:S(2)}) %collective-permute-start.1) | collective-permute-done | bytes 393248 | tf_op jit(solution)/shard_map/ppermute | solution.py:285
  32.8 0.6 shard_map.82
  33.4 0.1 collective-permute-start.4
  33.5 0.1 collective-permute-start.6
  33.5 1.6 %collective-permute-done.4.arrived = f32[2,96,512]{2,1,0:T(8,128)S(1)} collective-permute-done((f32[2,96,512]{2,1,0:T(8,128)S(1)}, f32[2,96,512]{2,1,0:T(8,128)S(1)}, u32[]{:S(2)}, u32[]{:S(2)}) %collective-permute-start.4) | collective-permute-done | bytes 393248 | tf_op jit(solution)/shard_map/ppermute | solution.py:282
  35.2 1.4 %shard_map.83 = (f32[2,96,512]{2,1,0:T(8,128)S(1)}, f32[8,512]{1,0:T(8,128)S(1)}) custom-call(f32[2,96,512]{2,1,0:T(8,128)S(1)} %collective-permute-done.4.arrived, f32[1,1,5,2,96,512]{5,4,3,2,1,0:T(8,128)S(1)} %copy-done.1, f32[1,512]{1,0:T(1,128)S(1)} %copy-done.4, s32[4,96]{1,0:T(4,128)S(1)} %copy-done.5, ...), custom_call_target="tpu_custom_call", output_to_operand_aliasing={{1}: (7, {})} | custom-call | flops 1 | bytes 1 | tf_op jit(solution)/shard_map/pallas_call | solution.py:163
  36.6 7.8 %collective-permute-done.6.arrived = f32[2,96,512]{2,1,0:T(8,128)S(1)} collective-permute-done((f32[2,96,512]{2,1,0:T(8,128)S(1)}, f32[2,96,512]{2,1,0:T(8,128)S(1)}, u32[]{:S(2)}, u32[]{:S(2)}) %collective-permute-start.6) | collective-permute-done | bytes 393248 | tf_op jit(solution)/shard_map/ppermute | solution.py:285
  44.4 0.6 shard_map.84
  45.0 0.1 collective-permute-start.7
  45.0 0.1 collective-permute-start.5
  45.1 1.6 %collective-permute-done.7.from_mate.refs_1_ = f32[2,96,512]{2,1,0:T(8,128)S(1)} collective-permute-done((f32[2,96,512]{2,1,0:T(8,128)S(1)}, f32[2,96,512]{2,1,0:T(8,128)S(1)}, u32[]{:S(2)}, u32[]{:S(2)}) %collective-permute-start.7) | collective-permute-done | bytes 393248 | tf_op jit(solution)/shard_map/ppermute | solution.py:282
  46.7 9.2 %collective-permute-done.5.from_above.refs_0_ = f32[2,96,512]{2,1,0:T(8,128)S(1)} collective-permute-done((f32[2,96,512]{2,1,0:T(8,128)S(1)}, f32[2,96,512]{2,1,0:T(8,128)S(1)}, u32[]{:S(2)}, u32[]{:S(2)}) %collective-permute-start.5) | collective-permute-done | bytes 393248 | tf_op jit(solution)/shard_map/ppermute | solution.py:285
  55.9 0.6 %shard_map.86 = (f32[1,256]{1,0:T(1,128)S(1)}, f32[1,256]{1,0:T(1,128)S(1)}) custom-call(f32[2,96,512]{2,1,0:T(8,128)S(1)} %collective-permute-done.5.from_above.refs_0_, f32[2,96,512]{2,1,0:T(8,128)S(1)} %collective-permute-done.7.from_mate.refs_1_, f32[1,1,5,2,96,512]{5,4,3,2,1,0:T(8,128)S(1)} %copy-done.1, f32[1,512]{1,0:T(1,128)S(1)} %copy-done.4, ...), custom_call_target="tpu_custom_call" | custom-call | flops 1 | bytes 1 | tf_op jit(solution)/shard_map/pallas_call | solution.py:210
  56.6 1.3 %collective-permute-start.8 = (f32[1,256]{1,0:T(1,128)S(1)}, f32[1,256]{1,0:T(1,128)S(1)}, u32[]{:S(2)}, u32[]{:S(2)}) collective-permute-start(f32[1,256]{1,0:T(1,128)S(1)} %get-tuple-element.45), channel_id=1, source_target_pairs={{0,1},{1,0},{2,3},{3,2},{4,5},{5,4},{6,7},{7,6},{8,9},{9,8},{10,11... | collective-permute-start | bytes 3080 | tf_op jit(solution)/shard_map/ppermute | solution.py:306
  57.8 2.2 %shard_map.85 = f32[2,96,512]{2,1,0:T(8,128)} custom-call(f32[2,96,512]{2,1,0:T(8,128)S(1)} %collective-permute-done.5.from_above.refs_0_, f32[2,96,512]{2,1,0:T(8,128)S(1)} %collective-permute-done.7.from_mate.refs_1_, f32[1,1,5,2,96,512]{5,4,3,2,1,0:T(8,128)S(1)} %copy-done.1, f32[1,512]{1,0:T(1,128)S(1)} %copy-done.4, s32[4,96]{1,0:T(4,128)S(1)} %copy-done.5, ...), custom_call_target="tpu_custom_call" | custom-call | flops 1 | bytes 1 | tf_op jit(solution)/shard_map/pallas_call | solution.py:239
  60.0 0.0 collective-permute-done.8
  60.0 0.6 add.3
  (1 shorter events, 0.0 us)
Async XLA Ops:
  0.6 1.5 %copy-start = (f32[1,1,5,2,96,512]{5,4,3,2,1,0:T(8,128)S(1)}, f32[1,1,5,2,96,512]{5,4,3,2,1,0:T(8,128)}, u32[]{:S(2)}) copy-start(f32[1,1,5,2,96,512]{5,4,3,2,1,0:T(8,128)} %refs_2_.5) | copy-start | bytes 5898244
  2.2 1.6 %copy-start.2 = (f32[1,1,2,512,512]{4,3,2,1,0:T(8,128)S(1)}, f32[1,1,2,512,512]{4,3,2,1,0:T(8,128)}, u32[]{:S(2)}) copy-start(f32[1,1,2,512,512]{4,3,2,1,0:T(8,128)} %refs_0_.3) | copy-start | bytes 6291460
  3.8 1.0 %copy-start.3 = (f32[1,1,2,96,512]{4,3,2,1,0:T(8,128)S(1)}, f32[1,1,2,96,512]{4,3,2,1,0:T(8,128)}, u32[]{:S(2)}) copy-start(f32[1,1,2,96,512]{4,3,2,1,0:T(8,128)} %refs_3_.4) | copy-start | bytes 1179652
  4.8 0.7 %copy-start.4 = (f32[1,512]{1,0:T(1,128)S(1)}, f32[1,512]{1,0:T(1,128)}, u32[]{:S(2)}) copy-start(f32[1,512]{1,0:T(1,128)} %refs_3_.5) | copy-start | bytes 6148
  7.1 10.7 %collective-permute-start.2 = (f32[2,96,512]{2,1,0:T(8,128)S(1)}, f32[2,96,512]{2,1,0:T(8,128)S(1)}, u32[]{:S(2)}, u32[]{:S(2)}) collective-permute-start(f32[2,96,512]{2,1,0:T(8,128)S(1)} %get-tuple-element.24.refs_4_), channel_id=1, source_target_pairs={{0,2},{2,4},{4,6},{6,8},{8,0},{10,12},{12,14},{14,16},{16,10},{18,... | collective-permute-start | bytes 1179656 | tf_op jit(solution)/shard_map/ppermute | solution.py:285
  17.9 1.8 %copy-start.1 = (f32[1,1,5,2,96,512]{5,4,3,2,1,0:T(8,128)S(1)}, f32[1,1,5,2,96,512]{5,4,3,2,1,0:T(8,128)}, u32[]{:S(2)}) copy-start(f32[1,1,5,2,96,512]{5,4,3,2,1,0:T(8,128)} %refs_2_.5) | copy-start | bytes 5898244
  17.9 1.8 %copy-start.5 = (s32[4,96]{1,0:T(4,128)S(1)}, s32[4,96]{1,0:T(4,128)}, u32[]{:S(2)}) copy-start(s32[4,96]{1,0:T(4,128)} %refs_4_.1) | copy-start | bytes 4612
  17.9 1.8 %copy-start.6 = (f32[1,4,2]{1,2,0:T(2,128)S(1)}, f32[1,4,2]{1,2,0:T(2,128)}, u32[]{:S(2)}) copy-start(f32[1,4,2]{1,2,0:T(2,128)} %param.11) | copy-start | bytes 100
  17.9 1.8 %collective-permute-start = (f32[2,96,512]{2,1,0:T(8,128)S(1)}, f32[2,96,512]{2,1,0:T(8,128)S(1)}, u32[]{:S(2)}, u32[]{:S(2)}) collective-permute-start(f32[2,96,512]{2,1,0:T(8,128)S(1)} %get-tuple-element.28), channel_id=1, source_target_pairs={{0,2},{2,0},{4,6},{6,4},{8,10},{10,8},{12,14},{14,12},{16,18},{18,... | collective-permute-start | bytes 1179656 | tf_op jit(solution)/shard_map/ppermute | solution.py:282
  21.6 1.8 %collective-permute-start.3 = (f32[2,96,512]{2,1,0:T(8,128)S(1)}, f32[2,96,512]{2,1,0:T(8,128)S(1)}, u32[]{:S(2)}, u32[]{:S(2)}) collective-permute-start(f32[2,96,512]{2,1,0:T(8,128)S(1)} %get-tuple-element.34), channel_id=1, source_target_pairs={{0,2},{2,0},{4,6},{6,4},{8,10},{10,8},{12,14},{14,12},{16,18},{18,... | collective-permute-start | bytes 1179656 | tf_op jit(solution)/shard_map/ppermute | solution.py:282
  22.0 10.8 %collective-permute-start.1 = (f32[2,96,512]{2,1,0:T(8,128)S(1)}, f32[2,96,512]{2,1,0:T(8,128)S(1)}, u32[]{:S(2)}, u32[]{:S(2)}) collective-permute-start(f32[2,96,512]{2,1,0:T(8,128)S(1)} %get-tuple-element.32), channel_id=1, source_target_pairs={{0,2},{2,4},{4,6},{6,8},{8,0},{10,12},{12,14},{14,16},{16,10},{18,... | collective-permute-start | bytes 1179656 | tf_op jit(solution)/shard_map/ppermute | solution.py:285
  33.4 1.8 %collective-permute-start.4 = (f32[2,96,512]{2,1,0:T(8,128)S(1)}, f32[2,96,512]{2,1,0:T(8,128)S(1)}, u32[]{:S(2)}, u32[]{:S(2)}) collective-permute-start(f32[2,96,512]{2,1,0:T(8,128)S(1)} %get-tuple-element.37), channel_id=1, source_target_pairs={{0,2},{2,0},{4,6},{6,4},{8,10},{10,8},{12,14},{14,12},{16,18},{18,... | collective-permute-start | bytes 1179656 | tf_op jit(solution)/shard_map/ppermute | solution.py:282
  33.5 10.9 %collective-permute-start.6 = (f32[2,96,512]{2,1,0:T(8,128)S(1)}, f32[2,96,512]{2,1,0:T(8,128)S(1)}, u32[]{:S(2)}, u32[]{:S(2)}) collective-permute-start(f32[2,96,512]{2,1,0:T(8,128)S(1)} %get-tuple-element.40), channel_id=1, source_target_pairs={{0,2},{2,4},{4,6},{6,8},{8,0},{10,12},{12,14},{14,16},{16,10},{18,... | collective-permute-start | bytes 1179656 | tf_op jit(solution)/shard_map/ppermute | solution.py:285
  45.0 1.8 %collective-permute-start.7 = (f32[2,96,512]{2,1,0:T(8,128)S(1)}, f32[2,96,512]{2,1,0:T(8,128)S(1)}, u32[]{:S(2)}, u32[]{:S(2)}) collective-permute-start(f32[2,96,512]{2,1,0:T(8,128)S(1)} %get-tuple-element.42), channel_id=1, source_target_pairs={{0,2},{2,0},{4,6},{6,4},{8,10},{10,8},{12,14},{14,12},{16,18},{18,... | collective-permute-start | bytes 1179656 | tf_op jit(solution)/shard_map/ppermute | solution.py:282
  45.0 10.9 %collective-permute-start.5 = (f32[2,96,512]{2,1,0:T(8,128)S(1)}, f32[2,96,512]{2,1,0:T(8,128)S(1)}, u32[]{:S(2)}, u32[]{:S(2)}) collective-permute-start(f32[2,96,512]{2,1,0:T(8,128)S(1)} %get-tuple-element.39), channel_id=1, source_target_pairs={{0,2},{2,4},{4,6},{6,8},{8,0},{10,12},{12,14},{14,16},{16,10},{18,... | collective-permute-start | bytes 1179656 | tf_op jit(solution)/shard_map/ppermute | solution.py:285
  56.6 3.5 %collective-permute-start.8 = (f32[1,256]{1,0:T(1,128)S(1)}, f32[1,256]{1,0:T(1,128)S(1)}, u32[]{:S(2)}, u32[]{:S(2)}) collective-permute-start(f32[1,256]{1,0:T(1,128)S(1)} %get-tuple-element.45), channel_id=1, source_target_pairs={{0,1},{1,0},{2,3},{3,2},{4,5},{5,4},{6,7},{7,6},{8,9},{9,8},{10,11... | collective-permute-start | bytes 3080 | tf_op jit(solution)/shard_map/ppermute | solution.py:306

commit v4 on v3

v4 whole, which is shorter than its diff:
```python
import functools
import math

import jax
import jax.numpy as jnp
from jax import lax
from jax.experimental import pallas as pl
from jax.experimental.pallas import tpu as pltpu
from jax.sharding import PartitionSpec as P

TICKS = 5
VMEM_LIMIT = 24 * 1024 * 1024
QUICK = pl.CostEstimate(flops=1, bytes_accessed=1, transcendentals=0)
LONGER = pl.CostEstimate(flops=500000000, bytes_accessed=1, transcendentals=0)
PARAMS = pltpu.CompilerParams(vmem_limit_bytes=VMEM_LIMIT)


def pinned(value):
    return pltpu.with_memory_space_constraint(value, pltpu.VMEM)


def kept(value):
    return pltpu.with_memory_space_constraint(value, pltpu.HBM)


IN_VMEM = pl.BlockSpec(memory_space=pltpu.VMEM)
IN_HBM = pl.BlockSpec(memory_space=pltpu.HBM)


def is_odd():
    return lax.axis_index("depth") % 2 == 1


def split(value):
    high = value.astype(jnp.bfloat16)
    low = (value - high.astype(jnp.float32)).astype(jnp.bfloat16)
    return high, low


def fold(product):
    return jnp.sum(product.reshape(-1, 8, product.shape[1]), axis=0)


def take(pair, waves, contrast, grad_in, grad, left):
    if grad is not None:
        term = fold(pair[0] * waves[0]) + fold(pair[1] * waves[1])
        grad[...] = term if grad_in is None else grad_in[...] + term
    if left is not None:
        shots = pair[0].shape[0]
        for part in range(2):
            high, low = split(pair[part] + contrast[...] * waves[part])
            left[pl.ds(part * shots, shots), :] = high
            left[pl.ds((2 + part) * shots, shots), :] = low


def multiply(left, high, low, columns):
    shots = left.shape[0] // 4
    dot = functools.partial(jnp.dot, preferred_element_type=jnp.float32)

    def by(part):
        big = dot(left[...], high[part, :, columns])
        small = dot(left[pl.ds(0, 2 * shots), :], low[part, :, columns])
        real = big[:shots] + (big[2 * shots : 3 * shots] + small[:shots])
        imag = big[shots : 2 * shots] + (big[3 * shots :] + small[shots:])
        return real, imag

    real_real, imag_real = by(0)
    real_imag, imag_imag = by(1)
    return real_real - imag_imag, real_imag + imag_real


def injected(tick, sites, pulse, shape):
    shots, breadth = shape
    row = lax.broadcasted_iota(jnp.int32, (shots, shots), 0)
    column = lax.broadcasted_iota(jnp.int32, (shots, shots), 1)
    spread = jnp.broadcast_to(sites[pl.ds(tick - 1, 1), :], (shots, shots)).astype(jnp.float32)
    site = jnp.sum(jnp.where(row == column, spread, 0.0), axis=1, keepdims=True)
    lanes = lax.broadcasted_iota(jnp.int32, (shots, breadth), 1).astype(jnp.float32)
    hit = lanes == site
    return [jnp.where(hit, pulse[pl.ds(part, 1), pl.ds(tick - 1, 1)], 0.0) for part in range(2)]


def first_kernel(parity, chained, *refs):
    operator, contrast, residual, panel = refs[:4]
    outs = 2 - parity
    refs = refs[7:] if chained else refs[4:]
    out = refs[:outs]
    high, low, grad, whole, wave, arrived, left, sems = refs[outs:]

    @pl.when(is_odd() if parity else jnp.logical_not(is_odd()))
    def _():
        copies = [
            pltpu.make_async_copy(residual.at[0, 0, 0], wave, sems.at[0]),
            pltpu.make_async_copy(panel.at[0, 0], arrived, sems.at[1]),
            pltpu.make_async_copy(operator.at[0, 0, 0], whole.at[0], sems.at[2]),
            pltpu.make_async_copy(operator.at[0, 0, 1], whole.at[1], sems.at[3]),
        ]
        for copy in copies:
            copy.start()
        copies[0].wait()
        copies[1].wait()
        take(arrived, wave, contrast, None, grad, left)
        for part in range(2):
            copies[2 + part].wait()
            high[part], low[part] = split(whole[part])
        store(out, multiply(left, high, low, slice(None)))


def store(out, pair):
    if len(out) == 1:
        out[0][0], out[0][1] = pair
    else:
        out[0][...], out[1][...] = pair


def panel_shape(parity, shots, breadth):
    if parity:
        return [pltpu.VMEM((2, shots, breadth), jnp.float32)]
    return [pltpu.VMEM((shots, breadth), jnp.float32)] * 2


def first(parity, operator, contrast, residual, panel, carried):
    shots, breadth = panel.shape[3:]
    half = pltpu.VMEM((2, breadth, breadth), jnp.bfloat16)
    outs = panel_shape(parity, shots, breadth)
    return pl.pallas_call(
        functools.partial(first_kernel, parity, bool(carried)),
        out_shape=(*outs, half, half, pltpu.VMEM((8, breadth), jnp.float32)),
        in_specs=[IN_HBM, IN_VMEM, IN_HBM, IN_HBM] + [IN_VMEM] * len(carried),
        out_specs=(IN_VMEM,) * (len(outs) + 3),
        scratch_shapes=[
            pltpu.VMEM((2, breadth, breadth), jnp.float32),
            pltpu.VMEM((2, shots, breadth), jnp.float32),
            pltpu.VMEM((2, shots, breadth), jnp.float32),
            pltpu.VMEM((4 * shots, breadth), jnp.bfloat16),
            pltpu.SemaphoreType.DMA((4,)),
        ],
        input_output_aliases={4 + i: len(outs) + i for i in range(len(carried))},
        compiler_params=PARAMS,
        cost_estimate=QUICK if parity else LONGER,
        name=f"first_{parity}",
    )(kept(operator), contrast, kept(residual), kept(panel), *[pinned(value) for value in carried])


def arrive(tick, parity, panel, shared, grad_in, grad, left):
    residual, contrast, sites, pulse = shared
    waves = residual.at[0, 0, tick]
    if parity:
        take([part[...] for part in panel], waves, contrast, grad_in, grad, left)
        return
    surface = lax.axis_index("depth") == 0

    @pl.when(surface)
    def _():
        take(injected(tick, sites, pulse, panel.shape[1:]), waves, contrast, grad_in, grad, left)

    @pl.when(jnp.logical_not(surface))
    def _():
        take(panel, waves, contrast, grad_in, grad, left)


def step_kernel(tick, parity, *refs):
    panels = 1 + parity
    panel = refs[:panels] if parity else refs[0]
    shared, (high, low, grad_in) = refs[panels : panels + 4], refs[panels + 4 : panels + 7]
    *out, grad, left = refs[panels + 7 :]

    @pl.when(is_odd() if parity else jnp.logical_not(is_odd()))
    def _():
        arrive(tick, parity, panel, shared, grad_in, grad, left)
        store(out, multiply(left, high, low, slice(None)))


def step(tick, parity, panel, shared, high, low, grad):
    shots, breadth = panel[0].shape[-2:]
    outs = panel_shape(parity, shots, breadth)
    operands = [pinned(value) for value in (*panel, *shared, high, low, grad)]
    return pl.pallas_call(
        functools.partial(step_kernel, tick, parity),
        out_shape=(*outs, pltpu.VMEM(grad.shape, jnp.float32)),
        in_specs=[IN_VMEM] * len(operands),
        out_specs=(IN_VMEM,) * (len(outs) + 1),
        scratch_shapes=[pltpu.VMEM((4 * shots, breadth), jnp.bfloat16)],
        input_output_aliases={len(operands) - 1: len(outs)},
        compiler_params=PARAMS,
        cost_estimate=QUICK if parity else LONGER,
        name=f"step_{tick}_{parity}",
    )(*operands)


def final_arrive(refs, grad_in, grad, left):
    from_above, from_mate, shared = refs[0], refs[1:3], refs[3:7]

    @pl.when(is_odd())
    def _():
        arrive(TICKS - 1, 1, from_mate, shared, grad_in, grad, left)

    @pl.when(jnp.logical_not(is_odd()))
    def _():
        arrive(TICKS - 1, 0, from_above, shared, grad_in, grad, left)


def gradient_chunks(panels, shared, grad, scale):
    breadth = grad.shape[1]
    count = lax.axis_size("freq")
    width = breadth // count

    def body(*refs):
        chunks, total = refs[8 : 8 + count], refs[8 + count]
        final_arrive(refs, refs[7], total, None)
        gradient = jnp.sum(total[...], axis=0, keepdims=True) * scale
        me = lax.axis_index("freq")
        for distance in range(count):
            owner = lax.rem(me + distance, count)
            chunk = jnp.zeros((1, width), jnp.float32)
            for place in range(count):
                piece = gradient[:, place * width : (place + 1) * width]
                chunk = jnp.where(owner == place, piece, chunk)
            chunks[distance][...] = chunk

    operands = [pinned(value) for value in (*panels, *shared, grad)]
    return pl.pallas_call(
        body,
        out_shape=(pltpu.VMEM((1, width), jnp.float32),) * count,
        in_specs=[IN_VMEM] * len(operands),
        out_specs=(IN_VMEM,) * count,
        scratch_shapes=[pltpu.VMEM(grad.shape, jnp.float32)],
        compiler_params=PARAMS,
        cost_estimate=QUICK,
        name="gradient",
    )(*operands)


def last_kernel(*refs):
    high, low, out, left, held, sems = refs[7:]
    final_arrive(refs, None, None, left)
    halves = held.shape[0]
    width = held.shape[3]
    copies = []
    for half in range(halves):
        columns = pl.ds(half * width, width)
        held[half, 0], held[half, 1] = multiply(left, high, low, columns)
        copies.append(pltpu.make_async_copy(held.at[half], out.at[:, :, columns], sems.at[half]))
        copies[-1].start()
    for copy in copies:
        copy.wait()


def last(panels, shared, high, low):
    shots, breadth = panels[0].shape[1:]
    operands = [pinned(value) for value in (*panels, *shared, high, low)]
    return pl.pallas_call(
        last_kernel,
        out_shape=jax.ShapeDtypeStruct((2, shots, breadth), jnp.float32),
        in_specs=[IN_VMEM] * len(operands),
        out_specs=IN_HBM,
        scratch_shapes=[
            pltpu.VMEM((4 * shots, breadth), jnp.bfloat16),
            pltpu.VMEM((2, 2, shots, breadth // 2), jnp.float32),
            pltpu.SemaphoreType.DMA((2,)),
        ],
        compiler_params=PARAMS,
        cost_estimate=QUICK,
        name="last",
    )(*operands)


def cross_route(levels):
    route = {level: (level + 1) % levels for level in range(levels)}
    chips = levels // 2
    if chips % 2 == 0:
        for chip in range(chips - 1, 1, -2):
            route[levels - 1 if chip == chips - 1 else 2 * chip] = 2 * (chip - 2) + 1
        route[2 if chips > 2 else levels - 1] = 0
    return sorted(route.items())


def local(
    extrapolation_operator,
    impedance_contrast,
    ascending_residual,
    arriving_downward_matrices,
    shot_node_indices,
    emitted_pulse,
):
    levels = lax.axis_size("depth")
    freqs = lax.axis_size("freq")
    shots = arriving_downward_matrices.shape[3]
    mate_route = [(level, level ^ 1) for level in range(levels)]
    down_route = cross_route(levels)
    shared = (ascending_residual, impedance_contrast, shot_node_indices, emitted_pulse[0].T)

    def mate(parts):
        return [lax.ppermute(part, "depth", mate_route) for part in parts]

    def down(panel):
        return lax.ppermute(panel, "depth", down_route)

    start = (extrapolation_operator, pinned(impedance_contrast), ascending_residual, arriving_downward_matrices)
    odd, *carried = first(1, *start, ())
    from_above = down(odd)
    *even, high, low, grad = first(0, *start, carried)
    from_mate = mate(even)
    for tick in range(1, TICKS - 1):
        odd, grad = step(tick, 1, from_mate, shared, high, low, grad)
        later = down(odd)
        *even, grad = step(tick, 0, [from_above], shared, high, low, grad)
        from_mate = mate(even)
        from_above = later

    panels = (from_above, *from_mate)
    chunks = gradient_chunks(panels, shared, grad, 1.0 / math.sqrt(shots * TICKS))
    out = last(panels, shared, high, low)
    gradient = chunks[0]
    for distance in range(1, freqs):
        route = [(i, (i + distance) % freqs) for i in range(freqs)]
        gradient = gradient + lax.ppermute(chunks[distance], "freq", route)
    return (out[None, None], gradient)


def solution(mesh):
    placed = (
        P("freq", "depth", None, None, None),
        P("depth", None),
        P("freq", "depth", None, None, None, None),
        P("freq", "depth", None, None, None),
        P(),
        P("freq", None, None),
    )
    return jax.shard_map(
        local,
        mesh=mesh,
        in_specs=placed,
        out_specs=(P("freq", "depth", None, None, None), P("depth", "freq")),
        check_vma=False,
    )
```

time: 60.8 us -> 32.6 us (0.54)
  the two profiles are of different devices: /device:TPU:25 before, /device:TPU:0 now
where the time goes in v4:
time: 32.6 us; the launch traced here: 32.5 us
  waiting for transfers between devices  11.6 us (36%)
  starting transfers between devices  11.1 us (34%)
  Pallas kernels  7.77 us (24%)
  between operations  0.75 us (2%)
  local copies, waits for them, and re-layouts  0.69 us (2%)
  other arithmetic  0.57 us (2%)
    ppermute x4, waiting for transfers between devices, down(): return lax.ppermute(panel, 'depth', down_route)  7.96 us
    ppermute x4, starting transfers between devices, down(): return lax.ppermute(panel, 'depth', down_route)  6.42 us
    ppermute x8, waiting for transfers between devices, mate(): return [lax.ppermute(part, 'depth', mate_route) for part in parts]  3.64 us
    pallas_call x6, Pallas kernels, step(): pl.pallas_call(functools.partial(step_kernel, tick, parity), out_shape=(*...  3.02 us
    pallas_call x2, Pallas kernels, first(): pl.pallas_call(functools.partial(first_kernel, parity, bool(carried)), ou...  2.83 us
    ppermute x1, starting transfers between devices, local(): gradient = gradient + lax.ppermute(chunks[distance], 'freq', route)  2.39 us
    ppermute x8, starting transfers between devices, mate(): return [lax.ppermute(part, 'depth', mate_route) for part in parts]  2.27 us
    pallas_call x1, Pallas kernels, last(): pl.pallas_call(last_kernel, out_shape=jax.ShapeDtypeStruct((2, shots, bre...  1.73 us
  transfers between devices with their start and end apart: 13, of which 9 were waited for; matrix products, arithmetic and copies ran while one was open for 0% of the time, Pallas kernels for 23%

profile of v4, /device:TPU:0, one launch (start us, length us, event | category | flops | bytes accessed | tf_op | source)
XLA Modules:
  0.0 32.5 jit_solution(6314801368192413803)
XLA Ops:
  0.6 0.0 copy-start.1
  0.6 0.7 %copy-done.1 = f32[1,512]{1,0:T(1,128)S(1)} copy-done((f32[1,512]{1,0:T(1,128)S(1)}, f32[1,512]{1,0:T(1,128)}, u32[]{:S(2)}) %copy-start.1) | copy-done | bytes 2072
  1.4 3.1 %collective-permute-start.3 = (f32[2,96,512]{2,1,0:T(8,128)S(1)}, f32[2,96,512]{2,1,0:T(8,128)S(1)}, u32[]{:S(2)}, u32[]{:S(2)}) collective-permute-start(f32[2,96,512]{2,1,0:T(8,128)S(1)} %get-tuple-element.37), channel_id=1, source_target_pairs={{0,2},{2,4},{4,0},{6,8},{8,10},{10,12},{12,6},{14,16},{16,18},{18,... | collective-permute-start | bytes 1179656 | tf_op jit(solution)/shard_map/ppermute | solution.py:297
  4.5 0.0 copy-start
  4.5 0.0 copy-start.2
  4.5 0.0 copy-start.3
  4.5 2.8 %first_0.1 = (f32[96,512]{1,0:T(8,128)S(1)}, f32[96,512]{1,0:T(8,128)S(1)}, bf16[2,512,512]{2,1,0:T(8,128)(2,1)S(1)}, bf16[2,512,512]{2,1,0:T(8,128)(2,1)S(1)}, f32[8,512]{1,0:T(8,128)S(1)}) custom-call(f32[1,1,2,512,512]{4,3,2,1,0:T(8,128)} %refs_0_.3, f32[1,512]{1,0:T(1,128)S(1)} %copy-done.1, ...), custom_call_target="tpu_custom_call", output_to_operand_aliasing={{2}: (4, {}), {3}: (5, {}), {4}: (6, {})} | custom-call | flops 500000000 | bytes 1 | tf_op jit(solution)/shard_map/first_0/pallas_call | solution.py:126
  7.3 0.1 collective-permute-start
  7.4 0.5 %collective-permute-start.1 = (f32[96,512]{1,0:T(8,128)S(1)}, f32[96,512]{1,0:T(8,128)S(1)}, u32[]{:S(2)}, u32[]{:S(2)}) collective-permute-start(f32[96,512]{1,0:T(8,128)S(1)} %get-tuple-element.32), channel_id=1, source_target_pairs={{0,2},{2,0},{4,6},{6,4},{8,10},{10,8},{12,14},{14,12},{16,18},{18,... | collective-permute-start | bytes 589832 | tf_op jit(solution)/shard_map/ppermute | solution.py:294
  7.9 0.9 %collective-permute-done.refs_0_ = f32[96,512]{1,0:T(8,128)S(1)} collective-permute-done((f32[96,512]{1,0:T(8,128)S(1)}, f32[96,512]{1,0:T(8,128)S(1)}, u32[]{:S(2)}, u32[]{:S(2)}) %collective-permute-start) | collective-permute-done | bytes 196640 | tf_op jit(solution)/shard_map/ppermute | solution.py:294
  8.8 0.3 collective-permute-done.1.refs_1_
  9.1 0.0 copy-done
  9.1 0.0 copy-done.2
  9.1 0.0 copy-done.3
  9.1 1.1 %collective-permute-start.2 = (f32[2,96,512]{2,1,0:T(8,128)S(1)}, f32[2,96,512]{2,1,0:T(8,128)S(1)}, u32[]{:S(2)}, u32[]{:S(2)}) collective-permute-start(f32[2,96,512]{2,1,0:T(8,128)S(1)} %get-tuple-element.36), channel_id=1, source_target_pairs={{0,2},{2,4},{4,0},{6,8},{8,10},{10,12},{12,6},{14,16},{16,18},{18,... | collective-permute-start | bytes 1179656 | tf_op jit(solution)/shard_map/ppermute | solution.py:297
  10.2 0.0 collective-permute-done.3.refs_0_
  10.2 1.0 %step_1_0.1 = (f32[96,512]{1,0:T(8,128)S(1)}, f32[96,512]{1,0:T(8,128)S(1)}, f32[8,512]{1,0:T(8,128)S(1)}) custom-call(f32[2,96,512]{2,1,0:T(8,128)S(1)} %collective-permute-done.3.refs_0_, f32[1,1,5,2,96,512]{5,4,3,2,1,0:T(8,128)S(1)} %copy-done, f32[1,512]{1,0:T(1,128)S(1)} %copy-done.1, s32[4,96]{1,0:T(4,128)S(1)} %copy-done.2, ...), custom_call_target="tpu_custom_call", output_to_operand_aliasing={{2}: (7, {})} | custom-call | flops 500000000 | bytes 1 | tf_op jit(solution)/shard_map/step_1_0/pallas_call | solution.py:178
  11.2 0.1 collective-permute-start.4
  11.3 0.5 %collective-permute-start.5 = (f32[96,512]{1,0:T(8,128)S(1)}, f32[96,512]{1,0:T(8,128)S(1)}, u32[]{:S(2)}, u32[]{:S(2)}) collective-permute-start(f32[96,512]{1,0:T(8,128)S(1)} %get-tuple-element.40), channel_id=1, source_target_pairs={{0,2},{2,0},{4,6},{6,4},{8,10},{10,8},{12,14},{14,12},{16,18},{18,... | collective-permute-start | bytes 589832 | tf_op jit(solution)/shard_map/ppermute | solution.py:294
  11.8 0.9 %collective-permute-done.4.refs_0_ = f32[96,512]{1,0:T(8,128)S(1)} collective-permute-done((f32[96,512]{1,0:T(8,128)S(1)}, f32[96,512]{1,0:T(8,128)S(1)}, u32[]{:S(2)}, u32[]{:S(2)}) %collective-permute-start.4) | collective-permute-done | bytes 196640 | tf_op jit(solution)/shard_map/ppermute | solution.py:294
  12.7 0.3 collective-permute-done.5.refs_1_
  13.0 1.1 %collective-permute-start.9 = (f32[2,96,512]{2,1,0:T(8,128)S(1)}, f32[2,96,512]{2,1,0:T(8,128)S(1)}, u32[]{:S(2)}, u32[]{:S(2)}) collective-permute-start(f32[2,96,512]{2,1,0:T(8,128)S(1)} %get-tuple-element.47), channel_id=1, source_target_pairs={{0,2},{2,4},{4,0},{6,8},{8,10},{10,12},{12,6},{14,16},{16,18},{18,... | collective-permute-start | bytes 1179656 | tf_op jit(solution)/shard_map/ppermute | solution.py:297
  14.1 2.9 %collective-permute-done.2.refs_0_ = f32[2,96,512]{2,1,0:T(8,128)S(1)} collective-permute-done((f32[2,96,512]{2,1,0:T(8,128)S(1)}, f32[2,96,512]{2,1,0:T(8,128)S(1)}, u32[]{:S(2)}, u32[]{:S(2)}) %collective-permute-start.2) | collective-permute-done | bytes 393248 | tf_op jit(solution)/shard_map/ppermute | solution.py:297
  17.0 1.0 %step_2_0.1 = (f32[96,512]{1,0:T(8,128)S(1)}, f32[96,512]{1,0:T(8,128)S(1)}, f32[8,512]{1,0:T(8,128)S(1)}) custom-call(f32[2,96,512]{2,1,0:T(8,128)S(1)} %collective-permute-done.2.refs_0_, f32[1,1,5,2,96,512]{5,4,3,2,1,0:T(8,128)S(1)} %copy-done, f32[1,512]{1,0:T(1,128)S(1)} %copy-done.1, s32[4,96]{1,0:T(4,128)S(1)} %copy-done.2, ...), custom_call_target="tpu_custom_call", output_to_operand_aliasing={{2}: (7, {})} | custom-call | flops 500000000 | bytes 1 | tf_op jit(solution)/shard_map/step_2_0/pallas_call | solution.py:178
  18.0 0.1 collective-permute-start.6
  18.1 0.5 %collective-permute-start.7 = (f32[96,512]{1,0:T(8,128)S(1)}, f32[96,512]{1,0:T(8,128)S(1)}, u32[]{:S(2)}, u32[]{:S(2)}) collective-permute-start(f32[96,512]{1,0:T(8,128)S(1)} %get-tuple-element.44), channel_id=1, source_target_pairs={{0,2},{2,0},{4,6},{6,4},{8,10},{10,8},{12,14},{14,12},{16,18},{18,... | collective-permute-start | bytes 589832 | tf_op jit(solution)/shard_map/ppermute | solution.py:294
  18.6 0.9 %collective-permute-done.6.refs_0_ = f32[96,512]{1,0:T(8,128)S(1)} collective-permute-done((f32[96,512]{1,0:T(8,128)S(1)}, f32[96,512]{1,0:T(8,128)S(1)}, u32[]{:S(2)}, u32[]{:S(2)}) %collective-permute-start.6) | collective-permute-done | bytes 196640 | tf_op jit(solution)/shard_map/ppermute | solution.py:294
  19.5 0.3 collective-permute-done.7.refs_1_
  19.8 1.1 %collective-permute-start.8 = (f32[2,96,512]{2,1,0:T(8,128)S(1)}, f32[2,96,512]{2,1,0:T(8,128)S(1)}, u32[]{:S(2)}, u32[]{:S(2)}) collective-permute-start(f32[2,96,512]{2,1,0:T(8,128)S(1)} %get-tuple-element.46), channel_id=1, source_target_pairs={{0,2},{2,4},{4,0},{6,8},{8,10},{10,12},{12,6},{14,16},{16,18},{18,... | collective-permute-start | bytes 1179656 | tf_op jit(solution)/shard_map/ppermute | solution.py:297
  20.9 0.7 %collective-permute-done.9.refs_0_ = f32[2,96,512]{2,1,0:T(8,128)S(1)} collective-permute-done((f32[2,96,512]{2,1,0:T(8,128)S(1)}, f32[2,96,512]{2,1,0:T(8,128)S(1)}, u32[]{:S(2)}, u32[]{:S(2)}) %collective-permute-start.9) | collective-permute-done | bytes 393248 | tf_op jit(solution)/shard_map/ppermute | solution.py:297
  21.5 1.0 %step_3_0.1 = (f32[96,512]{1,0:T(8,128)S(1)}, f32[96,512]{1,0:T(8,128)S(1)}, f32[8,512]{1,0:T(8,128)S(1)}) custom-call(f32[2,96,512]{2,1,0:T(8,128)S(1)} %collective-permute-done.9.refs_0_, f32[1,1,5,2,96,512]{5,4,3,2,1,0:T(8,128)S(1)} %copy-done, f32[1,512]{1,0:T(1,128)S(1)} %copy-done.1, s32[4,96]{1,0:T(4,128)S(1)} %copy-done.2, ...), custom_call_target="tpu_custom_call", output_to_operand_aliasing={{2}: (7, {})} | custom-call | flops 500000000 | bytes 1 | tf_op jit(solution)/shard_map/step_3_0/pallas_call | solution.py:178
  22.6 0.1 collective-permute-start.10
  22.6 0.5 %collective-permute-start.11 = (f32[96,512]{1,0:T(8,128)S(1)}, f32[96,512]{1,0:T(8,128)S(1)}, u32[]{:S(2)}, u32[]{:S(2)}) collective-permute-start(f32[96,512]{1,0:T(8,128)S(1)} %get-tuple-element.50), channel_id=1, source_target_pairs={{0,2},{2,0},{4,6},{6,4},{8,10},{10,8},{12,14},{14,12},{16,18},{18,... | collective-permute-start | bytes 589832 | tf_op jit(solution)/shard_map/ppermute | solution.py:294
  23.1 4.4 %collective-permute-done.8.refs_0_ = f32[2,96,512]{2,1,0:T(8,128)S(1)} collective-permute-done((f32[2,96,512]{2,1,0:T(8,128)S(1)}, f32[2,96,512]{2,1,0:T(8,128)S(1)}, u32[]{:S(2)}, u32[]{:S(2)}) %collective-permute-start.8) | collective-permute-done | bytes 393248 | tf_op jit(solution)/shard_map/ppermute | solution.py:297
  27.6 0.0 collective-permute-done.10.refs_1_
  27.6 0.0 collective-permute-done.11.refs_2_
  27.6 0.2 gradient.1
  27.7 2.4 %collective-permute-start.12 = (f32[1,256]{1,0:T(1,128)S(1)}, f32[1,256]{1,0:T(1,128)S(1)}, u32[]{:S(2)}, u32[]{:S(2)}) collective-permute-start(f32[1,256]{1,0:T(1,128)S(1)} %get-tuple-element.53), channel_id=1, source_target_pairs={{0,1},{1,0},{2,3},{3,2},{4,5},{5,4},{6,7},{7,6},{8,9},{9,8},{10,11... | collective-permute-start | bytes 3080 | tf_op jit(solution)/shard_map/ppermute | solution.py:317
  30.1 1.7 %last.1 = f32[2,96,512]{2,1,0:T(8,128)} custom-call(f32[2,96,512]{2,1,0:T(8,128)S(1)} %collective-permute-done.8.refs_0_, f32[96,512]{1,0:T(8,128)S(1)} %collective-permute-done.10.refs_1_, f32[96,512]{1,0:T(8,128)S(1)} %collective-permute-done.11.refs_2_, f32[1,1,5,2,96,512]{5,4,3,2,1,0:T(8,128)S(1)} %copy-done, f32[1,512]{1,0:T(1,128)S(1)} %copy-done.1, ...), custom_call_target="tpu_custom_call" | custom-call | flops 1 | bytes 1 | tf_op jit(solution)/shard_map/last/pallas_call | solution.py:252
  31.9 0.0 collective-permute-done.12
  31.9 0.6 %add.3 = f32[1,256]{1,0:T(1,128)} add(f32[1,256]{1,0:T(1,128)S(1)} %get-tuple-element.52, f32[1,256]{1,0:T(1,128)S(1)} %collective-permute-done.12) | non-fusion elementwise | flops 256 | bytes 3072 | tf_op jit(solution)/shard_map/add | solution.py:317
  (4 shorter events, 0.1 us)
Async XLA Ops:
  0.6 0.7 %copy-start.1 = (f32[1,512]{1,0:T(1,128)S(1)}, f32[1,512]{1,0:T(1,128)}, u32[]{:S(2)}) copy-start(f32[1,512]{1,0:T(1,128)} %refs_4_.9) | copy-start | bytes 6148
  1.4 8.9 %collective-permute-start.3 = (f32[2,96,512]{2,1,0:T(8,128)S(1)}, f32[2,96,512]{2,1,0:T(8,128)S(1)}, u32[]{:S(2)}, u32[]{:S(2)}) collective-permute-start(f32[2,96,512]{2,1,0:T(8,128)S(1)} %get-tuple-element.37), channel_id=1, source_target_pairs={{0,2},{2,4},{4,0},{6,8},{8,10},{10,12},{12,6},{14,16},{16,18},{18,... | collective-permute-start | bytes 1179656 | tf_op jit(solution)/shard_map/ppermute | solution.py:297
  4.5 4.6 %copy-start = (f32[1,1,5,2,96,512]{5,4,3,2,1,0:T(8,128)S(1)}, f32[1,1,5,2,96,512]{5,4,3,2,1,0:T(8,128)}, u32[]{:S(2)}) copy-start(f32[1,1,5,2,96,512]{5,4,3,2,1,0:T(8,128)} %refs_3_.19) | copy-start | bytes 5898244
  4.5 4.6 %copy-start.2 = (s32[4,96]{1,0:T(4,128)S(1)}, s32[4,96]{1,0:T(4,128)}, u32[]{:S(2)}) copy-start(s32[4,96]{1,0:T(4,128)} %refs_5_.3) | copy-start | bytes 4612
  4.5 4.6 %copy-start.3 = (f32[1,4,2]{1,2,0:T(2,128)S(1)}, f32[1,4,2]{1,2,0:T(2,128)}, u32[]{:S(2)}) copy-start(f32[1,4,2]{1,2,0:T(2,128)} %param.11) | copy-start | bytes 100
  7.3 1.5 %collective-permute-start = (f32[96,512]{1,0:T(8,128)S(1)}, f32[96,512]{1,0:T(8,128)S(1)}, u32[]{:S(2)}, u32[]{:S(2)}) collective-permute-start(f32[96,512]{1,0:T(8,128)S(1)} %get-tuple-element.31), channel_id=1, source_target_pairs={{0,2},{2,0},{4,6},{6,4},{8,10},{10,8},{12,14},{14,12},{16,18},{18,... | collective-permute-start | bytes 589832 | tf_op jit(solution)/shard_map/ppermute | solution.py:294
  7.4 1.7 %collective-permute-start.1 = (f32[96,512]{1,0:T(8,128)S(1)}, f32[96,512]{1,0:T(8,128)S(1)}, u32[]{:S(2)}, u32[]{:S(2)}) collective-permute-start(f32[96,512]{1,0:T(8,128)S(1)} %get-tuple-element.32), channel_id=1, source_target_pairs={{0,2},{2,0},{4,6},{6,4},{8,10},{10,8},{12,14},{14,12},{16,18},{18,... | collective-permute-start | bytes 589832 | tf_op jit(solution)/shard_map/ppermute | solution.py:294
  9.1 7.8 %collective-permute-start.2 = (f32[2,96,512]{2,1,0:T(8,128)S(1)}, f32[2,96,512]{2,1,0:T(8,128)S(1)}, u32[]{:S(2)}, u32[]{:S(2)}) collective-permute-start(f32[2,96,512]{2,1,0:T(8,128)S(1)} %get-tuple-element.36), channel_id=1, source_target_pairs={{0,2},{2,4},{4,0},{6,8},{8,10},{10,12},{12,6},{14,16},{16,18},{18,... | collective-permute-start | bytes 1179656 | tf_op jit(solution)/shard_map/ppermute | solution.py:297
  11.2 1.5 %collective-permute-start.4 = (f32[96,512]{1,0:T(8,128)S(1)}, f32[96,512]{1,0:T(8,128)S(1)}, u32[]{:S(2)}, u32[]{:S(2)}) collective-permute-start(f32[96,512]{1,0:T(8,128)S(1)} %get-tuple-element.39), channel_id=1, source_target_pairs={{0,2},{2,0},{4,6},{6,4},{8,10},{10,8},{12,14},{14,12},{16,18},{18,... | collective-permute-start | bytes 589832 | tf_op jit(solution)/shard_map/ppermute | solution.py:294
  11.3 1.7 %collective-permute-start.5 = (f32[96,512]{1,0:T(8,128)S(1)}, f32[96,512]{1,0:T(8,128)S(1)}, u32[]{:S(2)}, u32[]{:S(2)}) collective-permute-start(f32[96,512]{1,0:T(8,128)S(1)} %get-tuple-element.40), channel_id=1, source_target_pairs={{0,2},{2,0},{4,6},{6,4},{8,10},{10,8},{12,14},{14,12},{16,18},{18,... | collective-permute-start | bytes 589832 | tf_op jit(solution)/shard_map/ppermute | solution.py:294
  13.0 8.5 %collective-permute-start.9 = (f32[2,96,512]{2,1,0:T(8,128)S(1)}, f32[2,96,512]{2,1,0:T(8,128)S(1)}, u32[]{:S(2)}, u32[]{:S(2)}) collective-permute-start(f32[2,96,512]{2,1,0:T(8,128)S(1)} %get-tuple-element.47), channel_id=1, source_target_pairs={{0,2},{2,4},{4,0},{6,8},{8,10},{10,12},{12,6},{14,16},{16,18},{18,... | collective-permute-start | bytes 1179656 | tf_op jit(solution)/shard_map/ppermute | solution.py:297
  18.0 1.5 %collective-permute-start.6 = (f32[96,512]{1,0:T(8,128)S(1)}, f32[96,512]{1,0:T(8,128)S(1)}, u32[]{:S(2)}, u32[]{:S(2)}) collective-permute-start(f32[96,512]{1,0:T(8,128)S(1)} %get-tuple-element.43), channel_id=1, source_target_pairs={{0,2},{2,0},{4,6},{6,4},{8,10},{10,8},{12,14},{14,12},{16,18},{18,... | collective-permute-start | bytes 589832 | tf_op jit(solution)/shard_map/ppermute | solution.py:294
  18.1 1.7 %collective-permute-start.7 = (f32[96,512]{1,0:T(8,128)S(1)}, f32[96,512]{1,0:T(8,128)S(1)}, u32[]{:S(2)}, u32[]{:S(2)}) collective-permute-start(f32[96,512]{1,0:T(8,128)S(1)} %get-tuple-element.44), channel_id=1, source_target_pairs={{0,2},{2,0},{4,6},{6,4},{8,10},{10,8},{12,14},{14,12},{16,18},{18,... | collective-permute-start | bytes 589832 | tf_op jit(solution)/shard_map/ppermute | solution.py:294
  19.8 7.8 %collective-permute-start.8 = (f32[2,96,512]{2,1,0:T(8,128)S(1)}, f32[2,96,512]{2,1,0:T(8,128)S(1)}, u32[]{:S(2)}, u32[]{:S(2)}) collective-permute-start(f32[2,96,512]{2,1,0:T(8,128)S(1)} %get-tuple-element.46), channel_id=1, source_target_pairs={{0,2},{2,4},{4,0},{6,8},{8,10},{10,12},{12,6},{14,16},{16,18},{18,... | collective-permute-start | bytes 1179656 | tf_op jit(solution)/shard_map/ppermute | solution.py:297
  22.6 5.0 %collective-permute-start.10 = (f32[96,512]{1,0:T(8,128)S(1)}, f32[96,512]{1,0:T(8,128)S(1)}, u32[]{:S(2)}, u32[]{:S(2)}) collective-permute-start(f32[96,512]{1,0:T(8,128)S(1)} %get-tuple-element.49), channel_id=1, source_target_pairs={{0,2},{2,0},{4,6},{6,4},{8,10},{10,8},{12,14},{14,12},{16,18},{18,... | collective-permute-start | bytes 589832 | tf_op jit(solution)/shard_map/ppermute | solution.py:294
  22.6 4.9 %collective-permute-start.11 = (f32[96,512]{1,0:T(8,128)S(1)}, f32[96,512]{1,0:T(8,128)S(1)}, u32[]{:S(2)}, u32[]{:S(2)}) collective-permute-start(f32[96,512]{1,0:T(8,128)S(1)} %get-tuple-element.50), channel_id=1, source_target_pairs={{0,2},{2,0},{4,6},{6,4},{8,10},{10,8},{12,14},{14,12},{16,18},{18,... | collective-permute-start | bytes 589832 | tf_op jit(solution)/shard_map/ppermute | solution.py:294
  27.7 4.1 %collective-permute-start.12 = (f32[1,256]{1,0:T(1,128)S(1)}, f32[1,256]{1,0:T(1,128)S(1)}, u32[]{:S(2)}, u32[]{:S(2)}) collective-permute-start(f32[1,256]{1,0:T(1,128)S(1)} %get-tuple-element.53), channel_id=1, source_target_pairs={{0,1},{1,0},{2,3},{3,2},{4,5},{5,4},{6,7},{7,6},{8,9},{9,8},{10,11... | collective-permute-start | bytes 3080 | tf_op jit(solution)/shard_map/ppermute | solution.py:317

commit v5 on v4

v5 whole, which is shorter than its diff:
```python
import functools
import math

import jax
import jax.numpy as jnp
from jax import lax
from jax.experimental import pallas as pl
from jax.experimental.pallas import tpu as pltpu
from jax.sharding import PartitionSpec as P

TICKS = 5
TAIL = 16
VMEM_LIMIT = 24 * 1024 * 1024
QUICK = pl.CostEstimate(flops=1, bytes_accessed=1, transcendentals=0)
LONGER = pl.CostEstimate(flops=500000000, bytes_accessed=1, transcendentals=0)
PARAMS = pltpu.CompilerParams(vmem_limit_bytes=VMEM_LIMIT)
IN_VMEM = pl.BlockSpec(memory_space=pltpu.VMEM)
IN_HBM = pl.BlockSpec(memory_space=pltpu.HBM)


def pinned(value):
    return pltpu.with_memory_space_constraint(value, pltpu.VMEM)


def kept(value):
    return pltpu.with_memory_space_constraint(value, pltpu.HBM)


def dot(left, right):
    return jnp.dot(left, right, preferred_element_type=jnp.float32)


def is_odd():
    return lax.axis_index("depth") % 2 == 1


def when_parity(parity):
    return pl.when(is_odd() if parity else jnp.logical_not(is_odd()))


def split(value):
    high = value.astype(jnp.bfloat16)
    low = (value - high.astype(jnp.float32)).astype(jnp.bfloat16)
    return high, low


def fold(product):
    return jnp.sum(product.reshape(-1, 8, product.shape[1]), axis=0)


def take(segments, waves, contrast, grad_in, grad, left):
    shots = left.shape[0] // 4
    total = None if grad_in is None else grad_in[...]
    for start, pair in segments:
        rows = pl.ds(start, pair[0].shape[0])
        for part in range(2):
            wave = waves[part, rows]
            term = fold(pair[part] * wave)
            total = term if total is None else total + term
            high, low = split(pair[part] + contrast[...] * wave)
            left[pl.ds(part * shots + start, rows.size), :] = high
            left[pl.ds((2 + part) * shots + start, rows.size), :] = low
    grad[...] = total


def multiply(left, high, low, columns):
    shots = left.shape[0] // 4

    def by(part):
        big = dot(left[...], high[part, :, columns])
        small = dot(left[pl.ds(0, 2 * shots), :], low[part, :, columns])
        total = big[: 2 * shots] + (big[2 * shots :] + small)
        return total[:shots], total[shots:]

    real_real, imag_real = by(0)
    real_imag, imag_imag = by(1)
    return real_real - imag_imag, real_imag + imag_real


def injected(tick, sites, pulse, shape):
    shots, breadth = shape
    row = lax.broadcasted_iota(jnp.int32, (shots, shots), 0)
    column = lax.broadcasted_iota(jnp.int32, (shots, shots), 1)
    spread = jnp.broadcast_to(sites[pl.ds(tick - 1, 1), :], (shots, shots)).astype(jnp.float32)
    site = jnp.sum(jnp.where(row == column, spread, 0.0), axis=1, keepdims=True)
    lanes = lax.broadcasted_iota(jnp.int32, (shots, breadth), 1).astype(jnp.float32)
    hit = lanes == site
    return [jnp.where(hit, pulse[pl.ds(part, 1), pl.ds(tick - 1, 1)], 0.0) for part in range(2)]


def first_kernel(parity, chained, *refs):
    operator, contrast, residual, panel = refs[:4]
    refs = refs[7:] if chained else refs[4:]
    out = refs[: 2 - parity]
    high, low, grad = refs[2 - parity : 5 - parity]
    whole, reflect, wave, arrived, left, sems = refs[-6:]
    shots, breadth = arrived.shape[1:]
    depth = breadth // 2

    @when_parity(parity)
    def _():
        copies = [
            pltpu.make_async_copy(contrast, reflect, sems.at[0]),
            pltpu.make_async_copy(residual.at[0, 0, 0], wave, sems.at[1]),
            pltpu.make_async_copy(panel.at[0, 0], arrived, sems.at[2]),
        ]
        pieces = [(part, pl.ds(half * depth, depth)) for half in range(2) for part in range(2)]
        for place, (part, rows) in enumerate(pieces):
            copies.append(
                pltpu.make_async_copy(operator.at[0, 0, part, rows], whole.at[part, rows], sems.at[3 + place])
            )
        for copy in copies:
            copy.start()
        for copy in copies[:3]:
            copy.wait()
        take([(0, arrived)], wave, reflect, None, grad, left)
        sums = [None, None]
        for place, (part, rows) in enumerate(pieces):
            copies[3 + place].wait()
            upper, lower = split(whole[part, rows])
            high[part, rows] = upper
            low[part, rows] = lower
            big = dot(left[:, rows], upper)
            small = dot(left[pl.ds(0, 2 * shots), rows], lower)
            total = big[: 2 * shots] + (big[2 * shots :] + small)
            sums[part] = total if sums[part] is None else sums[part] + total
        store(out, (sums[0][:shots] - sums[1][shots:], sums[1][:shots] + sums[0][shots:]))


def store(out, pair):
    start = 0
    for piece in out:
        for part in range(2):
            piece[part] = pair[part][start : start + piece.shape[1]]
        start += piece.shape[1]


def panel_shapes(parity, shots, breadth):
    rows = [shots] if parity else [shots - TAIL, TAIL]
    return tuple(pltpu.VMEM((2, count, breadth), jnp.float32) for count in rows)


def first(parity, operator, contrast, residual, panel, carried):
    shots, breadth = panel.shape[3:]
    half = pltpu.VMEM((2, breadth, breadth), jnp.bfloat16)
    outs = panel_shapes(parity, shots, breadth)
    return pl.pallas_call(
        functools.partial(first_kernel, parity, bool(carried)),
        out_shape=(*outs, half, half, pltpu.VMEM((8, breadth), jnp.float32)),
        in_specs=[IN_HBM] * 4 + [IN_VMEM] * len(carried),
        out_specs=(IN_VMEM,) * (len(outs) + 3),
        scratch_shapes=[
            pltpu.VMEM((2, breadth, breadth), jnp.float32),
            pltpu.VMEM((1, breadth), jnp.float32),
            pltpu.VMEM((2, shots, breadth), jnp.float32),
            pltpu.VMEM((2, shots, breadth), jnp.float32),
            pltpu.VMEM((4 * shots, breadth), jnp.bfloat16),
            pltpu.SemaphoreType.DMA((7,)),
        ],
        input_output_aliases={4 + i: len(outs) + i for i in range(len(carried))},
        compiler_params=PARAMS,
        cost_estimate=QUICK if parity else LONGER,
        name=f"first_{parity}",
    )(kept(operator), kept(contrast), kept(residual), kept(panel), *[pinned(value) for value in carried])


def arrive(tick, parity, panel, shared, grad_in, grad, left):
    residual, contrast, sites, pulse = shared
    rest = (residual.at[0, 0, tick], contrast, grad_in, grad, left)
    if parity:
        take([(0, panel[0]), (panel[0].shape[1], panel[1])], *rest)
        return
    surface = lax.axis_index("depth") == 0

    @pl.when(surface)
    def _():
        take([(0, injected(tick, sites, pulse, panel[0].shape[1:]))], *rest)

    @pl.when(jnp.logical_not(surface))
    def _():
        take([(0, panel[0])], *rest)


def step_kernel(tick, parity, *refs):
    panel, shared = refs[: 1 + parity], refs[1 + parity : 5 + parity]
    high, low, grad_in = refs[5 + parity : 8 + parity]
    *out, grad, left = refs[8 + parity :]

    @when_parity(parity)
    def _():
        arrive(tick, parity, panel, shared, grad_in, grad, left)
        store(out, multiply(left, high, low, slice(None)))


def step(tick, parity, panel, shared, high, low, grad, shots):
    breadth = grad.shape[1]
    outs = panel_shapes(parity, shots, breadth)
    operands = [pinned(value) for value in (*panel, *shared, high, low, grad)]
    return pl.pallas_call(
        functools.partial(step_kernel, tick, parity),
        out_shape=(*outs, pltpu.VMEM(grad.shape, jnp.float32)),
        in_specs=[IN_VMEM] * len(operands),
        out_specs=(IN_VMEM,) * (len(outs) + 1),
        scratch_shapes=[pltpu.VMEM((4 * shots, breadth), jnp.bfloat16)],
        input_output_aliases={len(operands) - 1: len(outs)},
        compiler_params=PARAMS,
        cost_estimate=QUICK if parity else LONGER,
        name=f"step_{tick}_{parity}",
    )(*operands)


def half_out(half, left, high, low, out, held, sem):
    width = held.shape[2]
    columns = pl.ds(half * width, width)
    held[0], held[1] = multiply(left, high, low, columns)
    return pltpu.make_async_copy(held, out.at[:, :, columns], sem)


def last_first(panels, shared, high, low, grad, scale):
    shots, breadth = panels[0].shape[1:]
    count = lax.axis_size("freq")
    width = breadth // count

    def body(from_above, from_mate, from_mate_tail, residual, contrast, sites, pulse, high, low, grad_in, out, left, *refs):
        chunks, (total, held, sem) = refs[:count], refs[count:]
        shared = (residual, contrast, sites, pulse)

        @when_parity(1)
        def _():
            arrive(TICKS - 1, 1, (from_mate, from_mate_tail), shared, grad_in, total, left)

        @when_parity(0)
        def _():
            arrive(TICKS - 1, 0, (from_above,), shared, grad_in, total, left)

        copy = half_out(0, left, high, low, out, held, sem)
        copy.start()
        gradient = jnp.sum(total[...], axis=0, keepdims=True) * scale
        me = lax.axis_index("freq")
        for distance in range(count):
            owner = lax.rem(me + distance, count)
            chunk = jnp.zeros((1, width), jnp.float32)
            for place in range(count):
                piece = gradient[:, place * width : (place + 1) * width]
                chunk = jnp.where(owner == place, piece, chunk)
            chunks[distance][...] = chunk
        copy.wait()

    operands = [pinned(value) for value in (*panels, *shared, high, low, grad)]
    chunk = pltpu.VMEM((1, width), jnp.float32)
    left = pltpu.VMEM((4 * shots, breadth), jnp.bfloat16)
    return pl.pallas_call(
        body,
        out_shape=(pltpu.HBM((2, shots, breadth), jnp.float32), left) + (chunk,) * count,
        in_specs=[IN_VMEM] * len(operands),
        out_specs=(IN_HBM,) + (IN_VMEM,) * (1 + count),
        scratch_shapes=[
            pltpu.VMEM(grad.shape, jnp.float32),
            pltpu.VMEM((2, shots, breadth // 2), jnp.float32),
            pltpu.SemaphoreType.DMA,
        ],
        compiler_params=PARAMS,
        cost_estimate=QUICK,
        name="last_first",
    )(*operands)


def last_second(out, left, high, low):
    def body(left, high, low, _, out, held, sem):
        copy = half_out(1, left, high, low, out, held, sem)
        copy.start()
        copy.wait()

    shots, breadth = out.shape[1:]
    return pl.pallas_call(
        body,
        out_shape=pltpu.HBM(out.shape, jnp.float32),
        in_specs=[IN_VMEM] * 3 + [IN_HBM],
        out_specs=IN_HBM,
        scratch_shapes=[pltpu.VMEM((2, shots, breadth // 2), jnp.float32), pltpu.SemaphoreType.DMA],
        input_output_aliases={3: 0},
        compiler_params=PARAMS,
        cost_estimate=QUICK,
        name="last_second",
    )(pinned(left), pinned(high), pinned(low), kept(out))


def cross_route(levels):
    route = {level: (level + 1) % levels for level in range(levels)}
    chips = levels // 2
    if chips % 2 == 0:
        for chip in range(chips - 1, 1, -2):
            route[levels - 1 if chip == chips - 1 else 2 * chip] = 2 * (chip - 2) + 1
        route[2 if chips > 2 else levels - 1] = 0
    return sorted(route.items())


def local(
    extrapolation_operator,
    impedance_contrast,
    ascending_residual,
    arriving_downward_matrices,
    shot_node_indices,
    emitted_pulse,
):
    levels = lax.axis_size("depth")
    freqs = lax.axis_size("freq")
    shots = arriving_downward_matrices.shape[3]
    mate_route = [(level, level ^ 1) for level in range(levels)]
    down_route = cross_route(levels)
    shared = (ascending_residual, impedance_contrast, shot_node_indices, emitted_pulse[0].T)

    def mate(pieces):
        return [lax.ppermute(piece, "depth", mate_route) for piece in pieces]

    def down(panel):
        return lax.ppermute(panel, "depth", down_route)

    start = (extrapolation_operator, impedance_contrast, ascending_residual, arriving_downward_matrices)
    odd, *carried = first(1, *start, ())
    from_above = down(odd)
    *even, high, low, grad = first(0, *start, carried)
    from_mate = mate(even)
    for tick in range(1, TICKS - 1):
        odd, grad = step(tick, 1, from_mate, shared, high, low, grad, shots)
        later = down(odd)
        *even, grad = step(tick, 0, (from_above,), shared, high, low, grad, shots)
        from_mate = mate(even)
        from_above = later

    scale = 1.0 / math.sqrt(shots * TICKS)
    out, left, *chunks = last_first((from_above, *from_mate), shared, high, low, grad, scale)
    gradient = chunks[0]
    for distance in range(1, freqs):
        route = [(i, (i + distance) % freqs) for i in range(freqs)]
        gradient = gradient + lax.ppermute(chunks[distance], "freq", route)
    out = last_second(out, left, high, low)
    return (out[None, None], gradient)


def solution(mesh):
    placed = (
        P("freq", "depth", None, None, None),
        P("depth", None),
        P("freq", "depth", None, None, None, None),
        P("freq", "depth", None, None, None),
        P(),
        P("freq", None, None),
    )
    return jax.shard_map(
        local,
        mesh=mesh,
        in_specs=placed,
        out_specs=(P("freq", "depth", None, None, None), P("depth", "freq")),
        check_vma=False,
    )
```

time: 32.6 us -> 32.6 us (level)
  waiting for transfers between devices: 11.6 us -> 12.3 us
  local copies, waits for them, and re-layouts: 0.69 us -> 0.01 us
  Pallas kernels: 7.77 us -> 8.3 us
  starting transfers between devices: 11.1 us -> 10.6 us
    ppermute x8, waiting for transfers between devices: 3.64 us -> 4.86 us  [mate(): return [lax.ppermute(piece, 'depth', mate_route) for piece in pieces]]
    ppermute x4, waiting for transfers between devices: 7.96 us -> 7.05 us  [down(): return lax.ppermute(panel, 'depth', down_route)]
    unnamed x8, local copies, waits for them, and re-layouts: 0.69 us -> 0.01 us
    pallas_call x2, Pallas kernels: 1.92 us -> 2.58 us  [the longest x1 1.41 us: last_first(): pl.pallas_call(body, out_shape=(pltpu.HBM((2, shots, breadth), jnp.float3...]
    ppermute x4, starting transfers between devices: 6.42 us -> 5.9 us  [down(): return lax.ppermute(panel, 'depth', down_route)]
    ppermute x1, waiting for transfers between devices: 0.01 us -> 0.37 us  [local(): gradient = gradient + lax.ppermute(chunks[distance], 'freq', route)]
  transfers between devices with their start and end apart: 13 -> 13, of which waited for: 9 -> 9; matrix products, arithmetic and copies ran while one was open for 0% -> 0% of each run, Pallas kernels for 23% -> 21%
where the time goes in v5:
time: 32.6 us; the launch traced here: 32.5 us
  waiting for transfers between devices  12.3 us (38%)
  starting transfers between devices  10.6 us (33%)
  Pallas kernels  8.3 us (25%)
  between operations  0.76 us (2%)
  other arithmetic  0.56 us (2%)
    ppermute x4, waiting for transfers between devices, down(): return lax.ppermute(panel, 'depth', down_route)  7.05 us
    ppermute x4, starting transfers between devices, down(): return lax.ppermute(panel, 'depth', down_route)  5.9 us
    ppermute x8, waiting for transfers between devices, mate(): return [lax.ppermute(piece, 'depth', mate_route) for piece in pieces]  4.86 us
    pallas_call x6, Pallas kernels, step(): pl.pallas_call(functools.partial(step_kernel, tick, parity), out_shape=(*...  3.01 us
    pallas_call x2, Pallas kernels, first(): pl.pallas_call(functools.partial(first_kernel, parity, bool(carried)), ou...  2.71 us
    ppermute x1, starting transfers between devices, local(): gradient = gradient + lax.ppermute(chunks[distance], 'freq', route)  2.38 us
    ppermute x8, starting transfers between devices, mate(): return [lax.ppermute(piece, 'depth', mate_route) for piece in pieces]  2.27 us
    pallas_call x1, Pallas kernels, last_first(): pl.pallas_call(body, out_shape=(pltpu.HBM((2, shots, breadth), jnp.float3...  1.41 us
  transfers between devices with their start and end apart: 13, of which 9 were waited for; matrix products, arithmetic and copies ran while one was open for 0% of the time, Pallas kernels for 21%

profile of v5, /device:TPU:0, one launch (start us, length us, event | category | flops | bytes accessed | tf_op | source)
XLA Modules:
  0.0 32.5 jit_solution(10975755460177484132)
XLA Ops:
  0.6 0.1 first_1.1
  0.7 2.9 %collective-permute-start.3 = (f32[2,96,512]{2,1,0:T(8,128)S(1)}, f32[2,96,512]{2,1,0:T(8,128)S(1)}, u32[]{:S(2)}, u32[]{:S(2)}) collective-permute-start(f32[2,96,512]{2,1,0:T(8,128)S(1)} %get-tuple-element.39), channel_id=1, source_target_pairs={{0,2},{2,4},{4,0},{6,8},{8,10},{10,12},{12,6},{14,16},{16,18},{18,... | collective-permute-start | bytes 1179656 | tf_op jit(solution)/shard_map/ppermute | solution.py:317
  3.6 0.0 copy-start
  3.6 0.0 copy-start.1
  3.6 0.0 copy-start.2
  3.6 0.0 copy-start.3
  3.6 2.6 %first_0.1 = (f32[2,80,512]{2,1,0:T(8,128)S(1)}, f32[2,16,512]{2,1,0:T(8,128)S(1)}, bf16[2,512,512]{2,1,0:T(8,128)(2,1)S(1)}, bf16[2,512,512]{2,1,0:T(8,128)(2,1)S(1)}, f32[8,512]{1,0:T(8,128)S(1)}) custom-call(f32[1,1,2,512,512]{4,3,2,1,0:T(8,128)} %refs_0_.3, f32[1,512]{1,0:T(1,128)} %contrast.1, ...), custom_call_target="tpu_custom_call", output_to_operand_aliasing={{2}: (4, {}), {3}: (5, {}), {4}: (6, {})} | custom-call | flops 500000000 | bytes 1 | tf_op jit(solution)/shard_map/first_0/pallas_call | solution.py:147
  6.3 0.1 collective-permute-start
  6.4 0.5 %collective-permute-start.1 = (f32[2,16,512]{2,1,0:T(8,128)S(1)}, f32[2,16,512]{2,1,0:T(8,128)S(1)}, u32[]{:S(2)}, u32[]{:S(2)}) collective-permute-start(f32[2,16,512]{2,1,0:T(8,128)S(1)} %get-tuple-element.34), channel_id=1, source_target_pairs={{0,2},{2,0},{4,6},{6,4},{8,10},{10,8},{12,14},{14,12},{16,18},{18,... | collective-permute-start | bytes 196616 | tf_op jit(solution)/shard_map/ppermute | solution.py:314
  6.9 1.2 %collective-permute-done.1.refs_1_ = f32[2,16,512]{2,1,0:T(8,128)S(1)} collective-permute-done((f32[2,16,512]{2,1,0:T(8,128)S(1)}, f32[2,16,512]{2,1,0:T(8,128)S(1)}, u32[]{:S(2)}, u32[]{:S(2)}) %collective-permute-start.1) | collective-permute-done | bytes 65568 | tf_op jit(solution)/shard_map/ppermute | solution.py:314
  8.1 0.0 collective-permute-done.refs_0_
  8.1 0.0 copy-done
  8.1 0.0 copy-done.1
  8.1 0.0 copy-done.2
  8.1 0.0 copy-done.3
  8.1 1.0 %collective-permute-start.2 = (f32[2,96,512]{2,1,0:T(8,128)S(1)}, f32[2,96,512]{2,1,0:T(8,128)S(1)}, u32[]{:S(2)}, u32[]{:S(2)}) collective-permute-start(f32[2,96,512]{2,1,0:T(8,128)S(1)} %get-tuple-element.38), channel_id=1, source_target_pairs={{0,2},{2,4},{4,0},{6,8},{8,10},{10,12},{12,6},{14,16},{16,18},{18,... | collective-permute-start | bytes 1179656 | tf_op jit(solution)/shard_map/ppermute | solution.py:317
  9.1 0.4 %collective-permute-done.3.refs_0_ = f32[2,96,512]{2,1,0:T(8,128)S(1)} collective-permute-done((f32[2,96,512]{2,1,0:T(8,128)S(1)}, f32[2,96,512]{2,1,0:T(8,128)S(1)}, u32[]{:S(2)}, u32[]{:S(2)}) %collective-permute-start.3) | collective-permute-done | bytes 393248 | tf_op jit(solution)/shard_map/ppermute | solution.py:317
  9.5 1.0 %step_1_0.1 = (f32[2,80,512]{2,1,0:T(8,128)S(1)}, f32[2,16,512]{2,1,0:T(8,128)S(1)}, f32[8,512]{1,0:T(8,128)S(1)}) custom-call(f32[2,96,512]{2,1,0:T(8,128)S(1)} %collective-permute-done.3.refs_0_, f32[1,1,5,2,96,512]{5,4,3,2,1,0:T(8,128)S(1)} %copy-done, f32[1,512]{1,0:T(1,128)S(1)} %copy-done.1, ...), custom_call_target="tpu_custom_call", output_to_operand_aliasing={{2}: (7, {})} | custom-call | flops 500000000 | bytes 1 | tf_op jit(solution)/shard_map/step_1_0/pallas_call | solution.py:199
  10.5 0.1 collective-permute-start.4
  10.6 0.5 %collective-permute-start.5 = (f32[2,16,512]{2,1,0:T(8,128)S(1)}, f32[2,16,512]{2,1,0:T(8,128)S(1)}, u32[]{:S(2)}, u32[]{:S(2)}) collective-permute-start(f32[2,16,512]{2,1,0:T(8,128)S(1)} %get-tuple-element.42), channel_id=1, source_target_pairs={{0,2},{2,0},{4,6},{6,4},{8,10},{10,8},{12,14},{14,12},{16,18},{18,... | collective-permute-start | bytes 196616 | tf_op jit(solution)/shard_map/ppermute | solution.py:314
  11.1 1.2 %collective-permute-done.5.refs_1_ = f32[2,16,512]{2,1,0:T(8,128)S(1)} collective-permute-done((f32[2,16,512]{2,1,0:T(8,128)S(1)}, f32[2,16,512]{2,1,0:T(8,128)S(1)}, u32[]{:S(2)}, u32[]{:S(2)}) %collective-permute-start.5) | collective-permute-done | bytes 65568 | tf_op jit(solution)/shard_map/ppermute | solution.py:314
  12.3 0.0 collective-permute-done.4.refs_0_
  12.3 1.0 %collective-permute-start.9 = (f32[2,96,512]{2,1,0:T(8,128)S(1)}, f32[2,96,512]{2,1,0:T(8,128)S(1)}, u32[]{:S(2)}, u32[]{:S(2)}) collective-permute-start(f32[2,96,512]{2,1,0:T(8,128)S(1)} %get-tuple-element.49), channel_id=1, source_target_pairs={{0,2},{2,4},{4,0},{6,8},{8,10},{10,12},{12,6},{14,16},{16,18},{18,... | collective-permute-start | bytes 1179656 | tf_op jit(solution)/shard_map/ppermute | solution.py:317
  13.3 2.7 %collective-permute-done.2.refs_0_ = f32[2,96,512]{2,1,0:T(8,128)S(1)} collective-permute-done((f32[2,96,512]{2,1,0:T(8,128)S(1)}, f32[2,96,512]{2,1,0:T(8,128)S(1)}, u32[]{:S(2)}, u32[]{:S(2)}) %collective-permute-start.2) | collective-permute-done | bytes 393248 | tf_op jit(solution)/shard_map/ppermute | solution.py:317
  16.0 1.0 %step_2_0.1 = (f32[2,80,512]{2,1,0:T(8,128)S(1)}, f32[2,16,512]{2,1,0:T(8,128)S(1)}, f32[8,512]{1,0:T(8,128)S(1)}) custom-call(f32[2,96,512]{2,1,0:T(8,128)S(1)} %collective-permute-done.2.refs_0_, f32[1,1,5,2,96,512]{5,4,3,2,1,0:T(8,128)S(1)} %copy-done, f32[1,512]{1,0:T(1,128)S(1)} %copy-done.1, ...), custom_call_target="tpu_custom_call", output_to_operand_aliasing={{2}: (7, {})} | custom-call | flops 500000000 | bytes 1 | tf_op jit(solution)/shard_map/step_2_0/pallas_call | solution.py:199
  17.0 0.1 collective-permute-start.6
  17.1 0.5 %collective-permute-start.7 = (f32[2,16,512]{2,1,0:T(8,128)S(1)}, f32[2,16,512]{2,1,0:T(8,128)S(1)}, u32[]{:S(2)}, u32[]{:S(2)}) collective-permute-start(f32[2,16,512]{2,1,0:T(8,128)S(1)} %get-tuple-element.46), channel_id=1, source_target_pairs={{0,2},{2,0},{4,6},{6,4},{8,10},{10,8},{12,14},{14,12},{16,18},{18,... | collective-permute-start | bytes 196616 | tf_op jit(solution)/shard_map/ppermute | solution.py:314
  17.6 1.2 %collective-permute-done.7.refs_1_ = f32[2,16,512]{2,1,0:T(8,128)S(1)} collective-permute-done((f32[2,16,512]{2,1,0:T(8,128)S(1)}, f32[2,16,512]{2,1,0:T(8,128)S(1)}, u32[]{:S(2)}, u32[]{:S(2)}) %collective-permute-start.7) | collective-permute-done | bytes 65568 | tf_op jit(solution)/shard_map/ppermute | solution.py:314
  18.8 0.0 collective-permute-done.6.refs_0_
  18.8 1.0 %collective-permute-start.8 = (f32[2,96,512]{2,1,0:T(8,128)S(1)}, f32[2,96,512]{2,1,0:T(8,128)S(1)}, u32[]{:S(2)}, u32[]{:S(2)}) collective-permute-start(f32[2,96,512]{2,1,0:T(8,128)S(1)} %get-tuple-element.48), channel_id=1, source_target_pairs={{0,2},{2,4},{4,0},{6,8},{8,10},{10,12},{12,6},{14,16},{16,18},{18,... | collective-permute-start | bytes 1179656 | tf_op jit(solution)/shard_map/ppermute | solution.py:317
  19.8 0.8 %collective-permute-done.9.refs_0_ = f32[2,96,512]{2,1,0:T(8,128)S(1)} collective-permute-done((f32[2,96,512]{2,1,0:T(8,128)S(1)}, f32[2,96,512]{2,1,0:T(8,128)S(1)}, u32[]{:S(2)}, u32[]{:S(2)}) %collective-permute-start.9) | collective-permute-done | bytes 393248 | tf_op jit(solution)/shard_map/ppermute | solution.py:317
  20.6 1.0 %step_3_0.1 = (f32[2,80,512]{2,1,0:T(8,128)S(1)}, f32[2,16,512]{2,1,0:T(8,128)S(1)}, f32[8,512]{1,0:T(8,128)S(1)}) custom-call(f32[2,96,512]{2,1,0:T(8,128)S(1)} %collective-permute-done.9.refs_0_, f32[1,1,5,2,96,512]{5,4,3,2,1,0:T(8,128)S(1)} %copy-done, f32[1,512]{1,0:T(1,128)S(1)} %copy-done.1, ...), custom_call_target="tpu_custom_call", output_to_operand_aliasing={{2}: (7, {})} | custom-call | flops 500000000 | bytes 1 | tf_op jit(solution)/shard_map/step_3_0/pallas_call | solution.py:199
  21.6 0.1 collective-permute-start.10
  21.7 0.5 %collective-permute-start.11 = (f32[2,16,512]{2,1,0:T(8,128)S(1)}, f32[2,16,512]{2,1,0:T(8,128)S(1)}, u32[]{:S(2)}, u32[]{:S(2)}) collective-permute-start(f32[2,16,512]{2,1,0:T(8,128)S(1)} %get-tuple-element.52), channel_id=1, source_target_pairs={{0,2},{2,0},{4,6},{6,4},{8,10},{10,8},{12,14},{14,12},{16,18},{18,... | collective-permute-start | bytes 196616 | tf_op jit(solution)/shard_map/ppermute | solution.py:314
  22.2 1.2 %collective-permute-done.11.from_mate_tail = f32[2,16,512]{2,1,0:T(8,128)S(1)} collective-permute-done((f32[2,16,512]{2,1,0:T(8,128)S(1)}, f32[2,16,512]{2,1,0:T(8,128)S(1)}, u32[]{:S(2)}, u32[]{:S(2)}) %collective-permute-start.11) | collective-permute-done | bytes 65568 | tf_op jit(solution)/shard_map/ppermute | solution.py:314
  23.4 3.2 %collective-permute-done.8.from_above = f32[2,96,512]{2,1,0:T(8,128)S(1)} collective-permute-done((f32[2,96,512]{2,1,0:T(8,128)S(1)}, f32[2,96,512]{2,1,0:T(8,128)S(1)}, u32[]{:S(2)}, u32[]{:S(2)}) %collective-permute-start.8) | collective-permute-done | bytes 393248 | tf_op jit(solution)/shard_map/ppermute | solution.py:317
  26.6 0.0 collective-permute-done.10.from_mate
  26.6 1.4 %last_first.1 = (f32[2,96,512]{2,1,0:T(8,128)}, bf16[384,512]{1,0:T(8,128)(2,1)S(1)}, f32[1,256]{1,0:T(1,128)S(1)}, f32[1,256]{1,0:T(1,128)S(1)}) custom-call(f32[2,96,512]{2,1,0:T(8,128)S(1)} %collective-permute-done.8.from_above, f32[2,80,512]{2,1,0:T(8,128)S(1)} %collective-permute-done.10.from_mate, ...), custom_call_target="tpu_custom_call" | custom-call | flops 1 | bytes 1 | tf_op jit(solution)/shard_map/last_first/pallas_call | solution.py:252
  28.0 2.4 %collective-permute-start.12 = (f32[1,256]{1,0:T(1,128)S(1)}, f32[1,256]{1,0:T(1,128)S(1)}, u32[]{:S(2)}, u32[]{:S(2)}) collective-permute-start(f32[1,256]{1,0:T(1,128)S(1)} %get-tuple-element.57), channel_id=1, source_target_pairs={{0,1},{1,0},{2,3},{3,2},{4,5},{5,4},{6,7},{7,6},{8,9},{9,8},{10,11... | collective-permute-start | bytes 3080 | tf_op jit(solution)/shard_map/ppermute | solution.py:336
  30.4 1.2 %last_second.1 = f32[2,96,512]{2,1,0:T(8,128)} custom-call(bf16[384,512]{1,0:T(8,128)(2,1)S(1)} %get-tuple-element.54.left, bf16[2,512,512]{2,1,0:T(8,128)(2,1)S(1)} %get-tuple-element.35.refs_6_.refs_5_.high, bf16[2,512,512]{2,1,0:T(8,128)(2,1)S(1)} %get-tuple-element.36.refs_7_.refs_6_.low, ...), custom_call_target="tpu_custom_call", output_to_operand_aliasing={{}: (3, {})} | custom-call | flops 1 | bytes 1 | tf_op jit(solution)/shard_map/last_second/pallas_call | solution.py:275
  31.5 0.4 %collective-permute-done.12 = f32[1,256]{1,0:T(1,128)S(1)} collective-permute-done((f32[1,256]{1,0:T(1,128)S(1)}, f32[1,256]{1,0:T(1,128)S(1)}, u32[]{:S(2)}, u32[]{:S(2)}) %collective-permute-start.12) | collective-permute-done | bytes 1056 | tf_op jit(solution)/shard_map/ppermute | solution.py:336
  31.9 0.6 %add.3 = f32[1,256]{1,0:T(1,128)} add(f32[1,256]{1,0:T(1,128)S(1)} %get-tuple-element.56, f32[1,256]{1,0:T(1,128)S(1)} %collective-permute-done.12) | non-fusion elementwise | flops 256 | bytes 3072 | tf_op jit(solution)/shard_map/add | solution.py:336
  (3 shorter events, 0.0 us)
Async XLA Ops:
  0.7 8.8 %collective-permute-start.3 = (f32[2,96,512]{2,1,0:T(8,128)S(1)}, f32[2,96,512]{2,1,0:T(8,128)S(1)}, u32[]{:S(2)}, u32[]{:S(2)}) collective-permute-start(f32[2,96,512]{2,1,0:T(8,128)S(1)} %get-tuple-element.39), channel_id=1, source_target_pairs={{0,2},{2,4},{4,0},{6,8},{8,10},{10,12},{12,6},{14,16},{16,18},{18,... | collective-permute-start | bytes 1179656 | tf_op jit(solution)/shard_map/ppermute | solution.py:317
  3.6 4.4 %copy-start = (f32[1,1,5,2,96,512]{5,4,3,2,1,0:T(8,128)S(1)}, f32[1,1,5,2,96,512]{5,4,3,2,1,0:T(8,128)}, u32[]{:S(2)}) copy-start(f32[1,1,5,2,96,512]{5,4,3,2,1,0:T(8,128)} %residual.1) | copy-start | bytes 5898244
  3.6 4.4 %copy-start.1 = (f32[1,512]{1,0:T(1,128)S(1)}, f32[1,512]{1,0:T(1,128)}, u32[]{:S(2)}) copy-start(f32[1,512]{1,0:T(1,128)} %contrast.1) | copy-start | bytes 6148
  3.6 4.4 %copy-start.2 = (s32[4,96]{1,0:T(4,128)S(1)}, s32[4,96]{1,0:T(4,128)}, u32[]{:S(2)}) copy-start(s32[4,96]{1,0:T(4,128)} %sites.1) | copy-start | bytes 4612
  3.6 4.4 %copy-start.3 = (f32[1,4,2]{1,2,0:T(2,128)S(1)}, f32[1,4,2]{1,2,0:T(2,128)}, u32[]{:S(2)}) copy-start(f32[1,4,2]{1,2,0:T(2,128)} %param.11) | copy-start | bytes 100
  6.3 1.8 %collective-permute-start = (f32[2,80,512]{2,1,0:T(8,128)S(1)}, f32[2,80,512]{2,1,0:T(8,128)S(1)}, u32[]{:S(2)}, u32[]{:S(2)}) collective-permute-start(f32[2,80,512]{2,1,0:T(8,128)S(1)} %get-tuple-element.33), channel_id=1, source_target_pairs={{0,2},{2,0},{4,6},{6,4},{8,10},{10,8},{12,14},{14,12},{16,18},{18,... | collective-permute-start | bytes 983048 | tf_op jit(solution)/shard_map/ppermute | solution.py:314
  6.4 1.7 %collective-permute-start.1 = (f32[2,16,512]{2,1,0:T(8,128)S(1)}, f32[2,16,512]{2,1,0:T(8,128)S(1)}, u32[]{:S(2)}, u32[]{:S(2)}) collective-permute-start(f32[2,16,512]{2,1,0:T(8,128)S(1)} %get-tuple-element.34), channel_id=1, source_target_pairs={{0,2},{2,0},{4,6},{6,4},{8,10},{10,8},{12,14},{14,12},{16,18},{18,... | collective-permute-start | bytes 196616 | tf_op jit(solution)/shard_map/ppermute | solution.py:314
  8.1 7.8 %collective-permute-start.2 = (f32[2,96,512]{2,1,0:T(8,128)S(1)}, f32[2,96,512]{2,1,0:T(8,128)S(1)}, u32[]{:S(2)}, u32[]{:S(2)}) collective-permute-start(f32[2,96,512]{2,1,0:T(8,128)S(1)} %get-tuple-element.38), channel_id=1, source_target_pairs={{0,2},{2,4},{4,0},{6,8},{8,10},{10,12},{12,6},{14,16},{16,18},{18,... | collective-permute-start | bytes 1179656 | tf_op jit(solution)/shard_map/ppermute | solution.py:317
  10.5 1.8 %collective-permute-start.4 = (f32[2,80,512]{2,1,0:T(8,128)S(1)}, f32[2,80,512]{2,1,0:T(8,128)S(1)}, u32[]{:S(2)}, u32[]{:S(2)}) collective-permute-start(f32[2,80,512]{2,1,0:T(8,128)S(1)} %get-tuple-element.41), channel_id=1, source_target_pairs={{0,2},{2,0},{4,6},{6,4},{8,10},{10,8},{12,14},{14,12},{16,18},{18,... | collective-permute-start | bytes 983048 | tf_op jit(solution)/shard_map/ppermute | solution.py:314
  10.6 1.7 %collective-permute-start.5 = (f32[2,16,512]{2,1,0:T(8,128)S(1)}, f32[2,16,512]{2,1,0:T(8,128)S(1)}, u32[]{:S(2)}, u32[]{:S(2)}) collective-permute-start(f32[2,16,512]{2,1,0:T(8,128)S(1)} %get-tuple-element.42), channel_id=1, source_target_pairs={{0,2},{2,0},{4,6},{6,4},{8,10},{10,8},{12,14},{14,12},{16,18},{18,... | collective-permute-start | bytes 196616 | tf_op jit(solution)/shard_map/ppermute | solution.py:314
  12.3 8.3 %collective-permute-start.9 = (f32[2,96,512]{2,1,0:T(8,128)S(1)}, f32[2,96,512]{2,1,0:T(8,128)S(1)}, u32[]{:S(2)}, u32[]{:S(2)}) collective-permute-start(f32[2,96,512]{2,1,0:T(8,128)S(1)} %get-tuple-element.49), channel_id=1, source_target_pairs={{0,2},{2,4},{4,0},{6,8},{8,10},{10,12},{12,6},{14,16},{16,18},{18,... | collective-permute-start | bytes 1179656 | tf_op jit(solution)/shard_map/ppermute | solution.py:317
  17.0 1.8 %collective-permute-start.6 = (f32[2,80,512]{2,1,0:T(8,128)S(1)}, f32[2,80,512]{2,1,0:T(8,128)S(1)}, u32[]{:S(2)}, u32[]{:S(2)}) collective-permute-start(f32[2,80,512]{2,1,0:T(8,128)S(1)} %get-tuple-element.45), channel_id=1, source_target_pairs={{0,2},{2,0},{4,6},{6,4},{8,10},{10,8},{12,14},{14,12},{16,18},{18,... | collective-permute-start | bytes 983048 | tf_op jit(solution)/shard_map/ppermute | solution.py:314
  17.1 1.7 %collective-permute-start.7 = (f32[2,16,512]{2,1,0:T(8,128)S(1)}, f32[2,16,512]{2,1,0:T(8,128)S(1)}, u32[]{:S(2)}, u32[]{:S(2)}) collective-permute-start(f32[2,16,512]{2,1,0:T(8,128)S(1)} %get-tuple-element.46), channel_id=1, source_target_pairs={{0,2},{2,0},{4,6},{6,4},{8,10},{10,8},{12,14},{14,12},{16,18},{18,... | collective-permute-start | bytes 196616 | tf_op jit(solution)/shard_map/ppermute | solution.py:314
  18.8 7.8 %collective-permute-start.8 = (f32[2,96,512]{2,1,0:T(8,128)S(1)}, f32[2,96,512]{2,1,0:T(8,128)S(1)}, u32[]{:S(2)}, u32[]{:S(2)}) collective-permute-start(f32[2,96,512]{2,1,0:T(8,128)S(1)} %get-tuple-element.48), channel_id=1, source_target_pairs={{0,2},{2,4},{4,0},{6,8},{8,10},{10,12},{12,6},{14,16},{16,18},{18,... | collective-permute-start | bytes 1179656 | tf_op jit(solution)/shard_map/ppermute | solution.py:317
  21.6 5.0 %collective-permute-start.10 = (f32[2,80,512]{2,1,0:T(8,128)S(1)}, f32[2,80,512]{2,1,0:T(8,128)S(1)}, u32[]{:S(2)}, u32[]{:S(2)}) collective-permute-start(f32[2,80,512]{2,1,0:T(8,128)S(1)} %get-tuple-element.51), channel_id=1, source_target_pairs={{0,2},{2,0},{4,6},{6,4},{8,10},{10,8},{12,14},{14,12},{16,18},{18,... | collective-permute-start | bytes 983048 | tf_op jit(solution)/shard_map/ppermute | solution.py:314
  21.7 1.7 %collective-permute-start.11 = (f32[2,16,512]{2,1,0:T(8,128)S(1)}, f32[2,16,512]{2,1,0:T(8,128)S(1)}, u32[]{:S(2)}, u32[]{:S(2)}) collective-permute-start(f32[2,16,512]{2,1,0:T(8,128)S(1)} %get-tuple-element.52), channel_id=1, source_target_pairs={{0,2},{2,0},{4,6},{6,4},{8,10},{10,8},{12,14},{14,12},{16,18},{18,... | collective-permute-start | bytes 196616 | tf_op jit(solution)/shard_map/ppermute | solution.py:314
  28.0 3.9 %collective-permute-start.12 = (f32[1,256]{1,0:T(1,128)S(1)}, f32[1,256]{1,0:T(1,128)S(1)}, u32[]{:S(2)}, u32[]{:S(2)}) collective-permute-start(f32[1,256]{1,0:T(1,128)S(1)} %get-tuple-element.57), channel_id=1, source_target_pairs={{0,1},{1,0},{2,3},{3,2},{4,5},{5,4},{6,7},{7,6},{8,9},{9,8},{10,11... | collective-permute-start | bytes 3080 | tf_op jit(solution)/shard_map/ppermute | solution.py:336

commit v6 on v5

v6 whole, which is shorter than its diff:
```python
import functools
import math

import jax
import jax.numpy as jnp
from jax import lax
from jax.experimental import pallas as pl
from jax.experimental.pallas import tpu as pltpu
from jax.sharding import PartitionSpec as P

TICKS = 5
HALVES = 2
TAIL = 16
VMEM_LIMIT = 24 * 1024 * 1024
WEIGHTS = {"step_1_0": 10000000, "step_0_1": 1000000, "step_1_1": 200000000, "last_0": 200000000, "gradient": 10000000}
PARAMS = pltpu.CompilerParams(vmem_limit_bytes=VMEM_LIMIT)
IN_VMEM = pl.BlockSpec(memory_space=pltpu.VMEM)
IN_HBM = pl.BlockSpec(memory_space=pltpu.HBM)


def pinned(value):
    return pltpu.with_memory_space_constraint(value, pltpu.VMEM)


def kept(value):
    return pltpu.with_memory_space_constraint(value, pltpu.HBM)


def cost(kind):
    return pl.CostEstimate(flops=WEIGHTS.get(kind, 1), bytes_accessed=1, transcendentals=0)


def dot(left, right):
    return jnp.dot(left, right, preferred_element_type=jnp.float32)


def is_odd():
    return lax.axis_index("depth") % 2 == 1


def when_parity(parity):
    return pl.when(is_odd() if parity else jnp.logical_not(is_odd()))


def split(value):
    high = value.astype(jnp.bfloat16)
    low = (value - high.astype(jnp.float32)).astype(jnp.bfloat16)
    return high, low


def fold(product):
    return jnp.sum(product.reshape(-1, 8, product.shape[1]), axis=0)


def take(pair, start, waves, contrast, grad_in, grad, left, offset=0):
    count = pair[0].shape[0]
    total = None if grad_in is None else grad_in[...]
    for part in range(2):
        wave = waves[part, pl.ds(start + offset, count)]
        if grad is not None:
            term = fold(pair[part] * wave)
            total = term if total is None else total + term
        if left is not None:
            shots = left.shape[0] // 4
            high, low = split(pair[part] + contrast[...] * wave)
            left[pl.ds(part * shots + offset, count), :] = high
            left[pl.ds((2 + part) * shots + offset, count), :] = low
    if grad is not None:
        grad[...] = total


def multiply(left, high, low, columns):
    shots = left.shape[0] // 4

    def by(part):
        big = dot(left[...], high[part, :, columns])
        small = dot(left[pl.ds(0, 2 * shots), :], low[part, :, columns])
        total = big[: 2 * shots] + (big[2 * shots :] + small)
        return total[:shots], total[shots:]

    real_real, imag_real = by(0)
    real_imag, imag_imag = by(1)
    return real_real - imag_imag, real_imag + imag_real


def injected(tick, start, sites, pulse, shape):
    rows, breadth = shape
    shots = sites.shape[1]
    row = lax.broadcasted_iota(jnp.int32, (rows, shots), 0) + start
    column = lax.broadcasted_iota(jnp.int32, (rows, shots), 1)
    spread = jnp.broadcast_to(sites[pl.ds(tick - 1, 1), :], (rows, shots)).astype(jnp.float32)
    site = jnp.sum(jnp.where(row == column, spread, 0.0), axis=1, keepdims=True)
    lanes = lax.broadcasted_iota(jnp.int32, (rows, breadth), 1).astype(jnp.float32)
    hit = lanes == site
    return [jnp.where(hit, pulse[pl.ds(part, 1), pl.ds(tick - 1, 1)], 0.0) for part in range(2)]


def first_kernel(parity, chained, *refs):
    operator, contrast, residual, panel = refs[:4]
    refs = refs[7:] if chained else refs[4:]
    pieces = HALVES * (2 - parity)
    out = refs[:pieces]
    high, low, grad = refs[pieces : pieces + 3]
    whole, reflect, wave, arrived, left, sems = refs[-6:]
    shots, breadth = arrived.shape[1:]
    depth = breadth // 2

    @when_parity(parity)
    def _():
        copies = [
            pltpu.make_async_copy(contrast, reflect, sems.at[0]),
            pltpu.make_async_copy(residual.at[0, 0, 0], wave, sems.at[1]),
            pltpu.make_async_copy(panel.at[0, 0], arrived, sems.at[2]),
        ]
        pieces = [(part, pl.ds(half * depth, depth)) for half in range(2) for part in range(2)]
        for place, (part, rows) in enumerate(pieces):
            copies.append(
                pltpu.make_async_copy(operator.at[0, 0, part, rows], whole.at[part, rows], sems.at[3 + place])
            )
        for copy in copies:
            copy.start()
        for copy in copies[:3]:
            copy.wait()
        take(arrived, 0, wave, reflect, None, grad, left)
        sums = [None, None]
        for place, (part, rows) in enumerate(pieces):
            copies[3 + place].wait()
            upper, lower = split(whole[part, rows])
            high[part, rows] = upper
            low[part, rows] = lower
            big = dot(left[:, rows], upper)
            small = dot(left[pl.ds(0, 2 * shots), rows], lower)
            total = big[: 2 * shots] + (big[2 * shots :] + small)
            sums[part] = total if sums[part] is None else sums[part] + total
        parts = sums[0][:shots] - sums[1][shots:], sums[1][:shots] + sums[0][shots:]
        store(out, parts)


def store(out, parts):
    start = 0
    for piece in out:
        for part in range(2):
            piece[part] = parts[part][start : start + piece.shape[1]]
        start += piece.shape[1]


def piece_shapes(parity, rows, breadth):
    counts = [rows] if parity else [rows - TAIL, TAIL]
    return tuple(pltpu.VMEM((2, count, breadth), jnp.float32) for count in counts)


def first(parity, operator, contrast, residual, panel, carried):
    shots, breadth = panel.shape[3:]
    half = pltpu.VMEM((2, breadth, breadth), jnp.bfloat16)
    outs = piece_shapes(parity, shots // HALVES, breadth) * HALVES
    return pl.pallas_call(
        functools.partial(first_kernel, parity, bool(carried)),
        out_shape=(*outs, half, half, pltpu.VMEM((8, breadth), jnp.float32)),
        in_specs=[IN_HBM] * 4 + [IN_VMEM] * len(carried),
        out_specs=(IN_VMEM,) * (len(outs) + 3),
        scratch_shapes=[
            pltpu.VMEM((2, breadth, breadth), jnp.float32),
            pltpu.VMEM((1, breadth), jnp.float32),
            pltpu.VMEM((2, shots, breadth), jnp.float32),
            pltpu.VMEM((2, shots, breadth), jnp.float32),
            pltpu.VMEM((4 * shots, breadth), jnp.bfloat16),
            pltpu.SemaphoreType.DMA((7,)),
        ],
        input_output_aliases={4 + i: len(outs) + i for i in range(len(carried))},
        compiler_params=PARAMS,
        cost_estimate=cost(f"first_{parity}"),
        name=f"first_{parity}",
    )(kept(operator), kept(contrast), kept(residual), kept(panel), *[pinned(value) for value in carried])


def arrive(tick, half, parity, panel, shared, grad_in, grad, left):
    residual, contrast, sites, pulse = shared
    rows = sum(piece.shape[1] for piece in panel)
    start = half * rows
    waves = residual.at[0, 0, tick]
    rest = (start, waves, contrast, grad_in, grad, left)
    if parity:
        take(panel[0], *rest)
        take(panel[1], start, waves, contrast, grad, grad, left, panel[0].shape[1])
        return
    surface = lax.axis_index("depth") == 0

    @pl.when(surface)
    def _():
        take(injected(tick, start, sites, pulse, panel[0].shape[1:]), *rest)

    @pl.when(jnp.logical_not(surface))
    def _():
        take(panel[0], *rest)


def arrive_either(half, above, mate, shared, grad_in, grad, left):
    @when_parity(1)
    def _():
        arrive(TICKS - 1, half, 1, mate, shared, grad_in, grad, left)

    @when_parity(0)
    def _():
        arrive(TICKS - 1, half, 0, (above,), shared, grad_in, grad, left)


def step_kernel(tick, half, parity, *refs):
    panel, refs = refs[: 1 + parity], refs[1 + parity :]
    shared, (high, low, grad_in) = refs[:4], refs[4:7]
    *out, grad, left = refs[7:]

    @when_parity(parity)
    def _():
        arrive(tick, half, parity, panel, shared, grad_in, grad, left)
        store(out, multiply(left, high, low, slice(None)))


def step(tick, half, parity, panel, shared, high, low, grad, rows):
    breadth = grad.shape[1]
    outs = piece_shapes(parity, rows, breadth)
    operands = [pinned(value) for value in (*panel, *shared, high, low, grad)]
    return pl.pallas_call(
        functools.partial(step_kernel, tick, half, parity),
        out_shape=(*outs, pltpu.VMEM(grad.shape, jnp.float32)),
        in_specs=[IN_VMEM] * len(operands),
        out_specs=(IN_VMEM,) * (len(outs) + 1),
        scratch_shapes=[pltpu.VMEM((4 * rows, breadth), jnp.bfloat16)],
        input_output_aliases={len(operands) - 1: len(outs)},
        compiler_params=PARAMS,
        cost_estimate=cost(f"step_{half}_{parity}"),
        name=f"step_{tick}_{half}_{parity}",
    )(*operands)


def gradient_chunks(above, mate, shared, grad, scale):
    breadth = grad.shape[1]
    count = lax.axis_size("freq")
    width = breadth // count

    def body(above, mate, mate_tail, residual, contrast, sites, pulse, grad_in, *refs):
        chunks, total = refs[:count], refs[count]
        arrive_either(HALVES - 1, above, (mate, mate_tail), (residual, contrast, sites, pulse), grad_in, total, None)
        gradient = jnp.sum(total[...], axis=0, keepdims=True) * scale
        me = lax.axis_index("freq")
        for distance in range(count):
            owner = lax.rem(me + distance, count)
            chunk = jnp.zeros((1, width), jnp.float32)
            for place in range(count):
                piece = gradient[:, place * width : (place + 1) * width]
                chunk = jnp.where(owner == place, piece, chunk)
            chunks[distance][...] = chunk

    operands = [pinned(value) for value in (above, *mate, *shared, grad)]
    return pl.pallas_call(
        body,
        out_shape=(pltpu.VMEM((1, width), jnp.float32),) * count,
        in_specs=[IN_VMEM] * len(operands),
        out_specs=(IN_VMEM,) * count,
        scratch_shapes=[pltpu.VMEM(grad.shape, jnp.float32)],
        compiler_params=PARAMS,
        cost_estimate=cost("gradient"),
        name="gradient",
    )(*operands)


def last_kernel(half, chained, above, mate, mate_tail, *refs):
    shared, high, low = refs[:4], refs[4], refs[5]
    if chained:
        out, left, held, sem = refs[7:]
        grad_in = grad = None
    else:
        grad_in, out, grad, left, held, sem = refs[6:]
    arrive_either(half, above, (mate, mate_tail), shared, grad_in, grad, left)
    held[0], held[1] = multiply(left, high, low, slice(None))
    rows = held.shape[1]
    copy = pltpu.make_async_copy(held, out.at[:, pl.ds(half * rows, rows)], sem)
    copy.start()
    copy.wait()


def last(half, above, mate, shared, high, low, grad, out):
    rows, breadth = above.shape[1:]
    operands = [pinned(value) for value in (above, *mate, *shared, high, low)]
    whole = pltpu.HBM((2, rows * HALVES, breadth), jnp.float32)
    if out is None:
        operands.append(pinned(grad))
        out_shape, aliases = (whole, pltpu.VMEM(grad.shape, jnp.float32)), {9: 1}
    else:
        operands.append(kept(out))
        out_shape, aliases = (whole,), {9: 0}
    return pl.pallas_call(
        functools.partial(last_kernel, half, out is not None),
        out_shape=out_shape,
        in_specs=[IN_VMEM] * 9 + [IN_VMEM if out is None else IN_HBM],
        out_specs=(IN_HBM, IN_VMEM)[: len(out_shape)],
        scratch_shapes=[
            pltpu.VMEM((4 * rows, breadth), jnp.bfloat16),
            pltpu.VMEM((2, rows, breadth), jnp.float32),
            pltpu.SemaphoreType.DMA,
        ],
        input_output_aliases=aliases,
        compiler_params=PARAMS,
        cost_estimate=cost(f"last_{half}"),
        name=f"last_{half}",
    )(*operands)


def cross_route(levels):
    route = {level: (level + 1) % levels for level in range(levels)}
    chips = levels // 2
    if chips % 2 == 0:
        for chip in range(chips - 1, 1, -2):
            route[levels - 1 if chip == chips - 1 else 2 * chip] = 2 * (chip - 2) + 1
        route[2 if chips > 2 else levels - 1] = 0
    return sorted(route.items())


def local(
    extrapolation_operator,
    impedance_contrast,
    ascending_residual,
    arriving_downward_matrices,
    shot_node_indices,
    emitted_pulse,
):
    levels = lax.axis_size("depth")
    freqs = lax.axis_size("freq")
    shots = arriving_downward_matrices.shape[3]
    mate_route = [(level, level ^ 1) for level in range(levels)]
    down_route = cross_route(levels)
    shared = (ascending_residual, impedance_contrast, shot_node_indices, emitted_pulse[0].T)

    def mate(pieces):
        return [lax.ppermute(piece, "depth", mate_route) for piece in pieces]

    def down(piece):
        return lax.ppermute(piece, "depth", down_route)

    rows = shots // HALVES
    start = (extrapolation_operator, impedance_contrast, ascending_residual, arriving_downward_matrices)
    results = first(1, *start, ())
    above = [down(piece) for piece in results[:HALVES]]
    *even, high, low, grad = first(0, *start, results[HALVES:])
    beside = [mate(even[2 * half : 2 * half + 2]) for half in range(HALVES)]
    for tick in range(1, TICKS - 1):
        later = []
        for half in range(HALVES):
            odd, grad = step(tick, half, 1, beside[half], shared, high, low, grad, rows)
            later.append(down(odd))
        beside = []
        for half in range(HALVES):
            *even, grad = step(tick, half, 0, (above[half],), shared, high, low, grad, rows)
            beside.append(mate(even))
        above = later

    scale = 1.0 / math.sqrt(shots * TICKS)
    out, grad = last(0, above[0], beside[0], shared, high, low, grad, None)
    chunks = gradient_chunks(above[1], beside[1], shared, grad, scale)
    gradient = chunks[0]
    for distance in range(1, freqs):
        route = [(i, (i + distance) % freqs) for i in range(freqs)]
        gradient = gradient + lax.ppermute(chunks[distance], "freq", route)
    (out,) = last(1, above[1], beside[1], shared, high, low, None, out)
    return (out[None, None], gradient)


def solution(mesh):
    placed = (
        P("freq", "depth", None, None, None),
        P("depth", None),
        P("freq", "depth", None, None, None, None),
        P("freq", "depth", None, None, None),
        P(),
        P("freq", None, None),
    )
    return jax.shard_map(
        local,
        mesh=mesh,
        in_specs=placed,
        out_specs=(P("freq", "depth", None, None, None), P("depth", "freq")),
        check_vma=False,
    )
```

time: 32.6 us -> 31.6 us (0.969)
  waiting for transfers between devices: 12.3 us -> 3.61 us
  starting transfers between devices: 10.6 us -> 16.8 us
  Pallas kernels: 8.3 us -> 9.63 us
    ppermute x4 -> x8, waiting for transfers between devices: 7.05 us -> 1.77 us  [down(): return lax.ppermute(piece, 'depth', down_route)]
    ppermute x4 -> x8, starting transfers between devices: 5.9 us -> 9.74 us  [down(): return lax.ppermute(piece, 'depth', down_route)]
    ppermute x8 -> x16, waiting for transfers between devices: 4.86 us -> 1.66 us  [mate(): return [lax.ppermute(piece, 'depth', mate_route) for piece in pieces]]
    ppermute x8 -> x16, starting transfers between devices: 2.27 us -> 4.81 us  [mate(): return [lax.ppermute(piece, 'depth', mate_route) for piece in pieces]]
    pallas_call x8 -> x15, Pallas kernels: 5.59 us -> 6.92 us  [the longest x12 4.05 us: step(): pl.pallas_call(functools.partial(step_kernel, tick, half, parity), out_sh...]
  transfers between devices with their start and end apart: 13 -> 25, of which waited for: 9 -> 9; matrix products, arithmetic and copies ran while one was open for 0% -> 0% of each run, Pallas kernels for 21% -> 30%
where the time goes in v6:
time: 31.6 us; the launch traced here: 31.4 us
  starting transfers between devices  16.8 us (53%)
  Pallas kernels  9.63 us (30%)
  waiting for transfers between devices  3.61 us (11%)
  between operations  0.83 us (3%)
  other arithmetic  0.56 us (2%)
    ppermute x8, starting transfers between devices, down(): return lax.ppermute(piece, 'depth', down_route)  9.74 us
    ppermute x16, starting transfers between devices, mate(): return [lax.ppermute(piece, 'depth', mate_route) for piece in pieces]  4.81 us
    pallas_call x12, Pallas kernels, step(): pl.pallas_call(functools.partial(step_kernel, tick, half, parity), out_sh...  4.05 us
    pallas_call x2, Pallas kernels, last(): pl.pallas_call(functools.partial(last_kernel, half, out is not None), out...  2.72 us
    pallas_call x2, Pallas kernels, first(): pl.pallas_call(functools.partial(first_kernel, parity, bool(carried)), ou...  2.71 us
    ppermute x1, starting transfers between devices, local(): gradient = gradient + lax.ppermute(chunks[distance], 'freq', route)  2.23 us
    ppermute x8, waiting for transfers between devices, down(): return lax.ppermute(piece, 'depth', down_route)  1.77 us
    ppermute x16, waiting for transfers between devices, mate(): return [lax.ppermute(piece, 'depth', mate_route) for piece in pieces]  1.66 us
  transfers between devices with their start and end apart: 25, of which 9 were waited for; matrix products, arithmetic and copies ran while one was open for 0% of the time, Pallas kernels for 30%

profile of v6, /device:TPU:0, one launch (start us, length us, event | category | flops | bytes accessed | tf_op | source)
XLA Modules:
  0.0 31.4 jit_solution(15950036205158564522)
XLA Ops:
  0.6 0.1 first_1.1
  0.7 2.9 %collective-permute-start.7 = (f32[2,48,512]{2,1,0:T(8,128)S(1)}, f32[2,48,512]{2,1,0:T(8,128)S(1)}, u32[]{:S(2)}, u32[]{:S(2)}) collective-permute-start(f32[2,48,512]{2,1,0:T(8,128)S(1)} %get-tuple-element.62), channel_id=1, source_target_pairs={{0,2},{2,4},{4,0},{6,8},{8,10},{10,12},{12,6},{14,16},{16,18},{18,... | collective-permute-start | bytes 589832 | tf_op jit(solution)/shard_map/ppermute | solution.py:337
  3.6 0.2 collective-permute-start.6
  3.9 2.6 %first_0.1 = (f32[2,32,512]{2,1,0:T(8,128)S(1)}, f32[2,16,512]{2,1,0:T(8,128)S(1)}, f32[2,32,512]{2,1,0:T(8,128)S(1)}, f32[2,16,512]{2,1,0:T(8,128)S(1)}, bf16[2...) custom-call(f32[1,1,2,512,512]{4,3,2,1,0:T(8,128)} %refs_0_.5, ...), custom_call_target="tpu_custom_call", output_to_operand_aliasing={{4}: (4, {}), {5}: (5, {}), {6}: (6, {})} | custom-call | flops 1 | bytes 1 | tf_op jit(solution)/shard_map/first_0/pallas_call | solution.py:156
  6.5 0.1 collective-permute-start.2
  6.6 0.5 %collective-permute-start.3 = (f32[2,16,512]{2,1,0:T(8,128)S(1)}, f32[2,16,512]{2,1,0:T(8,128)S(1)}, u32[]{:S(2)}, u32[]{:S(2)}) collective-permute-start(f32[2,16,512]{2,1,0:T(8,128)S(1)} %get-tuple-element.56), channel_id=1, source_target_pairs={{0,2},{2,0},{4,6},{6,4},{8,10},{10,8},{12,14},{14,12},{16,18},{18,... | collective-permute-start | bytes 196616 | tf_op jit(solution)/shard_map/ppermute | solution.py:334
  7.1 0.1 collective-permute-start
  7.2 0.9 %collective-permute-done.3.refs_1_ = f32[2,16,512]{2,1,0:T(8,128)S(1)} collective-permute-done((f32[2,16,512]{2,1,0:T(8,128)S(1)}, f32[2,16,512]{2,1,0:T(8,128)S(1)}, u32[]{:S(2)}, u32[]{:S(2)}) %collective-permute-start.3) | collective-permute-done | bytes 65568 | tf_op jit(solution)/shard_map/ppermute | solution.py:334
  8.0 0.3 %collective-permute-start.1 = (f32[2,16,512]{2,1,0:T(8,128)S(1)}, f32[2,16,512]{2,1,0:T(8,128)S(1)}, u32[]{:S(2)}, u32[]{:S(2)}) collective-permute-start(f32[2,16,512]{2,1,0:T(8,128)S(1)} %get-tuple-element.52), channel_id=1, source_target_pairs={{0,2},{2,0},{4,6},{6,4},{8,10},{10,8},{12,14},{14,12},{16,18},{18,... | collective-permute-start | bytes 196616 | tf_op jit(solution)/shard_map/ppermute | solution.py:334
  8.3 0.0 collective-permute-done.2.refs_0_
  8.3 0.0 copy-done
  8.3 0.0 copy-done.1
  8.4 0.8 %collective-permute-start.5 = (f32[2,48,512]{2,1,0:T(8,128)S(1)}, f32[2,48,512]{2,1,0:T(8,128)S(1)}, u32[]{:S(2)}, u32[]{:S(2)}) collective-permute-start(f32[2,48,512]{2,1,0:T(8,128)S(1)} %get-tuple-element.60), channel_id=1, source_target_pairs={{0,2},{2,4},{4,0},{6,8},{8,10},{10,12},{12,6},{14,16},{16,18},{18,... | collective-permute-start | bytes 589832 | tf_op jit(solution)/shard_map/ppermute | solution.py:337
  9.2 0.1 collective-permute-done.1.refs_1_
  9.3 0.0 collective-permute-done.refs_0_
  9.3 1.7 %collective-permute-start.4 = (f32[2,48,512]{2,1,0:T(8,128)S(1)}, f32[2,48,512]{2,1,0:T(8,128)S(1)}, u32[]{:S(2)}, u32[]{:S(2)}) collective-permute-start(f32[2,48,512]{2,1,0:T(8,128)S(1)} %get-tuple-element.59), channel_id=1, source_target_pairs={{0,2},{2,4},{4,0},{6,8},{8,10},{10,12},{12,6},{14,16},{16,18},{18,... | collective-permute-start | bytes 589832 | tf_op jit(solution)/shard_map/ppermute | solution.py:337
  11.0 0.0 collective-permute-done.7.refs_0_
  11.0 0.7 %step_1_0_0.1 = (f32[2,32,512]{2,1,0:T(8,128)S(1)}, f32[2,16,512]{2,1,0:T(8,128)S(1)}, f32[8,512]{1,0:T(8,128)S(1)}) custom-call(f32[2,48,512]{2,1,0:T(8,128)S(1)} %collective-permute-done.7.refs_0_, f32[1,1,5,2,96,512]{5,4,3,2,1,0:T(8,128)S(1)} %copy-done, f32[1,512]{1,0:T(1,128)S(1)} %copy-done.1, ...), custom_call_target="tpu_custom_call", output_to_operand_aliasing={{2}: (7, {})} | custom-call | flops 1 | bytes 1 | tf_op jit(solution)/shard_map/step_1_0_0/pallas_call | solution.py:222
  11.6 0.1 collective-permute-start.11
  11.7 0.5 %collective-permute-start.10 = (f32[2,32,512]{2,1,0:T(8,128)S(1)}, f32[2,32,512]{2,1,0:T(8,128)S(1)}, u32[]{:S(2)}, u32[]{:S(2)}) collective-permute-start(f32[2,32,512]{2,1,0:T(8,128)S(1)} %get-tuple-element.67), channel_id=1, source_target_pairs={{0,2},{2,0},{4,6},{6,4},{8,10},{10,8},{12,14},{14,12},{16,18},{18,... | collective-permute-start | bytes 393224 | tf_op jit(solution)/shard_map/ppermute | solution.py:334
  12.2 0.0 collective-permute-done.6.refs_0_
  12.2 0.7 %step_1_1_0.1 = (f32[2,32,512]{2,1,0:T(8,128)S(1)}, f32[2,16,512]{2,1,0:T(8,128)S(1)}, f32[8,512]{1,0:T(8,128)S(1)}) custom-call(f32[2,48,512]{2,1,0:T(8,128)S(1)} %collective-permute-done.6.refs_0_, f32[1,1,5,2,96,512]{5,4,3,2,1,0:T(8,128)S(1)} %copy-done, f32[1,512]{1,0:T(1,128)S(1)} %copy-done.1, ...), custom_call_target="tpu_custom_call", output_to_operand_aliasing={{2}: (7, {})} | custom-call | flops 10000000 | bytes 1 | tf_op jit(solution)/shard_map/step_1_1_0/pallas_call | solution.py:222
  12.9 0.1 collective-permute-start.8
  12.9 0.0 collective-permute-done.11.refs_1_
  13.0 0.5 %collective-permute-start.9 = (f32[2,16,512]{2,1,0:T(8,128)S(1)}, f32[2,16,512]{2,1,0:T(8,128)S(1)}, u32[]{:S(2)}, u32[]{:S(2)}) collective-permute-start(f32[2,16,512]{2,1,0:T(8,128)S(1)} %get-tuple-element.66), channel_id=1, source_target_pairs={{0,2},{2,0},{4,6},{6,4},{8,10},{10,8},{12,14},{14,12},{16,18},{18,... | collective-permute-start | bytes 196616 | tf_op jit(solution)/shard_map/ppermute | solution.py:334
  13.4 0.0 collective-permute-done.10.refs_0_
  13.4 0.7 %collective-permute-start.18 = (f32[2,48,512]{2,1,0:T(8,128)S(1)}, f32[2,48,512]{2,1,0:T(8,128)S(1)}, u32[]{:S(2)}, u32[]{:S(2)}) collective-permute-start(f32[2,48,512]{2,1,0:T(8,128)S(1)} %get-tuple-element.81), channel_id=1, source_target_pairs={{0,2},{2,4},{4,0},{6,8},{8,10},{10,12},{12,6},{14,16},{16,18},{18,... | collective-permute-start | bytes 589832 | tf_op jit(solution)/shard_map/ppermute | solution.py:337
  14.1 0.2 collective-permute-done.9.refs_1_
  14.4 0.0 collective-permute-done.8.refs_0_
  14.4 0.0 collective-permute-done.5.refs_0_
  14.4 0.7 %step_2_0_0.1 = (f32[2,32,512]{2,1,0:T(8,128)S(1)}, f32[2,16,512]{2,1,0:T(8,128)S(1)}, f32[8,512]{1,0:T(8,128)S(1)}) custom-call(f32[2,48,512]{2,1,0:T(8,128)S(1)} %collective-permute-done.5.refs_0_, f32[1,1,5,2,96,512]{5,4,3,2,1,0:T(8,128)S(1)} %copy-done, f32[1,512]{1,0:T(1,128)S(1)} %copy-done.1, ...), custom_call_target="tpu_custom_call", output_to_operand_aliasing={{2}: (7, {})} | custom-call | flops 1 | bytes 1 | tf_op jit(solution)/shard_map/step_2_0_0/pallas_call | solution.py:222
  15.1 0.3 collective-permute-start.15
  15.3 0.3 collective-permute-start.14
  15.7 0.6 %collective-permute-done.4.refs_0_ = f32[2,48,512]{2,1,0:T(8,128)S(1)} collective-permute-done((f32[2,48,512]{2,1,0:T(8,128)S(1)}, f32[2,48,512]{2,1,0:T(8,128)S(1)}, u32[]{:S(2)}, u32[]{:S(2)}) %collective-permute-start.4) | collective-permute-done | bytes 196640 | tf_op jit(solution)/shard_map/ppermute | solution.py:337
  16.2 0.7 %step_2_1_0.1 = (f32[2,32,512]{2,1,0:T(8,128)S(1)}, f32[2,16,512]{2,1,0:T(8,128)S(1)}, f32[8,512]{1,0:T(8,128)S(1)}) custom-call(f32[2,48,512]{2,1,0:T(8,128)S(1)} %collective-permute-done.4.refs_0_, f32[1,1,5,2,96,512]{5,4,3,2,1,0:T(8,128)S(1)} %copy-done, f32[1,512]{1,0:T(1,128)S(1)} %copy-done.1, ...), custom_call_target="tpu_custom_call", output_to_operand_aliasing={{2}: (7, {})} | custom-call | flops 10000000 | bytes 1 | tf_op jit(solution)/shard_map/step_2_1_0/pallas_call | solution.py:222
  16.9 0.1 collective-permute-start.12
  17.0 0.5 %collective-permute-start.17 = (f32[2,48,512]{2,1,0:T(8,128)S(1)}, f32[2,48,512]{2,1,0:T(8,128)S(1)}, u32[]{:S(2)}, u32[]{:S(2)}) collective-permute-start(f32[2,48,512]{2,1,0:T(8,128)S(1)} %get-tuple-element.80), channel_id=1, source_target_pairs={{0,2},{2,4},{4,0},{6,8},{8,10},{10,12},{12,6},{14,16},{16,18},{18,... | collective-permute-start | bytes 589832 | tf_op jit(solution)/shard_map/ppermute | solution.py:337
  17.5 0.0 collective-permute-done.15.refs_1_
  17.5 1.1 %collective-permute-start.13 = (f32[2,16,512]{2,1,0:T(8,128)S(1)}, f32[2,16,512]{2,1,0:T(8,128)S(1)}, u32[]{:S(2)}, u32[]{:S(2)}) collective-permute-start(f32[2,16,512]{2,1,0:T(8,128)S(1)} %get-tuple-element.74), channel_id=1, source_target_pairs={{0,2},{2,0},{4,6},{6,4},{8,10},{10,8},{12,14},{14,12},{16,18},{18,... | collective-permute-start | bytes 196616 | tf_op jit(solution)/shard_map/ppermute | solution.py:334
  18.6 0.0 collective-permute-done.14.refs_0_
  18.6 0.6 %collective-permute-start.21 = (f32[2,48,512]{2,1,0:T(8,128)S(1)}, f32[2,48,512]{2,1,0:T(8,128)S(1)}, u32[]{:S(2)}, u32[]{:S(2)}) collective-permute-start(f32[2,48,512]{2,1,0:T(8,128)S(1)} %get-tuple-element.86), channel_id=1, source_target_pairs={{0,2},{2,4},{4,0},{6,8},{8,10},{10,12},{12,6},{14,16},{16,18},{18,... | collective-permute-start | bytes 589832 | tf_op jit(solution)/shard_map/ppermute | solution.py:337
  19.2 0.3 collective-permute-done.13.refs_1_
  19.5 0.0 collective-permute-done.12.refs_0_
  19.5 2.3 %collective-permute-start.16 = (f32[2,48,512]{2,1,0:T(8,128)S(1)}, f32[2,48,512]{2,1,0:T(8,128)S(1)}, u32[]{:S(2)}, u32[]{:S(2)}) collective-permute-start(f32[2,48,512]{2,1,0:T(8,128)S(1)} %get-tuple-element.79), channel_id=1, source_target_pairs={{0,2},{2,4},{4,0},{6,8},{8,10},{10,12},{12,6},{14,16},{16,18},{18,... | collective-permute-start | bytes 589832 | tf_op jit(solution)/shard_map/ppermute | solution.py:337
  21.8 0.0 collective-permute-done.18.refs_0_
  21.8 0.7 %step_3_0_0.1 = (f32[2,32,512]{2,1,0:T(8,128)S(1)}, f32[2,16,512]{2,1,0:T(8,128)S(1)}, f32[8,512]{1,0:T(8,128)S(1)}) custom-call(f32[2,48,512]{2,1,0:T(8,128)S(1)} %collective-permute-done.18.refs_0_, f32[1,1,5,2,96,512]{5,4,3,2,1,0:T(8,128)S(1)} %copy-done, f32[1,512]{1,0:T(1,128)S(1)} %copy-done.1, ...), custom_call_target="tpu_custom_call", output_to_operand_aliasing={{2}: (7, {})} | custom-call | flops 1 | bytes 1 | tf_op jit(solution)/shard_map/step_3_0_0/pallas_call | solution.py:222
  22.5 0.1 collective-permute-start.22
  22.6 0.5 %collective-permute-start.23 = (f32[2,16,512]{2,1,0:T(8,128)S(1)}, f32[2,16,512]{2,1,0:T(8,128)S(1)}, u32[]{:S(2)}, u32[]{:S(2)}) collective-permute-start(f32[2,16,512]{2,1,0:T(8,128)S(1)} %get-tuple-element.88), channel_id=1, source_target_pairs={{0,2},{2,0},{4,6},{6,4},{8,10},{10,8},{12,14},{14,12},{16,18},{18,... | collective-permute-start | bytes 196616 | tf_op jit(solution)/shard_map/ppermute | solution.py:334
  23.1 0.0 collective-permute-done.17.refs_0_
  23.1 0.7 %step_3_1_0.1 = (f32[2,32,512]{2,1,0:T(8,128)S(1)}, f32[2,16,512]{2,1,0:T(8,128)S(1)}, f32[8,512]{1,0:T(8,128)S(1)}) custom-call(f32[2,48,512]{2,1,0:T(8,128)S(1)} %collective-permute-done.17.refs_0_, f32[1,1,5,2,96,512]{5,4,3,2,1,0:T(8,128)S(1)} %copy-done, f32[1,512]{1,0:T(1,128)S(1)} %copy-done.1, ...), custom_call_target="tpu_custom_call", output_to_operand_aliasing={{2}: (7, {})} | custom-call | flops 10000000 | bytes 1 | tf_op jit(solution)/shard_map/step_3_1_0/pallas_call | solution.py:222
  23.8 0.1 collective-permute-start.19
  23.9 0.2 collective-permute-done.23.mate_tail
  24.0 0.3 %collective-permute-start.20 = (f32[2,16,512]{2,1,0:T(8,128)S(1)}, f32[2,16,512]{2,1,0:T(8,128)S(1)}, u32[]{:S(2)}, u32[]{:S(2)}) collective-permute-start(f32[2,16,512]{2,1,0:T(8,128)S(1)} %get-tuple-element.85), channel_id=1, source_target_pairs={{0,2},{2,0},{4,6},{6,4},{8,10},{10,8},{12,14},{14,12},{16,18},{18,... | collective-permute-start | bytes 196616 | tf_op jit(solution)/shard_map/ppermute | solution.py:334
  24.4 0.0 collective-permute-done.22.mate
  24.4 0.5 %collective-permute-done.21.above = f32[2,48,512]{2,1,0:T(8,128)S(1)} collective-permute-done((f32[2,48,512]{2,1,0:T(8,128)S(1)}, f32[2,48,512]{2,1,0:T(8,128)S(1)}, u32[]{:S(2)}, u32[]{:S(2)}) %collective-permute-start.21) | collective-permute-done | bytes 196640 | tf_op jit(solution)/shard_map/ppermute | solution.py:337
  24.8 1.4 %last_0.1 = (f32[2,96,512]{2,1,0:T(8,128)}, f32[8,512]{1,0:T(8,128)S(1)}) custom-call(f32[2,48,512]{2,1,0:T(8,128)S(1)} %collective-permute-done.21.above, f32[2,32,512]{2,1,0:T(8,128)S(1)} %collective-permute-done.22.mate, f32[2,16,512]{2,1,0:T(8,128)S(1)} %collective-permute-done.23.mate_tail, ...), custom_call_target="tpu_custom_call", output_to_operand_aliasing={{1}: (9, {})} | custom-call | flops 200000000 | bytes 1 | tf_op jit(solution)/shard_map/last_0/pallas_call | solution.py:291
  26.2 0.0 collective-permute-done.20.mate_tail
  26.2 0.0 collective-permute-done.19.mate
  26.2 0.7 %collective-permute-done.16.above = f32[2,48,512]{2,1,0:T(8,128)S(1)} collective-permute-done((f32[2,48,512]{2,1,0:T(8,128)S(1)}, f32[2,48,512]{2,1,0:T(8,128)S(1)}, u32[]{:S(2)}, u32[]{:S(2)}) %collective-permute-start.16) | collective-permute-done | bytes 196640 | tf_op jit(solution)/shard_map/ppermute | solution.py:337
  26.9 0.1 gradient.1
  27.1 2.2 %collective-permute-start.24 = (f32[1,256]{1,0:T(1,128)S(1)}, f32[1,256]{1,0:T(1,128)S(1)}, u32[]{:S(2)}, u32[]{:S(2)}) collective-permute-start(f32[1,256]{1,0:T(1,128)S(1)} %get-tuple-element.93), channel_id=1, source_target_pairs={{0,1},{1,0},{2,3},{3,2},{4,5},{5,4},{6,7},{7,6},{8,9},{9,8},{10,11... | collective-permute-start | bytes 3080 | tf_op jit(solution)/shard_map/ppermute | solution.py:362
  29.3 1.4 %last_1.1 = f32[2,96,512]{2,1,0:T(8,128)} custom-call(f32[2,48,512]{2,1,0:T(8,128)S(1)} %collective-permute-done.16.above, f32[2,32,512]{2,1,0:T(8,128)S(1)} %collective-permute-done.19.mate, f32[2,16,512]{2,1,0:T(8,128)S(1)} %collective-permute-done.20.mate_tail, f32[1,1,5,2,96,512]{5,4,3,2,1,0:T(8,128)S(1)} %copy-done, ...), custom_call_target="tpu_custom_call", output_to_operand_aliasing={{}: (9, {})} | custom-call | flops 1 | bytes 1 | tf_op jit(solution)/shard_map/last_1/pallas_call | solution.py:291
  30.7 0.2 collective-permute-done.24
  30.9 0.6 %add.3 = f32[1,256]{1,0:T(1,128)} add(f32[1,256]{1,0:T(1,128)S(1)} %get-tuple-element.92, f32[1,256]{1,0:T(1,128)S(1)} %collective-permute-done.24) | non-fusion elementwise | flops 256 | bytes 3072 | tf_op jit(solution)/shard_map/add | solution.py:362
  (12 shorter events, 0.0 us)
Async XLA Ops:
  0.7 10.2 %collective-permute-start.7 = (f32[2,48,512]{2,1,0:T(8,128)S(1)}, f32[2,48,512]{2,1,0:T(8,128)S(1)}, u32[]{:S(2)}, u32[]{:S(2)}) collective-permute-start(f32[2,48,512]{2,1,0:T(8,128)S(1)} %get-tuple-element.62), channel_id=1, source_target_pairs={{0,2},{2,4},{4,0},{6,8},{8,10},{10,12},{12,6},{14,16},{16,18},{18,... | collective-permute-start | bytes 589832 | tf_op jit(solution)/shard_map/ppermute | solution.py:337
  3.6 8.6 %collective-permute-start.6 = (f32[2,48,512]{2,1,0:T(8,128)S(1)}, f32[2,48,512]{2,1,0:T(8,128)S(1)}, u32[]{:S(2)}, u32[]{:S(2)}) collective-permute-start(f32[2,48,512]{2,1,0:T(8,128)S(1)} %get-tuple-element.61), channel_id=1, source_target_pairs={{0,2},{2,4},{4,0},{6,8},{8,10},{10,12},{12,6},{14,16},{16,18},{18,... | collective-permute-start | bytes 589832 | tf_op jit(solution)/shard_map/ppermute | solution.py:337
  3.9 4.5 %copy-start = (f32[1,1,5,2,96,512]{5,4,3,2,1,0:T(8,128)S(1)}, f32[1,1,5,2,96,512]{5,4,3,2,1,0:T(8,128)}, u32[]{:S(2)}) copy-start(f32[1,1,5,2,96,512]{5,4,3,2,1,0:T(8,128)} %residual.1) | copy-start | bytes 5898244
  3.9 4.5 %copy-start.1 = (f32[1,512]{1,0:T(1,128)S(1)}, f32[1,512]{1,0:T(1,128)}, u32[]{:S(2)}) copy-start(f32[1,512]{1,0:T(1,128)} %contrast.1) | copy-start | bytes 6148
  3.9 4.5 %copy-start.2 = (s32[4,96]{1,0:T(4,128)S(1)}, s32[4,96]{1,0:T(4,128)}, u32[]{:S(2)}) copy-start(s32[4,96]{1,0:T(4,128)} %sites.1) | copy-start | bytes 4612
  3.9 4.5 %copy-start.3 = (f32[1,4,2]{1,2,0:T(2,128)S(1)}, f32[1,4,2]{1,2,0:T(2,128)}, u32[]{:S(2)}) copy-start(f32[1,4,2]{1,2,0:T(2,128)} %param.11) | copy-start | bytes 100
  6.5 1.8 %collective-permute-start.2 = (f32[2,32,512]{2,1,0:T(8,128)S(1)}, f32[2,32,512]{2,1,0:T(8,128)S(1)}, u32[]{:S(2)}, u32[]{:S(2)}) collective-permute-start(f32[2,32,512]{2,1,0:T(8,128)S(1)} %get-tuple-element.55), channel_id=1, source_target_pairs={{0,2},{2,0},{4,6},{6,4},{8,10},{10,8},{12,14},{14,12},{16,18},{18,... | collective-permute-start | bytes 393224 | tf_op jit(solution)/shard_map/ppermute | solution.py:334
  6.6 1.4 %collective-permute-start.3 = (f32[2,16,512]{2,1,0:T(8,128)S(1)}, f32[2,16,512]{2,1,0:T(8,128)S(1)}, u32[]{:S(2)}, u32[]{:S(2)}) collective-permute-start(f32[2,16,512]{2,1,0:T(8,128)S(1)} %get-tuple-element.56), channel_id=1, source_target_pairs={{0,2},{2,0},{4,6},{6,4},{8,10},{10,8},{12,14},{14,12},{16,18},{18,... | collective-permute-start | bytes 196616 | tf_op jit(solution)/shard_map/ppermute | solution.py:334
  7.1 2.2 %collective-permute-start = (f32[2,32,512]{2,1,0:T(8,128)S(1)}, f32[2,32,512]{2,1,0:T(8,128)S(1)}, u32[]{:S(2)}, u32[]{:S(2)}) collective-permute-start(f32[2,32,512]{2,1,0:T(8,128)S(1)} %get-tuple-element.51), channel_id=1, source_target_pairs={{0,2},{2,0},{4,6},{6,4},{8,10},{10,8},{12,14},{14,12},{16,18},{18,... | collective-permute-start | bytes 393224 | tf_op jit(solution)/shard_map/ppermute | solution.py:334
  8.0 1.3 %collective-permute-start.1 = (f32[2,16,512]{2,1,0:T(8,128)S(1)}, f32[2,16,512]{2,1,0:T(8,128)S(1)}, u32[]{:S(2)}, u32[]{:S(2)}) collective-permute-start(f32[2,16,512]{2,1,0:T(8,128)S(1)} %get-tuple-element.52), channel_id=1, source_target_pairs={{0,2},{2,0},{4,6},{6,4},{8,10},{10,8},{12,14},{14,12},{16,18},{18,... | collective-permute-start | bytes 196616 | tf_op jit(solution)/shard_map/ppermute | solution.py:334
  8.4 6.0 %collective-permute-start.5 = (f32[2,48,512]{2,1,0:T(8,128)S(1)}, f32[2,48,512]{2,1,0:T(8,128)S(1)}, u32[]{:S(2)}, u32[]{:S(2)}) collective-permute-start(f32[2,48,512]{2,1,0:T(8,128)S(1)} %get-tuple-element.60), channel_id=1, source_target_pairs={{0,2},{2,4},{4,0},{6,8},{8,10},{10,12},{12,6},{14,16},{16,18},{18,... | collective-permute-start | bytes 589832 | tf_op jit(solution)/shard_map/ppermute | solution.py:337
  9.3 7.0 %collective-permute-start.4 = (f32[2,48,512]{2,1,0:T(8,128)S(1)}, f32[2,48,512]{2,1,0:T(8,128)S(1)}, u32[]{:S(2)}, u32[]{:S(2)}) collective-permute-start(f32[2,48,512]{2,1,0:T(8,128)S(1)} %get-tuple-element.59), channel_id=1, source_target_pairs={{0,2},{2,4},{4,0},{6,8},{8,10},{10,12},{12,6},{14,16},{16,18},{18,... | collective-permute-start | bytes 589832 | tf_op jit(solution)/shard_map/ppermute | solution.py:337
  11.6 1.3 %collective-permute-start.11 = (f32[2,16,512]{2,1,0:T(8,128)S(1)}, f32[2,16,512]{2,1,0:T(8,128)S(1)}, u32[]{:S(2)}, u32[]{:S(2)}) collective-permute-start(f32[2,16,512]{2,1,0:T(8,128)S(1)} %get-tuple-element.68), channel_id=1, source_target_pairs={{0,2},{2,0},{4,6},{6,4},{8,10},{10,8},{12,14},{14,12},{16,18},{18,... | collective-permute-start | bytes 196616 | tf_op jit(solution)/shard_map/ppermute | solution.py:334
  11.7 1.7 %collective-permute-start.10 = (f32[2,32,512]{2,1,0:T(8,128)S(1)}, f32[2,32,512]{2,1,0:T(8,128)S(1)}, u32[]{:S(2)}, u32[]{:S(2)}) collective-permute-start(f32[2,32,512]{2,1,0:T(8,128)S(1)} %get-tuple-element.67), channel_id=1, source_target_pairs={{0,2},{2,0},{4,6},{6,4},{8,10},{10,8},{12,14},{14,12},{16,18},{18,... | collective-permute-start | bytes 393224 | tf_op jit(solution)/shard_map/ppermute | solution.py:334
  12.9 1.5 %collective-permute-start.8 = (f32[2,32,512]{2,1,0:T(8,128)S(1)}, f32[2,32,512]{2,1,0:T(8,128)S(1)}, u32[]{:S(2)}, u32[]{:S(2)}) collective-permute-start(f32[2,32,512]{2,1,0:T(8,128)S(1)} %get-tuple-element.65), channel_id=1, source_target_pairs={{0,2},{2,0},{4,6},{6,4},{8,10},{10,8},{12,14},{14,12},{16,18},{18,... | collective-permute-start | bytes 393224 | tf_op jit(solution)/shard_map/ppermute | solution.py:334
  13.0 1.4 %collective-permute-start.9 = (f32[2,16,512]{2,1,0:T(8,128)S(1)}, f32[2,16,512]{2,1,0:T(8,128)S(1)}, u32[]{:S(2)}, u32[]{:S(2)}) collective-permute-start(f32[2,16,512]{2,1,0:T(8,128)S(1)} %get-tuple-element.66), channel_id=1, source_target_pairs={{0,2},{2,0},{4,6},{6,4},{8,10},{10,8},{12,14},{14,12},{16,18},{18,... | collective-permute-start | bytes 196616 | tf_op jit(solution)/shard_map/ppermute | solution.py:334
  13.4 8.4 %collective-permute-start.18 = (f32[2,48,512]{2,1,0:T(8,128)S(1)}, f32[2,48,512]{2,1,0:T(8,128)S(1)}, u32[]{:S(2)}, u32[]{:S(2)}) collective-permute-start(f32[2,48,512]{2,1,0:T(8,128)S(1)} %get-tuple-element.81), channel_id=1, source_target_pairs={{0,2},{2,4},{4,0},{6,8},{8,10},{10,12},{12,6},{14,16},{16,18},{18,... | collective-permute-start | bytes 589832 | tf_op jit(solution)/shard_map/ppermute | solution.py:337
  15.1 2.4 %collective-permute-start.15 = (f32[2,16,512]{2,1,0:T(8,128)S(1)}, f32[2,16,512]{2,1,0:T(8,128)S(1)}, u32[]{:S(2)}, u32[]{:S(2)}) collective-permute-start(f32[2,16,512]{2,1,0:T(8,128)S(1)} %get-tuple-element.76), channel_id=1, source_target_pairs={{0,2},{2,0},{4,6},{6,4},{8,10},{10,8},{12,14},{14,12},{16,18},{18,... | collective-permute-start | bytes 196616 | tf_op jit(solution)/shard_map/ppermute | solution.py:334
  15.3 3.2 %collective-permute-start.14 = (f32[2,32,512]{2,1,0:T(8,128)S(1)}, f32[2,32,512]{2,1,0:T(8,128)S(1)}, u32[]{:S(2)}, u32[]{:S(2)}) collective-permute-start(f32[2,32,512]{2,1,0:T(8,128)S(1)} %get-tuple-element.75), channel_id=1, source_target_pairs={{0,2},{2,0},{4,6},{6,4},{8,10},{10,8},{12,14},{14,12},{16,18},{18,... | collective-permute-start | bytes 393224 | tf_op jit(solution)/shard_map/ppermute | solution.py:334
  16.9 2.6 %collective-permute-start.12 = (f32[2,32,512]{2,1,0:T(8,128)S(1)}, f32[2,32,512]{2,1,0:T(8,128)S(1)}, u32[]{:S(2)}, u32[]{:S(2)}) collective-permute-start(f32[2,32,512]{2,1,0:T(8,128)S(1)} %get-tuple-element.73), channel_id=1, source_target_pairs={{0,2},{2,0},{4,6},{6,4},{8,10},{10,8},{12,14},{14,12},{16,18},{18,... | collective-permute-start | bytes 393224 | tf_op jit(solution)/shard_map/ppermute | solution.py:334
  17.0 6.1 %collective-permute-start.17 = (f32[2,48,512]{2,1,0:T(8,128)S(1)}, f32[2,48,512]{2,1,0:T(8,128)S(1)}, u32[]{:S(2)}, u32[]{:S(2)}) collective-permute-start(f32[2,48,512]{2,1,0:T(8,128)S(1)} %get-tuple-element.80), channel_id=1, source_target_pairs={{0,2},{2,4},{4,0},{6,8},{8,10},{10,12},{12,6},{14,16},{16,18},{18,... | collective-permute-start | bytes 589832 | tf_op jit(solution)/shard_map/ppermute | solution.py:337
  17.5 2.0 %collective-permute-start.13 = (f32[2,16,512]{2,1,0:T(8,128)S(1)}, f32[2,16,512]{2,1,0:T(8,128)S(1)}, u32[]{:S(2)}, u32[]{:S(2)}) collective-permute-start(f32[2,16,512]{2,1,0:T(8,128)S(1)} %get-tuple-element.74), channel_id=1, source_target_pairs={{0,2},{2,0},{4,6},{6,4},{8,10},{10,8},{12,14},{14,12},{16,18},{18,... | collective-permute-start | bytes 196616 | tf_op jit(solution)/shard_map/ppermute | solution.py:334
  18.6 6.2 %collective-permute-start.21 = (f32[2,48,512]{2,1,0:T(8,128)S(1)}, f32[2,48,512]{2,1,0:T(8,128)S(1)}, u32[]{:S(2)}, u32[]{:S(2)}) collective-permute-start(f32[2,48,512]{2,1,0:T(8,128)S(1)} %get-tuple-element.86), channel_id=1, source_target_pairs={{0,2},{2,4},{4,0},{6,8},{8,10},{10,12},{12,6},{14,16},{16,18},{18,... | collective-permute-start | bytes 589832 | tf_op jit(solution)/shard_map/ppermute | solution.py:337
  19.5 7.5 %collective-permute-start.16 = (f32[2,48,512]{2,1,0:T(8,128)S(1)}, f32[2,48,512]{2,1,0:T(8,128)S(1)}, u32[]{:S(2)}, u32[]{:S(2)}) collective-permute-start(f32[2,48,512]{2,1,0:T(8,128)S(1)} %get-tuple-element.79), channel_id=1, source_target_pairs={{0,2},{2,4},{4,0},{6,8},{8,10},{10,12},{12,6},{14,16},{16,18},{18,... | collective-permute-start | bytes 589832 | tf_op jit(solution)/shard_map/ppermute | solution.py:337
  22.5 1.9 %collective-permute-start.22 = (f32[2,32,512]{2,1,0:T(8,128)S(1)}, f32[2,32,512]{2,1,0:T(8,128)S(1)}, u32[]{:S(2)}, u32[]{:S(2)}) collective-permute-start(f32[2,32,512]{2,1,0:T(8,128)S(1)} %get-tuple-element.87), channel_id=1, source_target_pairs={{0,2},{2,0},{4,6},{6,4},{8,10},{10,8},{12,14},{14,12},{16,18},{18,... | collective-permute-start | bytes 393224 | tf_op jit(solution)/shard_map/ppermute | solution.py:334
  22.6 1.4 %collective-permute-start.23 = (f32[2,16,512]{2,1,0:T(8,128)S(1)}, f32[2,16,512]{2,1,0:T(8,128)S(1)}, u32[]{:S(2)}, u32[]{:S(2)}) collective-permute-start(f32[2,16,512]{2,1,0:T(8,128)S(1)} %get-tuple-element.88), channel_id=1, source_target_pairs={{0,2},{2,0},{4,6},{6,4},{8,10},{10,8},{12,14},{14,12},{16,18},{18,... | collective-permute-start | bytes 196616 | tf_op jit(solution)/shard_map/ppermute | solution.py:334
  23.8 2.4 %collective-permute-start.19 = (f32[2,32,512]{2,1,0:T(8,128)S(1)}, f32[2,32,512]{2,1,0:T(8,128)S(1)}, u32[]{:S(2)}, u32[]{:S(2)}) collective-permute-start(f32[2,32,512]{2,1,0:T(8,128)S(1)} %get-tuple-element.84), channel_id=1, source_target_pairs={{0,2},{2,0},{4,6},{6,4},{8,10},{10,8},{12,14},{14,12},{16,18},{18,... | collective-permute-start | bytes 393224 | tf_op jit(solution)/shard_map/ppermute | solution.py:334
  24.0 2.2 %collective-permute-start.20 = (f32[2,16,512]{2,1,0:T(8,128)S(1)}, f32[2,16,512]{2,1,0:T(8,128)S(1)}, u32[]{:S(2)}, u32[]{:S(2)}) collective-permute-start(f32[2,16,512]{2,1,0:T(8,128)S(1)} %get-tuple-element.85), channel_id=1, source_target_pairs={{0,2},{2,0},{4,6},{6,4},{8,10},{10,8},{12,14},{14,12},{16,18},{18,... | collective-permute-start | bytes 196616 | tf_op jit(solution)/shard_map/ppermute | solution.py:334
  27.1 3.8 %collective-permute-start.24 = (f32[1,256]{1,0:T(1,128)S(1)}, f32[1,256]{1,0:T(1,128)S(1)}, u32[]{:S(2)}, u32[]{:S(2)}) collective-permute-start(f32[1,256]{1,0:T(1,128)S(1)} %get-tuple-element.93), channel_id=1, source_target_pairs={{0,1},{1,0},{2,3},{3,2},{4,5},{5,4},{6,7},{7,6},{8,9},{9,8},{10,11... | collective-permute-start | bytes 3080 | tf_op jit(solution)/shard_map/ppermute | solution.py:362

commit v7 on v6

--- a/solution.py
+++ b/solution.py
@@ -12,7 +12,21 @@
 HALVES = 2
 TAIL = 16
 VMEM_LIMIT = 24 * 1024 * 1024
-WEIGHTS = {"step_1_0": 10000000, "step_0_1": 1000000, "step_1_1": 200000000, "last_0": 200000000, "gradient": 10000000}
+WEIGHTS = {
+    "first_0": 30000000,
+    "first_1": 30000000,
+    "step_1_0_0": 1000000,
+    "step_1_1_0": 1000000,
+    "step_2_0_0": 1000000,
+    "step_2_1_0": 1000000000,
+    "step_2_1_1": 500000000,
+    "step_3_0_0": 1000000,
+    "step_3_0_1": 500000000,
+    "step_3_1_0": 500000000,
+    "step_3_1_1": 1000000,
+    "last_0": 30000000,
+    "gradient": 100000000,
+}
 PARAMS = pltpu.CompilerParams(vmem_limit_bytes=VMEM_LIMIT)
 IN_VMEM = pl.BlockSpec(memory_space=pltpu.VMEM)
 IN_HBM = pl.BlockSpec(memory_space=pltpu.HBM)
@@ -227,7 +241,7 @@
         scratch_shapes=[pltpu.VMEM((4 * rows, breadth), jnp.bfloat16)],
         input_output_aliases={len(operands) - 1: len(outs)},
         compiler_params=PARAMS,
-        cost_estimate=cost(f"step_{half}_{parity}"),
+        cost_estimate=cost(f"step_{tick}_{half}_{parity}"),
         name=f"step_{tick}_{half}_{parity}",
     )(*operands)
 
@@ -263,41 +277,43 @@
     )(*operands)
 
 
-def last_kernel(half, chained, above, mate, mate_tail, *refs):
+def last_kernel(half, above, mate, mate_tail, *refs):
     shared, high, low = refs[:4], refs[4], refs[5]
-    if chained:
-        out, left, held, sem = refs[7:]
-        grad_in = grad = None
+    if half == 0:
+        grad_in, held, grad, left = refs[6:]
+        arrive_either(half, above, (mate, mate_tail), shared, grad_in, grad, left)
+        held[0], held[1] = multiply(left, high, low, slice(None))
+        return
+    before, out, left, held, sems = refs[6:]
+    rows = held.shape[1]
+    copies = [
+        pltpu.make_async_copy(piece, out.at[:, pl.ds(place * rows, rows)], sems.at[place])
+        for place, piece in enumerate((before, held))
+    ]
+    copies[0].start()
+    arrive_either(half, above, (mate, mate_tail), shared, None, None, left)
+    held[0], held[1] = multiply(left, high, low, slice(None))
+    copies[1].start()
+    for copy in copies:
+        copy.wait()
+
+
+def last(half, above, mate, shared, high, low, grad, held):
+    rows, breadth = above.shape[1:]
+    left = pltpu.VMEM((4 * rows, breadth), jnp.bfloat16)
+    piece = pltpu.VMEM((2, rows, breadth), jnp.float32)
+    if half == 0:
+        out_shape, out_specs, scratch, aliases = (piece, pltpu.VMEM(grad.shape, jnp.float32)), (IN_VMEM,) * 2, [left], {9: 1}
     else:
-        grad_in, out, grad, left, held, sem = refs[6:]
-    arrive_either(half, above, (mate, mate_tail), shared, grad_in, grad, left)
-    held[0], held[1] = multiply(left, high, low, slice(None))
-    rows = held.shape[1]
-    copy = pltpu.make_async_copy(held, out.at[:, pl.ds(half * rows, rows)], sem)
-    copy.start()
-    copy.wait()
-
-
-def last(half, above, mate, shared, high, low, grad, out):
-    rows, breadth = above.shape[1:]
-    operands = [pinned(value) for value in (above, *mate, *shared, high, low)]
-    whole = pltpu.HBM((2, rows * HALVES, breadth), jnp.float32)
-    if out is None:
-        operands.append(pinned(grad))
-        out_shape, aliases = (whole, pltpu.VMEM(grad.shape, jnp.float32)), {9: 1}
-    else:
-        operands.append(kept(out))
-        out_shape, aliases = (whole,), {9: 0}
+        out_shape, out_specs, aliases = (pltpu.HBM((2, rows * HALVES, breadth), jnp.float32),), (IN_HBM,), {}
+        scratch = [left, piece, pltpu.SemaphoreType.DMA((HALVES,))]
+    operands = [pinned(value) for value in (above, *mate, *shared, high, low, grad if half == 0 else held)]
     return pl.pallas_call(
-        functools.partial(last_kernel, half, out is not None),
+        functools.partial(last_kernel, half),
         out_shape=out_shape,
-        in_specs=[IN_VMEM] * 9 + [IN_VMEM if out is None else IN_HBM],
-        out_specs=(IN_HBM, IN_VMEM)[: len(out_shape)],
-        scratch_shapes=[
-            pltpu.VMEM((4 * rows, breadth), jnp.bfloat16),
-            pltpu.VMEM((2, rows, breadth), jnp.float32),
-            pltpu.SemaphoreType.DMA,
-        ],
+        in_specs=[IN_VMEM] * len(operands),
+        out_specs=out_specs,
+        scratch_shapes=scratch,
         input_output_aliases=aliases,
         compiler_params=PARAMS,
         cost_estimate=cost(f"last_{half}"),
@@ -342,25 +358,29 @@
     above = [down(piece) for piece in results[:HALVES]]
     *even, high, low, grad = first(0, *start, results[HALVES:])
     beside = [mate(even[2 * half : 2 * half + 2]) for half in range(HALVES)]
+    grads = [grad]
+
+    def odd_step(tick, half):
+        odd, grads[0] = step(tick, half, 1, beside[half], shared, high, low, grads[0], rows)
+        return down(odd)
+
+    def even_step(tick, half):
+        *even, grads[0] = step(tick, half, 0, (above[half],), shared, high, low, grads[0], rows)
+        return mate(even)
+
     for tick in range(1, TICKS - 1):
-        later = []
-        for half in range(HALVES):
-            odd, grad = step(tick, half, 1, beside[half], shared, high, low, grad, rows)
-            later.append(down(odd))
-        beside = []
-        for half in range(HALVES):
-            *even, grad = step(tick, half, 0, (above[half],), shared, high, low, grad, rows)
-            beside.append(mate(even))
+        later = [odd_step(tick, half) for half in range(HALVES)]
+        beside[:] = [even_step(tick, half) for half in range(HALVES)]
         above = later
 
     scale = 1.0 / math.sqrt(shots * TICKS)
-    out, grad = last(0, above[0], beside[0], shared, high, low, grad, None)
+    held, grad = last(0, above[0], beside[0], shared, high, low, grads[0], None)
     chunks = gradient_chunks(above[1], beside[1], shared, grad, scale)
     gradient = chunks[0]
     for distance in range(1, freqs):
         route = [(i, (i + distance) % freqs) for i in range(freqs)]
         gradient = gradient + lax.ppermute(chunks[distance], "freq", route)
-    (out,) = last(1, above[1], beside[1], shared, high, low, None, out)
+    (out,) = last(1, above[1], beside[1], shared, high, low, None, held)
     return (out[None, None], gradient)
 
 

time: 31.6 us -> 31.2 us (0.987)
  waiting for transfers between devices: 3.61 us -> 4.63 us
  starting transfers between devices: 16.8 us -> 16.1 us
  Pallas kernels: 9.63 us -> 8.94 us
    ppermute x16, waiting for transfers between devices: 1.66 us -> 2.37 us  [mate(): return [lax.ppermute(piece, 'depth', mate_route) for piece in pieces]]
    pallas_call x2, Pallas kernels: 2.72 us -> 2.05 us  [last(): pl.pallas_call(functools.partial(last_kernel, half), out_shape=out_shape,...]
    ppermute x16, starting transfers between devices: 4.81 us -> 4.36 us  [mate(): return [lax.ppermute(piece, 'depth', mate_route) for piece in pieces]]
    ppermute x8, starting transfers between devices: 9.74 us -> 9.31 us  [down(): return lax.ppermute(piece, 'depth', down_route)]
    ppermute x8, waiting for transfers between devices: 1.77 us -> 2.09 us  [down(): return lax.ppermute(piece, 'depth', down_route)]
  transfers between devices with their start and end apart: 25 -> 25, of which waited for: 9 -> 8; matrix products, arithmetic and copies ran while one was open for 0% -> 0% of each run, Pallas kernels for 30% -> 28%
where the time goes in v7:
time: 31.2 us; the launch traced here: 31 us
  starting transfers between devices  16.1 us (52%)
  Pallas kernels  8.94 us (29%)
  waiting for transfers between devices  4.63 us (15%)
  between operations  0.82 us (3%)
  other arithmetic  0.56 us (2%)
    ppermute x8, starting transfers between devices, down(): return lax.ppermute(piece, 'depth', down_route)  9.31 us
    ppermute x16, starting transfers between devices, mate(): return [lax.ppermute(piece, 'depth', mate_route) for piece in pieces]  4.36 us
    pallas_call x12, Pallas kernels, step(): pl.pallas_call(functools.partial(step_kernel, tick, half, parity), out_sh...  4.04 us
    pallas_call x2, Pallas kernels, first(): pl.pallas_call(functools.partial(first_kernel, parity, bool(carried)), ou...  2.71 us
    ppermute x1, starting transfers between devices, local(): gradient = gradient + lax.ppermute(chunks[distance], 'freq', route)  2.39 us
    ppermute x16, waiting for transfers between devices, mate(): return [lax.ppermute(piece, 'depth', mate_route) for piece in pieces]  2.37 us
    ppermute x8, waiting for transfers between devices, down(): return lax.ppermute(piece, 'depth', down_route)  2.09 us
    pallas_call x2, Pallas kernels, last(): pl.pallas_call(functools.partial(last_kernel, half), out_shape=out_shape,...  2.05 us
  transfers between devices with their start and end apart: 25, of which 8 were waited for; matrix products, arithmetic and copies ran while one was open for 0% of the time, Pallas kernels for 28%

profile of v7, /device:TPU:0, one launch (start us, length us, event | category | flops | bytes accessed | tf_op | source)
XLA Modules:
  0.0 31.0 jit_solution(12267620463184861625)
XLA Ops:
  0.6 0.1 first_1.1
  0.7 2.9 %collective-permute-start.7 = (f32[2,48,512]{2,1,0:T(8,128)S(1)}, f32[2,48,512]{2,1,0:T(8,128)S(1)}, u32[]{:S(2)}, u32[]{:S(2)}) collective-permute-start(f32[2,48,512]{2,1,0:T(8,128)S(1)} %get-tuple-element.62), channel_id=1, source_target_pairs={{0,2},{2,4},{4,0},{6,8},{8,10},{10,12},{12,6},{14,16},{16,18},{18,... | collective-permute-start | bytes 589832 | tf_op jit(solution)/shard_map/ppermute | solution.py:353
  3.6 0.2 collective-permute-start.6
  3.9 2.6 %first_0.1 = (f32[2,32,512]{2,1,0:T(8,128)S(1)}, f32[2,16,512]{2,1,0:T(8,128)S(1)}, f32[2,32,512]{2,1,0:T(8,128)S(1)}, f32[2,16,512]{2,1,0:T(8,128)S(1)}, bf16[2...) custom-call(f32[1,1,2,512,512]{4,3,2,1,0:T(8,128)} %refs_0_.5, ...), custom_call_target="tpu_custom_call", output_to_operand_aliasing={{4}: (4, {}), {5}: (5, {}), {6}: (6, {})} | custom-call | flops 30000000 | bytes 1 | tf_op jit(solution)/shard_map/first_0/pallas_call | solution.py:170
  6.5 0.1 collective-permute-start.2
  6.6 0.5 %collective-permute-start.3 = (f32[2,16,512]{2,1,0:T(8,128)S(1)}, f32[2,16,512]{2,1,0:T(8,128)S(1)}, u32[]{:S(2)}, u32[]{:S(2)}) collective-permute-start(f32[2,16,512]{2,1,0:T(8,128)S(1)} %get-tuple-element.56), channel_id=1, source_target_pairs={{0,2},{2,0},{4,6},{6,4},{8,10},{10,8},{12,14},{14,12},{16,18},{18,... | collective-permute-start | bytes 196616 | tf_op jit(solution)/shard_map/ppermute | solution.py:350
  7.1 0.1 collective-permute-start
  7.2 0.9 %collective-permute-done.3.refs_1_ = f32[2,16,512]{2,1,0:T(8,128)S(1)} collective-permute-done((f32[2,16,512]{2,1,0:T(8,128)S(1)}, f32[2,16,512]{2,1,0:T(8,128)S(1)}, u32[]{:S(2)}, u32[]{:S(2)}) %collective-permute-start.3) | collective-permute-done | bytes 65568 | tf_op jit(solution)/shard_map/ppermute | solution.py:350
  8.0 0.3 %collective-permute-start.1 = (f32[2,16,512]{2,1,0:T(8,128)S(1)}, f32[2,16,512]{2,1,0:T(8,128)S(1)}, u32[]{:S(2)}, u32[]{:S(2)}) collective-permute-start(f32[2,16,512]{2,1,0:T(8,128)S(1)} %get-tuple-element.52), channel_id=1, source_target_pairs={{0,2},{2,0},{4,6},{6,4},{8,10},{10,8},{12,14},{14,12},{16,18},{18,... | collective-permute-start | bytes 196616 | tf_op jit(solution)/shard_map/ppermute | solution.py:350
  8.3 0.0 collective-permute-done.2.refs_0_
  8.3 0.0 copy-done.2
  8.4 0.0 copy-done.3
  8.4 0.8 %collective-permute-start.5 = (f32[2,48,512]{2,1,0:T(8,128)S(1)}, f32[2,48,512]{2,1,0:T(8,128)S(1)}, u32[]{:S(2)}, u32[]{:S(2)}) collective-permute-start(f32[2,48,512]{2,1,0:T(8,128)S(1)} %get-tuple-element.60), channel_id=1, source_target_pairs={{0,2},{2,4},{4,0},{6,8},{8,10},{10,12},{12,6},{14,16},{16,18},{18,... | collective-permute-start | bytes 589832 | tf_op jit(solution)/shard_map/ppermute | solution.py:353
  9.2 0.1 collective-permute-done.1.refs_1_
  9.3 0.0 collective-permute-done.refs_0_
  9.3 1.7 %collective-permute-start.4 = (f32[2,48,512]{2,1,0:T(8,128)S(1)}, f32[2,48,512]{2,1,0:T(8,128)S(1)}, u32[]{:S(2)}, u32[]{:S(2)}) collective-permute-start(f32[2,48,512]{2,1,0:T(8,128)S(1)} %get-tuple-element.59), channel_id=1, source_target_pairs={{0,2},{2,4},{4,0},{6,8},{8,10},{10,12},{12,6},{14,16},{16,18},{18,... | collective-permute-start | bytes 589832 | tf_op jit(solution)/shard_map/ppermute | solution.py:353
  11.0 0.0 collective-permute-done.7.refs_0_
  11.0 0.7 %step_1_0_0.1 = (f32[2,32,512]{2,1,0:T(8,128)S(1)}, f32[2,16,512]{2,1,0:T(8,128)S(1)}, f32[8,512]{1,0:T(8,128)S(1)}) custom-call(f32[2,48,512]{2,1,0:T(8,128)S(1)} %collective-permute-done.7.refs_0_, f32[1,1,5,2,96,512]{5,4,3,2,1,0:T(8,128)S(1)} %copy-done, f32[1,512]{1,0:T(1,128)S(1)} %copy-done.1, ...), custom_call_target="tpu_custom_call", output_to_operand_aliasing={{2}: (7, {})} | custom-call | flops 1000000 | bytes 1 | tf_op jit(solution)/shard_map/step_1_0_0/pallas_call | solution.py:236
  11.6 0.1 collective-permute-start.11
  11.7 0.5 %collective-permute-start.10 = (f32[2,32,512]{2,1,0:T(8,128)S(1)}, f32[2,32,512]{2,1,0:T(8,128)S(1)}, u32[]{:S(2)}, u32[]{:S(2)}) collective-permute-start(f32[2,32,512]{2,1,0:T(8,128)S(1)} %get-tuple-element.67), channel_id=1, source_target_pairs={{0,2},{2,0},{4,6},{6,4},{8,10},{10,8},{12,14},{14,12},{16,18},{18,... | collective-permute-start | bytes 393224 | tf_op jit(solution)/shard_map/ppermute | solution.py:350
  12.2 0.0 collective-permute-done.6.refs_0_
  12.2 0.7 %step_1_1_0.1 = (f32[2,32,512]{2,1,0:T(8,128)S(1)}, f32[2,16,512]{2,1,0:T(8,128)S(1)}, f32[8,512]{1,0:T(8,128)S(1)}) custom-call(f32[2,48,512]{2,1,0:T(8,128)S(1)} %collective-permute-done.6.refs_0_, f32[1,1,5,2,96,512]{5,4,3,2,1,0:T(8,128)S(1)} %copy-done, f32[1,512]{1,0:T(1,128)S(1)} %copy-done.1, ...), custom_call_target="tpu_custom_call", output_to_operand_aliasing={{2}: (7, {})} | custom-call | flops 1000000 | bytes 1 | tf_op jit(solution)/shard_map/step_1_1_0/pallas_call | solution.py:236
  12.9 0.1 collective-permute-start.8
  13.0 0.0 collective-permute-done.11.refs_1_
  13.0 0.5 %collective-permute-start.9 = (f32[2,16,512]{2,1,0:T(8,128)S(1)}, f32[2,16,512]{2,1,0:T(8,128)S(1)}, u32[]{:S(2)}, u32[]{:S(2)}) collective-permute-start(f32[2,16,512]{2,1,0:T(8,128)S(1)} %get-tuple-element.66), channel_id=1, source_target_pairs={{0,2},{2,0},{4,6},{6,4},{8,10},{10,8},{12,14},{14,12},{16,18},{18,... | collective-permute-start | bytes 196616 | tf_op jit(solution)/shard_map/ppermute | solution.py:350
  13.5 0.0 collective-permute-done.10.refs_0_
  13.5 0.9 %collective-permute-done.9.refs_1_ = f32[2,16,512]{2,1,0:T(8,128)S(1)} collective-permute-done((f32[2,16,512]{2,1,0:T(8,128)S(1)}, f32[2,16,512]{2,1,0:T(8,128)S(1)}, u32[]{:S(2)}, u32[]{:S(2)}) %collective-permute-start.9) | collective-permute-done | bytes 65568 | tf_op jit(solution)/shard_map/ppermute | solution.py:350
  14.4 0.0 collective-permute-done.8.refs_0_
  14.4 0.9 %collective-permute-start.17 = (f32[2,48,512]{2,1,0:T(8,128)S(1)}, f32[2,48,512]{2,1,0:T(8,128)S(1)}, u32[]{:S(2)}, u32[]{:S(2)}) collective-permute-start(f32[2,48,512]{2,1,0:T(8,128)S(1)} %get-tuple-element.80), channel_id=1, source_target_pairs={{0,2},{2,4},{4,0},{6,8},{8,10},{10,12},{12,6},{14,16},{16,18},{18,... | collective-permute-start | bytes 589832 | tf_op jit(solution)/shard_map/ppermute | solution.py:353
  15.3 0.1 collective-permute-start.18
  15.4 0.0 collective-permute-done.5.refs_0_
  15.4 0.7 %step_2_0_0.1 = (f32[2,32,512]{2,1,0:T(8,128)S(1)}, f32[2,16,512]{2,1,0:T(8,128)S(1)}, f32[8,512]{1,0:T(8,128)S(1)}) custom-call(f32[2,48,512]{2,1,0:T(8,128)S(1)} %collective-permute-done.5.refs_0_, f32[1,1,5,2,96,512]{5,4,3,2,1,0:T(8,128)S(1)} %copy-done, f32[1,512]{1,0:T(1,128)S(1)} %copy-done.1, ...), custom_call_target="tpu_custom_call", output_to_operand_aliasing={{2}: (7, {})} | custom-call | flops 1000000 | bytes 1 | tf_op jit(solution)/shard_map/step_2_0_0/pallas_call | solution.py:236
  16.1 0.5 %collective-permute-start.15 = (f32[2,16,512]{2,1,0:T(8,128)S(1)}, f32[2,16,512]{2,1,0:T(8,128)S(1)}, u32[]{:S(2)}, u32[]{:S(2)}) collective-permute-start(f32[2,16,512]{2,1,0:T(8,128)S(1)} %get-tuple-element.76), channel_id=1, source_target_pairs={{0,2},{2,0},{4,6},{6,4},{8,10},{10,8},{12,14},{14,12},{16,18},{18,... | collective-permute-start | bytes 196616 | tf_op jit(solution)/shard_map/ppermute | solution.py:350
  16.5 0.1 collective-permute-start.14
  16.7 0.0 collective-permute-done.4.refs_0_
  16.7 0.7 %step_2_1_0.1 = (f32[2,32,512]{2,1,0:T(8,128)S(1)}, f32[2,16,512]{2,1,0:T(8,128)S(1)}, f32[8,512]{1,0:T(8,128)S(1)}) custom-call(f32[2,48,512]{2,1,0:T(8,128)S(1)} %collective-permute-done.4.refs_0_, f32[1,1,5,2,96,512]{5,4,3,2,1,0:T(8,128)S(1)} %copy-done, f32[1,512]{1,0:T(1,128)S(1)} %copy-done.1, ...), custom_call_target="tpu_custom_call", output_to_operand_aliasing={{2}: (7, {})} | custom-call | flops 1000000000 | bytes 1 | tf_op jit(solution)/shard_map/step_2_1_0/pallas_call | solution.py:236
  17.3 0.1 collective-permute-start.12
  17.4 0.0 collective-permute-done.15.refs_1_
  17.4 0.5 %collective-permute-start.13 = (f32[2,16,512]{2,1,0:T(8,128)S(1)}, f32[2,16,512]{2,1,0:T(8,128)S(1)}, u32[]{:S(2)}, u32[]{:S(2)}) collective-permute-start(f32[2,16,512]{2,1,0:T(8,128)S(1)} %get-tuple-element.74), channel_id=1, source_target_pairs={{0,2},{2,0},{4,6},{6,4},{8,10},{10,8},{12,14},{14,12},{16,18},{18,... | collective-permute-start | bytes 196616 | tf_op jit(solution)/shard_map/ppermute | solution.py:350
  17.9 0.0 collective-permute-done.14.refs_0_
  17.9 0.7 %collective-permute-start.21 = (f32[2,48,512]{2,1,0:T(8,128)S(1)}, f32[2,48,512]{2,1,0:T(8,128)S(1)}, u32[]{:S(2)}, u32[]{:S(2)}) collective-permute-start(f32[2,48,512]{2,1,0:T(8,128)S(1)} %get-tuple-element.86), channel_id=1, source_target_pairs={{0,2},{2,4},{4,0},{6,8},{8,10},{10,12},{12,6},{14,16},{16,18},{18,... | collective-permute-start | bytes 589832 | tf_op jit(solution)/shard_map/ppermute | solution.py:353
  18.6 0.2 collective-permute-done.13.refs_1_
  18.8 0.0 collective-permute-done.12.refs_0_
  18.9 2.0 %collective-permute-start.16 = (f32[2,48,512]{2,1,0:T(8,128)S(1)}, f32[2,48,512]{2,1,0:T(8,128)S(1)}, u32[]{:S(2)}, u32[]{:S(2)}) collective-permute-start(f32[2,48,512]{2,1,0:T(8,128)S(1)} %get-tuple-element.79), channel_id=1, source_target_pairs={{0,2},{2,4},{4,0},{6,8},{8,10},{10,12},{12,6},{14,16},{16,18},{18,... | collective-permute-start | bytes 589832 | tf_op jit(solution)/shard_map/ppermute | solution.py:353
  20.8 1.3 %collective-permute-done.18.refs_0_ = f32[2,48,512]{2,1,0:T(8,128)S(1)} collective-permute-done((f32[2,48,512]{2,1,0:T(8,128)S(1)}, f32[2,48,512]{2,1,0:T(8,128)S(1)}, u32[]{:S(2)}, u32[]{:S(2)}) %collective-permute-start.18) | collective-permute-done | bytes 196640 | tf_op jit(solution)/shard_map/ppermute | solution.py:353
  22.2 0.7 %step_3_0_0.1 = (f32[2,32,512]{2,1,0:T(8,128)S(1)}, f32[2,16,512]{2,1,0:T(8,128)S(1)}, f32[8,512]{1,0:T(8,128)S(1)}) custom-call(f32[2,48,512]{2,1,0:T(8,128)S(1)} %collective-permute-done.18.refs_0_, f32[1,1,5,2,96,512]{5,4,3,2,1,0:T(8,128)S(1)} %copy-done, f32[1,512]{1,0:T(1,128)S(1)} %copy-done.1, ...), custom_call_target="tpu_custom_call", output_to_operand_aliasing={{2}: (7, {})} | custom-call | flops 1000000 | bytes 1 | tf_op jit(solution)/shard_map/step_3_0_0/pallas_call | solution.py:236
  22.8 0.1 collective-permute-start.23
  22.9 0.5 %collective-permute-start.22 = (f32[2,32,512]{2,1,0:T(8,128)S(1)}, f32[2,32,512]{2,1,0:T(8,128)S(1)}, u32[]{:S(2)}, u32[]{:S(2)}) collective-permute-start(f32[2,32,512]{2,1,0:T(8,128)S(1)} %get-tuple-element.87), channel_id=1, source_target_pairs={{0,2},{2,0},{4,6},{6,4},{8,10},{10,8},{12,14},{14,12},{16,18},{18,... | collective-permute-start | bytes 393224 | tf_op jit(solution)/shard_map/ppermute | solution.py:350
  23.4 0.0 collective-permute-done.17.refs_0_
  23.4 0.7 %step_3_1_0.1 = (f32[2,32,512]{2,1,0:T(8,128)S(1)}, f32[2,16,512]{2,1,0:T(8,128)S(1)}, f32[8,512]{1,0:T(8,128)S(1)}) custom-call(f32[2,48,512]{2,1,0:T(8,128)S(1)} %collective-permute-done.17.refs_0_, f32[1,1,5,2,96,512]{5,4,3,2,1,0:T(8,128)S(1)} %copy-done, f32[1,512]{1,0:T(1,128)S(1)} %copy-done.1, ...), custom_call_target="tpu_custom_call", output_to_operand_aliasing={{2}: (7, {})} | custom-call | flops 500000000 | bytes 1 | tf_op jit(solution)/shard_map/step_3_1_0/pallas_call | solution.py:236
  24.1 0.1 collective-permute-start.19
  24.2 0.0 collective-permute-done.23.mate_tail
  24.2 0.5 %collective-permute-start.20 = (f32[2,16,512]{2,1,0:T(8,128)S(1)}, f32[2,16,512]{2,1,0:T(8,128)S(1)}, u32[]{:S(2)}, u32[]{:S(2)}) collective-permute-start(f32[2,16,512]{2,1,0:T(8,128)S(1)} %get-tuple-element.85), channel_id=1, source_target_pairs={{0,2},{2,0},{4,6},{6,4},{8,10},{10,8},{12,14},{14,12},{16,18},{18,... | collective-permute-start | bytes 196616 | tf_op jit(solution)/shard_map/ppermute | solution.py:350
  24.7 0.0 collective-permute-done.22.mate
  24.7 0.0 collective-permute-done.21.above
  24.7 0.7 %last_0.1 = (f32[2,48,512]{2,1,0:T(8,128)S(1)}, f32[8,512]{1,0:T(8,128)S(1)}) custom-call(f32[2,48,512]{2,1,0:T(8,128)S(1)} %collective-permute-done.21.above, f32[2,32,512]{2,1,0:T(8,128)S(1)} %collective-permute-done.22.mate, f32[2,16,512]{2,1,0:T(8,128)S(1)} %collective-permute-done.23.mate_tail, ...), custom_call_target="tpu_custom_call", output_to_operand_aliasing={{1}: (9, {})} | custom-call | flops 30000000 | bytes 1 | tf_op jit(solution)/shard_map/last_0/pallas_call | solution.py:311
  25.4 0.2 collective-permute-done.20.mate_tail
  25.6 0.0 collective-permute-done.19.mate
  25.6 0.8 %collective-permute-done.16.above = f32[2,48,512]{2,1,0:T(8,128)S(1)} collective-permute-done((f32[2,48,512]{2,1,0:T(8,128)S(1)}, f32[2,48,512]{2,1,0:T(8,128)S(1)}, u32[]{:S(2)}, u32[]{:S(2)}) %collective-permute-start.16) | collective-permute-done | bytes 196640 | tf_op jit(solution)/shard_map/ppermute | solution.py:353
  26.4 0.1 gradient.1
  26.5 2.4 %collective-permute-start.24 = (f32[1,256]{1,0:T(1,128)S(1)}, f32[1,256]{1,0:T(1,128)S(1)}, u32[]{:S(2)}, u32[]{:S(2)}) collective-permute-start(f32[1,256]{1,0:T(1,128)S(1)} %get-tuple-element.93), channel_id=1, source_target_pairs={{0,1},{1,0},{2,3},{3,2},{4,5},{5,4},{6,7},{7,6},{8,9},{9,8},{10,11... | collective-permute-start | bytes 3080 | tf_op jit(solution)/shard_map/ppermute | solution.py:382
  28.9 1.4 %last_1.1 = f32[2,96,512]{2,1,0:T(8,128)} custom-call(f32[2,48,512]{2,1,0:T(8,128)S(1)} %collective-permute-done.16.above, f32[2,32,512]{2,1,0:T(8,128)S(1)} %collective-permute-done.19.mate, f32[2,16,512]{2,1,0:T(8,128)S(1)} %collective-permute-done.20.mate_tail, f32[1,1,5,2,96,512]{5,4,3,2,1,0:T(8,128)S(1)} %copy-done, f32[1,512]{1,0:T(1,128)S(1)} %copy-done.1, ...), custom_call_target="tpu_custom_call" | custom-call | flops 1 | bytes 1 | tf_op jit(solution)/shard_map/last_1/pallas_call | solution.py:311
  30.3 0.2 collective-permute-done.24
  30.5 0.6 %add.3 = f32[1,256]{1,0:T(1,128)} add(f32[1,256]{1,0:T(1,128)S(1)} %get-tuple-element.92, f32[1,256]{1,0:T(1,128)S(1)} %collective-permute-done.24) | non-fusion elementwise | flops 256 | bytes 3072 | tf_op jit(solution)/shard_map/add | solution.py:382
  (12 shorter events, 0.0 us)
Async XLA Ops:
  0.7 10.3 %collective-permute-start.7 = (f32[2,48,512]{2,1,0:T(8,128)S(1)}, f32[2,48,512]{2,1,0:T(8,128)S(1)}, u32[]{:S(2)}, u32[]{:S(2)}) collective-permute-start(f32[2,48,512]{2,1,0:T(8,128)S(1)} %get-tuple-element.62), channel_id=1, source_target_pairs={{0,2},{2,4},{4,0},{6,8},{8,10},{10,12},{12,6},{14,16},{16,18},{18,... | collective-permute-start | bytes 589832 | tf_op jit(solution)/shard_map/ppermute | solution.py:353
  3.6 8.6 %collective-permute-start.6 = (f32[2,48,512]{2,1,0:T(8,128)S(1)}, f32[2,48,512]{2,1,0:T(8,128)S(1)}, u32[]{:S(2)}, u32[]{:S(2)}) collective-permute-start(f32[2,48,512]{2,1,0:T(8,128)S(1)} %get-tuple-element.61), channel_id=1, source_target_pairs={{0,2},{2,4},{4,0},{6,8},{8,10},{10,12},{12,6},{14,16},{16,18},{18,... | collective-permute-start | bytes 589832 | tf_op jit(solution)/shard_map/ppermute | solution.py:353
  3.9 4.5 %copy-start = (f32[1,1,5,2,96,512]{5,4,3,2,1,0:T(8,128)S(1)}, f32[1,1,5,2,96,512]{5,4,3,2,1,0:T(8,128)}, u32[]{:S(2)}) copy-start(f32[1,1,5,2,96,512]{5,4,3,2,1,0:T(8,128)} %residual.1) | copy-start | bytes 5898244
  3.9 4.5 %copy-start.1 = (f32[1,512]{1,0:T(1,128)S(1)}, f32[1,512]{1,0:T(1,128)}, u32[]{:S(2)}) copy-start(f32[1,512]{1,0:T(1,128)} %contrast.1) | copy-start | bytes 6148
  3.9 4.5 %copy-start.2 = (s32[4,96]{1,0:T(4,128)S(1)}, s32[4,96]{1,0:T(4,128)}, u32[]{:S(2)}) copy-start(s32[4,96]{1,0:T(4,128)} %sites.1) | copy-start | bytes 4612
  3.9 4.5 %copy-start.3 = (f32[1,4,2]{1,2,0:T(2,128)S(1)}, f32[1,4,2]{1,2,0:T(2,128)}, u32[]{:S(2)}) copy-start(f32[1,4,2]{1,2,0:T(2,128)} %param.11) | copy-start | bytes 100
  6.5 1.8 %collective-permute-start.2 = (f32[2,32,512]{2,1,0:T(8,128)S(1)}, f32[2,32,512]{2,1,0:T(8,128)S(1)}, u32[]{:S(2)}, u32[]{:S(2)}) collective-permute-start(f32[2,32,512]{2,1,0:T(8,128)S(1)} %get-tuple-element.55), channel_id=1, source_target_pairs={{0,2},{2,0},{4,6},{6,4},{8,10},{10,8},{12,14},{14,12},{16,18},{18,... | collective-permute-start | bytes 393224 | tf_op jit(solution)/shard_map/ppermute | solution.py:350
  6.6 1.4 %collective-permute-start.3 = (f32[2,16,512]{2,1,0:T(8,128)S(1)}, f32[2,16,512]{2,1,0:T(8,128)S(1)}, u32[]{:S(2)}, u32[]{:S(2)}) collective-permute-start(f32[2,16,512]{2,1,0:T(8,128)S(1)} %get-tuple-element.56), channel_id=1, source_target_pairs={{0,2},{2,0},{4,6},{6,4},{8,10},{10,8},{12,14},{14,12},{16,18},{18,... | collective-permute-start | bytes 196616 | tf_op jit(solution)/shard_map/ppermute | solution.py:350
  7.1 2.2 %collective-permute-start = (f32[2,32,512]{2,1,0:T(8,128)S(1)}, f32[2,32,512]{2,1,0:T(8,128)S(1)}, u32[]{:S(2)}, u32[]{:S(2)}) collective-permute-start(f32[2,32,512]{2,1,0:T(8,128)S(1)} %get-tuple-element.51), channel_id=1, source_target_pairs={{0,2},{2,0},{4,6},{6,4},{8,10},{10,8},{12,14},{14,12},{16,18},{18,... | collective-permute-start | bytes 393224 | tf_op jit(solution)/shard_map/ppermute | solution.py:350
  8.0 1.3 %collective-permute-start.1 = (f32[2,16,512]{2,1,0:T(8,128)S(1)}, f32[2,16,512]{2,1,0:T(8,128)S(1)}, u32[]{:S(2)}, u32[]{:S(2)}) collective-permute-start(f32[2,16,512]{2,1,0:T(8,128)S(1)} %get-tuple-element.52), channel_id=1, source_target_pairs={{0,2},{2,0},{4,6},{6,4},{8,10},{10,8},{12,14},{14,12},{16,18},{18,... | collective-permute-start | bytes 196616 | tf_op jit(solution)/shard_map/ppermute | solution.py:350
  8.4 7.0 %collective-permute-start.5 = (f32[2,48,512]{2,1,0:T(8,128)S(1)}, f32[2,48,512]{2,1,0:T(8,128)S(1)}, u32[]{:S(2)}, u32[]{:S(2)}) collective-permute-start(f32[2,48,512]{2,1,0:T(8,128)S(1)} %get-tuple-element.60), channel_id=1, source_target_pairs={{0,2},{2,4},{4,0},{6,8},{8,10},{10,12},{12,6},{14,16},{16,18},{18,... | collective-permute-start | bytes 589832 | tf_op jit(solution)/shard_map/ppermute | solution.py:353
  9.3 7.4 %collective-permute-start.4 = (f32[2,48,512]{2,1,0:T(8,128)S(1)}, f32[2,48,512]{2,1,0:T(8,128)S(1)}, u32[]{:S(2)}, u32[]{:S(2)}) collective-permute-start(f32[2,48,512]{2,1,0:T(8,128)S(1)} %get-tuple-element.59), channel_id=1, source_target_pairs={{0,2},{2,4},{4,0},{6,8},{8,10},{10,12},{12,6},{14,16},{16,18},{18,... | collective-permute-start | bytes 589832 | tf_op jit(solution)/shard_map/ppermute | solution.py:353
  11.6 1.3 %collective-permute-start.11 = (f32[2,16,512]{2,1,0:T(8,128)S(1)}, f32[2,16,512]{2,1,0:T(8,128)S(1)}, u32[]{:S(2)}, u32[]{:S(2)}) collective-permute-start(f32[2,16,512]{2,1,0:T(8,128)S(1)} %get-tuple-element.68), channel_id=1, source_target_pairs={{0,2},{2,0},{4,6},{6,4},{8,10},{10,8},{12,14},{14,12},{16,18},{18,... | collective-permute-start | bytes 196616 | tf_op jit(solution)/shard_map/ppermute | solution.py:350
  11.7 1.7 %collective-permute-start.10 = (f32[2,32,512]{2,1,0:T(8,128)S(1)}, f32[2,32,512]{2,1,0:T(8,128)S(1)}, u32[]{:S(2)}, u32[]{:S(2)}) collective-permute-start(f32[2,32,512]{2,1,0:T(8,128)S(1)} %get-tuple-element.67), channel_id=1, source_target_pairs={{0,2},{2,0},{4,6},{6,4},{8,10},{10,8},{12,14},{14,12},{16,18},{18,... | collective-permute-start | bytes 393224 | tf_op jit(solution)/shard_map/ppermute | solution.py:350
  12.9 1.5 %collective-permute-start.8 = (f32[2,32,512]{2,1,0:T(8,128)S(1)}, f32[2,32,512]{2,1,0:T(8,128)S(1)}, u32[]{:S(2)}, u32[]{:S(2)}) collective-permute-start(f32[2,32,512]{2,1,0:T(8,128)S(1)} %get-tuple-element.65), channel_id=1, source_target_pairs={{0,2},{2,0},{4,6},{6,4},{8,10},{10,8},{12,14},{14,12},{16,18},{18,... | collective-permute-start | bytes 393224 | tf_op jit(solution)/shard_map/ppermute | solution.py:350
  13.0 1.4 %collective-permute-start.9 = (f32[2,16,512]{2,1,0:T(8,128)S(1)}, f32[2,16,512]{2,1,0:T(8,128)S(1)}, u32[]{:S(2)}, u32[]{:S(2)}) collective-permute-start(f32[2,16,512]{2,1,0:T(8,128)S(1)} %get-tuple-element.66), channel_id=1, source_target_pairs={{0,2},{2,0},{4,6},{6,4},{8,10},{10,8},{12,14},{14,12},{16,18},{18,... | collective-permute-start | bytes 196616 | tf_op jit(solution)/shard_map/ppermute | solution.py:350
  14.4 9.0 %collective-permute-start.17 = (f32[2,48,512]{2,1,0:T(8,128)S(1)}, f32[2,48,512]{2,1,0:T(8,128)S(1)}, u32[]{:S(2)}, u32[]{:S(2)}) collective-permute-start(f32[2,48,512]{2,1,0:T(8,128)S(1)} %get-tuple-element.80), channel_id=1, source_target_pairs={{0,2},{2,4},{4,0},{6,8},{8,10},{10,12},{12,6},{14,16},{16,18},{18,... | collective-permute-start | bytes 589832 | tf_op jit(solution)/shard_map/ppermute | solution.py:353
  15.3 6.9 %collective-permute-start.18 = (f32[2,48,512]{2,1,0:T(8,128)S(1)}, f32[2,48,512]{2,1,0:T(8,128)S(1)}, u32[]{:S(2)}, u32[]{:S(2)}) collective-permute-start(f32[2,48,512]{2,1,0:T(8,128)S(1)} %get-tuple-element.81), channel_id=1, source_target_pairs={{0,2},{2,4},{4,0},{6,8},{8,10},{10,12},{12,6},{14,16},{16,18},{18,... | collective-permute-start | bytes 589832 | tf_op jit(solution)/shard_map/ppermute | solution.py:353
  16.1 1.4 %collective-permute-start.15 = (f32[2,16,512]{2,1,0:T(8,128)S(1)}, f32[2,16,512]{2,1,0:T(8,128)S(1)}, u32[]{:S(2)}, u32[]{:S(2)}) collective-permute-start(f32[2,16,512]{2,1,0:T(8,128)S(1)} %get-tuple-element.76), channel_id=1, source_target_pairs={{0,2},{2,0},{4,6},{6,4},{8,10},{10,8},{12,14},{14,12},{16,18},{18,... | collective-permute-start | bytes 196616 | tf_op jit(solution)/shard_map/ppermute | solution.py:350
  16.5 1.4 %collective-permute-start.14 = (f32[2,32,512]{2,1,0:T(8,128)S(1)}, f32[2,32,512]{2,1,0:T(8,128)S(1)}, u32[]{:S(2)}, u32[]{:S(2)}) collective-permute-start(f32[2,32,512]{2,1,0:T(8,128)S(1)} %get-tuple-element.75), channel_id=1, source_target_pairs={{0,2},{2,0},{4,6},{6,4},{8,10},{10,8},{12,14},{14,12},{16,18},{18,... | collective-permute-start | bytes 393224 | tf_op jit(solution)/shard_map/ppermute | solution.py:350
  17.3 1.5 %collective-permute-start.12 = (f32[2,32,512]{2,1,0:T(8,128)S(1)}, f32[2,32,512]{2,1,0:T(8,128)S(1)}, u32[]{:S(2)}, u32[]{:S(2)}) collective-permute-start(f32[2,32,512]{2,1,0:T(8,128)S(1)} %get-tuple-element.73), channel_id=1, source_target_pairs={{0,2},{2,0},{4,6},{6,4},{8,10},{10,8},{12,14},{14,12},{16,18},{18,... | collective-permute-start | bytes 393224 | tf_op jit(solution)/shard_map/ppermute | solution.py:350
  17.4 1.4 %collective-permute-start.13 = (f32[2,16,512]{2,1,0:T(8,128)S(1)}, f32[2,16,512]{2,1,0:T(8,128)S(1)}, u32[]{:S(2)}, u32[]{:S(2)}) collective-permute-start(f32[2,16,512]{2,1,0:T(8,128)S(1)} %get-tuple-element.74), channel_id=1, source_target_pairs={{0,2},{2,0},{4,6},{6,4},{8,10},{10,8},{12,14},{14,12},{16,18},{18,... | collective-permute-start | bytes 196616 | tf_op jit(solution)/shard_map/ppermute | solution.py:350
  17.9 6.8 %collective-permute-start.21 = (f32[2,48,512]{2,1,0:T(8,128)S(1)}, f32[2,48,512]{2,1,0:T(8,128)S(1)}, u32[]{:S(2)}, u32[]{:S(2)}) collective-permute-start(f32[2,48,512]{2,1,0:T(8,128)S(1)} %get-tuple-element.86), channel_id=1, source_target_pairs={{0,2},{2,4},{4,0},{6,8},{8,10},{10,12},{12,6},{14,16},{16,18},{18,... | collective-permute-start | bytes 589832 | tf_op jit(solution)/shard_map/ppermute | solution.py:353
  18.9 7.5 %collective-permute-start.16 = (f32[2,48,512]{2,1,0:T(8,128)S(1)}, f32[2,48,512]{2,1,0:T(8,128)S(1)}, u32[]{:S(2)}, u32[]{:S(2)}) collective-permute-start(f32[2,48,512]{2,1,0:T(8,128)S(1)} %get-tuple-element.79), channel_id=1, source_target_pairs={{0,2},{2,4},{4,0},{6,8},{8,10},{10,12},{12,6},{14,16},{16,18},{18,... | collective-permute-start | bytes 589832 | tf_op jit(solution)/shard_map/ppermute | solution.py:353
  22.8 1.3 %collective-permute-start.23 = (f32[2,16,512]{2,1,0:T(8,128)S(1)}, f32[2,16,512]{2,1,0:T(8,128)S(1)}, u32[]{:S(2)}, u32[]{:S(2)}) collective-permute-start(f32[2,16,512]{2,1,0:T(8,128)S(1)} %get-tuple-element.88), channel_id=1, source_target_pairs={{0,2},{2,0},{4,6},{6,4},{8,10},{10,8},{12,14},{14,12},{16,18},{18,... | collective-permute-start | bytes 196616 | tf_op jit(solution)/shard_map/ppermute | solution.py:350
  22.9 1.8 %collective-permute-start.22 = (f32[2,32,512]{2,1,0:T(8,128)S(1)}, f32[2,32,512]{2,1,0:T(8,128)S(1)}, u32[]{:S(2)}, u32[]{:S(2)}) collective-permute-start(f32[2,32,512]{2,1,0:T(8,128)S(1)} %get-tuple-element.87), channel_id=1, source_target_pairs={{0,2},{2,0},{4,6},{6,4},{8,10},{10,8},{12,14},{14,12},{16,18},{18,... | collective-permute-start | bytes 393224 | tf_op jit(solution)/shard_map/ppermute | solution.py:350
  24.1 1.5 %collective-permute-start.19 = (f32[2,32,512]{2,1,0:T(8,128)S(1)}, f32[2,32,512]{2,1,0:T(8,128)S(1)}, u32[]{:S(2)}, u32[]{:S(2)}) collective-permute-start(f32[2,32,512]{2,1,0:T(8,128)S(1)} %get-tuple-element.84), channel_id=1, source_target_pairs={{0,2},{2,0},{4,6},{6,4},{8,10},{10,8},{12,14},{14,12},{16,18},{18,... | collective-permute-start | bytes 393224 | tf_op jit(solution)/shard_map/ppermute | solution.py:350
  24.2 1.4 %collective-permute-start.20 = (f32[2,16,512]{2,1,0:T(8,128)S(1)}, f32[2,16,512]{2,1,0:T(8,128)S(1)}, u32[]{:S(2)}, u32[]{:S(2)}) collective-permute-start(f32[2,16,512]{2,1,0:T(8,128)S(1)} %get-tuple-element.85), channel_id=1, source_target_pairs={{0,2},{2,0},{4,6},{6,4},{8,10},{10,8},{12,14},{14,12},{16,18},{18,... | collective-permute-start | bytes 196616 | tf_op jit(solution)/shard_map/ppermute | solution.py:350
  26.5 3.9 %collective-permute-start.24 = (f32[1,256]{1,0:T(1,128)S(1)}, f32[1,256]{1,0:T(1,128)S(1)}, u32[]{:S(2)}, u32[]{:S(2)}) collective-permute-start(f32[1,256]{1,0:T(1,128)S(1)} %get-tuple-element.93), channel_id=1, source_target_pairs={{0,1},{1,0},{2,3},{3,2},{4,5},{5,4},{6,7},{7,6},{8,9},{9,8},{10,11... | collective-permute-start | bytes 3080 | tf_op jit(solution)/shard_map/ppermute | solution.py:382

commit v8 on v7

--- a/solution.py
+++ b/solution.py
@@ -14,18 +14,20 @@
 VMEM_LIMIT = 24 * 1024 * 1024
 WEIGHTS = {
     "first_0": 30000000,
-    "first_1": 30000000,
-    "step_1_0_0": 1000000,
-    "step_1_1_0": 1000000,
+    "first_1": 200000000,
+    "step_1_0_0": 500000000,
+    "step_1_0_1": 10000000,
+    "step_1_1_0": 30000000,
     "step_2_0_0": 1000000,
-    "step_2_1_0": 1000000000,
-    "step_2_1_1": 500000000,
-    "step_3_0_0": 1000000,
-    "step_3_0_1": 500000000,
-    "step_3_1_0": 500000000,
+    "step_2_0_1": 100000000,
+    "step_2_1_0": 30000000,
+    "step_2_1_1": 30000000,
+    "step_3_0_0": 500000000,
+    "step_3_0_1": 1000000,
+    "step_3_1_0": 1000000000,
     "step_3_1_1": 1000000,
-    "last_0": 30000000,
-    "gradient": 100000000,
+    "last_0": 1000000000,
+    "gradient": 500000000,
 }
 PARAMS = pltpu.CompilerParams(vmem_limit_bytes=VMEM_LIMIT)
 IN_VMEM = pl.BlockSpec(memory_space=pltpu.VMEM)
@@ -112,7 +114,7 @@
 def first_kernel(parity, chained, *refs):
     operator, contrast, residual, panel = refs[:4]
     refs = refs[7:] if chained else refs[4:]
-    pieces = HALVES * (2 - parity)
+    pieces = 1 if parity else 2 * HALVES
     out = refs[:pieces]
     high, low, grad = refs[pieces : pieces + 3]
     whole, reflect, wave, arrived, left, sems = refs[-6:]
@@ -166,7 +168,7 @@
 def first(parity, operator, contrast, residual, panel, carried):
     shots, breadth = panel.shape[3:]
     half = pltpu.VMEM((2, breadth, breadth), jnp.bfloat16)
-    outs = piece_shapes(parity, shots // HALVES, breadth) * HALVES
+    outs = piece_shapes(1, shots, breadth) if parity else piece_shapes(0, shots // HALVES, breadth) * HALVES
     return pl.pallas_call(
         functools.partial(first_kernel, parity, bool(carried)),
         out_shape=(*outs, half, half, pltpu.VMEM((8, breadth), jnp.float32)),
@@ -189,7 +191,7 @@
 
 def arrive(tick, half, parity, panel, shared, grad_in, grad, left):
     residual, contrast, sites, pulse = shared
-    rows = sum(piece.shape[1] for piece in panel)
+    rows = left.shape[0] // 4 if left is not None else sum(piece.shape[1] for piece in panel)
     start = half * rows
     waves = residual.at[0, 0, tick]
     rest = (start, waves, contrast, grad_in, grad, left)
@@ -199,13 +201,17 @@
         return
     surface = lax.axis_index("depth") == 0
 
+    piece = panel[0]
+    if piece.shape[1] > rows:
+        piece = piece.at[:, pl.ds(start, rows)]
+
     @pl.when(surface)
     def _():
-        take(injected(tick, start, sites, pulse, panel[0].shape[1:]), *rest)
+        take(injected(tick, start, sites, pulse, (rows, piece.shape[2])), *rest)
 
     @pl.when(jnp.logical_not(surface))
     def _():
-        take(panel[0], *rest)
+        take(piece, *rest)
 
 
 def arrive_either(half, above, mate, shared, grad_in, grad, left):
@@ -344,25 +350,26 @@
     shots = arriving_downward_matrices.shape[3]
     mate_route = [(level, level ^ 1) for level in range(levels)]
     down_route = cross_route(levels)
+    open_route = [(level, level + 1) for level in range(1, levels - 1, 2)]
     shared = (ascending_residual, impedance_contrast, shot_node_indices, emitted_pulse[0].T)
 
     def mate(pieces):
         return [lax.ppermute(piece, "depth", mate_route) for piece in pieces]
 
-    def down(piece):
-        return lax.ppermute(piece, "depth", down_route)
+    def down(piece, closed=True):
+        return lax.ppermute(piece, "depth", down_route if closed else open_route)
 
     rows = shots // HALVES
     start = (extrapolation_operator, impedance_contrast, ascending_residual, arriving_downward_matrices)
-    results = first(1, *start, ())
-    above = [down(piece) for piece in results[:HALVES]]
-    *even, high, low, grad = first(0, *start, results[HALVES:])
+    odd, *carried = first(1, *start, ())
+    above = [down(odd, closed=False)] * HALVES
+    *even, high, low, grad = first(0, *start, carried)
     beside = [mate(even[2 * half : 2 * half + 2]) for half in range(HALVES)]
     grads = [grad]
 
     def odd_step(tick, half):
         odd, grads[0] = step(tick, half, 1, beside[half], shared, high, low, grads[0], rows)
-        return down(odd)
+        return down(odd, closed=tick < TICKS - 2 or half < HALVES - 1)
 
     def even_step(tick, half):
         *even, grads[0] = step(tick, half, 0, (above[half],), shared, high, low, grads[0], rows)

time: 31.2 us -> 32.3 us (1.035)
  starting transfers between devices: 16.1 us -> 19.2 us
  waiting for transfers between devices: 4.63 us -> 2.54 us
    ppermute x16, starting transfers between devices: 4.36 us -> 13.8 us  [mate(): return [lax.ppermute(piece, 'depth', mate_route) for piece in pieces]]
    ppermute x8 -> x7, starting transfers between devices: 9.31 us -> 3.84 us  [down(): return lax.ppermute(piece, 'depth', down_route if closed else open_route)]
    ppermute x8 -> x7, waiting for transfers between devices: 2.09 us -> 0.02 us  [down(): return lax.ppermute(piece, 'depth', down_route if closed else open_route)]
    ppermute x1, starting transfers between devices: 2.39 us -> 1.55 us  [local(): gradient = gradient + lax.ppermute(chunks[distance], 'freq', route)]
    ppermute x16, waiting for transfers between devices: 2.37 us -> 1.82 us  [mate(): return [lax.ppermute(piece, 'depth', mate_route) for piece in pieces]]
    ppermute x1, waiting for transfers between devices: 0.17 us -> 0.71 us  [local(): gradient = gradient + lax.ppermute(chunks[distance], 'freq', route)]
  transfers between devices with their start and end apart: 25 -> 24, of which waited for: 8 -> 8; matrix products, arithmetic and copies ran while one was open for 0% -> 0% of each run, Pallas kernels for 28% -> 27%
where the time goes in v8:
time: 32.3 us; the launch traced here: 32.1 us
  starting transfers between devices  19.2 us (59%)
  Pallas kernels  9 us (28%)
  waiting for transfers between devices  2.54 us (8%)
  between operations  0.83 us (3%)
  other arithmetic  0.56 us (2%)
    ppermute x16, starting transfers between devices, mate(): return [lax.ppermute(piece, 'depth', mate_route) for piece in pieces]  13.8 us
    pallas_call x12, Pallas kernels, step(): pl.pallas_call(functools.partial(step_kernel, tick, half, parity), out_sh...  4.1 us
    ppermute x7, starting transfers between devices, down(): return lax.ppermute(piece, 'depth', down_route if closed else open_route)  3.84 us
    pallas_call x2, Pallas kernels, first(): pl.pallas_call(functools.partial(first_kernel, parity, bool(carried)), ou...  2.7 us
    pallas_call x2, Pallas kernels, last(): pl.pallas_call(functools.partial(last_kernel, half), out_shape=out_shape,...  2.05 us
    ppermute x16, waiting for transfers between devices, mate(): return [lax.ppermute(piece, 'depth', mate_route) for piece in pieces]  1.82 us
    ppermute x1, starting transfers between devices, local(): gradient = gradient + lax.ppermute(chunks[distance], 'freq', route)  1.55 us
    ppermute x1, waiting for transfers between devices, local(): gradient = gradient + lax.ppermute(chunks[distance], 'freq', route)  0.71 us
  transfers between devices with their start and end apart: 24, of which 8 were waited for; matrix products, arithmetic and copies ran while one was open for 0% of the time, Pallas kernels for 27%

profile of v8, /device:TPU:0, one launch (start us, length us, event | category | flops | bytes accessed | tf_op | source)
XLA Modules:
  0.0 32.1 jit_solution(17826096224860840202)
XLA Ops:
  0.6 0.1 first_1.1
  0.7 0.7 %collective-permute-start.6 = (f32[2,96,512]{2,1,0:T(8,128)S(1)}, f32[2,96,512]{2,1,0:T(8,128)S(1)}, u32[]{:S(2)}, u32[]{:S(2)}) collective-permute-start(f32[2,96,512]{2,1,0:T(8,128)S(1)} %get-tuple-element.60), channel_id=1, source_target_pairs={{2,4},{6,8},{10,12},{14,16},{18,20},{22,24},{26,28},{3,5},{7,9},{1... | collective-permute-start | bytes 1179656 | tf_op jit(solution)/shard_map/ppermute | solution.py:360
  1.4 0.0 copy-start
  1.4 0.0 copy-start.1
  1.4 0.0 copy-start.2
  1.5 0.0 copy-start.3
  1.5 2.6 %first_0.1 = (f32[2,32,512]{2,1,0:T(8,128)S(1)}, f32[2,16,512]{2,1,0:T(8,128)S(1)}, f32[2,32,512]{2,1,0:T(8,128)S(1)}, f32[2,16,512]{2,1,0:T(8,128)S(1)}, bf16[2...) custom-call(f32[1,1,2,512,512]{4,3,2,1,0:T(8,128)} %refs_0_.5, ...), custom_call_target="tpu_custom_call", output_to_operand_aliasing={{4}: (4, {}), {5}: (5, {}), {6}: (6, {})} | custom-call | flops 30000000 | bytes 1 | tf_op jit(solution)/shard_map/first_0/pallas_call | solution.py:172
  4.1 1.9 %collective-permute-start.2 = (f32[2,32,512]{2,1,0:T(8,128)S(1)}, f32[2,32,512]{2,1,0:T(8,128)S(1)}, u32[]{:S(2)}, u32[]{:S(2)}) collective-permute-start(f32[2,32,512]{2,1,0:T(8,128)S(1)} %get-tuple-element.54), channel_id=1, source_target_pairs={{0,2},{2,0},{4,6},{6,4},{8,10},{10,8},{12,14},{14,12},{16,18},{18,... | collective-permute-start | bytes 393224 | tf_op jit(solution)/shard_map/ppermute | solution.py:357
  5.9 0.1 collective-permute-start
  6.0 0.4 %collective-permute-start.3 = (f32[2,16,512]{2,1,0:T(8,128)S(1)}, f32[2,16,512]{2,1,0:T(8,128)S(1)}, u32[]{:S(2)}, u32[]{:S(2)}) collective-permute-start(f32[2,16,512]{2,1,0:T(8,128)S(1)} %get-tuple-element.55), channel_id=1, source_target_pairs={{0,2},{2,0},{4,6},{6,4},{8,10},{10,8},{12,14},{14,12},{16,18},{18,... | collective-permute-start | bytes 196616 | tf_op jit(solution)/shard_map/ppermute | solution.py:357
  6.5 0.1 collective-permute-start.1
  6.5 0.9 %collective-permute-done.3.refs_1_ = f32[2,16,512]{2,1,0:T(8,128)S(1)} collective-permute-done((f32[2,16,512]{2,1,0:T(8,128)S(1)}, f32[2,16,512]{2,1,0:T(8,128)S(1)}, u32[]{:S(2)}, u32[]{:S(2)}) %collective-permute-start.3) | collective-permute-done | bytes 65568 | tf_op jit(solution)/shard_map/ppermute | solution.py:357
  7.4 0.0 collective-permute-done.2.refs_0_
  7.5 0.9 %collective-permute-start.5 = (f32[2,48,512]{2,1,0:T(8,128)S(1)}, f32[2,48,512]{2,1,0:T(8,128)S(1)}, u32[]{:S(2)}, u32[]{:S(2)}) collective-permute-start(f32[2,48,512]{2,1,0:T(8,128)S(1)} %get-tuple-element.59), channel_id=1, source_target_pairs={{0,2},{2,4},{4,0},{6,8},{8,10},{10,12},{12,6},{14,16},{16,18},{18,... | collective-permute-start | bytes 589832 | tf_op jit(solution)/shard_map/ppermute | solution.py:360
  8.4 0.0 collective-permute-done.1.refs_1_
  8.4 0.0 collective-permute-done.refs_0_
  8.4 0.0 collective-permute-done.6.refs_0_
  8.4 0.7 %step_1_0_0.1 = (f32[2,32,512]{2,1,0:T(8,128)S(1)}, f32[2,16,512]{2,1,0:T(8,128)S(1)}, f32[8,512]{1,0:T(8,128)S(1)}) custom-call(f32[2,96,512]{2,1,0:T(8,128)S(1)} %collective-permute-done.6.refs_0_, f32[1,1,5,2,96,512]{5,4,3,2,1,0:T(8,128)S(1)} %copy-done, f32[1,512]{1,0:T(1,128)S(1)} %copy-done.1, ...), custom_call_target="tpu_custom_call", output_to_operand_aliasing={{2}: (7, {})} | custom-call | flops 500000000 | bytes 1 | tf_op jit(solution)/shard_map/step_1_0_0/pallas_call | solution.py:242
  9.0 1.4 %collective-permute-start.9 = (f32[2,32,512]{2,1,0:T(8,128)S(1)}, f32[2,32,512]{2,1,0:T(8,128)S(1)}, u32[]{:S(2)}, u32[]{:S(2)}) collective-permute-start(f32[2,32,512]{2,1,0:T(8,128)S(1)} %get-tuple-element.65), channel_id=1, source_target_pairs={{0,2},{2,0},{4,6},{6,4},{8,10},{10,8},{12,14},{14,12},{16,18},{18,... | collective-permute-start | bytes 393224 | tf_op jit(solution)/shard_map/ppermute | solution.py:357
  10.4 0.0 collective-permute-start.4
  10.5 3.2 %collective-permute-start.10 = (f32[2,16,512]{2,1,0:T(8,128)S(1)}, f32[2,16,512]{2,1,0:T(8,128)S(1)}, u32[]{:S(2)}, u32[]{:S(2)}) collective-permute-start(f32[2,16,512]{2,1,0:T(8,128)S(1)} %get-tuple-element.66), channel_id=1, source_target_pairs={{0,2},{2,0},{4,6},{6,4},{8,10},{10,8},{12,14},{14,12},{16,18},{18,... | collective-permute-start | bytes 196616 | tf_op jit(solution)/shard_map/ppermute | solution.py:357
  13.6 0.7 %step_1_1_0.1 = (f32[2,32,512]{2,1,0:T(8,128)S(1)}, f32[2,16,512]{2,1,0:T(8,128)S(1)}, f32[8,512]{1,0:T(8,128)S(1)}) custom-call(f32[2,96,512]{2,1,0:T(8,128)S(1)} %collective-permute-done.6.refs_0_, f32[1,1,5,2,96,512]{5,4,3,2,1,0:T(8,128)S(1)} %copy-done, f32[1,512]{1,0:T(1,128)S(1)} %copy-done.1, ...), custom_call_target="tpu_custom_call", output_to_operand_aliasing={{2}: (7, {})} | custom-call | flops 30000000 | bytes 1 | tf_op jit(solution)/shard_map/step_1_1_0/pallas_call | solution.py:242
  14.3 0.1 collective-permute-start.7
  14.4 0.2 collective-permute-done.10.refs_1_
  14.5 0.4 %collective-permute-start.8 = (f32[2,16,512]{2,1,0:T(8,128)S(1)}, f32[2,16,512]{2,1,0:T(8,128)S(1)}, u32[]{:S(2)}, u32[]{:S(2)}) collective-permute-start(f32[2,16,512]{2,1,0:T(8,128)S(1)} %get-tuple-element.64), channel_id=1, source_target_pairs={{0,2},{2,0},{4,6},{6,4},{8,10},{10,8},{12,14},{14,12},{16,18},{18,... | collective-permute-start | bytes 196616 | tf_op jit(solution)/shard_map/ppermute | solution.py:357
  14.9 0.0 collective-permute-done.9.refs_0_
  14.9 0.7 %collective-permute-start.17 = (f32[2,48,512]{2,1,0:T(8,128)S(1)}, f32[2,48,512]{2,1,0:T(8,128)S(1)}, u32[]{:S(2)}, u32[]{:S(2)}) collective-permute-start(f32[2,48,512]{2,1,0:T(8,128)S(1)} %get-tuple-element.79), channel_id=1, source_target_pairs={{0,2},{2,4},{4,0},{6,8},{8,10},{10,12},{12,6},{14,16},{16,18},{18,... | collective-permute-start | bytes 589832 | tf_op jit(solution)/shard_map/ppermute | solution.py:360
  15.6 0.2 collective-permute-done.8.refs_1_
  15.8 0.0 collective-permute-done.7.refs_0_
  15.8 0.0 collective-permute-done.5.refs_0_
  15.8 0.7 %step_2_0_0.1 = (f32[2,32,512]{2,1,0:T(8,128)S(1)}, f32[2,16,512]{2,1,0:T(8,128)S(1)}, f32[8,512]{1,0:T(8,128)S(1)}) custom-call(f32[2,48,512]{2,1,0:T(8,128)S(1)} %collective-permute-done.5.refs_0_, f32[1,1,5,2,96,512]{5,4,3,2,1,0:T(8,128)S(1)} %copy-done, f32[1,512]{1,0:T(1,128)S(1)} %copy-done.1, ...), custom_call_target="tpu_custom_call", output_to_operand_aliasing={{2}: (7, {})} | custom-call | flops 1000000 | bytes 1 | tf_op jit(solution)/shard_map/step_2_0_0/pallas_call | solution.py:242
  16.5 1.6 %collective-permute-start.13 = (f32[2,32,512]{2,1,0:T(8,128)S(1)}, f32[2,32,512]{2,1,0:T(8,128)S(1)}, u32[]{:S(2)}, u32[]{:S(2)}) collective-permute-start(f32[2,32,512]{2,1,0:T(8,128)S(1)} %get-tuple-element.73), channel_id=1, source_target_pairs={{0,2},{2,0},{4,6},{6,4},{8,10},{10,8},{12,14},{14,12},{16,18},{18,... | collective-permute-start | bytes 393224 | tf_op jit(solution)/shard_map/ppermute | solution.py:357
  18.1 0.1 collective-permute-start.16
  18.1 1.2 %collective-permute-start.14 = (f32[2,16,512]{2,1,0:T(8,128)S(1)}, f32[2,16,512]{2,1,0:T(8,128)S(1)}, u32[]{:S(2)}, u32[]{:S(2)}) collective-permute-start(f32[2,16,512]{2,1,0:T(8,128)S(1)} %get-tuple-element.74), channel_id=1, source_target_pairs={{0,2},{2,0},{4,6},{6,4},{8,10},{10,8},{12,14},{14,12},{16,18},{18,... | collective-permute-start | bytes 196616 | tf_op jit(solution)/shard_map/ppermute | solution.py:357
  19.3 0.0 collective-permute-done.4.refs_0_
  19.3 0.7 %step_2_1_0.1 = (f32[2,32,512]{2,1,0:T(8,128)S(1)}, f32[2,16,512]{2,1,0:T(8,128)S(1)}, f32[8,512]{1,0:T(8,128)S(1)}) custom-call(f32[2,48,512]{2,1,0:T(8,128)S(1)} %collective-permute-done.4.refs_0_, f32[1,1,5,2,96,512]{5,4,3,2,1,0:T(8,128)S(1)} %copy-done, f32[1,512]{1,0:T(1,128)S(1)} %copy-done.1, ...), custom_call_target="tpu_custom_call", output_to_operand_aliasing={{2}: (7, {})} | custom-call | flops 30000000 | bytes 1 | tf_op jit(solution)/shard_map/step_2_1_0/pallas_call | solution.py:242
  20.0 0.1 collective-permute-start.11
  20.1 0.1 collective-permute-done.14.refs_1_
  20.2 0.4 %collective-permute-start.12 = (f32[2,16,512]{2,1,0:T(8,128)S(1)}, f32[2,16,512]{2,1,0:T(8,128)S(1)}, u32[]{:S(2)}, u32[]{:S(2)}) collective-permute-start(f32[2,16,512]{2,1,0:T(8,128)S(1)} %get-tuple-element.72), channel_id=1, source_target_pairs={{0,2},{2,0},{4,6},{6,4},{8,10},{10,8},{12,14},{14,12},{16,18},{18,... | collective-permute-start | bytes 196616 | tf_op jit(solution)/shard_map/ppermute | solution.py:357
  20.6 0.0 collective-permute-done.13.refs_0_
  20.6 0.7 %collective-permute-start.20 = (f32[2,48,512]{2,1,0:T(8,128)S(1)}, f32[2,48,512]{2,1,0:T(8,128)S(1)}, u32[]{:S(2)}, u32[]{:S(2)}) collective-permute-start(f32[2,48,512]{2,1,0:T(8,128)S(1)} %get-tuple-element.84), channel_id=1, source_target_pairs={{0,2},{2,4},{4,0},{6,8},{8,10},{10,12},{12,6},{14,16},{16,18},{18,... | collective-permute-start | bytes 589832 | tf_op jit(solution)/shard_map/ppermute | solution.py:360
  21.3 0.2 collective-permute-done.12.refs_1_
  21.5 0.0 collective-permute-done.11.refs_0_
  21.5 0.7 %collective-permute-start.15 = (f32[2,48,512]{2,1,0:T(8,128)S(1)}, f32[2,48,512]{2,1,0:T(8,128)S(1)}, u32[]{:S(2)}, u32[]{:S(2)}) collective-permute-start(f32[2,48,512]{2,1,0:T(8,128)S(1)} %get-tuple-element.77), channel_id=1, source_target_pairs={{2,4},{6,8},{10,12},{14,16},{18,20},{22,24},{26,28},{3,5},{7,9},{1... | collective-permute-start | bytes 589832 | tf_op jit(solution)/shard_map/ppermute | solution.py:360
  22.2 0.0 collective-permute-done.17.refs_0_
  22.2 0.7 %step_3_0_0.1 = (f32[2,32,512]{2,1,0:T(8,128)S(1)}, f32[2,16,512]{2,1,0:T(8,128)S(1)}, f32[8,512]{1,0:T(8,128)S(1)}) custom-call(f32[2,48,512]{2,1,0:T(8,128)S(1)} %collective-permute-done.17.refs_0_, f32[1,1,5,2,96,512]{5,4,3,2,1,0:T(8,128)S(1)} %copy-done, f32[1,512]{1,0:T(1,128)S(1)} %copy-done.1, ...), custom_call_target="tpu_custom_call", output_to_operand_aliasing={{2}: (7, {})} | custom-call | flops 500000000 | bytes 1 | tf_op jit(solution)/shard_map/step_3_0_0/pallas_call | solution.py:242
  22.9 2.6 %collective-permute-start.22 = (f32[2,16,512]{2,1,0:T(8,128)S(1)}, f32[2,16,512]{2,1,0:T(8,128)S(1)}, u32[]{:S(2)}, u32[]{:S(2)}) collective-permute-start(f32[2,16,512]{2,1,0:T(8,128)S(1)} %get-tuple-element.86), channel_id=1, source_target_pairs={{0,2},{2,0},{4,6},{6,4},{8,10},{10,8},{12,14},{14,12},{16,18},{18,... | collective-permute-start | bytes 196616 | tf_op jit(solution)/shard_map/ppermute | solution.py:357
  25.5 0.1 collective-permute-start.21
  25.6 0.0 collective-permute-done.16.refs_0_
  25.6 0.7 %step_3_1_0.1 = (f32[2,32,512]{2,1,0:T(8,128)S(1)}, f32[2,16,512]{2,1,0:T(8,128)S(1)}, f32[8,512]{1,0:T(8,128)S(1)}) custom-call(f32[2,48,512]{2,1,0:T(8,128)S(1)} %collective-permute-done.16.refs_0_, f32[1,1,5,2,96,512]{5,4,3,2,1,0:T(8,128)S(1)} %copy-done, f32[1,512]{1,0:T(1,128)S(1)} %copy-done.1, ...), custom_call_target="tpu_custom_call", output_to_operand_aliasing={{2}: (7, {})} | custom-call | flops 1000000000 | bytes 1 | tf_op jit(solution)/shard_map/step_3_1_0/pallas_call | solution.py:242
  26.3 0.1 collective-permute-start.18
  26.4 0.1 collective-permute-done.22.mate_tail
  26.4 0.4 %collective-permute-start.19 = (f32[2,16,512]{2,1,0:T(8,128)S(1)}, f32[2,16,512]{2,1,0:T(8,128)S(1)}, u32[]{:S(2)}, u32[]{:S(2)}) collective-permute-start(f32[2,16,512]{2,1,0:T(8,128)S(1)} %get-tuple-element.83), channel_id=1, source_target_pairs={{0,2},{2,0},{4,6},{6,4},{8,10},{10,8},{12,14},{14,12},{16,18},{18,... | collective-permute-start | bytes 196616 | tf_op jit(solution)/shard_map/ppermute | solution.py:357
  26.9 0.0 collective-permute-done.20.above
  26.9 0.0 collective-permute-done.21.mate
  26.9 0.7 %last_0.1 = (f32[2,48,512]{2,1,0:T(8,128)S(1)}, f32[8,512]{1,0:T(8,128)S(1)}) custom-call(f32[2,48,512]{2,1,0:T(8,128)S(1)} %collective-permute-done.20.above, f32[2,32,512]{2,1,0:T(8,128)S(1)} %collective-permute-done.21.mate, f32[2,16,512]{2,1,0:T(8,128)S(1)} %collective-permute-done.22.mate_tail, ...), custom_call_target="tpu_custom_call", output_to_operand_aliasing={{1}: (9, {})} | custom-call | flops 1000000000 | bytes 1 | tf_op jit(solution)/shard_map/last_0/pallas_call | solution.py:317
  27.5 0.2 collective-permute-done.19.mate_tail
  27.8 0.0 collective-permute-done.15.above
  27.8 0.0 collective-permute-done.18.mate
  27.8 0.1 gradient.1
  27.9 1.6 %collective-permute-start.23 = (f32[1,256]{1,0:T(1,128)S(1)}, f32[1,256]{1,0:T(1,128)S(1)}, u32[]{:S(2)}, u32[]{:S(2)}) collective-permute-start(f32[1,256]{1,0:T(1,128)S(1)} %get-tuple-element.91), channel_id=1, source_target_pairs={{0,1},{1,0},{2,3},{3,2},{4,5},{5,4},{6,7},{7,6},{8,9},{9,8},{10,11... | collective-permute-start | bytes 3080 | tf_op jit(solution)/shard_map/ppermute | solution.py:389
  29.5 1.4 %last_1.1 = f32[2,96,512]{2,1,0:T(8,128)} custom-call(f32[2,48,512]{2,1,0:T(8,128)S(1)} %collective-permute-done.15.above, f32[2,32,512]{2,1,0:T(8,128)S(1)} %collective-permute-done.18.mate, f32[2,16,512]{2,1,0:T(8,128)S(1)} %collective-permute-done.19.mate_tail, f32[1,1,5,2,96,512]{5,4,3,2,1,0:T(8,128)S(1)} %copy-done, f32[1,512]{1,0:T(1,128)S(1)} %copy-done.1, ...), custom_call_target="tpu_custom_call" | custom-call | flops 1 | bytes 1 | tf_op jit(solution)/shard_map/last_1/pallas_call | solution.py:317
  30.9 0.7 %collective-permute-done.23 = f32[1,256]{1,0:T(1,128)S(1)} collective-permute-done((f32[1,256]{1,0:T(1,128)S(1)}, f32[1,256]{1,0:T(1,128)S(1)}, u32[]{:S(2)}, u32[]{:S(2)}) %collective-permute-start.23) | collective-permute-done | bytes 1056 | tf_op jit(solution)/shard_map/ppermute | solution.py:389
  31.6 0.6 %add.3 = f32[1,256]{1,0:T(1,128)} add(f32[1,256]{1,0:T(1,128)S(1)} %get-tuple-element.90, f32[1,256]{1,0:T(1,128)S(1)} %collective-permute-done.23) | non-fusion elementwise | flops 256 | bytes 3072 | tf_op jit(solution)/shard_map/add | solution.py:389
  (10 shorter events, 0.0 us)
Async XLA Ops:
  0.7 7.6 %collective-permute-start.6 = (f32[2,96,512]{2,1,0:T(8,128)S(1)}, f32[2,96,512]{2,1,0:T(8,128)S(1)}, u32[]{:S(2)}, u32[]{:S(2)}) collective-permute-start(f32[2,96,512]{2,1,0:T(8,128)S(1)} %get-tuple-element.60), channel_id=1, source_target_pairs={{2,4},{6,8},{10,12},{14,16},{18,20},{22,24},{26,28},{3,5},{7,9},{1... | collective-permute-start | bytes 1179656 | tf_op jit(solution)/shard_map/ppermute | solution.py:360
  1.4 6.0 %copy-start = (f32[1,1,5,2,96,512]{5,4,3,2,1,0:T(8,128)S(1)}, f32[1,1,5,2,96,512]{5,4,3,2,1,0:T(8,128)}, u32[]{:S(2)}) copy-start(f32[1,1,5,2,96,512]{5,4,3,2,1,0:T(8,128)} %residual.1) | copy-start | bytes 5898244
  1.4 6.0 %copy-start.1 = (f32[1,512]{1,0:T(1,128)S(1)}, f32[1,512]{1,0:T(1,128)}, u32[]{:S(2)}) copy-start(f32[1,512]{1,0:T(1,128)} %contrast.1) | copy-start | bytes 6148
  1.4 6.0 %copy-start.2 = (s32[4,96]{1,0:T(4,128)S(1)}, s32[4,96]{1,0:T(4,128)}, u32[]{:S(2)}) copy-start(s32[4,96]{1,0:T(4,128)} %sites.1) | copy-start | bytes 4612
  1.5 6.0 %copy-start.3 = (f32[1,4,2]{1,2,0:T(2,128)S(1)}, f32[1,4,2]{1,2,0:T(2,128)}, u32[]{:S(2)}) copy-start(f32[1,4,2]{1,2,0:T(2,128)} %param.11) | copy-start | bytes 100
  4.1 3.3 %collective-permute-start.2 = (f32[2,32,512]{2,1,0:T(8,128)S(1)}, f32[2,32,512]{2,1,0:T(8,128)S(1)}, u32[]{:S(2)}, u32[]{:S(2)}) collective-permute-start(f32[2,32,512]{2,1,0:T(8,128)S(1)} %get-tuple-element.54), channel_id=1, source_target_pairs={{0,2},{2,0},{4,6},{6,4},{8,10},{10,8},{12,14},{14,12},{16,18},{18,... | collective-permute-start | bytes 393224 | tf_op jit(solution)/shard_map/ppermute | solution.py:357
  5.9 2.4 %collective-permute-start = (f32[2,32,512]{2,1,0:T(8,128)S(1)}, f32[2,32,512]{2,1,0:T(8,128)S(1)}, u32[]{:S(2)}, u32[]{:S(2)}) collective-permute-start(f32[2,32,512]{2,1,0:T(8,128)S(1)} %get-tuple-element.50), channel_id=1, source_target_pairs={{0,2},{2,0},{4,6},{6,4},{8,10},{10,8},{12,14},{14,12},{16,18},{18,... | collective-permute-start | bytes 393224 | tf_op jit(solution)/shard_map/ppermute | solution.py:357
  6.0 1.4 %collective-permute-start.3 = (f32[2,16,512]{2,1,0:T(8,128)S(1)}, f32[2,16,512]{2,1,0:T(8,128)S(1)}, u32[]{:S(2)}, u32[]{:S(2)}) collective-permute-start(f32[2,16,512]{2,1,0:T(8,128)S(1)} %get-tuple-element.55), channel_id=1, source_target_pairs={{0,2},{2,0},{4,6},{6,4},{8,10},{10,8},{12,14},{14,12},{16,18},{18,... | collective-permute-start | bytes 196616 | tf_op jit(solution)/shard_map/ppermute | solution.py:357
  6.5 1.9 %collective-permute-start.1 = (f32[2,16,512]{2,1,0:T(8,128)S(1)}, f32[2,16,512]{2,1,0:T(8,128)S(1)}, u32[]{:S(2)}, u32[]{:S(2)}) collective-permute-start(f32[2,16,512]{2,1,0:T(8,128)S(1)} %get-tuple-element.51), channel_id=1, source_target_pairs={{0,2},{2,0},{4,6},{6,4},{8,10},{10,8},{12,14},{14,12},{16,18},{18,... | collective-permute-start | bytes 196616 | tf_op jit(solution)/shard_map/ppermute | solution.py:357
  7.5 8.3 %collective-permute-start.5 = (f32[2,48,512]{2,1,0:T(8,128)S(1)}, f32[2,48,512]{2,1,0:T(8,128)S(1)}, u32[]{:S(2)}, u32[]{:S(2)}) collective-permute-start(f32[2,48,512]{2,1,0:T(8,128)S(1)} %get-tuple-element.59), channel_id=1, source_target_pairs={{0,2},{2,4},{4,0},{6,8},{8,10},{10,12},{12,6},{14,16},{16,18},{18,... | collective-permute-start | bytes 589832 | tf_op jit(solution)/shard_map/ppermute | solution.py:360
  9.0 5.8 %collective-permute-start.9 = (f32[2,32,512]{2,1,0:T(8,128)S(1)}, f32[2,32,512]{2,1,0:T(8,128)S(1)}, u32[]{:S(2)}, u32[]{:S(2)}) collective-permute-start(f32[2,32,512]{2,1,0:T(8,128)S(1)} %get-tuple-element.65), channel_id=1, source_target_pairs={{0,2},{2,0},{4,6},{6,4},{8,10},{10,8},{12,14},{14,12},{16,18},{18,... | collective-permute-start | bytes 393224 | tf_op jit(solution)/shard_map/ppermute | solution.py:357
  10.4 8.9 %collective-permute-start.4 = (f32[2,48,512]{2,1,0:T(8,128)S(1)}, f32[2,48,512]{2,1,0:T(8,128)S(1)}, u32[]{:S(2)}, u32[]{:S(2)}) collective-permute-start(f32[2,48,512]{2,1,0:T(8,128)S(1)} %get-tuple-element.58), channel_id=1, source_target_pairs={{0,2},{2,4},{4,0},{6,8},{8,10},{10,12},{12,6},{14,16},{16,18},{18,... | collective-permute-start | bytes 589832 | tf_op jit(solution)/shard_map/ppermute | solution.py:360
  10.5 4.1 %collective-permute-start.10 = (f32[2,16,512]{2,1,0:T(8,128)S(1)}, f32[2,16,512]{2,1,0:T(8,128)S(1)}, u32[]{:S(2)}, u32[]{:S(2)}) collective-permute-start(f32[2,16,512]{2,1,0:T(8,128)S(1)} %get-tuple-element.66), channel_id=1, source_target_pairs={{0,2},{2,0},{4,6},{6,4},{8,10},{10,8},{12,14},{14,12},{16,18},{18,... | collective-permute-start | bytes 196616 | tf_op jit(solution)/shard_map/ppermute | solution.py:357
  14.3 1.5 %collective-permute-start.7 = (f32[2,32,512]{2,1,0:T(8,128)S(1)}, f32[2,32,512]{2,1,0:T(8,128)S(1)}, u32[]{:S(2)}, u32[]{:S(2)}) collective-permute-start(f32[2,32,512]{2,1,0:T(8,128)S(1)} %get-tuple-element.63), channel_id=1, source_target_pairs={{0,2},{2,0},{4,6},{6,4},{8,10},{10,8},{12,14},{14,12},{16,18},{18,... | collective-permute-start | bytes 393224 | tf_op jit(solution)/shard_map/ppermute | solution.py:357
  14.5 1.3 %collective-permute-start.8 = (f32[2,16,512]{2,1,0:T(8,128)S(1)}, f32[2,16,512]{2,1,0:T(8,128)S(1)}, u32[]{:S(2)}, u32[]{:S(2)}) collective-permute-start(f32[2,16,512]{2,1,0:T(8,128)S(1)} %get-tuple-element.64), channel_id=1, source_target_pairs={{0,2},{2,0},{4,6},{6,4},{8,10},{10,8},{12,14},{14,12},{16,18},{18,... | collective-permute-start | bytes 196616 | tf_op jit(solution)/shard_map/ppermute | solution.py:357
  14.9 7.3 %collective-permute-start.17 = (f32[2,48,512]{2,1,0:T(8,128)S(1)}, f32[2,48,512]{2,1,0:T(8,128)S(1)}, u32[]{:S(2)}, u32[]{:S(2)}) collective-permute-start(f32[2,48,512]{2,1,0:T(8,128)S(1)} %get-tuple-element.79), channel_id=1, source_target_pairs={{0,2},{2,4},{4,0},{6,8},{8,10},{10,12},{12,6},{14,16},{16,18},{18,... | collective-permute-start | bytes 589832 | tf_op jit(solution)/shard_map/ppermute | solution.py:360
  16.5 4.1 %collective-permute-start.13 = (f32[2,32,512]{2,1,0:T(8,128)S(1)}, f32[2,32,512]{2,1,0:T(8,128)S(1)}, u32[]{:S(2)}, u32[]{:S(2)}) collective-permute-start(f32[2,32,512]{2,1,0:T(8,128)S(1)} %get-tuple-element.73), channel_id=1, source_target_pairs={{0,2},{2,0},{4,6},{6,4},{8,10},{10,8},{12,14},{14,12},{16,18},{18,... | collective-permute-start | bytes 393224 | tf_op jit(solution)/shard_map/ppermute | solution.py:357
  18.1 7.5 %collective-permute-start.16 = (f32[2,48,512]{2,1,0:T(8,128)S(1)}, f32[2,48,512]{2,1,0:T(8,128)S(1)}, u32[]{:S(2)}, u32[]{:S(2)}) collective-permute-start(f32[2,48,512]{2,1,0:T(8,128)S(1)} %get-tuple-element.78), channel_id=1, source_target_pairs={{0,2},{2,4},{4,0},{6,8},{8,10},{10,12},{12,6},{14,16},{16,18},{18,... | collective-permute-start | bytes 589832 | tf_op jit(solution)/shard_map/ppermute | solution.py:360
  18.1 2.1 %collective-permute-start.14 = (f32[2,16,512]{2,1,0:T(8,128)S(1)}, f32[2,16,512]{2,1,0:T(8,128)S(1)}, u32[]{:S(2)}, u32[]{:S(2)}) collective-permute-start(f32[2,16,512]{2,1,0:T(8,128)S(1)} %get-tuple-element.74), channel_id=1, source_target_pairs={{0,2},{2,0},{4,6},{6,4},{8,10},{10,8},{12,14},{14,12},{16,18},{18,... | collective-permute-start | bytes 196616 | tf_op jit(solution)/shard_map/ppermute | solution.py:357
  20.0 1.5 %collective-permute-start.11 = (f32[2,32,512]{2,1,0:T(8,128)S(1)}, f32[2,32,512]{2,1,0:T(8,128)S(1)}, u32[]{:S(2)}, u32[]{:S(2)}) collective-permute-start(f32[2,32,512]{2,1,0:T(8,128)S(1)} %get-tuple-element.71), channel_id=1, source_target_pairs={{0,2},{2,0},{4,6},{6,4},{8,10},{10,8},{12,14},{14,12},{16,18},{18,... | collective-permute-start | bytes 393224 | tf_op jit(solution)/shard_map/ppermute | solution.py:357
  20.2 1.3 %collective-permute-start.12 = (f32[2,16,512]{2,1,0:T(8,128)S(1)}, f32[2,16,512]{2,1,0:T(8,128)S(1)}, u32[]{:S(2)}, u32[]{:S(2)}) collective-permute-start(f32[2,16,512]{2,1,0:T(8,128)S(1)} %get-tuple-element.72), channel_id=1, source_target_pairs={{0,2},{2,0},{4,6},{6,4},{8,10},{10,8},{12,14},{14,12},{16,18},{18,... | collective-permute-start | bytes 196616 | tf_op jit(solution)/shard_map/ppermute | solution.py:357
  20.6 6.3 %collective-permute-start.20 = (f32[2,48,512]{2,1,0:T(8,128)S(1)}, f32[2,48,512]{2,1,0:T(8,128)S(1)}, u32[]{:S(2)}, u32[]{:S(2)}) collective-permute-start(f32[2,48,512]{2,1,0:T(8,128)S(1)} %get-tuple-element.84), channel_id=1, source_target_pairs={{0,2},{2,4},{4,0},{6,8},{8,10},{10,12},{12,6},{14,16},{16,18},{18,... | collective-permute-start | bytes 589832 | tf_op jit(solution)/shard_map/ppermute | solution.py:360
  21.5 6.3 %collective-permute-start.15 = (f32[2,48,512]{2,1,0:T(8,128)S(1)}, f32[2,48,512]{2,1,0:T(8,128)S(1)}, u32[]{:S(2)}, u32[]{:S(2)}) collective-permute-start(f32[2,48,512]{2,1,0:T(8,128)S(1)} %get-tuple-element.77), channel_id=1, source_target_pairs={{2,4},{6,8},{10,12},{14,16},{18,20},{22,24},{26,28},{3,5},{7,9},{1... | collective-permute-start | bytes 589832 | tf_op jit(solution)/shard_map/ppermute | solution.py:360
  22.9 3.5 %collective-permute-start.22 = (f32[2,16,512]{2,1,0:T(8,128)S(1)}, f32[2,16,512]{2,1,0:T(8,128)S(1)}, u32[]{:S(2)}, u32[]{:S(2)}) collective-permute-start(f32[2,16,512]{2,1,0:T(8,128)S(1)} %get-tuple-element.86), channel_id=1, source_target_pairs={{0,2},{2,0},{4,6},{6,4},{8,10},{10,8},{12,14},{14,12},{16,18},{18,... | collective-permute-start | bytes 196616 | tf_op jit(solution)/shard_map/ppermute | solution.py:357
  25.5 1.4 %collective-permute-start.21 = (f32[2,32,512]{2,1,0:T(8,128)S(1)}, f32[2,32,512]{2,1,0:T(8,128)S(1)}, u32[]{:S(2)}, u32[]{:S(2)}) collective-permute-start(f32[2,32,512]{2,1,0:T(8,128)S(1)} %get-tuple-element.85), channel_id=1, source_target_pairs={{0,2},{2,0},{4,6},{6,4},{8,10},{10,8},{12,14},{14,12},{16,18},{18,... | collective-permute-start | bytes 393224 | tf_op jit(solution)/shard_map/ppermute | solution.py:357
  26.3 1.5 %collective-permute-start.18 = (f32[2,32,512]{2,1,0:T(8,128)S(1)}, f32[2,32,512]{2,1,0:T(8,128)S(1)}, u32[]{:S(2)}, u32[]{:S(2)}) collective-permute-start(f32[2,32,512]{2,1,0:T(8,128)S(1)} %get-tuple-element.82), channel_id=1, source_target_pairs={{0,2},{2,0},{4,6},{6,4},{8,10},{10,8},{12,14},{14,12},{16,18},{18,... | collective-permute-start | bytes 393224 | tf_op jit(solution)/shard_map/ppermute | solution.py:357
  26.4 1.4 %collective-permute-start.19 = (f32[2,16,512]{2,1,0:T(8,128)S(1)}, f32[2,16,512]{2,1,0:T(8,128)S(1)}, u32[]{:S(2)}, u32[]{:S(2)}) collective-permute-start(f32[2,16,512]{2,1,0:T(8,128)S(1)} %get-tuple-element.83), channel_id=1, source_target_pairs={{0,2},{2,0},{4,6},{6,4},{8,10},{10,8},{12,14},{14,12},{16,18},{18,... | collective-permute-start | bytes 196616 | tf_op jit(solution)/shard_map/ppermute | solution.py:357
  27.9 3.6 %collective-permute-start.23 = (f32[1,256]{1,0:T(1,128)S(1)}, f32[1,256]{1,0:T(1,128)S(1)}, u32[]{:S(2)}, u32[]{:S(2)}) collective-permute-start(f32[1,256]{1,0:T(1,128)S(1)} %get-tuple-element.91), channel_id=1, source_target_pairs={{0,1},{1,0},{2,3},{3,2},{4,5},{5,4},{6,7},{7,6},{8,9},{9,8},{10,11... | collective-permute-start | bytes 3080 | tf_op jit(solution)/shard_map/ppermute | solution.py:389

commit v9 on v7

--- a/solution.py
+++ b/solution.py
@@ -344,13 +344,14 @@
     shots = arriving_downward_matrices.shape[3]
     mate_route = [(level, level ^ 1) for level in range(levels)]
     down_route = cross_route(levels)
+    open_route = [(level, level + 1) for level in range(1, levels - 1, 2)]
     shared = (ascending_residual, impedance_contrast, shot_node_indices, emitted_pulse[0].T)
 
     def mate(pieces):
         return [lax.ppermute(piece, "depth", mate_route) for piece in pieces]
 
-    def down(piece):
-        return lax.ppermute(piece, "depth", down_route)
+    def down(piece, closed=True):
+        return lax.ppermute(piece, "depth", down_route if closed else open_route)
 
     rows = shots // HALVES
     start = (extrapolation_operator, impedance_contrast, ascending_residual, arriving_downward_matrices)
@@ -362,7 +363,7 @@
 
     def odd_step(tick, half):
         odd, grads[0] = step(tick, half, 1, beside[half], shared, high, low, grads[0], rows)
-        return down(odd)
+        return down(odd, closed=tick < TICKS - 2 or half < HALVES - 1)
 
     def even_step(tick, half):
         *even, grads[0] = step(tick, half, 0, (above[half],), shared, high, low, grads[0], rows)

time: 31.2 us -> 30.4 us (0.974)
  starting transfers between devices: 16.1 us -> 14.7 us
  waiting for transfers between devices: 4.63 us -> 5.2 us
    ppermute x8, starting transfers between devices: 9.31 us -> 7.98 us  [down(): return lax.ppermute(piece, 'depth', down_route if closed else open_route)]
    ppermute x8, waiting for transfers between devices: 2.09 us -> 2.66 us  [down(): return lax.ppermute(piece, 'depth', down_route if closed else open_route)]
  transfers between devices with their start and end apart: 25 -> 25, of which waited for: 8 -> 7; matrix products, arithmetic and copies ran while one was open for 0% -> 0% of each run, Pallas kernels for 28% -> 29%
where the time goes in v9:
time: 30.4 us; the launch traced here: 30.3 us
  starting transfers between devices  14.7 us (48%)
  Pallas kernels  8.94 us (29%)
  waiting for transfers between devices  5.2 us (17%)
  between operations  0.82 us (3%)
  other arithmetic  0.56 us (2%)
    ppermute x8, starting transfers between devices, down(): return lax.ppermute(piece, 'depth', down_route if closed else open_route)  7.98 us
    ppermute x16, starting transfers between devices, mate(): return [lax.ppermute(piece, 'depth', mate_route) for piece in pieces]  4.36 us
    pallas_call x12, Pallas kernels, step(): pl.pallas_call(functools.partial(step_kernel, tick, half, parity), out_sh...  4.04 us
    pallas_call x2, Pallas kernels, first(): pl.pallas_call(functools.partial(first_kernel, parity, bool(carried)), ou...  2.71 us
    ppermute x8, waiting for transfers between devices, down(): return lax.ppermute(piece, 'depth', down_route if closed else open_route)  2.66 us
    ppermute x1, starting transfers between devices, local(): gradient = gradient + lax.ppermute(chunks[distance], 'freq', route)  2.39 us
    ppermute x16, waiting for transfers between devices, mate(): return [lax.ppermute(piece, 'depth', mate_route) for piece in pieces]  2.37 us
    pallas_call x2, Pallas kernels, last(): pl.pallas_call(functools.partial(last_kernel, half), out_shape=out_shape,...  2.05 us
  transfers between devices with their start and end apart: 25, of which 7 were waited for; matrix products, arithmetic and copies ran while one was open for 0% of the time, Pallas kernels for 29%

profile of v9, /device:TPU:0, one launch (start us, length us, event | category | flops | bytes accessed | tf_op | source)
XLA Modules:
  0.0 30.3 jit_solution(7603690338122322071)
XLA Ops:
  0.6 0.1 first_1.1
  0.7 2.9 %collective-permute-start.7 = (f32[2,48,512]{2,1,0:T(8,128)S(1)}, f32[2,48,512]{2,1,0:T(8,128)S(1)}, u32[]{:S(2)}, u32[]{:S(2)}) collective-permute-start(f32[2,48,512]{2,1,0:T(8,128)S(1)} %get-tuple-element.62), channel_id=1, source_target_pairs={{0,2},{2,4},{4,0},{6,8},{8,10},{10,12},{12,6},{14,16},{16,18},{18,... | collective-permute-start | bytes 589832 | tf_op jit(solution)/shard_map/ppermute | solution.py:354
  3.6 0.2 collective-permute-start.6
  3.9 2.6 %first_0.1 = (f32[2,32,512]{2,1,0:T(8,128)S(1)}, f32[2,16,512]{2,1,0:T(8,128)S(1)}, f32[2,32,512]{2,1,0:T(8,128)S(1)}, f32[2,16,512]{2,1,0:T(8,128)S(1)}, bf16[2...) custom-call(f32[1,1,2,512,512]{4,3,2,1,0:T(8,128)} %refs_0_.5, ...), custom_call_target="tpu_custom_call", output_to_operand_aliasing={{4}: (4, {}), {5}: (5, {}), {6}: (6, {})} | custom-call | flops 30000000 | bytes 1 | tf_op jit(solution)/shard_map/first_0/pallas_call | solution.py:170
  6.5 0.1 collective-permute-start.2
  6.6 0.5 %collective-permute-start.3 = (f32[2,16,512]{2,1,0:T(8,128)S(1)}, f32[2,16,512]{2,1,0:T(8,128)S(1)}, u32[]{:S(2)}, u32[]{:S(2)}) collective-permute-start(f32[2,16,512]{2,1,0:T(8,128)S(1)} %get-tuple-element.56), channel_id=1, source_target_pairs={{0,2},{2,0},{4,6},{6,4},{8,10},{10,8},{12,14},{14,12},{16,18},{18,... | collective-permute-start | bytes 196616 | tf_op jit(solution)/shard_map/ppermute | solution.py:351
  7.1 0.1 collective-permute-start
  7.2 0.9 %collective-permute-done.3.refs_1_ = f32[2,16,512]{2,1,0:T(8,128)S(1)} collective-permute-done((f32[2,16,512]{2,1,0:T(8,128)S(1)}, f32[2,16,512]{2,1,0:T(8,128)S(1)}, u32[]{:S(2)}, u32[]{:S(2)}) %collective-permute-start.3) | collective-permute-done | bytes 65568 | tf_op jit(solution)/shard_map/ppermute | solution.py:351
  8.0 0.3 %collective-permute-start.1 = (f32[2,16,512]{2,1,0:T(8,128)S(1)}, f32[2,16,512]{2,1,0:T(8,128)S(1)}, u32[]{:S(2)}, u32[]{:S(2)}) collective-permute-start(f32[2,16,512]{2,1,0:T(8,128)S(1)} %get-tuple-element.52), channel_id=1, source_target_pairs={{0,2},{2,0},{4,6},{6,4},{8,10},{10,8},{12,14},{14,12},{16,18},{18,... | collective-permute-start | bytes 196616 | tf_op jit(solution)/shard_map/ppermute | solution.py:351
  8.3 0.0 collective-permute-done.2.refs_0_
  8.3 0.0 copy-done
  8.3 0.0 copy-done.1
  8.4 0.8 %collective-permute-start.5 = (f32[2,48,512]{2,1,0:T(8,128)S(1)}, f32[2,48,512]{2,1,0:T(8,128)S(1)}, u32[]{:S(2)}, u32[]{:S(2)}) collective-permute-start(f32[2,48,512]{2,1,0:T(8,128)S(1)} %get-tuple-element.60), channel_id=1, source_target_pairs={{0,2},{2,4},{4,0},{6,8},{8,10},{10,12},{12,6},{14,16},{16,18},{18,... | collective-permute-start | bytes 589832 | tf_op jit(solution)/shard_map/ppermute | solution.py:354
  9.2 0.1 collective-permute-done.1.refs_1_
  9.3 0.0 collective-permute-done.refs_0_
  9.3 1.7 %collective-permute-start.4 = (f32[2,48,512]{2,1,0:T(8,128)S(1)}, f32[2,48,512]{2,1,0:T(8,128)S(1)}, u32[]{:S(2)}, u32[]{:S(2)}) collective-permute-start(f32[2,48,512]{2,1,0:T(8,128)S(1)} %get-tuple-element.59), channel_id=1, source_target_pairs={{0,2},{2,4},{4,0},{6,8},{8,10},{10,12},{12,6},{14,16},{16,18},{18,... | collective-permute-start | bytes 589832 | tf_op jit(solution)/shard_map/ppermute | solution.py:354
  11.0 0.0 collective-permute-done.7.refs_0_
  11.0 0.7 %step_1_0_0.1 = (f32[2,32,512]{2,1,0:T(8,128)S(1)}, f32[2,16,512]{2,1,0:T(8,128)S(1)}, f32[8,512]{1,0:T(8,128)S(1)}) custom-call(f32[2,48,512]{2,1,0:T(8,128)S(1)} %collective-permute-done.7.refs_0_, f32[1,1,5,2,96,512]{5,4,3,2,1,0:T(8,128)S(1)} %copy-done, f32[1,512]{1,0:T(1,128)S(1)} %copy-done.1, ...), custom_call_target="tpu_custom_call", output_to_operand_aliasing={{2}: (7, {})} | custom-call | flops 1000000 | bytes 1 | tf_op jit(solution)/shard_map/step_1_0_0/pallas_call | solution.py:236
  11.6 0.1 collective-permute-start.11
  11.7 0.5 %collective-permute-start.10 = (f32[2,32,512]{2,1,0:T(8,128)S(1)}, f32[2,32,512]{2,1,0:T(8,128)S(1)}, u32[]{:S(2)}, u32[]{:S(2)}) collective-permute-start(f32[2,32,512]{2,1,0:T(8,128)S(1)} %get-tuple-element.67), channel_id=1, source_target_pairs={{0,2},{2,0},{4,6},{6,4},{8,10},{10,8},{12,14},{14,12},{16,18},{18,... | collective-permute-start | bytes 393224 | tf_op jit(solution)/shard_map/ppermute | solution.py:351
  12.2 0.0 collective-permute-done.6.refs_0_
  12.2 0.7 %step_1_1_0.1 = (f32[2,32,512]{2,1,0:T(8,128)S(1)}, f32[2,16,512]{2,1,0:T(8,128)S(1)}, f32[8,512]{1,0:T(8,128)S(1)}) custom-call(f32[2,48,512]{2,1,0:T(8,128)S(1)} %collective-permute-done.6.refs_0_, f32[1,1,5,2,96,512]{5,4,3,2,1,0:T(8,128)S(1)} %copy-done, f32[1,512]{1,0:T(1,128)S(1)} %copy-done.1, ...), custom_call_target="tpu_custom_call", output_to_operand_aliasing={{2}: (7, {})} | custom-call | flops 1000000 | bytes 1 | tf_op jit(solution)/shard_map/step_1_1_0/pallas_call | solution.py:236
  12.9 0.1 collective-permute-start.8
  13.0 0.0 collective-permute-done.11.refs_1_
  13.0 0.5 %collective-permute-start.9 = (f32[2,16,512]{2,1,0:T(8,128)S(1)}, f32[2,16,512]{2,1,0:T(8,128)S(1)}, u32[]{:S(2)}, u32[]{:S(2)}) collective-permute-start(f32[2,16,512]{2,1,0:T(8,128)S(1)} %get-tuple-element.66), channel_id=1, source_target_pairs={{0,2},{2,0},{4,6},{6,4},{8,10},{10,8},{12,14},{14,12},{16,18},{18,... | collective-permute-start | bytes 196616 | tf_op jit(solution)/shard_map/ppermute | solution.py:351
  13.5 0.0 collective-permute-done.10.refs_0_
  13.5 0.9 %collective-permute-done.9.refs_1_ = f32[2,16,512]{2,1,0:T(8,128)S(1)} collective-permute-done((f32[2,16,512]{2,1,0:T(8,128)S(1)}, f32[2,16,512]{2,1,0:T(8,128)S(1)}, u32[]{:S(2)}, u32[]{:S(2)}) %collective-permute-start.9) | collective-permute-done | bytes 65568 | tf_op jit(solution)/shard_map/ppermute | solution.py:351
  14.4 0.0 collective-permute-done.8.refs_0_
  14.4 0.9 %collective-permute-start.17 = (f32[2,48,512]{2,1,0:T(8,128)S(1)}, f32[2,48,512]{2,1,0:T(8,128)S(1)}, u32[]{:S(2)}, u32[]{:S(2)}) collective-permute-start(f32[2,48,512]{2,1,0:T(8,128)S(1)} %get-tuple-element.80), channel_id=1, source_target_pairs={{0,2},{2,4},{4,0},{6,8},{8,10},{10,12},{12,6},{14,16},{16,18},{18,... | collective-permute-start | bytes 589832 | tf_op jit(solution)/shard_map/ppermute | solution.py:354
  15.3 0.1 collective-permute-start.18
  15.4 0.0 collective-permute-done.5.refs_0_
  15.4 0.7 %step_2_0_0.1 = (f32[2,32,512]{2,1,0:T(8,128)S(1)}, f32[2,16,512]{2,1,0:T(8,128)S(1)}, f32[8,512]{1,0:T(8,128)S(1)}) custom-call(f32[2,48,512]{2,1,0:T(8,128)S(1)} %collective-permute-done.5.refs_0_, f32[1,1,5,2,96,512]{5,4,3,2,1,0:T(8,128)S(1)} %copy-done, f32[1,512]{1,0:T(1,128)S(1)} %copy-done.1, ...), custom_call_target="tpu_custom_call", output_to_operand_aliasing={{2}: (7, {})} | custom-call | flops 1000000 | bytes 1 | tf_op jit(solution)/shard_map/step_2_0_0/pallas_call | solution.py:236
  16.1 0.5 %collective-permute-start.15 = (f32[2,16,512]{2,1,0:T(8,128)S(1)}, f32[2,16,512]{2,1,0:T(8,128)S(1)}, u32[]{:S(2)}, u32[]{:S(2)}) collective-permute-start(f32[2,16,512]{2,1,0:T(8,128)S(1)} %get-tuple-element.76), channel_id=1, source_target_pairs={{0,2},{2,0},{4,6},{6,4},{8,10},{10,8},{12,14},{14,12},{16,18},{18,... | collective-permute-start | bytes 196616 | tf_op jit(solution)/shard_map/ppermute | solution.py:351
  16.5 0.1 collective-permute-start.14
  16.7 0.0 collective-permute-done.4.refs_0_
  16.7 0.7 %step_2_1_0.1 = (f32[2,32,512]{2,1,0:T(8,128)S(1)}, f32[2,16,512]{2,1,0:T(8,128)S(1)}, f32[8,512]{1,0:T(8,128)S(1)}) custom-call(f32[2,48,512]{2,1,0:T(8,128)S(1)} %collective-permute-done.4.refs_0_, f32[1,1,5,2,96,512]{5,4,3,2,1,0:T(8,128)S(1)} %copy-done, f32[1,512]{1,0:T(1,128)S(1)} %copy-done.1, ...), custom_call_target="tpu_custom_call", output_to_operand_aliasing={{2}: (7, {})} | custom-call | flops 1000000000 | bytes 1 | tf_op jit(solution)/shard_map/step_2_1_0/pallas_call | solution.py:236
  17.3 0.1 collective-permute-start.12
  17.4 0.0 collective-permute-done.15.refs_1_
  17.4 0.5 %collective-permute-start.13 = (f32[2,16,512]{2,1,0:T(8,128)S(1)}, f32[2,16,512]{2,1,0:T(8,128)S(1)}, u32[]{:S(2)}, u32[]{:S(2)}) collective-permute-start(f32[2,16,512]{2,1,0:T(8,128)S(1)} %get-tuple-element.74), channel_id=1, source_target_pairs={{0,2},{2,0},{4,6},{6,4},{8,10},{10,8},{12,14},{14,12},{16,18},{18,... | collective-permute-start | bytes 196616 | tf_op jit(solution)/shard_map/ppermute | solution.py:351
  17.9 0.0 collective-permute-done.14.refs_0_
  17.9 0.7 %collective-permute-start.21 = (f32[2,48,512]{2,1,0:T(8,128)S(1)}, f32[2,48,512]{2,1,0:T(8,128)S(1)}, u32[]{:S(2)}, u32[]{:S(2)}) collective-permute-start(f32[2,48,512]{2,1,0:T(8,128)S(1)} %get-tuple-element.86), channel_id=1, source_target_pairs={{0,2},{2,4},{4,0},{6,8},{8,10},{10,12},{12,6},{14,16},{16,18},{18,... | collective-permute-start | bytes 589832 | tf_op jit(solution)/shard_map/ppermute | solution.py:354
  18.6 0.2 collective-permute-done.13.refs_1_
  18.8 0.0 collective-permute-done.12.refs_0_
  18.9 0.7 %collective-permute-start.16 = (f32[2,48,512]{2,1,0:T(8,128)S(1)}, f32[2,48,512]{2,1,0:T(8,128)S(1)}, u32[]{:S(2)}, u32[]{:S(2)}) collective-permute-start(f32[2,48,512]{2,1,0:T(8,128)S(1)} %get-tuple-element.79), channel_id=1, source_target_pairs={{2,4},{6,8},{10,12},{14,16},{18,20},{22,24},{26,28},{3,5},{7,9},{1... | collective-permute-start | bytes 589832 | tf_op jit(solution)/shard_map/ppermute | solution.py:354
  19.5 2.6 %collective-permute-done.18.refs_0_ = f32[2,48,512]{2,1,0:T(8,128)S(1)} collective-permute-done((f32[2,48,512]{2,1,0:T(8,128)S(1)}, f32[2,48,512]{2,1,0:T(8,128)S(1)}, u32[]{:S(2)}, u32[]{:S(2)}) %collective-permute-start.18) | collective-permute-done | bytes 196640 | tf_op jit(solution)/shard_map/ppermute | solution.py:354
  22.2 0.7 %step_3_0_0.1 = (f32[2,32,512]{2,1,0:T(8,128)S(1)}, f32[2,16,512]{2,1,0:T(8,128)S(1)}, f32[8,512]{1,0:T(8,128)S(1)}) custom-call(f32[2,48,512]{2,1,0:T(8,128)S(1)} %collective-permute-done.18.refs_0_, f32[1,1,5,2,96,512]{5,4,3,2,1,0:T(8,128)S(1)} %copy-done, f32[1,512]{1,0:T(1,128)S(1)} %copy-done.1, ...), custom_call_target="tpu_custom_call", output_to_operand_aliasing={{2}: (7, {})} | custom-call | flops 1000000 | bytes 1 | tf_op jit(solution)/shard_map/step_3_0_0/pallas_call | solution.py:236
  22.8 0.2 collective-permute-start.23
  23.1 0.4 %collective-permute-start.22 = (f32[2,32,512]{2,1,0:T(8,128)S(1)}, f32[2,32,512]{2,1,0:T(8,128)S(1)}, u32[]{:S(2)}, u32[]{:S(2)}) collective-permute-start(f32[2,32,512]{2,1,0:T(8,128)S(1)} %get-tuple-element.87), channel_id=1, source_target_pairs={{0,2},{2,0},{4,6},{6,4},{8,10},{10,8},{12,14},{14,12},{16,18},{18,... | collective-permute-start | bytes 393224 | tf_op jit(solution)/shard_map/ppermute | solution.py:351
  23.4 0.0 collective-permute-done.17.refs_0_
  23.4 0.7 %step_3_1_0.1 = (f32[2,32,512]{2,1,0:T(8,128)S(1)}, f32[2,16,512]{2,1,0:T(8,128)S(1)}, f32[8,512]{1,0:T(8,128)S(1)}) custom-call(f32[2,48,512]{2,1,0:T(8,128)S(1)} %collective-permute-done.17.refs_0_, f32[1,1,5,2,96,512]{5,4,3,2,1,0:T(8,128)S(1)} %copy-done, f32[1,512]{1,0:T(1,128)S(1)} %copy-done.1, ...), custom_call_target="tpu_custom_call", output_to_operand_aliasing={{2}: (7, {})} | custom-call | flops 500000000 | bytes 1 | tf_op jit(solution)/shard_map/step_3_1_0/pallas_call | solution.py:236
  24.1 0.1 collective-permute-start.19
  24.2 0.0 collective-permute-done.23.mate_tail
  24.2 0.5 %collective-permute-start.20 = (f32[2,16,512]{2,1,0:T(8,128)S(1)}, f32[2,16,512]{2,1,0:T(8,128)S(1)}, u32[]{:S(2)}, u32[]{:S(2)}) collective-permute-start(f32[2,16,512]{2,1,0:T(8,128)S(1)} %get-tuple-element.85), channel_id=1, source_target_pairs={{0,2},{2,0},{4,6},{6,4},{8,10},{10,8},{12,14},{14,12},{16,18},{18,... | collective-permute-start | bytes 196616 | tf_op jit(solution)/shard_map/ppermute | solution.py:351
  24.7 0.0 collective-permute-done.22.mate
  24.7 0.0 collective-permute-done.21.above
  24.7 0.7 %last_0.1 = (f32[2,48,512]{2,1,0:T(8,128)S(1)}, f32[8,512]{1,0:T(8,128)S(1)}) custom-call(f32[2,48,512]{2,1,0:T(8,128)S(1)} %collective-permute-done.21.above, f32[2,32,512]{2,1,0:T(8,128)S(1)} %collective-permute-done.22.mate, f32[2,16,512]{2,1,0:T(8,128)S(1)} %collective-permute-done.23.mate_tail, ...), custom_call_target="tpu_custom_call", output_to_operand_aliasing={{1}: (9, {})} | custom-call | flops 30000000 | bytes 1 | tf_op jit(solution)/shard_map/last_0/pallas_call | solution.py:311
  25.4 0.2 collective-permute-done.20.mate_tail
  25.6 0.0 collective-permute-done.19.mate
  25.6 0.0 collective-permute-done.16.above
  25.6 0.1 gradient.1
  25.8 2.4 %collective-permute-start.24 = (f32[1,256]{1,0:T(1,128)S(1)}, f32[1,256]{1,0:T(1,128)S(1)}, u32[]{:S(2)}, u32[]{:S(2)}) collective-permute-start(f32[1,256]{1,0:T(1,128)S(1)} %get-tuple-element.93), channel_id=1, source_target_pairs={{0,1},{1,0},{2,3},{3,2},{4,5},{5,4},{6,7},{7,6},{8,9},{9,8},{10,11... | collective-permute-start | bytes 3080 | tf_op jit(solution)/shard_map/ppermute | solution.py:383
  28.2 1.4 %last_1.1 = f32[2,96,512]{2,1,0:T(8,128)} custom-call(f32[2,48,512]{2,1,0:T(8,128)S(1)} %collective-permute-done.16.above, f32[2,32,512]{2,1,0:T(8,128)S(1)} %collective-permute-done.19.mate, f32[2,16,512]{2,1,0:T(8,128)S(1)} %collective-permute-done.20.mate_tail, f32[1,1,5,2,96,512]{5,4,3,2,1,0:T(8,128)S(1)} %copy-done, f32[1,512]{1,0:T(1,128)S(1)} %copy-done.1, ...), custom_call_target="tpu_custom_call" | custom-call | flops 1 | bytes 1 | tf_op jit(solution)/shard_map/last_1/pallas_call | solution.py:311
  29.5 0.2 collective-permute-done.24
  29.7 0.6 %add.3 = f32[1,256]{1,0:T(1,128)} add(f32[1,256]{1,0:T(1,128)S(1)} %get-tuple-element.92, f32[1,256]{1,0:T(1,128)S(1)} %collective-permute-done.24) | non-fusion elementwise | flops 256 | bytes 3072 | tf_op jit(solution)/shard_map/add | solution.py:383
  (12 shorter events, 0.0 us)
Async XLA Ops:
  0.7 10.3 %collective-permute-start.7 = (f32[2,48,512]{2,1,0:T(8,128)S(1)}, f32[2,48,512]{2,1,0:T(8,128)S(1)}, u32[]{:S(2)}, u32[]{:S(2)}) collective-permute-start(f32[2,48,512]{2,1,0:T(8,128)S(1)} %get-tuple-element.62), channel_id=1, source_target_pairs={{0,2},{2,4},{4,0},{6,8},{8,10},{10,12},{12,6},{14,16},{16,18},{18,... | collective-permute-start | bytes 589832 | tf_op jit(solution)/shard_map/ppermute | solution.py:354
  3.6 8.6 %collective-permute-start.6 = (f32[2,48,512]{2,1,0:T(8,128)S(1)}, f32[2,48,512]{2,1,0:T(8,128)S(1)}, u32[]{:S(2)}, u32[]{:S(2)}) collective-permute-start(f32[2,48,512]{2,1,0:T(8,128)S(1)} %get-tuple-element.61), channel_id=1, source_target_pairs={{0,2},{2,4},{4,0},{6,8},{8,10},{10,12},{12,6},{14,16},{16,18},{18,... | collective-permute-start | bytes 589832 | tf_op jit(solution)/shard_map/ppermute | solution.py:354
  3.9 4.5 %copy-start = (f32[1,1,5,2,96,512]{5,4,3,2,1,0:T(8,128)S(1)}, f32[1,1,5,2,96,512]{5,4,3,2,1,0:T(8,128)}, u32[]{:S(2)}) copy-start(f32[1,1,5,2,96,512]{5,4,3,2,1,0:T(8,128)} %residual.1) | copy-start | bytes 5898244
  3.9 4.5 %copy-start.1 = (f32[1,512]{1,0:T(1,128)S(1)}, f32[1,512]{1,0:T(1,128)}, u32[]{:S(2)}) copy-start(f32[1,512]{1,0:T(1,128)} %contrast.1) | copy-start | bytes 6148
  3.9 4.5 %copy-start.2 = (s32[4,96]{1,0:T(4,128)S(1)}, s32[4,96]{1,0:T(4,128)}, u32[]{:S(2)}) copy-start(s32[4,96]{1,0:T(4,128)} %sites.1) | copy-start | bytes 4612
  3.9 4.5 %copy-start.3 = (f32[1,4,2]{1,2,0:T(2,128)S(1)}, f32[1,4,2]{1,2,0:T(2,128)}, u32[]{:S(2)}) copy-start(f32[1,4,2]{1,2,0:T(2,128)} %param.11) | copy-start | bytes 100
  6.5 1.8 %collective-permute-start.2 = (f32[2,32,512]{2,1,0:T(8,128)S(1)}, f32[2,32,512]{2,1,0:T(8,128)S(1)}, u32[]{:S(2)}, u32[]{:S(2)}) collective-permute-start(f32[2,32,512]{2,1,0:T(8,128)S(1)} %get-tuple-element.55), channel_id=1, source_target_pairs={{0,2},{2,0},{4,6},{6,4},{8,10},{10,8},{12,14},{14,12},{16,18},{18,... | collective-permute-start | bytes 393224 | tf_op jit(solution)/shard_map/ppermute | solution.py:351
  6.6 1.4 %collective-permute-start.3 = (f32[2,16,512]{2,1,0:T(8,128)S(1)}, f32[2,16,512]{2,1,0:T(8,128)S(1)}, u32[]{:S(2)}, u32[]{:S(2)}) collective-permute-start(f32[2,16,512]{2,1,0:T(8,128)S(1)} %get-tuple-element.56), channel_id=1, source_target_pairs={{0,2},{2,0},{4,6},{6,4},{8,10},{10,8},{12,14},{14,12},{16,18},{18,... | collective-permute-start | bytes 196616 | tf_op jit(solution)/shard_map/ppermute | solution.py:351
  7.1 2.2 %collective-permute-start = (f32[2,32,512]{2,1,0:T(8,128)S(1)}, f32[2,32,512]{2,1,0:T(8,128)S(1)}, u32[]{:S(2)}, u32[]{:S(2)}) collective-permute-start(f32[2,32,512]{2,1,0:T(8,128)S(1)} %get-tuple-element.51), channel_id=1, source_target_pairs={{0,2},{2,0},{4,6},{6,4},{8,10},{10,8},{12,14},{14,12},{16,18},{18,... | collective-permute-start | bytes 393224 | tf_op jit(solution)/shard_map/ppermute | solution.py:351
  8.0 1.3 %collective-permute-start.1 = (f32[2,16,512]{2,1,0:T(8,128)S(1)}, f32[2,16,512]{2,1,0:T(8,128)S(1)}, u32[]{:S(2)}, u32[]{:S(2)}) collective-permute-start(f32[2,16,512]{2,1,0:T(8,128)S(1)} %get-tuple-element.52), channel_id=1, source_target_pairs={{0,2},{2,0},{4,6},{6,4},{8,10},{10,8},{12,14},{14,12},{16,18},{18,... | collective-permute-start | bytes 196616 | tf_op jit(solution)/shard_map/ppermute | solution.py:351
  8.4 7.0 %collective-permute-start.5 = (f32[2,48,512]{2,1,0:T(8,128)S(1)}, f32[2,48,512]{2,1,0:T(8,128)S(1)}, u32[]{:S(2)}, u32[]{:S(2)}) collective-permute-start(f32[2,48,512]{2,1,0:T(8,128)S(1)} %get-tuple-element.60), channel_id=1, source_target_pairs={{0,2},{2,4},{4,0},{6,8},{8,10},{10,12},{12,6},{14,16},{16,18},{18,... | collective-permute-start | bytes 589832 | tf_op jit(solution)/shard_map/ppermute | solution.py:354
  9.3 7.4 %collective-permute-start.4 = (f32[2,48,512]{2,1,0:T(8,128)S(1)}, f32[2,48,512]{2,1,0:T(8,128)S(1)}, u32[]{:S(2)}, u32[]{:S(2)}) collective-permute-start(f32[2,48,512]{2,1,0:T(8,128)S(1)} %get-tuple-element.59), channel_id=1, source_target_pairs={{0,2},{2,4},{4,0},{6,8},{8,10},{10,12},{12,6},{14,16},{16,18},{18,... | collective-permute-start | bytes 589832 | tf_op jit(solution)/shard_map/ppermute | solution.py:354
  11.6 1.3 %collective-permute-start.11 = (f32[2,16,512]{2,1,0:T(8,128)S(1)}, f32[2,16,512]{2,1,0:T(8,128)S(1)}, u32[]{:S(2)}, u32[]{:S(2)}) collective-permute-start(f32[2,16,512]{2,1,0:T(8,128)S(1)} %get-tuple-element.68), channel_id=1, source_target_pairs={{0,2},{2,0},{4,6},{6,4},{8,10},{10,8},{12,14},{14,12},{16,18},{18,... | collective-permute-start | bytes 196616 | tf_op jit(solution)/shard_map/ppermute | solution.py:351
  11.7 1.7 %collective-permute-start.10 = (f32[2,32,512]{2,1,0:T(8,128)S(1)}, f32[2,32,512]{2,1,0:T(8,128)S(1)}, u32[]{:S(2)}, u32[]{:S(2)}) collective-permute-start(f32[2,32,512]{2,1,0:T(8,128)S(1)} %get-tuple-element.67), channel_id=1, source_target_pairs={{0,2},{2,0},{4,6},{6,4},{8,10},{10,8},{12,14},{14,12},{16,18},{18,... | collective-permute-start | bytes 393224 | tf_op jit(solution)/shard_map/ppermute | solution.py:351
  12.9 1.5 %collective-permute-start.8 = (f32[2,32,512]{2,1,0:T(8,128)S(1)}, f32[2,32,512]{2,1,0:T(8,128)S(1)}, u32[]{:S(2)}, u32[]{:S(2)}) collective-permute-start(f32[2,32,512]{2,1,0:T(8,128)S(1)} %get-tuple-element.65), channel_id=1, source_target_pairs={{0,2},{2,0},{4,6},{6,4},{8,10},{10,8},{12,14},{14,12},{16,18},{18,... | collective-permute-start | bytes 393224 | tf_op jit(solution)/shard_map/ppermute | solution.py:351
  13.0 1.4 %collective-permute-start.9 = (f32[2,16,512]{2,1,0:T(8,128)S(1)}, f32[2,16,512]{2,1,0:T(8,128)S(1)}, u32[]{:S(2)}, u32[]{:S(2)}) collective-permute-start(f32[2,16,512]{2,1,0:T(8,128)S(1)} %get-tuple-element.66), channel_id=1, source_target_pairs={{0,2},{2,0},{4,6},{6,4},{8,10},{10,8},{12,14},{14,12},{16,18},{18,... | collective-permute-start | bytes 196616 | tf_op jit(solution)/shard_map/ppermute | solution.py:351
  14.4 9.0 %collective-permute-start.17 = (f32[2,48,512]{2,1,0:T(8,128)S(1)}, f32[2,48,512]{2,1,0:T(8,128)S(1)}, u32[]{:S(2)}, u32[]{:S(2)}) collective-permute-start(f32[2,48,512]{2,1,0:T(8,128)S(1)} %get-tuple-element.80), channel_id=1, source_target_pairs={{0,2},{2,4},{4,0},{6,8},{8,10},{10,12},{12,6},{14,16},{16,18},{18,... | collective-permute-start | bytes 589832 | tf_op jit(solution)/shard_map/ppermute | solution.py:354
  15.3 6.9 %collective-permute-start.18 = (f32[2,48,512]{2,1,0:T(8,128)S(1)}, f32[2,48,512]{2,1,0:T(8,128)S(1)}, u32[]{:S(2)}, u32[]{:S(2)}) collective-permute-start(f32[2,48,512]{2,1,0:T(8,128)S(1)} %get-tuple-element.81), channel_id=1, source_target_pairs={{0,2},{2,4},{4,0},{6,8},{8,10},{10,12},{12,6},{14,16},{16,18},{18,... | collective-permute-start | bytes 589832 | tf_op jit(solution)/shard_map/ppermute | solution.py:354
  16.1 1.4 %collective-permute-start.15 = (f32[2,16,512]{2,1,0:T(8,128)S(1)}, f32[2,16,512]{2,1,0:T(8,128)S(1)}, u32[]{:S(2)}, u32[]{:S(2)}) collective-permute-start(f32[2,16,512]{2,1,0:T(8,128)S(1)} %get-tuple-element.76), channel_id=1, source_target_pairs={{0,2},{2,0},{4,6},{6,4},{8,10},{10,8},{12,14},{14,12},{16,18},{18,... | collective-permute-start | bytes 196616 | tf_op jit(solution)/shard_map/ppermute | solution.py:351
  16.5 1.4 %collective-permute-start.14 = (f32[2,32,512]{2,1,0:T(8,128)S(1)}, f32[2,32,512]{2,1,0:T(8,128)S(1)}, u32[]{:S(2)}, u32[]{:S(2)}) collective-permute-start(f32[2,32,512]{2,1,0:T(8,128)S(1)} %get-tuple-element.75), channel_id=1, source_target_pairs={{0,2},{2,0},{4,6},{6,4},{8,10},{10,8},{12,14},{14,12},{16,18},{18,... | collective-permute-start | bytes 393224 | tf_op jit(solution)/shard_map/ppermute | solution.py:351
  17.3 1.5 %collective-permute-start.12 = (f32[2,32,512]{2,1,0:T(8,128)S(1)}, f32[2,32,512]{2,1,0:T(8,128)S(1)}, u32[]{:S(2)}, u32[]{:S(2)}) collective-permute-start(f32[2,32,512]{2,1,0:T(8,128)S(1)} %get-tuple-element.73), channel_id=1, source_target_pairs={{0,2},{2,0},{4,6},{6,4},{8,10},{10,8},{12,14},{14,12},{16,18},{18,... | collective-permute-start | bytes 393224 | tf_op jit(solution)/shard_map/ppermute | solution.py:351
  17.4 1.4 %collective-permute-start.13 = (f32[2,16,512]{2,1,0:T(8,128)S(1)}, f32[2,16,512]{2,1,0:T(8,128)S(1)}, u32[]{:S(2)}, u32[]{:S(2)}) collective-permute-start(f32[2,16,512]{2,1,0:T(8,128)S(1)} %get-tuple-element.74), channel_id=1, source_target_pairs={{0,2},{2,0},{4,6},{6,4},{8,10},{10,8},{12,14},{14,12},{16,18},{18,... | collective-permute-start | bytes 196616 | tf_op jit(solution)/shard_map/ppermute | solution.py:351
  17.9 6.8 %collective-permute-start.21 = (f32[2,48,512]{2,1,0:T(8,128)S(1)}, f32[2,48,512]{2,1,0:T(8,128)S(1)}, u32[]{:S(2)}, u32[]{:S(2)}) collective-permute-start(f32[2,48,512]{2,1,0:T(8,128)S(1)} %get-tuple-element.86), channel_id=1, source_target_pairs={{0,2},{2,4},{4,0},{6,8},{8,10},{10,12},{12,6},{14,16},{16,18},{18,... | collective-permute-start | bytes 589832 | tf_op jit(solution)/shard_map/ppermute | solution.py:354
  18.9 6.8 %collective-permute-start.16 = (f32[2,48,512]{2,1,0:T(8,128)S(1)}, f32[2,48,512]{2,1,0:T(8,128)S(1)}, u32[]{:S(2)}, u32[]{:S(2)}) collective-permute-start(f32[2,48,512]{2,1,0:T(8,128)S(1)} %get-tuple-element.79), channel_id=1, source_target_pairs={{2,4},{6,8},{10,12},{14,16},{18,20},{22,24},{26,28},{3,5},{7,9},{1... | collective-permute-start | bytes 589832 | tf_op jit(solution)/shard_map/ppermute | solution.py:354
  22.8 1.3 %collective-permute-start.23 = (f32[2,16,512]{2,1,0:T(8,128)S(1)}, f32[2,16,512]{2,1,0:T(8,128)S(1)}, u32[]{:S(2)}, u32[]{:S(2)}) collective-permute-start(f32[2,16,512]{2,1,0:T(8,128)S(1)} %get-tuple-element.88), channel_id=1, source_target_pairs={{0,2},{2,0},{4,6},{6,4},{8,10},{10,8},{12,14},{14,12},{16,18},{18,... | collective-permute-start | bytes 196616 | tf_op jit(solution)/shard_map/ppermute | solution.py:351
  23.1 1.6 %collective-permute-start.22 = (f32[2,32,512]{2,1,0:T(8,128)S(1)}, f32[2,32,512]{2,1,0:T(8,128)S(1)}, u32[]{:S(2)}, u32[]{:S(2)}) collective-permute-start(f32[2,32,512]{2,1,0:T(8,128)S(1)} %get-tuple-element.87), channel_id=1, source_target_pairs={{0,2},{2,0},{4,6},{6,4},{8,10},{10,8},{12,14},{14,12},{16,18},{18,... | collective-permute-start | bytes 393224 | tf_op jit(solution)/shard_map/ppermute | solution.py:351
  24.1 1.5 %collective-permute-start.19 = (f32[2,32,512]{2,1,0:T(8,128)S(1)}, f32[2,32,512]{2,1,0:T(8,128)S(1)}, u32[]{:S(2)}, u32[]{:S(2)}) collective-permute-start(f32[2,32,512]{2,1,0:T(8,128)S(1)} %get-tuple-element.84), channel_id=1, source_target_pairs={{0,2},{2,0},{4,6},{6,4},{8,10},{10,8},{12,14},{14,12},{16,18},{18,... | collective-permute-start | bytes 393224 | tf_op jit(solution)/shard_map/ppermute | solution.py:351
  24.2 1.4 %collective-permute-start.20 = (f32[2,16,512]{2,1,0:T(8,128)S(1)}, f32[2,16,512]{2,1,0:T(8,128)S(1)}, u32[]{:S(2)}, u32[]{:S(2)}) collective-permute-start(f32[2,16,512]{2,1,0:T(8,128)S(1)} %get-tuple-element.85), channel_id=1, source_target_pairs={{0,2},{2,0},{4,6},{6,4},{8,10},{10,8},{12,14},{14,12},{16,18},{18,... | collective-permute-start | bytes 196616 | tf_op jit(solution)/shard_map/ppermute | solution.py:351
  25.8 3.9 %collective-permute-start.24 = (f32[1,256]{1,0:T(1,128)S(1)}, f32[1,256]{1,0:T(1,128)S(1)}, u32[]{:S(2)}, u32[]{:S(2)}) collective-permute-start(f32[1,256]{1,0:T(1,128)S(1)} %get-tuple-element.93), channel_id=1, source_target_pairs={{0,1},{1,0},{2,3},{3,2},{4,5},{5,4},{6,7},{7,6},{8,9},{9,8},{10,11... | collective-permute-start | bytes 3080 | tf_op jit(solution)/shard_map/ppermute | solution.py:383

commit v10 on v9

--- a/solution.py
+++ b/solution.py
@@ -13,19 +13,21 @@
 TAIL = 16
 VMEM_LIMIT = 24 * 1024 * 1024
 WEIGHTS = {
-    "first_0": 30000000,
-    "first_1": 30000000,
+    "first_0": 500000000,
+    "first_1": 1000000000,
     "step_1_0_0": 1000000,
-    "step_1_1_0": 1000000,
-    "step_2_0_0": 1000000,
-    "step_2_1_0": 1000000000,
-    "step_2_1_1": 500000000,
-    "step_3_0_0": 1000000,
-    "step_3_0_1": 500000000,
-    "step_3_1_0": 500000000,
-    "step_3_1_1": 1000000,
-    "last_0": 30000000,
-    "gradient": 100000000,
+    "step_1_0_1": 1000000000,
+    "step_1_1_0": 1000000000,
+    "step_1_1_1": 30000000,
+    "step_2_0_0": 10000000,
+    "step_2_0_1": 1000000,
+    "step_2_1_0": 30000000,
+    "step_2_1_1": 30000000,
+    "step_3_0_0": 10000000,
+    "step_3_0_1": 30000000,
+    "step_3_1_0": 200000000,
+    "last_0": 100000000,
+    "gradient": 200000000,
 }
 PARAMS = pltpu.CompilerParams(vmem_limit_bytes=VMEM_LIMIT)
 IN_VMEM = pl.BlockSpec(memory_space=pltpu.VMEM)
@@ -187,62 +189,67 @@
     )(kept(operator), kept(contrast), kept(residual), kept(panel), *[pinned(value) for value in carried])
 
 
-def arrive(tick, half, parity, panel, shared, grad_in, grad, left):
+def arrive(tick, start, parity, pieces, shared, grad_in, grad, left):
     residual, contrast, sites, pulse = shared
-    rows = sum(piece.shape[1] for piece in panel)
-    start = half * rows
     waves = residual.at[0, 0, tick]
-    rest = (start, waves, contrast, grad_in, grad, left)
+
+    def take_pieces():
+        offset = 0
+        for piece in pieces:
+            take(piece, start, waves, contrast, grad if offset else grad_in, grad, left, offset)
+            offset += piece.shape[1]
+
     if parity:
-        take(panel[0], *rest)
-        take(panel[1], start, waves, contrast, grad, grad, left, panel[0].shape[1])
+        take_pieces()
         return
     surface = lax.axis_index("depth") == 0
+    shape = sum(piece.shape[1] for piece in pieces), pieces[0].shape[2]
 
     @pl.when(surface)
     def _():
-        take(injected(tick, start, sites, pulse, panel[0].shape[1:]), *rest)
-
-    @pl.when(jnp.logical_not(surface))
-    def _():
-        take(panel[0], *rest)
+        take(injected(tick, start, sites, pulse, shape), start, waves, contrast, grad_in, grad, left)
+
+    pl.when(jnp.logical_not(surface))(take_pieces)
 
 
 def arrive_either(half, above, mate, shared, grad_in, grad, left):
+    start = half * above.shape[1]
+
     @when_parity(1)
     def _():
-        arrive(TICKS - 1, half, 1, mate, shared, grad_in, grad, left)
+        arrive(TICKS - 1, start, 1, mate, shared, grad_in, grad, left)
 
     @when_parity(0)
     def _():
-        arrive(TICKS - 1, half, 0, (above,), shared, grad_in, grad, left)
-
-
-def step_kernel(tick, half, parity, *refs):
-    panel, refs = refs[: 1 + parity], refs[1 + parity :]
+        arrive(TICKS - 1, start, 0, (above,), shared, grad_in, grad, left)
+
+
+def step_kernel(tick, start, parity, count, *refs):
+    pieces, refs = refs[:count], refs[count:]
     shared, (high, low, grad_in) = refs[:4], refs[4:7]
     *out, grad, left = refs[7:]
 
     @when_parity(parity)
     def _():
-        arrive(tick, half, parity, panel, shared, grad_in, grad, left)
+        arrive(tick, start, parity, pieces, shared, grad_in, grad, left)
         store(out, multiply(left, high, low, slice(None)))
 
 
-def step(tick, half, parity, panel, shared, high, low, grad, rows):
+def step(tick, start, parity, pieces, shared, high, low, grad, half):
     breadth = grad.shape[1]
-    outs = piece_shapes(parity, rows, breadth)
-    operands = [pinned(value) for value in (*panel, *shared, high, low, grad)]
+    rows = sum(piece.shape[1] for piece in pieces)
+    outs = piece_shapes(1, rows, breadth) if parity else piece_shapes(0, half, breadth) * (rows // half)
+    operands = [pinned(value) for value in (*pieces, *shared, high, low, grad)]
     return pl.pallas_call(
-        functools.partial(step_kernel, tick, half, parity),
+        functools.partial(step_kernel, tick, start, parity, len(pieces)),
         out_shape=(*outs, pltpu.VMEM(grad.shape, jnp.float32)),
         in_specs=[IN_VMEM] * len(operands),
         out_specs=(IN_VMEM,) * (len(outs) + 1),
         scratch_shapes=[pltpu.VMEM((4 * rows, breadth), jnp.bfloat16)],
         input_output_aliases={len(operands) - 1: len(outs)},
         compiler_params=PARAMS,
-        cost_estimate=cost(f"step_{tick}_{half}_{parity}"),
-        name=f"step_{tick}_{half}_{parity}",
+        cost_estimate=cost(f"step_{tick}_{start // half}_{parity}"),
+        name=f"step_{tick}_{start // half}_{parity}",
     )(*operands)
 
 
@@ -361,17 +368,24 @@
     beside = [mate(even[2 * half : 2 * half + 2]) for half in range(HALVES)]
     grads = [grad]
 
-    def odd_step(tick, half):
-        odd, grads[0] = step(tick, half, 1, beside[half], shared, high, low, grads[0], rows)
-        return down(odd, closed=tick < TICKS - 2 or half < HALVES - 1)
-
-    def even_step(tick, half):
-        *even, grads[0] = step(tick, half, 0, (above[half],), shared, high, low, grads[0], rows)
+    def odd_step(tick, start, pieces, closed=True):
+        odd, grads[0] = step(tick, start, 1, pieces, shared, high, low, grads[0], rows)
+        return down(odd, closed)
+
+    def even_step(tick, start, pieces):
+        *even, grads[0] = step(tick, start, 0, pieces, shared, high, low, grads[0], rows)
         return mate(even)
 
-    for tick in range(1, TICKS - 1):
-        later = [odd_step(tick, half) for half in range(HALVES)]
-        beside[:] = [even_step(tick, half) for half in range(HALVES)]
+    later, latest = [], []
+    for half in range(HALVES):
+        later.append(odd_step(1, half * rows, beside[half]))
+        latest.append(even_step(1, half * rows, [above[half]]))
+    above, beside = later, latest
+    for tick in range(2, TICKS - 1):
+        later = [
+            odd_step(tick, half * rows, beside[half], tick < TICKS - 2 or half < HALVES - 1) for half in range(HALVES)
+        ]
+        beside = [even_step(tick, half * rows, [above[half]]) for half in range(HALVES)]
         above = later
 
     scale = 1.0 / math.sqrt(shots * TICKS)

time: 30.4 us -> 31.1 us (1.023)
  the two profiles are of different devices: /device:TPU:0 before, /device:TPU:10 now
where the time goes in v10:
time: 31.1 us; the launch traced here: 30.9 us
  starting transfers between devices  12.4 us (40%)
  waiting for transfers between devices  8.97 us (29%)
  Pallas kernels  8.13 us (26%)
  between operations  0.88 us (3%)
  other arithmetic  0.56 us (2%)
    ppermute x8, starting transfers between devices, down(): return lax.ppermute(piece, 'depth', down_route if closed else open_route)  6.71 us
    ppermute x8, waiting for transfers between devices, down(): return lax.ppermute(piece, 'depth', down_route if closed else open_route)  5.54 us
    ppermute x16, starting transfers between devices, mate(): return [lax.ppermute(piece, 'depth', mate_route) for piece in pieces]  5.07 us
    pallas_call x12, Pallas kernels, step(): pl.pallas_call(functools.partial(step_kernel, tick, start, parity, len(pi...  3.53 us
    pallas_call x2, Pallas kernels, first(): pl.pallas_call(functools.partial(first_kernel, parity, bool(carried)), ou...  2.7 us
    pallas_call x2, Pallas kernels, last(): pl.pallas_call(functools.partial(last_kernel, half), out_shape=out_shape,...  1.84 us
    ppermute x1, waiting for transfers between devices, local(): gradient = gradient + lax.ppermute(chunks[distance], 'freq', route)  1.77 us
    ppermute x16, waiting for transfers between devices, mate(): return [lax.ppermute(piece, 'depth', mate_route) for piece in pieces]  1.65 us
  transfers between devices with their start and end apart: 25, of which 11 were waited for; matrix products, arithmetic and copies ran while one was open for 0% of the time, Pallas kernels for 17%

profile of v10, /device:TPU:10, one launch (start us, length us, event | category | flops | bytes accessed | tf_op | source)
XLA Modules:
  0.0 30.9 jit_solution(18306626830501156791)
XLA Ops:
  0.6 0.1 first_1.1
  0.7 0.0 copy-start
  0.7 0.0 copy-start.1
  0.7 0.0 copy-start.2
  0.8 0.0 copy-start.3
  0.8 2.6 %first_0.1 = (f32[2,32,512]{2,1,0:T(8,128)S(1)}, f32[2,16,512]{2,1,0:T(8,128)S(1)}, f32[2,32,512]{2,1,0:T(8,128)S(1)}, f32[2,16,512]{2,1,0:T(8,128)S(1)}, bf16[2...) custom-call(f32[1,1,2,512,512]{4,3,2,1,0:T(8,128)} %refs_0_.5, ...), custom_call_target="tpu_custom_call", output_to_operand_aliasing={{4}: (4, {}), {5}: (5, {}), {6}: (6, {})} | custom-call | flops 500000000 | bytes 1 | tf_op jit(solution)/shard_map/first_0/pallas_call | solution.py:172
  3.4 0.1 collective-permute-start.3
  3.5 0.5 %collective-permute-start.2 = (f32[2,48,512]{2,1,0:T(8,128)S(1)}, f32[2,48,512]{2,1,0:T(8,128)S(1)}, u32[]{:S(2)}, u32[]{:S(2)}) collective-permute-start(f32[2,48,512]{2,1,0:T(8,128)S(1)} %get-tuple-element.55), channel_id=1, source_target_pairs={{0,2},{2,4},{4,0},{6,8},{8,10},{10,12},{12,6},{14,16},{16,18},{18,... | collective-permute-start | bytes 589832 | tf_op jit(solution)/shard_map/ppermute | solution.py:361
  4.0 1.2 %collective-permute-start.7 = (f32[2,48,512]{2,1,0:T(8,128)S(1)}, f32[2,48,512]{2,1,0:T(8,128)S(1)}, u32[]{:S(2)}, u32[]{:S(2)}) collective-permute-start(f32[2,48,512]{2,1,0:T(8,128)S(1)} %get-tuple-element.63), channel_id=1, source_target_pairs={{0,2},{2,4},{4,0},{6,8},{8,10},{10,12},{12,6},{14,16},{16,18},{18,... | collective-permute-start | bytes 589832 | tf_op jit(solution)/shard_map/ppermute | solution.py:361
  5.2 0.5 %collective-permute-start.4 = (f32[2,16,512]{2,1,0:T(8,128)S(1)}, f32[2,16,512]{2,1,0:T(8,128)S(1)}, u32[]{:S(2)}, u32[]{:S(2)}) collective-permute-start(f32[2,16,512]{2,1,0:T(8,128)S(1)} %get-tuple-element.57), channel_id=1, source_target_pairs={{0,2},{2,0},{4,6},{6,4},{8,10},{10,8},{12,14},{14,12},{16,18},{18,... | collective-permute-start | bytes 196616 | tf_op jit(solution)/shard_map/ppermute | solution.py:358
  5.7 0.0 collective-permute-start
  5.7 0.9 %collective-permute-done.4.refs_1_ = f32[2,16,512]{2,1,0:T(8,128)S(1)} collective-permute-done((f32[2,16,512]{2,1,0:T(8,128)S(1)}, f32[2,16,512]{2,1,0:T(8,128)S(1)}, u32[]{:S(2)}, u32[]{:S(2)}) %collective-permute-start.4) | collective-permute-done | bytes 65568 | tf_op jit(solution)/shard_map/ppermute | solution.py:358
  6.6 0.4 %collective-permute-start.1 = (f32[2,16,512]{2,1,0:T(8,128)S(1)}, f32[2,16,512]{2,1,0:T(8,128)S(1)}, u32[]{:S(2)}, u32[]{:S(2)}) collective-permute-start(f32[2,16,512]{2,1,0:T(8,128)S(1)} %get-tuple-element.52), channel_id=1, source_target_pairs={{0,2},{2,0},{4,6},{6,4},{8,10},{10,8},{12,14},{14,12},{16,18},{18,... | collective-permute-start | bytes 196616 | tf_op jit(solution)/shard_map/ppermute | solution.py:358
  6.9 0.0 collective-permute-done.3.refs_0_
  7.0 0.7 %collective-permute-start.6 = (f32[2,48,512]{2,1,0:T(8,128)S(1)}, f32[2,48,512]{2,1,0:T(8,128)S(1)}, u32[]{:S(2)}, u32[]{:S(2)}) collective-permute-start(f32[2,48,512]{2,1,0:T(8,128)S(1)} %get-tuple-element.62), channel_id=1, source_target_pairs={{0,2},{2,4},{4,0},{6,8},{8,10},{10,12},{12,6},{14,16},{16,18},{18,... | collective-permute-start | bytes 589832 | tf_op jit(solution)/shard_map/ppermute | solution.py:361
  7.7 1.8 %collective-permute-done.2.refs_0_ = f32[2,48,512]{2,1,0:T(8,128)S(1)} collective-permute-done((f32[2,48,512]{2,1,0:T(8,128)S(1)}, f32[2,48,512]{2,1,0:T(8,128)S(1)}, u32[]{:S(2)}, u32[]{:S(2)}) %collective-permute-start.2) | collective-permute-done | bytes 196640 | tf_op jit(solution)/shard_map/ppermute | solution.py:361
  9.5 0.6 %step_1_0_0.1 = (f32[2,32,512]{2,1,0:T(8,128)S(1)}, f32[2,16,512]{2,1,0:T(8,128)S(1)}, f32[8,512]{1,0:T(8,128)S(1)}) custom-call(f32[2,48,512]{2,1,0:T(8,128)S(1)} %collective-permute-done.2.refs_0_, f32[1,1,5,2,96,512]{5,4,3,2,1,0:T(8,128)S(1)} %copy-done, f32[1,512]{1,0:T(1,128)S(1)} %copy-done.1, ...), custom_call_target="tpu_custom_call", output_to_operand_aliasing={{2}: (7, {})} | custom-call | flops 1000000 | bytes 1 | tf_op jit(solution)/shard_map/step_1_0_0/pallas_call | solution.py:243
  10.1 0.1 collective-permute-start.11
  10.2 0.0 collective-permute-done.1.refs_1_
  10.2 0.5 %collective-permute-start.10 = (f32[2,32,512]{2,1,0:T(8,128)S(1)}, f32[2,32,512]{2,1,0:T(8,128)S(1)}, u32[]{:S(2)}, u32[]{:S(2)}) collective-permute-start(f32[2,32,512]{2,1,0:T(8,128)S(1)} %get-tuple-element.67), channel_id=1, source_target_pairs={{0,2},{2,0},{4,6},{6,4},{8,10},{10,8},{12,14},{14,12},{16,18},{18,... | collective-permute-start | bytes 393224 | tf_op jit(solution)/shard_map/ppermute | solution.py:358
  10.7 0.0 collective-permute-done.refs_0_
  10.7 0.7 %collective-permute-start.5 = (f32[2,48,512]{2,1,0:T(8,128)S(1)}, f32[2,48,512]{2,1,0:T(8,128)S(1)}, u32[]{:S(2)}, u32[]{:S(2)}) collective-permute-start(f32[2,48,512]{2,1,0:T(8,128)S(1)} %get-tuple-element.61), channel_id=1, source_target_pairs={{0,2},{2,4},{4,0},{6,8},{8,10},{10,12},{12,6},{14,16},{16,18},{18,... | collective-permute-start | bytes 589832 | tf_op jit(solution)/shard_map/ppermute | solution.py:361
  11.4 0.2 collective-permute-done.7.refs_0_
  11.6 0.6 %step_1_1_0.1 = (f32[2,32,512]{2,1,0:T(8,128)S(1)}, f32[2,16,512]{2,1,0:T(8,128)S(1)}, f32[8,512]{1,0:T(8,128)S(1)}) custom-call(f32[2,48,512]{2,1,0:T(8,128)S(1)} %collective-permute-done.7.refs_0_, f32[1,1,5,2,96,512]{5,4,3,2,1,0:T(8,128)S(1)} %copy-done, f32[1,512]{1,0:T(1,128)S(1)} %copy-done.1, ...), custom_call_target="tpu_custom_call", output_to_operand_aliasing={{2}: (7, {})} | custom-call | flops 1000000000 | bytes 1 | tf_op jit(solution)/shard_map/step_1_1_0/pallas_call | solution.py:243
  12.2 0.1 collective-permute-start.8
  12.3 0.0 collective-permute-done.11.refs_1_
  12.3 0.5 %collective-permute-start.9 = (f32[2,16,512]{2,1,0:T(8,128)S(1)}, f32[2,16,512]{2,1,0:T(8,128)S(1)}, u32[]{:S(2)}, u32[]{:S(2)}) collective-permute-start(f32[2,16,512]{2,1,0:T(8,128)S(1)} %get-tuple-element.66), channel_id=1, source_target_pairs={{0,2},{2,0},{4,6},{6,4},{8,10},{10,8},{12,14},{14,12},{16,18},{18,... | collective-permute-start | bytes 196616 | tf_op jit(solution)/shard_map/ppermute | solution.py:358
  12.8 0.0 collective-permute-done.10.refs_0_
  12.8 0.7 %collective-permute-start.18 = (f32[2,48,512]{2,1,0:T(8,128)S(1)}, f32[2,48,512]{2,1,0:T(8,128)S(1)}, u32[]{:S(2)}, u32[]{:S(2)}) collective-permute-start(f32[2,48,512]{2,1,0:T(8,128)S(1)} %get-tuple-element.81), channel_id=1, source_target_pairs={{0,2},{2,4},{4,0},{6,8},{8,10},{10,12},{12,6},{14,16},{16,18},{18,... | collective-permute-start | bytes 589832 | tf_op jit(solution)/shard_map/ppermute | solution.py:361
  13.5 0.2 collective-permute-done.9.refs_1_
  13.7 0.0 collective-permute-done.8.refs_0_
  13.7 1.0 %collective-permute-start.17 = (f32[2,48,512]{2,1,0:T(8,128)S(1)}, f32[2,48,512]{2,1,0:T(8,128)S(1)}, u32[]{:S(2)}, u32[]{:S(2)}) collective-permute-start(f32[2,48,512]{2,1,0:T(8,128)S(1)} %get-tuple-element.80), channel_id=1, source_target_pairs={{0,2},{2,4},{4,0},{6,8},{8,10},{10,12},{12,6},{14,16},{16,18},{18,... | collective-permute-start | bytes 589832 | tf_op jit(solution)/shard_map/ppermute | solution.py:361
  14.7 0.0 collective-permute-done.6.refs_0_
  14.7 0.6 %step_2_0_0.1 = (f32[2,32,512]{2,1,0:T(8,128)S(1)}, f32[2,16,512]{2,1,0:T(8,128)S(1)}, f32[8,512]{1,0:T(8,128)S(1)}) custom-call(f32[2,48,512]{2,1,0:T(8,128)S(1)} %collective-permute-done.6.refs_0_, f32[1,1,5,2,96,512]{5,4,3,2,1,0:T(8,128)S(1)} %copy-done, f32[1,512]{1,0:T(1,128)S(1)} %copy-done.1, ...), custom_call_target="tpu_custom_call", output_to_operand_aliasing={{2}: (7, {})} | custom-call | flops 10000000 | bytes 1 | tf_op jit(solution)/shard_map/step_2_0_0/pallas_call | solution.py:243
  15.3 0.1 collective-permute-start.14
  15.3 0.5 %collective-permute-start.15 = (f32[2,16,512]{2,1,0:T(8,128)S(1)}, f32[2,16,512]{2,1,0:T(8,128)S(1)}, u32[]{:S(2)}, u32[]{:S(2)}) collective-permute-start(f32[2,16,512]{2,1,0:T(8,128)S(1)} %get-tuple-element.76), channel_id=1, source_target_pairs={{0,2},{2,0},{4,6},{6,4},{8,10},{10,8},{12,14},{14,12},{16,18},{18,... | collective-permute-start | bytes 196616 | tf_op jit(solution)/shard_map/ppermute | solution.py:358
  15.8 0.9 %collective-permute-done.5.refs_0_ = f32[2,48,512]{2,1,0:T(8,128)S(1)} collective-permute-done((f32[2,48,512]{2,1,0:T(8,128)S(1)}, f32[2,48,512]{2,1,0:T(8,128)S(1)}, u32[]{:S(2)}, u32[]{:S(2)}) %collective-permute-start.5) | collective-permute-done | bytes 196640 | tf_op jit(solution)/shard_map/ppermute | solution.py:361
  16.7 0.6 %step_2_1_0.1 = (f32[2,32,512]{2,1,0:T(8,128)S(1)}, f32[2,16,512]{2,1,0:T(8,128)S(1)}, f32[8,512]{1,0:T(8,128)S(1)}) custom-call(f32[2,48,512]{2,1,0:T(8,128)S(1)} %collective-permute-done.5.refs_0_, f32[1,1,5,2,96,512]{5,4,3,2,1,0:T(8,128)S(1)} %copy-done, f32[1,512]{1,0:T(1,128)S(1)} %copy-done.1, ...), custom_call_target="tpu_custom_call", output_to_operand_aliasing={{2}: (7, {})} | custom-call | flops 30000000 | bytes 1 | tf_op jit(solution)/shard_map/step_2_1_0/pallas_call | solution.py:243
  17.3 0.1 collective-permute-start.12
  17.4 0.5 %collective-permute-start.13 = (f32[2,16,512]{2,1,0:T(8,128)S(1)}, f32[2,16,512]{2,1,0:T(8,128)S(1)}, u32[]{:S(2)}, u32[]{:S(2)}) collective-permute-start(f32[2,16,512]{2,1,0:T(8,128)S(1)} %get-tuple-element.74), channel_id=1, source_target_pairs={{0,2},{2,0},{4,6},{6,4},{8,10},{10,8},{12,14},{14,12},{16,18},{18,... | collective-permute-start | bytes 196616 | tf_op jit(solution)/shard_map/ppermute | solution.py:358
  17.9 0.0 collective-permute-done.14.refs_0_
  17.9 0.7 %collective-permute-start.21 = (f32[2,48,512]{2,1,0:T(8,128)S(1)}, f32[2,48,512]{2,1,0:T(8,128)S(1)}, u32[]{:S(2)}, u32[]{:S(2)}) collective-permute-start(f32[2,48,512]{2,1,0:T(8,128)S(1)} %get-tuple-element.86), channel_id=1, source_target_pairs={{0,2},{2,4},{4,0},{6,8},{8,10},{10,12},{12,6},{14,16},{16,18},{18,... | collective-permute-start | bytes 589832 | tf_op jit(solution)/shard_map/ppermute | solution.py:361
  18.5 0.2 collective-permute-done.13.refs_1_
  18.8 0.0 collective-permute-done.12.refs_0_
  18.8 1.3 %collective-permute-start.16 = (f32[2,48,512]{2,1,0:T(8,128)S(1)}, f32[2,48,512]{2,1,0:T(8,128)S(1)}, u32[]{:S(2)}, u32[]{:S(2)}) collective-permute-start(f32[2,48,512]{2,1,0:T(8,128)S(1)} %get-tuple-element.79), channel_id=1, source_target_pairs={{2,4},{6,8},{10,12},{14,16},{18,20},{22,24},{26,28},{3,5},{7,9},{1... | collective-permute-start | bytes 589832 | tf_op jit(solution)/shard_map/ppermute | solution.py:361
  20.1 0.0 collective-permute-done.18.refs_0_
  20.1 0.6 %step_3_0_0.1 = (f32[2,32,512]{2,1,0:T(8,128)S(1)}, f32[2,16,512]{2,1,0:T(8,128)S(1)}, f32[8,512]{1,0:T(8,128)S(1)}) custom-call(f32[2,48,512]{2,1,0:T(8,128)S(1)} %collective-permute-done.18.refs_0_, f32[1,1,5,2,96,512]{5,4,3,2,1,0:T(8,128)S(1)} %copy-done, f32[1,512]{1,0:T(1,128)S(1)} %copy-done.1, ...), custom_call_target="tpu_custom_call", output_to_operand_aliasing={{2}: (7, {})} | custom-call | flops 10000000 | bytes 1 | tf_op jit(solution)/shard_map/step_3_0_0/pallas_call | solution.py:243
  20.7 1.4 %collective-permute-start.23 = (f32[2,16,512]{2,1,0:T(8,128)S(1)}, f32[2,16,512]{2,1,0:T(8,128)S(1)}, u32[]{:S(2)}, u32[]{:S(2)}) collective-permute-start(f32[2,16,512]{2,1,0:T(8,128)S(1)} %get-tuple-element.88), channel_id=1, source_target_pairs={{0,2},{2,0},{4,6},{6,4},{8,10},{10,8},{12,14},{14,12},{16,18},{18,... | collective-permute-start | bytes 196616 | tf_op jit(solution)/shard_map/ppermute | solution.py:358
  22.1 0.1 collective-permute-start.22
  22.2 0.0 collective-permute-done.17.refs_0_
  22.2 0.6 %step_3_1_0.1 = (f32[2,32,512]{2,1,0:T(8,128)S(1)}, f32[2,16,512]{2,1,0:T(8,128)S(1)}, f32[8,512]{1,0:T(8,128)S(1)}) custom-call(f32[2,48,512]{2,1,0:T(8,128)S(1)} %collective-permute-done.17.refs_0_, f32[1,1,5,2,96,512]{5,4,3,2,1,0:T(8,128)S(1)} %copy-done, f32[1,512]{1,0:T(1,128)S(1)} %copy-done.1, ...), custom_call_target="tpu_custom_call", output_to_operand_aliasing={{2}: (7, {})} | custom-call | flops 200000000 | bytes 1 | tf_op jit(solution)/shard_map/step_3_1_0/pallas_call | solution.py:243
  22.8 0.1 collective-permute-start.19
  22.8 0.2 collective-permute-done.23.mate_tail
  23.0 0.4 %collective-permute-start.20 = (f32[2,16,512]{2,1,0:T(8,128)S(1)}, f32[2,16,512]{2,1,0:T(8,128)S(1)}, u32[]{:S(2)}, u32[]{:S(2)}) collective-permute-start(f32[2,16,512]{2,1,0:T(8,128)S(1)} %get-tuple-element.85), channel_id=1, source_target_pairs={{0,2},{2,0},{4,6},{6,4},{8,10},{10,8},{12,14},{14,12},{16,18},{18,... | collective-permute-start | bytes 196616 | tf_op jit(solution)/shard_map/ppermute | solution.py:358
  23.3 0.1 collective-permute-done.22.mate
  23.4 0.4 %collective-permute-done.21.above = f32[2,48,512]{2,1,0:T(8,128)S(1)} collective-permute-done((f32[2,48,512]{2,1,0:T(8,128)S(1)}, f32[2,48,512]{2,1,0:T(8,128)S(1)}, u32[]{:S(2)}, u32[]{:S(2)}) %collective-permute-start.21) | collective-permute-done | bytes 196640 | tf_op jit(solution)/shard_map/ppermute | solution.py:361
  23.9 0.6 %last_0.1 = (f32[2,48,512]{2,1,0:T(8,128)S(1)}, f32[8,512]{1,0:T(8,128)S(1)}) custom-call(f32[2,48,512]{2,1,0:T(8,128)S(1)} %collective-permute-done.21.above, f32[2,32,512]{2,1,0:T(8,128)S(1)} %collective-permute-done.22.mate, f32[2,16,512]{2,1,0:T(8,128)S(1)} %collective-permute-done.23.mate_tail, ...), custom_call_target="tpu_custom_call", output_to_operand_aliasing={{1}: (9, {})} | custom-call | flops 100000000 | bytes 1 | tf_op jit(solution)/shard_map/last_0/pallas_call | solution.py:318
  24.4 0.0 collective-permute-done.20.mate_tail
  24.5 2.2 %collective-permute-done.16.above = f32[2,48,512]{2,1,0:T(8,128)S(1)} collective-permute-done((f32[2,48,512]{2,1,0:T(8,128)S(1)}, f32[2,48,512]{2,1,0:T(8,128)S(1)}, u32[]{:S(2)}, u32[]{:S(2)}) %collective-permute-start.16) | collective-permute-done | bytes 196640 | tf_op jit(solution)/shard_map/ppermute | solution.py:361
  26.7 0.1 gradient.1
  26.7 0.6 %collective-permute-start.24 = (f32[1,256]{1,0:T(1,128)S(1)}, f32[1,256]{1,0:T(1,128)S(1)}, u32[]{:S(2)}, u32[]{:S(2)}) collective-permute-start(f32[1,256]{1,0:T(1,128)S(1)} %get-tuple-element.93), channel_id=1, source_target_pairs={{0,1},{1,0},{2,3},{3,2},{4,5},{5,4},{6,7},{7,6},{8,9},{9,8},{10,11... | collective-permute-start | bytes 3080 | tf_op jit(solution)/shard_map/ppermute | solution.py:397
  27.3 1.3 %last_1.1 = f32[2,96,512]{2,1,0:T(8,128)} custom-call(f32[2,48,512]{2,1,0:T(8,128)S(1)} %collective-permute-done.16.above, f32[2,32,512]{2,1,0:T(8,128)S(1)} %collective-permute-done.19.mate, f32[2,16,512]{2,1,0:T(8,128)S(1)} %collective-permute-done.20.mate_tail, f32[1,1,5,2,96,512]{5,4,3,2,1,0:T(8,128)S(1)} %copy-done, f32[1,512]{1,0:T(1,128)S(1)} %copy-done.1, ...), custom_call_target="tpu_custom_call" | custom-call | flops 1 | bytes 1 | tf_op jit(solution)/shard_map/last_1/pallas_call | solution.py:318
  28.6 1.8 %collective-permute-done.24 = f32[1,256]{1,0:T(1,128)S(1)} collective-permute-done((f32[1,256]{1,0:T(1,128)S(1)}, f32[1,256]{1,0:T(1,128)S(1)}, u32[]{:S(2)}, u32[]{:S(2)}) %collective-permute-start.24) | collective-permute-done | bytes 1056 | tf_op jit(solution)/shard_map/ppermute | solution.py:397
  30.4 0.6 %add.3 = f32[1,256]{1,0:T(1,128)} add(f32[1,256]{1,0:T(1,128)S(1)} %get-tuple-element.92, f32[1,256]{1,0:T(1,128)S(1)} %collective-permute-done.24) | non-fusion elementwise | flops 256 | bytes 3072 | tf_op jit(solution)/shard_map/add | solution.py:397
  (12 shorter events, 0.0 us)
Async XLA Ops:
  0.7 6.2 %copy-start = (f32[1,1,5,2,96,512]{5,4,3,2,1,0:T(8,128)S(1)}, f32[1,1,5,2,96,512]{5,4,3,2,1,0:T(8,128)}, u32[]{:S(2)}) copy-start(f32[1,1,5,2,96,512]{5,4,3,2,1,0:T(8,128)} %residual.1) | copy-start | bytes 5898244
  0.7 6.2 %copy-start.1 = (f32[1,512]{1,0:T(1,128)S(1)}, f32[1,512]{1,0:T(1,128)}, u32[]{:S(2)}) copy-start(f32[1,512]{1,0:T(1,128)} %contrast.1) | copy-start | bytes 6148
  0.7 6.2 %copy-start.2 = (s32[4,96]{1,0:T(4,128)S(1)}, s32[4,96]{1,0:T(4,128)}, u32[]{:S(2)}) copy-start(s32[4,96]{1,0:T(4,128)} %sites.1) | copy-start | bytes 4612
  0.8 6.2 %copy-start.3 = (f32[1,4,2]{1,2,0:T(2,128)S(1)}, f32[1,4,2]{1,2,0:T(2,128)}, u32[]{:S(2)}) copy-start(f32[1,4,2]{1,2,0:T(2,128)} %param.11) | copy-start | bytes 100
  3.4 3.5 %collective-permute-start.3 = (f32[2,32,512]{2,1,0:T(8,128)S(1)}, f32[2,32,512]{2,1,0:T(8,128)S(1)}, u32[]{:S(2)}, u32[]{:S(2)}) collective-permute-start(f32[2,32,512]{2,1,0:T(8,128)S(1)} %get-tuple-element.56), channel_id=1, source_target_pairs={{0,2},{2,0},{4,6},{6,4},{8,10},{10,8},{12,14},{14,12},{16,18},{18,... | collective-permute-start | bytes 393224 | tf_op jit(solution)/shard_map/ppermute | solution.py:358
  3.5 6.1 %collective-permute-start.2 = (f32[2,48,512]{2,1,0:T(8,128)S(1)}, f32[2,48,512]{2,1,0:T(8,128)S(1)}, u32[]{:S(2)}, u32[]{:S(2)}) collective-permute-start(f32[2,48,512]{2,1,0:T(8,128)S(1)} %get-tuple-element.55), channel_id=1, source_target_pairs={{0,2},{2,4},{4,0},{6,8},{8,10},{10,12},{12,6},{14,16},{16,18},{18,... | collective-permute-start | bytes 589832 | tf_op jit(solution)/shard_map/ppermute | solution.py:361
  4.0 7.7 %collective-permute-start.7 = (f32[2,48,512]{2,1,0:T(8,128)S(1)}, f32[2,48,512]{2,1,0:T(8,128)S(1)}, u32[]{:S(2)}, u32[]{:S(2)}) collective-permute-start(f32[2,48,512]{2,1,0:T(8,128)S(1)} %get-tuple-element.63), channel_id=1, source_target_pairs={{0,2},{2,4},{4,0},{6,8},{8,10},{10,12},{12,6},{14,16},{16,18},{18,... | collective-permute-start | bytes 589832 | tf_op jit(solution)/shard_map/ppermute | solution.py:361
  5.2 1.4 %collective-permute-start.4 = (f32[2,16,512]{2,1,0:T(8,128)S(1)}, f32[2,16,512]{2,1,0:T(8,128)S(1)}, u32[]{:S(2)}, u32[]{:S(2)}) collective-permute-start(f32[2,16,512]{2,1,0:T(8,128)S(1)} %get-tuple-element.57), channel_id=1, source_target_pairs={{0,2},{2,0},{4,6},{6,4},{8,10},{10,8},{12,14},{14,12},{16,18},{18,... | collective-permute-start | bytes 196616 | tf_op jit(solution)/shard_map/ppermute | solution.py:358
  5.7 5.0 %collective-permute-start = (f32[2,32,512]{2,1,0:T(8,128)S(1)}, f32[2,32,512]{2,1,0:T(8,128)S(1)}, u32[]{:S(2)}, u32[]{:S(2)}) collective-permute-start(f32[2,32,512]{2,1,0:T(8,128)S(1)} %get-tuple-element.51), channel_id=1, source_target_pairs={{0,2},{2,0},{4,6},{6,4},{8,10},{10,8},{12,14},{14,12},{16,18},{18,... | collective-permute-start | bytes 393224 | tf_op jit(solution)/shard_map/ppermute | solution.py:358
  6.6 3.6 %collective-permute-start.1 = (f32[2,16,512]{2,1,0:T(8,128)S(1)}, f32[2,16,512]{2,1,0:T(8,128)S(1)}, u32[]{:S(2)}, u32[]{:S(2)}) collective-permute-start(f32[2,16,512]{2,1,0:T(8,128)S(1)} %get-tuple-element.52), channel_id=1, source_target_pairs={{0,2},{2,0},{4,6},{6,4},{8,10},{10,8},{12,14},{14,12},{16,18},{18,... | collective-permute-start | bytes 196616 | tf_op jit(solution)/shard_map/ppermute | solution.py:358
  7.0 7.7 %collective-permute-start.6 = (f32[2,48,512]{2,1,0:T(8,128)S(1)}, f32[2,48,512]{2,1,0:T(8,128)S(1)}, u32[]{:S(2)}, u32[]{:S(2)}) collective-permute-start(f32[2,48,512]{2,1,0:T(8,128)S(1)} %get-tuple-element.62), channel_id=1, source_target_pairs={{0,2},{2,4},{4,0},{6,8},{8,10},{10,12},{12,6},{14,16},{16,18},{18,... | collective-permute-start | bytes 589832 | tf_op jit(solution)/shard_map/ppermute | solution.py:361
  10.1 2.2 %collective-permute-start.11 = (f32[2,16,512]{2,1,0:T(8,128)S(1)}, f32[2,16,512]{2,1,0:T(8,128)S(1)}, u32[]{:S(2)}, u32[]{:S(2)}) collective-permute-start(f32[2,16,512]{2,1,0:T(8,128)S(1)} %get-tuple-element.68), channel_id=1, source_target_pairs={{0,2},{2,0},{4,6},{6,4},{8,10},{10,8},{12,14},{14,12},{16,18},{18,... | collective-permute-start | bytes 196616 | tf_op jit(solution)/shard_map/ppermute | solution.py:358
  10.2 2.6 %collective-permute-start.10 = (f32[2,32,512]{2,1,0:T(8,128)S(1)}, f32[2,32,512]{2,1,0:T(8,128)S(1)}, u32[]{:S(2)}, u32[]{:S(2)}) collective-permute-start(f32[2,32,512]{2,1,0:T(8,128)S(1)} %get-tuple-element.67), channel_id=1, source_target_pairs={{0,2},{2,0},{4,6},{6,4},{8,10},{10,8},{12,14},{14,12},{16,18},{18,... | collective-permute-start | bytes 393224 | tf_op jit(solution)/shard_map/ppermute | solution.py:358
  10.7 6.0 %collective-permute-start.5 = (f32[2,48,512]{2,1,0:T(8,128)S(1)}, f32[2,48,512]{2,1,0:T(8,128)S(1)}, u32[]{:S(2)}, u32[]{:S(2)}) collective-permute-start(f32[2,48,512]{2,1,0:T(8,128)S(1)} %get-tuple-element.61), channel_id=1, source_target_pairs={{0,2},{2,4},{4,0},{6,8},{8,10},{10,12},{12,6},{14,16},{16,18},{18,... | collective-permute-start | bytes 589832 | tf_op jit(solution)/shard_map/ppermute | solution.py:361
  12.2 1.5 %collective-permute-start.8 = (f32[2,32,512]{2,1,0:T(8,128)S(1)}, f32[2,32,512]{2,1,0:T(8,128)S(1)}, u32[]{:S(2)}, u32[]{:S(2)}) collective-permute-start(f32[2,32,512]{2,1,0:T(8,128)S(1)} %get-tuple-element.65), channel_id=1, source_target_pairs={{0,2},{2,0},{4,6},{6,4},{8,10},{10,8},{12,14},{14,12},{16,18},{18,... | collective-permute-start | bytes 393224 | tf_op jit(solution)/shard_map/ppermute | solution.py:358
  12.3 1.4 %collective-permute-start.9 = (f32[2,16,512]{2,1,0:T(8,128)S(1)}, f32[2,16,512]{2,1,0:T(8,128)S(1)}, u32[]{:S(2)}, u32[]{:S(2)}) collective-permute-start(f32[2,16,512]{2,1,0:T(8,128)S(1)} %get-tuple-element.66), channel_id=1, source_target_pairs={{0,2},{2,0},{4,6},{6,4},{8,10},{10,8},{12,14},{14,12},{16,18},{18,... | collective-permute-start | bytes 196616 | tf_op jit(solution)/shard_map/ppermute | solution.py:358
  12.8 7.3 %collective-permute-start.18 = (f32[2,48,512]{2,1,0:T(8,128)S(1)}, f32[2,48,512]{2,1,0:T(8,128)S(1)}, u32[]{:S(2)}, u32[]{:S(2)}) collective-permute-start(f32[2,48,512]{2,1,0:T(8,128)S(1)} %get-tuple-element.81), channel_id=1, source_target_pairs={{0,2},{2,4},{4,0},{6,8},{8,10},{10,12},{12,6},{14,16},{16,18},{18,... | collective-permute-start | bytes 589832 | tf_op jit(solution)/shard_map/ppermute | solution.py:361
  13.7 8.4 %collective-permute-start.17 = (f32[2,48,512]{2,1,0:T(8,128)S(1)}, f32[2,48,512]{2,1,0:T(8,128)S(1)}, u32[]{:S(2)}, u32[]{:S(2)}) collective-permute-start(f32[2,48,512]{2,1,0:T(8,128)S(1)} %get-tuple-element.80), channel_id=1, source_target_pairs={{0,2},{2,4},{4,0},{6,8},{8,10},{10,12},{12,6},{14,16},{16,18},{18,... | collective-permute-start | bytes 589832 | tf_op jit(solution)/shard_map/ppermute | solution.py:361
  15.3 2.6 %collective-permute-start.14 = (f32[2,32,512]{2,1,0:T(8,128)S(1)}, f32[2,32,512]{2,1,0:T(8,128)S(1)}, u32[]{:S(2)}, u32[]{:S(2)}) collective-permute-start(f32[2,32,512]{2,1,0:T(8,128)S(1)} %get-tuple-element.75), channel_id=1, source_target_pairs={{0,2},{2,0},{4,6},{6,4},{8,10},{10,8},{12,14},{14,12},{16,18},{18,... | collective-permute-start | bytes 393224 | tf_op jit(solution)/shard_map/ppermute | solution.py:358
  15.3 2.0 %collective-permute-start.15 = (f32[2,16,512]{2,1,0:T(8,128)S(1)}, f32[2,16,512]{2,1,0:T(8,128)S(1)}, u32[]{:S(2)}, u32[]{:S(2)}) collective-permute-start(f32[2,16,512]{2,1,0:T(8,128)S(1)} %get-tuple-element.76), channel_id=1, source_target_pairs={{0,2},{2,0},{4,6},{6,4},{8,10},{10,8},{12,14},{14,12},{16,18},{18,... | collective-permute-start | bytes 196616 | tf_op jit(solution)/shard_map/ppermute | solution.py:358
  17.3 1.5 %collective-permute-start.12 = (f32[2,32,512]{2,1,0:T(8,128)S(1)}, f32[2,32,512]{2,1,0:T(8,128)S(1)}, u32[]{:S(2)}, u32[]{:S(2)}) collective-permute-start(f32[2,32,512]{2,1,0:T(8,128)S(1)} %get-tuple-element.73), channel_id=1, source_target_pairs={{0,2},{2,0},{4,6},{6,4},{8,10},{10,8},{12,14},{14,12},{16,18},{18,... | collective-permute-start | bytes 393224 | tf_op jit(solution)/shard_map/ppermute | solution.py:358
  17.4 1.4 %collective-permute-start.13 = (f32[2,16,512]{2,1,0:T(8,128)S(1)}, f32[2,16,512]{2,1,0:T(8,128)S(1)}, u32[]{:S(2)}, u32[]{:S(2)}) collective-permute-start(f32[2,16,512]{2,1,0:T(8,128)S(1)} %get-tuple-element.74), channel_id=1, source_target_pairs={{0,2},{2,0},{4,6},{6,4},{8,10},{10,8},{12,14},{14,12},{16,18},{18,... | collective-permute-start | bytes 196616 | tf_op jit(solution)/shard_map/ppermute | solution.py:358
  17.9 6.0 %collective-permute-start.21 = (f32[2,48,512]{2,1,0:T(8,128)S(1)}, f32[2,48,512]{2,1,0:T(8,128)S(1)}, u32[]{:S(2)}, u32[]{:S(2)}) collective-permute-start(f32[2,48,512]{2,1,0:T(8,128)S(1)} %get-tuple-element.86), channel_id=1, source_target_pairs={{0,2},{2,4},{4,0},{6,8},{8,10},{10,12},{12,6},{14,16},{16,18},{18,... | collective-permute-start | bytes 589832 | tf_op jit(solution)/shard_map/ppermute | solution.py:361
  18.8 7.9 %collective-permute-start.16 = (f32[2,48,512]{2,1,0:T(8,128)S(1)}, f32[2,48,512]{2,1,0:T(8,128)S(1)}, u32[]{:S(2)}, u32[]{:S(2)}) collective-permute-start(f32[2,48,512]{2,1,0:T(8,128)S(1)} %get-tuple-element.79), channel_id=1, source_target_pairs={{2,4},{6,8},{10,12},{14,16},{18,20},{22,24},{26,28},{3,5},{7,9},{1... | collective-permute-start | bytes 589832 | tf_op jit(solution)/shard_map/ppermute | solution.py:361
  20.7 2.3 %collective-permute-start.23 = (f32[2,16,512]{2,1,0:T(8,128)S(1)}, f32[2,16,512]{2,1,0:T(8,128)S(1)}, u32[]{:S(2)}, u32[]{:S(2)}) collective-permute-start(f32[2,16,512]{2,1,0:T(8,128)S(1)} %get-tuple-element.88), channel_id=1, source_target_pairs={{0,2},{2,0},{4,6},{6,4},{8,10},{10,8},{12,14},{14,12},{16,18},{18,... | collective-permute-start | bytes 196616 | tf_op jit(solution)/shard_map/ppermute | solution.py:358
  22.1 1.3 %collective-permute-start.22 = (f32[2,32,512]{2,1,0:T(8,128)S(1)}, f32[2,32,512]{2,1,0:T(8,128)S(1)}, u32[]{:S(2)}, u32[]{:S(2)}) collective-permute-start(f32[2,32,512]{2,1,0:T(8,128)S(1)} %get-tuple-element.87), channel_id=1, source_target_pairs={{0,2},{2,0},{4,6},{6,4},{8,10},{10,8},{12,14},{14,12},{16,18},{18,... | collective-permute-start | bytes 393224 | tf_op jit(solution)/shard_map/ppermute | solution.py:358
  22.8 1.7 %collective-permute-start.19 = (f32[2,32,512]{2,1,0:T(8,128)S(1)}, f32[2,32,512]{2,1,0:T(8,128)S(1)}, u32[]{:S(2)}, u32[]{:S(2)}) collective-permute-start(f32[2,32,512]{2,1,0:T(8,128)S(1)} %get-tuple-element.84), channel_id=1, source_target_pairs={{0,2},{2,0},{4,6},{6,4},{8,10},{10,8},{12,14},{14,12},{16,18},{18,... | collective-permute-start | bytes 393224 | tf_op jit(solution)/shard_map/ppermute | solution.py:358
  23.0 1.5 %collective-permute-start.20 = (f32[2,16,512]{2,1,0:T(8,128)S(1)}, f32[2,16,512]{2,1,0:T(8,128)S(1)}, u32[]{:S(2)}, u32[]{:S(2)}) collective-permute-start(f32[2,16,512]{2,1,0:T(8,128)S(1)} %get-tuple-element.85), channel_id=1, source_target_pairs={{0,2},{2,0},{4,6},{6,4},{8,10},{10,8},{12,14},{14,12},{16,18},{18,... | collective-permute-start | bytes 196616 | tf_op jit(solution)/shard_map/ppermute | solution.py:358
  26.7 3.6 %collective-permute-start.24 = (f32[1,256]{1,0:T(1,128)S(1)}, f32[1,256]{1,0:T(1,128)S(1)}, u32[]{:S(2)}, u32[]{:S(2)}) collective-permute-start(f32[1,256]{1,0:T(1,128)S(1)} %get-tuple-element.93), channel_id=1, source_target_pairs={{0,1},{1,0},{2,3},{3,2},{4,5},{5,4},{6,7},{7,6},{8,9},{9,8},{10,11... | collective-permute-start | bytes 3080 | tf_op jit(solution)/shard_map/ppermute | solution.py:397

commit v11 on v10

--- a/solution.py
+++ b/solution.py
@@ -15,8 +15,8 @@
 WEIGHTS = {
     "first_0": 500000000,
     "first_1": 1000000000,
-    "step_1_0_0": 1000000,
-    "step_1_0_1": 1000000000,
+    "step_1_0_0": 30000000,
+    "step_1_0_1": 10000000,
     "step_1_1_0": 1000000000,
     "step_1_1_1": 30000000,
     "step_2_0_0": 10000000,
@@ -26,6 +26,7 @@
     "step_3_0_0": 10000000,
     "step_3_0_1": 30000000,
     "step_3_1_0": 200000000,
+    "step_3_1_1": 30000000,
     "last_0": 100000000,
     "gradient": 200000000,
 }

time: 31.1 us -> 30.2 us (0.971)
  the two profiles are of different devices: /device:TPU:10 before, /device:TPU:16 now
where the time goes in v11:
time: 30.2 us; the launch traced here: 30 us
  starting transfers between devices  14.6 us (48%)
  Pallas kernels  8.12 us (27%)
  waiting for transfers between devices  5.92 us (20%)
  between operations  0.83 us (3%)
  other arithmetic  0.56 us (2%)
    ppermute x8, starting transfers between devices, down(): return lax.ppermute(piece, 'depth', down_route if closed else open_route)  8.1 us
    ppermute x16, starting transfers between devices, mate(): return [lax.ppermute(piece, 'depth', mate_route) for piece in pieces]  4.92 us
    ppermute x8, waiting for transfers between devices, down(): return lax.ppermute(piece, 'depth', down_route if closed else open_route)  3.58 us
    pallas_call x12, Pallas kernels, step(): pl.pallas_call(functools.partial(step_kernel, tick, start, parity, len(pi...  3.51 us
    pallas_call x2, Pallas kernels, first(): pl.pallas_call(functools.partial(first_kernel, parity, bool(carried)), ou...  2.71 us
    pallas_call x2, Pallas kernels, last(): pl.pallas_call(functools.partial(last_kernel, half), out_shape=out_shape,...  1.84 us
    ppermute x1, starting transfers between devices, local(): gradient = gradient + lax.ppermute(chunks[distance], 'freq', route)  1.55 us
    ppermute x16, waiting for transfers between devices, mate(): return [lax.ppermute(piece, 'depth', mate_route) for piece in pieces]  1.53 us
  transfers between devices with their start and end apart: 25, of which 9 were waited for; matrix products, arithmetic and copies ran while one was open for 0% of the time, Pallas kernels for 27%

profile of v11, /device:TPU:16, one launch (start us, length us, event | category | flops | bytes accessed | tf_op | source)
XLA Modules:
  0.0 30.0 jit_solution(10015130917090390316)
XLA Ops:
  0.6 0.1 first_1.1
  0.7 2.3 %collective-permute-start.2 = (f32[2,48,512]{2,1,0:T(8,128)S(1)}, f32[2,48,512]{2,1,0:T(8,128)S(1)}, u32[]{:S(2)}, u32[]{:S(2)}) collective-permute-start(f32[2,48,512]{2,1,0:T(8,128)S(1)} %get-tuple-element.55), channel_id=1, source_target_pairs={{0,2},{2,4},{4,0},{6,8},{8,10},{10,12},{12,6},{14,16},{16,18},{18,... | collective-permute-start | bytes 589832 | tf_op jit(solution)/shard_map/ppermute | solution.py:362
  3.0 0.1 collective-permute-start.7
  3.1 2.6 %first_0.1 = (f32[2,32,512]{2,1,0:T(8,128)S(1)}, f32[2,16,512]{2,1,0:T(8,128)S(1)}, f32[2,32,512]{2,1,0:T(8,128)S(1)}, f32[2,16,512]{2,1,0:T(8,128)S(1)}, bf16[2...) custom-call(f32[1,1,2,512,512]{4,3,2,1,0:T(8,128)} %refs_0_.5, ...), custom_call_target="tpu_custom_call", output_to_operand_aliasing={{4}: (4, {}), {5}: (5, {}), {6}: (6, {})} | custom-call | flops 500000000 | bytes 1 | tf_op jit(solution)/shard_map/first_0/pallas_call | solution.py:173
  5.7 0.1 collective-permute-start.3
  5.8 0.5 %collective-permute-start.4 = (f32[2,16,512]{2,1,0:T(8,128)S(1)}, f32[2,16,512]{2,1,0:T(8,128)S(1)}, u32[]{:S(2)}, u32[]{:S(2)}) collective-permute-start(f32[2,16,512]{2,1,0:T(8,128)S(1)} %get-tuple-element.57), channel_id=1, source_target_pairs={{0,2},{2,0},{4,6},{6,4},{8,10},{10,8},{12,14},{14,12},{16,18},{18,... | collective-permute-start | bytes 196616 | tf_op jit(solution)/shard_map/ppermute | solution.py:359
  6.3 0.1 collective-permute-start
  6.4 0.9 %collective-permute-done.4.refs_1_ = f32[2,16,512]{2,1,0:T(8,128)S(1)} collective-permute-done((f32[2,16,512]{2,1,0:T(8,128)S(1)}, f32[2,16,512]{2,1,0:T(8,128)S(1)}, u32[]{:S(2)}, u32[]{:S(2)}) %collective-permute-start.4) | collective-permute-done | bytes 65568 | tf_op jit(solution)/shard_map/ppermute | solution.py:359
  7.2 0.3 %collective-permute-start.1 = (f32[2,16,512]{2,1,0:T(8,128)S(1)}, f32[2,16,512]{2,1,0:T(8,128)S(1)}, u32[]{:S(2)}, u32[]{:S(2)}) collective-permute-start(f32[2,16,512]{2,1,0:T(8,128)S(1)} %get-tuple-element.52), channel_id=1, source_target_pairs={{0,2},{2,0},{4,6},{6,4},{8,10},{10,8},{12,14},{14,12},{16,18},{18,... | collective-permute-start | bytes 196616 | tf_op jit(solution)/shard_map/ppermute | solution.py:359
  7.6 0.0 collective-permute-done.3.refs_0_
  7.6 0.0 copy-done
  7.6 0.0 copy-done.1
  7.6 0.8 %collective-permute-start.6 = (f32[2,48,512]{2,1,0:T(8,128)S(1)}, f32[2,48,512]{2,1,0:T(8,128)S(1)}, u32[]{:S(2)}, u32[]{:S(2)}) collective-permute-start(f32[2,48,512]{2,1,0:T(8,128)S(1)} %get-tuple-element.62), channel_id=1, source_target_pairs={{0,2},{2,4},{4,0},{6,8},{8,10},{10,12},{12,6},{14,16},{16,18},{18,... | collective-permute-start | bytes 589832 | tf_op jit(solution)/shard_map/ppermute | solution.py:362
  8.4 0.0 collective-permute-done.2.refs_0_
  8.4 0.6 %step_1_0_0.1 = (f32[2,32,512]{2,1,0:T(8,128)S(1)}, f32[2,16,512]{2,1,0:T(8,128)S(1)}, f32[8,512]{1,0:T(8,128)S(1)}) custom-call(f32[2,48,512]{2,1,0:T(8,128)S(1)} %collective-permute-done.2.refs_0_, f32[1,1,5,2,96,512]{5,4,3,2,1,0:T(8,128)S(1)} %copy-done, f32[1,512]{1,0:T(1,128)S(1)} %copy-done.1, ...), custom_call_target="tpu_custom_call", output_to_operand_aliasing={{2}: (7, {})} | custom-call | flops 30000000 | bytes 1 | tf_op jit(solution)/shard_map/step_1_0_0/pallas_call | solution.py:244
  9.0 0.4 %collective-permute-start.11 = (f32[2,16,512]{2,1,0:T(8,128)S(1)}, f32[2,16,512]{2,1,0:T(8,128)S(1)}, u32[]{:S(2)}, u32[]{:S(2)}) collective-permute-start(f32[2,16,512]{2,1,0:T(8,128)S(1)} %get-tuple-element.68), channel_id=1, source_target_pairs={{0,2},{2,0},{4,6},{6,4},{8,10},{10,8},{12,14},{14,12},{16,18},{18,... | collective-permute-start | bytes 196616 | tf_op jit(solution)/shard_map/ppermute | solution.py:359
  9.4 0.0 collective-permute-done.1.refs_1_
  9.4 0.2 collective-permute-start.10
  9.6 0.0 collective-permute-done.refs_0_
  9.6 0.9 %collective-permute-start.5 = (f32[2,48,512]{2,1,0:T(8,128)S(1)}, f32[2,48,512]{2,1,0:T(8,128)S(1)}, u32[]{:S(2)}, u32[]{:S(2)}) collective-permute-start(f32[2,48,512]{2,1,0:T(8,128)S(1)} %get-tuple-element.61), channel_id=1, source_target_pairs={{0,2},{2,4},{4,0},{6,8},{8,10},{10,12},{12,6},{14,16},{16,18},{18,... | collective-permute-start | bytes 589832 | tf_op jit(solution)/shard_map/ppermute | solution.py:362
  10.5 0.0 collective-permute-done.7.refs_0_
  10.5 0.6 %step_1_1_0.1 = (f32[2,32,512]{2,1,0:T(8,128)S(1)}, f32[2,16,512]{2,1,0:T(8,128)S(1)}, f32[8,512]{1,0:T(8,128)S(1)}) custom-call(f32[2,48,512]{2,1,0:T(8,128)S(1)} %collective-permute-done.7.refs_0_, f32[1,1,5,2,96,512]{5,4,3,2,1,0:T(8,128)S(1)} %copy-done, f32[1,512]{1,0:T(1,128)S(1)} %copy-done.1, ...), custom_call_target="tpu_custom_call", output_to_operand_aliasing={{2}: (7, {})} | custom-call | flops 1000000000 | bytes 1 | tf_op jit(solution)/shard_map/step_1_1_0/pallas_call | solution.py:244
  11.1 0.2 collective-permute-start.8
  11.3 0.0 collective-permute-done.11.refs_1_
  11.3 0.3 %collective-permute-start.9 = (f32[2,16,512]{2,1,0:T(8,128)S(1)}, f32[2,16,512]{2,1,0:T(8,128)S(1)}, u32[]{:S(2)}, u32[]{:S(2)}) collective-permute-start(f32[2,16,512]{2,1,0:T(8,128)S(1)} %get-tuple-element.66), channel_id=1, source_target_pairs={{0,2},{2,0},{4,6},{6,4},{8,10},{10,8},{12,14},{14,12},{16,18},{18,... | collective-permute-start | bytes 196616 | tf_op jit(solution)/shard_map/ppermute | solution.py:359
  11.7 0.0 collective-permute-done.10.refs_0_
  11.7 0.8 %collective-permute-start.18 = (f32[2,48,512]{2,1,0:T(8,128)S(1)}, f32[2,48,512]{2,1,0:T(8,128)S(1)}, u32[]{:S(2)}, u32[]{:S(2)}) collective-permute-start(f32[2,48,512]{2,1,0:T(8,128)S(1)} %get-tuple-element.81), channel_id=1, source_target_pairs={{0,2},{2,4},{4,0},{6,8},{8,10},{10,12},{12,6},{14,16},{16,18},{18,... | collective-permute-start | bytes 589832 | tf_op jit(solution)/shard_map/ppermute | solution.py:362
  12.4 0.2 collective-permute-done.9.refs_1_
  12.6 0.0 collective-permute-done.8.refs_0_
  12.6 1.3 %collective-permute-start.17 = (f32[2,48,512]{2,1,0:T(8,128)S(1)}, f32[2,48,512]{2,1,0:T(8,128)S(1)}, u32[]{:S(2)}, u32[]{:S(2)}) collective-permute-start(f32[2,48,512]{2,1,0:T(8,128)S(1)} %get-tuple-element.80), channel_id=1, source_target_pairs={{0,2},{2,4},{4,0},{6,8},{8,10},{10,12},{12,6},{14,16},{16,18},{18,... | collective-permute-start | bytes 589832 | tf_op jit(solution)/shard_map/ppermute | solution.py:362
  13.9 0.0 collective-permute-done.6.refs_0_
  13.9 0.6 %step_2_0_0.1 = (f32[2,32,512]{2,1,0:T(8,128)S(1)}, f32[2,16,512]{2,1,0:T(8,128)S(1)}, f32[8,512]{1,0:T(8,128)S(1)}) custom-call(f32[2,48,512]{2,1,0:T(8,128)S(1)} %collective-permute-done.6.refs_0_, f32[1,1,5,2,96,512]{5,4,3,2,1,0:T(8,128)S(1)} %copy-done, f32[1,512]{1,0:T(1,128)S(1)} %copy-done.1, ...), custom_call_target="tpu_custom_call", output_to_operand_aliasing={{2}: (7, {})} | custom-call | flops 10000000 | bytes 1 | tf_op jit(solution)/shard_map/step_2_0_0/pallas_call | solution.py:244
  14.5 0.1 collective-permute-start.14
  14.6 0.5 %collective-permute-start.15 = (f32[2,16,512]{2,1,0:T(8,128)S(1)}, f32[2,16,512]{2,1,0:T(8,128)S(1)}, u32[]{:S(2)}, u32[]{:S(2)}) collective-permute-start(f32[2,16,512]{2,1,0:T(8,128)S(1)} %get-tuple-element.76), channel_id=1, source_target_pairs={{0,2},{2,0},{4,6},{6,4},{8,10},{10,8},{12,14},{14,12},{16,18},{18,... | collective-permute-start | bytes 196616 | tf_op jit(solution)/shard_map/ppermute | solution.py:359
  15.1 0.7 %collective-permute-done.5.refs_0_ = f32[2,48,512]{2,1,0:T(8,128)S(1)} collective-permute-done((f32[2,48,512]{2,1,0:T(8,128)S(1)}, f32[2,48,512]{2,1,0:T(8,128)S(1)}, u32[]{:S(2)}, u32[]{:S(2)}) %collective-permute-start.5) | collective-permute-done | bytes 196640 | tf_op jit(solution)/shard_map/ppermute | solution.py:362
  15.8 0.6 %step_2_1_0.1 = (f32[2,32,512]{2,1,0:T(8,128)S(1)}, f32[2,16,512]{2,1,0:T(8,128)S(1)}, f32[8,512]{1,0:T(8,128)S(1)}) custom-call(f32[2,48,512]{2,1,0:T(8,128)S(1)} %collective-permute-done.5.refs_0_, f32[1,1,5,2,96,512]{5,4,3,2,1,0:T(8,128)S(1)} %copy-done, f32[1,512]{1,0:T(1,128)S(1)} %copy-done.1, ...), custom_call_target="tpu_custom_call", output_to_operand_aliasing={{2}: (7, {})} | custom-call | flops 30000000 | bytes 1 | tf_op jit(solution)/shard_map/step_2_1_0/pallas_call | solution.py:244
  16.4 0.1 collective-permute-start.12
  16.4 0.0 collective-permute-done.15.refs_1_
  16.5 0.5 %collective-permute-start.13 = (f32[2,16,512]{2,1,0:T(8,128)S(1)}, f32[2,16,512]{2,1,0:T(8,128)S(1)}, u32[]{:S(2)}, u32[]{:S(2)}) collective-permute-start(f32[2,16,512]{2,1,0:T(8,128)S(1)} %get-tuple-element.74), channel_id=1, source_target_pairs={{0,2},{2,0},{4,6},{6,4},{8,10},{10,8},{12,14},{14,12},{16,18},{18,... | collective-permute-start | bytes 196616 | tf_op jit(solution)/shard_map/ppermute | solution.py:359
  16.9 0.0 collective-permute-done.14.refs_0_
  17.0 0.7 %collective-permute-start.21 = (f32[2,48,512]{2,1,0:T(8,128)S(1)}, f32[2,48,512]{2,1,0:T(8,128)S(1)}, u32[]{:S(2)}, u32[]{:S(2)}) collective-permute-start(f32[2,48,512]{2,1,0:T(8,128)S(1)} %get-tuple-element.86), channel_id=1, source_target_pairs={{0,2},{2,4},{4,0},{6,8},{8,10},{10,12},{12,6},{14,16},{16,18},{18,... | collective-permute-start | bytes 589832 | tf_op jit(solution)/shard_map/ppermute | solution.py:362
  17.6 0.2 collective-permute-done.13.refs_1_
  17.9 0.0 collective-permute-done.12.refs_0_
  17.9 1.3 %collective-permute-start.16 = (f32[2,48,512]{2,1,0:T(8,128)S(1)}, f32[2,48,512]{2,1,0:T(8,128)S(1)}, u32[]{:S(2)}, u32[]{:S(2)}) collective-permute-start(f32[2,48,512]{2,1,0:T(8,128)S(1)} %get-tuple-element.79), channel_id=1, source_target_pairs={{2,4},{6,8},{10,12},{14,16},{18,20},{22,24},{26,28},{3,5},{7,9},{1... | collective-permute-start | bytes 589832 | tf_op jit(solution)/shard_map/ppermute | solution.py:362
  19.2 0.0 collective-permute-done.18.refs_0_
  19.2 0.6 %step_3_0_0.1 = (f32[2,32,512]{2,1,0:T(8,128)S(1)}, f32[2,16,512]{2,1,0:T(8,128)S(1)}, f32[8,512]{1,0:T(8,128)S(1)}) custom-call(f32[2,48,512]{2,1,0:T(8,128)S(1)} %collective-permute-done.18.refs_0_, f32[1,1,5,2,96,512]{5,4,3,2,1,0:T(8,128)S(1)} %copy-done, f32[1,512]{1,0:T(1,128)S(1)} %copy-done.1, ...), custom_call_target="tpu_custom_call", output_to_operand_aliasing={{2}: (7, {})} | custom-call | flops 10000000 | bytes 1 | tf_op jit(solution)/shard_map/step_3_0_0/pallas_call | solution.py:244
  19.8 1.2 %collective-permute-start.23 = (f32[2,16,512]{2,1,0:T(8,128)S(1)}, f32[2,16,512]{2,1,0:T(8,128)S(1)}, u32[]{:S(2)}, u32[]{:S(2)}) collective-permute-start(f32[2,16,512]{2,1,0:T(8,128)S(1)} %get-tuple-element.88), channel_id=1, source_target_pairs={{0,2},{2,0},{4,6},{6,4},{8,10},{10,8},{12,14},{14,12},{16,18},{18,... | collective-permute-start | bytes 196616 | tf_op jit(solution)/shard_map/ppermute | solution.py:359
  21.0 0.1 collective-permute-start.22
  21.0 0.0 collective-permute-done.17.refs_0_
  21.0 0.6 %step_3_1_0.1 = (f32[2,32,512]{2,1,0:T(8,128)S(1)}, f32[2,16,512]{2,1,0:T(8,128)S(1)}, f32[8,512]{1,0:T(8,128)S(1)}) custom-call(f32[2,48,512]{2,1,0:T(8,128)S(1)} %collective-permute-done.17.refs_0_, f32[1,1,5,2,96,512]{5,4,3,2,1,0:T(8,128)S(1)} %copy-done, f32[1,512]{1,0:T(1,128)S(1)} %copy-done.1, ...), custom_call_target="tpu_custom_call", output_to_operand_aliasing={{2}: (7, {})} | custom-call | flops 200000000 | bytes 1 | tf_op jit(solution)/shard_map/step_3_1_0/pallas_call | solution.py:244
  21.6 0.1 collective-permute-start.19
  21.7 0.2 collective-permute-done.23.mate_tail
  21.9 0.4 %collective-permute-start.20 = (f32[2,16,512]{2,1,0:T(8,128)S(1)}, f32[2,16,512]{2,1,0:T(8,128)S(1)}, u32[]{:S(2)}, u32[]{:S(2)}) collective-permute-start(f32[2,16,512]{2,1,0:T(8,128)S(1)} %get-tuple-element.85), channel_id=1, source_target_pairs={{0,2},{2,0},{4,6},{6,4},{8,10},{10,8},{12,14},{14,12},{16,18},{18,... | collective-permute-start | bytes 196616 | tf_op jit(solution)/shard_map/ppermute | solution.py:359
  22.2 0.1 collective-permute-done.22.mate
  22.3 0.6 %collective-permute-done.21.above = f32[2,48,512]{2,1,0:T(8,128)S(1)} collective-permute-done((f32[2,48,512]{2,1,0:T(8,128)S(1)}, f32[2,48,512]{2,1,0:T(8,128)S(1)}, u32[]{:S(2)}, u32[]{:S(2)}) %collective-permute-start.21) | collective-permute-done | bytes 196640 | tf_op jit(solution)/shard_map/ppermute | solution.py:362
  22.9 0.6 %last_0.1 = (f32[2,48,512]{2,1,0:T(8,128)S(1)}, f32[8,512]{1,0:T(8,128)S(1)}) custom-call(f32[2,48,512]{2,1,0:T(8,128)S(1)} %collective-permute-done.21.above, f32[2,32,512]{2,1,0:T(8,128)S(1)} %collective-permute-done.22.mate, f32[2,16,512]{2,1,0:T(8,128)S(1)} %collective-permute-done.23.mate_tail, ...), custom_call_target="tpu_custom_call", output_to_operand_aliasing={{1}: (9, {})} | custom-call | flops 100000000 | bytes 1 | tf_op jit(solution)/shard_map/last_0/pallas_call | solution.py:319
  23.5 0.0 collective-permute-done.20.mate_tail
  23.5 0.0 collective-permute-done.19.mate
  23.6 2.2 %collective-permute-done.16.above = f32[2,48,512]{2,1,0:T(8,128)S(1)} collective-permute-done((f32[2,48,512]{2,1,0:T(8,128)S(1)}, f32[2,48,512]{2,1,0:T(8,128)S(1)}, u32[]{:S(2)}, u32[]{:S(2)}) %collective-permute-start.16) | collective-permute-done | bytes 196640 | tf_op jit(solution)/shard_map/ppermute | solution.py:362
  25.8 0.1 gradient.1
  25.8 1.6 %collective-permute-start.24 = (f32[1,256]{1,0:T(1,128)S(1)}, f32[1,256]{1,0:T(1,128)S(1)}, u32[]{:S(2)}, u32[]{:S(2)}) collective-permute-start(f32[1,256]{1,0:T(1,128)S(1)} %get-tuple-element.93), channel_id=1, source_target_pairs={{0,1},{1,0},{2,3},{3,2},{4,5},{5,4},{6,7},{7,6},{8,9},{9,8},{10,11... | collective-permute-start | bytes 3080 | tf_op jit(solution)/shard_map/ppermute | solution.py:398
  27.4 1.3 %last_1.1 = f32[2,96,512]{2,1,0:T(8,128)} custom-call(f32[2,48,512]{2,1,0:T(8,128)S(1)} %collective-permute-done.16.above, f32[2,32,512]{2,1,0:T(8,128)S(1)} %collective-permute-done.19.mate, f32[2,16,512]{2,1,0:T(8,128)S(1)} %collective-permute-done.20.mate_tail, f32[1,1,5,2,96,512]{5,4,3,2,1,0:T(8,128)S(1)} %copy-done, f32[1,512]{1,0:T(1,128)S(1)} %copy-done.1, ...), custom_call_target="tpu_custom_call" | custom-call | flops 1 | bytes 1 | tf_op jit(solution)/shard_map/last_1/pallas_call | solution.py:319
  28.6 0.8 %collective-permute-done.24 = f32[1,256]{1,0:T(1,128)S(1)} collective-permute-done((f32[1,256]{1,0:T(1,128)S(1)}, f32[1,256]{1,0:T(1,128)S(1)}, u32[]{:S(2)}, u32[]{:S(2)}) %collective-permute-start.24) | collective-permute-done | bytes 1056 | tf_op jit(solution)/shard_map/ppermute | solution.py:398
  29.4 0.6 %add.3 = f32[1,256]{1,0:T(1,128)} add(f32[1,256]{1,0:T(1,128)S(1)} %get-tuple-element.92, f32[1,256]{1,0:T(1,128)S(1)} %collective-permute-done.24) | non-fusion elementwise | flops 256 | bytes 3072 | tf_op jit(solution)/shard_map/add | solution.py:398
  (12 shorter events, 0.0 us)
Async XLA Ops:
  0.7 7.7 %collective-permute-start.2 = (f32[2,48,512]{2,1,0:T(8,128)S(1)}, f32[2,48,512]{2,1,0:T(8,128)S(1)}, u32[]{:S(2)}, u32[]{:S(2)}) collective-permute-start(f32[2,48,512]{2,1,0:T(8,128)S(1)} %get-tuple-element.55), channel_id=1, source_target_pairs={{0,2},{2,4},{4,0},{6,8},{8,10},{10,12},{12,6},{14,16},{16,18},{18,... | collective-permute-start | bytes 589832 | tf_op jit(solution)/shard_map/ppermute | solution.py:362
  3.0 7.5 %collective-permute-start.7 = (f32[2,48,512]{2,1,0:T(8,128)S(1)}, f32[2,48,512]{2,1,0:T(8,128)S(1)}, u32[]{:S(2)}, u32[]{:S(2)}) collective-permute-start(f32[2,48,512]{2,1,0:T(8,128)S(1)} %get-tuple-element.63), channel_id=1, source_target_pairs={{0,2},{2,4},{4,0},{6,8},{8,10},{10,12},{12,6},{14,16},{16,18},{18,... | collective-permute-start | bytes 589832 | tf_op jit(solution)/shard_map/ppermute | solution.py:362
  3.1 4.5 %copy-start = (f32[1,1,5,2,96,512]{5,4,3,2,1,0:T(8,128)S(1)}, f32[1,1,5,2,96,512]{5,4,3,2,1,0:T(8,128)}, u32[]{:S(2)}) copy-start(f32[1,1,5,2,96,512]{5,4,3,2,1,0:T(8,128)} %residual.1) | copy-start | bytes 5898244
  3.1 4.5 %copy-start.1 = (f32[1,512]{1,0:T(1,128)S(1)}, f32[1,512]{1,0:T(1,128)}, u32[]{:S(2)}) copy-start(f32[1,512]{1,0:T(1,128)} %contrast.1) | copy-start | bytes 6148
  3.1 4.5 %copy-start.2 = (s32[4,96]{1,0:T(4,128)S(1)}, s32[4,96]{1,0:T(4,128)}, u32[]{:S(2)}) copy-start(s32[4,96]{1,0:T(4,128)} %sites.1) | copy-start | bytes 4612
  3.1 4.5 %copy-start.3 = (f32[1,4,2]{1,2,0:T(2,128)S(1)}, f32[1,4,2]{1,2,0:T(2,128)}, u32[]{:S(2)}) copy-start(f32[1,4,2]{1,2,0:T(2,128)} %param.11) | copy-start | bytes 100
  5.7 1.8 %collective-permute-start.3 = (f32[2,32,512]{2,1,0:T(8,128)S(1)}, f32[2,32,512]{2,1,0:T(8,128)S(1)}, u32[]{:S(2)}, u32[]{:S(2)}) collective-permute-start(f32[2,32,512]{2,1,0:T(8,128)S(1)} %get-tuple-element.56), channel_id=1, source_target_pairs={{0,2},{2,0},{4,6},{6,4},{8,10},{10,8},{12,14},{14,12},{16,18},{18,... | collective-permute-start | bytes 393224 | tf_op jit(solution)/shard_map/ppermute | solution.py:359
  5.8 1.4 %collective-permute-start.4 = (f32[2,16,512]{2,1,0:T(8,128)S(1)}, f32[2,16,512]{2,1,0:T(8,128)S(1)}, u32[]{:S(2)}, u32[]{:S(2)}) collective-permute-start(f32[2,16,512]{2,1,0:T(8,128)S(1)} %get-tuple-element.57), channel_id=1, source_target_pairs={{0,2},{2,0},{4,6},{6,4},{8,10},{10,8},{12,14},{14,12},{16,18},{18,... | collective-permute-start | bytes 196616 | tf_op jit(solution)/shard_map/ppermute | solution.py:359
  6.3 3.3 %collective-permute-start = (f32[2,32,512]{2,1,0:T(8,128)S(1)}, f32[2,32,512]{2,1,0:T(8,128)S(1)}, u32[]{:S(2)}, u32[]{:S(2)}) collective-permute-start(f32[2,32,512]{2,1,0:T(8,128)S(1)} %get-tuple-element.51), channel_id=1, source_target_pairs={{0,2},{2,0},{4,6},{6,4},{8,10},{10,8},{12,14},{14,12},{16,18},{18,... | collective-permute-start | bytes 393224 | tf_op jit(solution)/shard_map/ppermute | solution.py:359
  7.2 2.1 %collective-permute-start.1 = (f32[2,16,512]{2,1,0:T(8,128)S(1)}, f32[2,16,512]{2,1,0:T(8,128)S(1)}, u32[]{:S(2)}, u32[]{:S(2)}) collective-permute-start(f32[2,16,512]{2,1,0:T(8,128)S(1)} %get-tuple-element.52), channel_id=1, source_target_pairs={{0,2},{2,0},{4,6},{6,4},{8,10},{10,8},{12,14},{14,12},{16,18},{18,... | collective-permute-start | bytes 196616 | tf_op jit(solution)/shard_map/ppermute | solution.py:359
  7.6 6.3 %collective-permute-start.6 = (f32[2,48,512]{2,1,0:T(8,128)S(1)}, f32[2,48,512]{2,1,0:T(8,128)S(1)}, u32[]{:S(2)}, u32[]{:S(2)}) collective-permute-start(f32[2,48,512]{2,1,0:T(8,128)S(1)} %get-tuple-element.62), channel_id=1, source_target_pairs={{0,2},{2,4},{4,0},{6,8},{8,10},{10,12},{12,6},{14,16},{16,18},{18,... | collective-permute-start | bytes 589832 | tf_op jit(solution)/shard_map/ppermute | solution.py:362
  9.0 2.3 %collective-permute-start.11 = (f32[2,16,512]{2,1,0:T(8,128)S(1)}, f32[2,16,512]{2,1,0:T(8,128)S(1)}, u32[]{:S(2)}, u32[]{:S(2)}) collective-permute-start(f32[2,16,512]{2,1,0:T(8,128)S(1)} %get-tuple-element.68), channel_id=1, source_target_pairs={{0,2},{2,0},{4,6},{6,4},{8,10},{10,8},{12,14},{14,12},{16,18},{18,... | collective-permute-start | bytes 196616 | tf_op jit(solution)/shard_map/ppermute | solution.py:359
  9.4 2.3 %collective-permute-start.10 = (f32[2,32,512]{2,1,0:T(8,128)S(1)}, f32[2,32,512]{2,1,0:T(8,128)S(1)}, u32[]{:S(2)}, u32[]{:S(2)}) collective-permute-start(f32[2,32,512]{2,1,0:T(8,128)S(1)} %get-tuple-element.67), channel_id=1, source_target_pairs={{0,2},{2,0},{4,6},{6,4},{8,10},{10,8},{12,14},{14,12},{16,18},{18,... | collective-permute-start | bytes 393224 | tf_op jit(solution)/shard_map/ppermute | solution.py:359
  9.6 6.2 %collective-permute-start.5 = (f32[2,48,512]{2,1,0:T(8,128)S(1)}, f32[2,48,512]{2,1,0:T(8,128)S(1)}, u32[]{:S(2)}, u32[]{:S(2)}) collective-permute-start(f32[2,48,512]{2,1,0:T(8,128)S(1)} %get-tuple-element.61), channel_id=1, source_target_pairs={{0,2},{2,4},{4,0},{6,8},{8,10},{10,12},{12,6},{14,16},{16,18},{18,... | collective-permute-start | bytes 589832 | tf_op jit(solution)/shard_map/ppermute | solution.py:362
  11.1 1.5 %collective-permute-start.8 = (f32[2,32,512]{2,1,0:T(8,128)S(1)}, f32[2,32,512]{2,1,0:T(8,128)S(1)}, u32[]{:S(2)}, u32[]{:S(2)}) collective-permute-start(f32[2,32,512]{2,1,0:T(8,128)S(1)} %get-tuple-element.65), channel_id=1, source_target_pairs={{0,2},{2,0},{4,6},{6,4},{8,10},{10,8},{12,14},{14,12},{16,18},{18,... | collective-permute-start | bytes 393224 | tf_op jit(solution)/shard_map/ppermute | solution.py:359
  11.3 1.3 %collective-permute-start.9 = (f32[2,16,512]{2,1,0:T(8,128)S(1)}, f32[2,16,512]{2,1,0:T(8,128)S(1)}, u32[]{:S(2)}, u32[]{:S(2)}) collective-permute-start(f32[2,16,512]{2,1,0:T(8,128)S(1)} %get-tuple-element.66), channel_id=1, source_target_pairs={{0,2},{2,0},{4,6},{6,4},{8,10},{10,8},{12,14},{14,12},{16,18},{18,... | collective-permute-start | bytes 196616 | tf_op jit(solution)/shard_map/ppermute | solution.py:359
  11.7 7.5 %collective-permute-start.18 = (f32[2,48,512]{2,1,0:T(8,128)S(1)}, f32[2,48,512]{2,1,0:T(8,128)S(1)}, u32[]{:S(2)}, u32[]{:S(2)}) collective-permute-start(f32[2,48,512]{2,1,0:T(8,128)S(1)} %get-tuple-element.81), channel_id=1, source_target_pairs={{0,2},{2,4},{4,0},{6,8},{8,10},{10,12},{12,6},{14,16},{16,18},{18,... | collective-permute-start | bytes 589832 | tf_op jit(solution)/shard_map/ppermute | solution.py:362
  12.6 8.5 %collective-permute-start.17 = (f32[2,48,512]{2,1,0:T(8,128)S(1)}, f32[2,48,512]{2,1,0:T(8,128)S(1)}, u32[]{:S(2)}, u32[]{:S(2)}) collective-permute-start(f32[2,48,512]{2,1,0:T(8,128)S(1)} %get-tuple-element.80), channel_id=1, source_target_pairs={{0,2},{2,4},{4,0},{6,8},{8,10},{10,12},{12,6},{14,16},{16,18},{18,... | collective-permute-start | bytes 589832 | tf_op jit(solution)/shard_map/ppermute | solution.py:362
  14.5 2.5 %collective-permute-start.14 = (f32[2,32,512]{2,1,0:T(8,128)S(1)}, f32[2,32,512]{2,1,0:T(8,128)S(1)}, u32[]{:S(2)}, u32[]{:S(2)}) collective-permute-start(f32[2,32,512]{2,1,0:T(8,128)S(1)} %get-tuple-element.75), channel_id=1, source_target_pairs={{0,2},{2,0},{4,6},{6,4},{8,10},{10,8},{12,14},{14,12},{16,18},{18,... | collective-permute-start | bytes 393224 | tf_op jit(solution)/shard_map/ppermute | solution.py:359
  14.6 1.9 %collective-permute-start.15 = (f32[2,16,512]{2,1,0:T(8,128)S(1)}, f32[2,16,512]{2,1,0:T(8,128)S(1)}, u32[]{:S(2)}, u32[]{:S(2)}) collective-permute-start(f32[2,16,512]{2,1,0:T(8,128)S(1)} %get-tuple-element.76), channel_id=1, source_target_pairs={{0,2},{2,0},{4,6},{6,4},{8,10},{10,8},{12,14},{14,12},{16,18},{18,... | collective-permute-start | bytes 196616 | tf_op jit(solution)/shard_map/ppermute | solution.py:359
  16.4 1.5 %collective-permute-start.12 = (f32[2,32,512]{2,1,0:T(8,128)S(1)}, f32[2,32,512]{2,1,0:T(8,128)S(1)}, u32[]{:S(2)}, u32[]{:S(2)}) collective-permute-start(f32[2,32,512]{2,1,0:T(8,128)S(1)} %get-tuple-element.73), channel_id=1, source_target_pairs={{0,2},{2,0},{4,6},{6,4},{8,10},{10,8},{12,14},{14,12},{16,18},{18,... | collective-permute-start | bytes 393224 | tf_op jit(solution)/shard_map/ppermute | solution.py:359
  16.5 1.4 %collective-permute-start.13 = (f32[2,16,512]{2,1,0:T(8,128)S(1)}, f32[2,16,512]{2,1,0:T(8,128)S(1)}, u32[]{:S(2)}, u32[]{:S(2)}) collective-permute-start(f32[2,16,512]{2,1,0:T(8,128)S(1)} %get-tuple-element.74), channel_id=1, source_target_pairs={{0,2},{2,0},{4,6},{6,4},{8,10},{10,8},{12,14},{14,12},{16,18},{18,... | collective-permute-start | bytes 196616 | tf_op jit(solution)/shard_map/ppermute | solution.py:359
  17.0 6.0 %collective-permute-start.21 = (f32[2,48,512]{2,1,0:T(8,128)S(1)}, f32[2,48,512]{2,1,0:T(8,128)S(1)}, u32[]{:S(2)}, u32[]{:S(2)}) collective-permute-start(f32[2,48,512]{2,1,0:T(8,128)S(1)} %get-tuple-element.86), channel_id=1, source_target_pairs={{0,2},{2,4},{4,0},{6,8},{8,10},{10,12},{12,6},{14,16},{16,18},{18,... | collective-permute-start | bytes 589832 | tf_op jit(solution)/shard_map/ppermute | solution.py:362
  17.9 7.9 %collective-permute-start.16 = (f32[2,48,512]{2,1,0:T(8,128)S(1)}, f32[2,48,512]{2,1,0:T(8,128)S(1)}, u32[]{:S(2)}, u32[]{:S(2)}) collective-permute-start(f32[2,48,512]{2,1,0:T(8,128)S(1)} %get-tuple-element.79), channel_id=1, source_target_pairs={{2,4},{6,8},{10,12},{14,16},{18,20},{22,24},{26,28},{3,5},{7,9},{1... | collective-permute-start | bytes 589832 | tf_op jit(solution)/shard_map/ppermute | solution.py:362
  19.8 2.1 %collective-permute-start.23 = (f32[2,16,512]{2,1,0:T(8,128)S(1)}, f32[2,16,512]{2,1,0:T(8,128)S(1)}, u32[]{:S(2)}, u32[]{:S(2)}) collective-permute-start(f32[2,16,512]{2,1,0:T(8,128)S(1)} %get-tuple-element.88), channel_id=1, source_target_pairs={{0,2},{2,0},{4,6},{6,4},{8,10},{10,8},{12,14},{14,12},{16,18},{18,... | collective-permute-start | bytes 196616 | tf_op jit(solution)/shard_map/ppermute | solution.py:359
  21.0 1.3 %collective-permute-start.22 = (f32[2,32,512]{2,1,0:T(8,128)S(1)}, f32[2,32,512]{2,1,0:T(8,128)S(1)}, u32[]{:S(2)}, u32[]{:S(2)}) collective-permute-start(f32[2,32,512]{2,1,0:T(8,128)S(1)} %get-tuple-element.87), channel_id=1, source_target_pairs={{0,2},{2,0},{4,6},{6,4},{8,10},{10,8},{12,14},{14,12},{16,18},{18,... | collective-permute-start | bytes 393224 | tf_op jit(solution)/shard_map/ppermute | solution.py:359
  21.6 1.9 %collective-permute-start.19 = (f32[2,32,512]{2,1,0:T(8,128)S(1)}, f32[2,32,512]{2,1,0:T(8,128)S(1)}, u32[]{:S(2)}, u32[]{:S(2)}) collective-permute-start(f32[2,32,512]{2,1,0:T(8,128)S(1)} %get-tuple-element.84), channel_id=1, source_target_pairs={{0,2},{2,0},{4,6},{6,4},{8,10},{10,8},{12,14},{14,12},{16,18},{18,... | collective-permute-start | bytes 393224 | tf_op jit(solution)/shard_map/ppermute | solution.py:359
  21.9 1.7 %collective-permute-start.20 = (f32[2,16,512]{2,1,0:T(8,128)S(1)}, f32[2,16,512]{2,1,0:T(8,128)S(1)}, u32[]{:S(2)}, u32[]{:S(2)}) collective-permute-start(f32[2,16,512]{2,1,0:T(8,128)S(1)} %get-tuple-element.85), channel_id=1, source_target_pairs={{0,2},{2,0},{4,6},{6,4},{8,10},{10,8},{12,14},{14,12},{16,18},{18,... | collective-permute-start | bytes 196616 | tf_op jit(solution)/shard_map/ppermute | solution.py:359
  25.8 3.6 %collective-permute-start.24 = (f32[1,256]{1,0:T(1,128)S(1)}, f32[1,256]{1,0:T(1,128)S(1)}, u32[]{:S(2)}, u32[]{:S(2)}) collective-permute-start(f32[1,256]{1,0:T(1,128)S(1)} %get-tuple-element.93), channel_id=1, source_target_pairs={{0,1},{1,0},{2,3},{3,2},{4,5},{5,4},{6,7},{7,6},{8,9},{9,8},{10,11... | collective-permute-start | bytes 3080 | tf_op jit(solution)/shard_map/ppermute | solution.py:398

commit v12 on v11

--- a/solution.py
+++ b/solution.py
@@ -10,6 +10,7 @@
 
 TICKS = 5
 HALVES = 2
+SHARES = 4
 TAIL = 16
 VMEM_LIMIT = 24 * 1024 * 1024
 WEIGHTS = {
@@ -124,24 +125,27 @@
 
     @when_parity(parity)
     def _():
-        copies = [
-            pltpu.make_async_copy(contrast, reflect, sems.at[0]),
-            pltpu.make_async_copy(residual.at[0, 0, 0], wave, sems.at[1]),
-            pltpu.make_async_copy(panel.at[0, 0], arrived, sems.at[2]),
-        ]
-        pieces = [(part, pl.ds(half * depth, depth)) for half in range(2) for part in range(2)]
-        for place, (part, rows) in enumerate(pieces):
-            copies.append(
-                pltpu.make_async_copy(operator.at[0, 0, part, rows], whole.at[part, rows], sems.at[3 + place])
-            )
+        copies = [pltpu.make_async_copy(contrast, reflect, sems.at[0])]
+        for part in range(2):
+            copies.append(pltpu.make_async_copy(residual.at[0, 0, 0, part], wave.at[part], sems.at[1 + part]))
+            copies.append(pltpu.make_async_copy(panel.at[0, 0, part], arrived.at[part], sems.at[3 + part]))
+        early = len(copies)
+        pieces = [(part, half * depth) for half in range(2) for part in range(2)]
+        for part, row in pieces:
+            for shift in range(0, depth, depth // SHARES):
+                rows = pl.ds(row + shift, depth // SHARES)
+                source, target = operator.at[0, 0, part, rows], whole.at[part, rows]
+                copies.append(pltpu.make_async_copy(source, target, sems.at[len(copies)]))
         for copy in copies:
             copy.start()
-        for copy in copies[:3]:
+        for copy in copies[:early]:
             copy.wait()
         take(arrived, 0, wave, reflect, None, grad, left)
         sums = [None, None]
-        for place, (part, rows) in enumerate(pieces):
-            copies[3 + place].wait()
+        for place, (part, row) in enumerate(pieces):
+            rows = pl.ds(row, depth)
+            for copy in copies[early + place * SHARES : early + (place + 1) * SHARES]:
+                copy.wait()
             upper, lower = split(whole[part, rows])
             high[part, rows] = upper
             low[part, rows] = lower
@@ -181,7 +185,7 @@
             pltpu.VMEM((2, shots, breadth), jnp.float32),
             pltpu.VMEM((2, shots, breadth), jnp.float32),
             pltpu.VMEM((4 * shots, breadth), jnp.bfloat16),
-            pltpu.SemaphoreType.DMA((7,)),
+            pltpu.SemaphoreType.DMA((5 + 4 * SHARES,)),
         ],
         input_output_aliases={4 + i: len(outs) + i for i in range(len(carried))},
         compiler_params=PARAMS,

time: 30.2 us -> 30.6 us (1.013)
  the two profiles are of different devices: /device:TPU:16 before, /device:TPU:24 now
where the time goes in v12:
time: 30.6 us; the launch traced here: 30.5 us
  starting transfers between devices  14.2 us (46%)
  Pallas kernels  8.48 us (28%)
  waiting for transfers between devices  6.37 us (21%)
  between operations  0.82 us (3%)
  other arithmetic  0.56 us (2%)
    ppermute x8, starting transfers between devices, down(): return lax.ppermute(piece, 'depth', down_route if closed else open_route)  7.98 us
    ppermute x16, starting transfers between devices, mate(): return [lax.ppermute(piece, 'depth', mate_route) for piece in pieces]  4.69 us
    ppermute x8, waiting for transfers between devices, down(): return lax.ppermute(piece, 'depth', down_route if closed else open_route)  3.97 us
    pallas_call x12, Pallas kernels, step(): pl.pallas_call(functools.partial(step_kernel, tick, start, parity, len(pi...  3.52 us
    pallas_call x2, Pallas kernels, first(): pl.pallas_call(functools.partial(first_kernel, parity, bool(carried)), ou...  3.06 us
    pallas_call x2, Pallas kernels, last(): pl.pallas_call(functools.partial(last_kernel, half), out_shape=out_shape,...  1.85 us
    ppermute x16, waiting for transfers between devices, mate(): return [lax.ppermute(piece, 'depth', mate_route) for piece in pieces]  1.6 us
    ppermute x1, starting transfers between devices, local(): gradient = gradient + lax.ppermute(chunks[distance], 'freq', route)  1.55 us
  transfers between devices with their start and end apart: 25, of which 9 were waited for; matrix products, arithmetic and copies ran while one was open for 0% of the time, Pallas kernels for 27%

profile of v12, /device:TPU:24, one launch (start us, length us, event | category | flops | bytes accessed | tf_op | source)
XLA Modules:
  0.0 30.5 jit_solution(4413330763408969459)
XLA Ops:
  0.6 0.2 first_1.1
  0.8 2.4 %collective-permute-start.2 = (f32[2,48,512]{2,1,0:T(8,128)S(1)}, f32[2,48,512]{2,1,0:T(8,128)S(1)}, u32[]{:S(2)}, u32[]{:S(2)}) collective-permute-start(f32[2,48,512]{2,1,0:T(8,128)S(1)} %get-tuple-element.55), channel_id=1, source_target_pairs={{0,2},{2,4},{4,0},{6,8},{8,10},{10,12},{12,6},{14,16},{16,18},{18,... | collective-permute-start | bytes 589832 | tf_op jit(solution)/shard_map/ppermute | solution.py:366
  3.2 0.1 collective-permute-start.7
  3.3 2.8 %first_0.1 = (f32[2,32,512]{2,1,0:T(8,128)S(1)}, f32[2,16,512]{2,1,0:T(8,128)S(1)}, f32[2,32,512]{2,1,0:T(8,128)S(1)}, f32[2,16,512]{2,1,0:T(8,128)S(1)}, bf16[2...) custom-call(f32[1,1,2,512,512]{4,3,2,1,0:T(8,128)} %refs_0_.5, ...), custom_call_target="tpu_custom_call", output_to_operand_aliasing={{4}: (4, {}), {5}: (5, {}), {6}: (6, {})} | custom-call | flops 500000000 | bytes 1 | tf_op jit(solution)/shard_map/first_0/pallas_call | solution.py:177
  6.2 0.1 collective-permute-start.3
  6.3 0.5 %collective-permute-start.4 = (f32[2,16,512]{2,1,0:T(8,128)S(1)}, f32[2,16,512]{2,1,0:T(8,128)S(1)}, u32[]{:S(2)}, u32[]{:S(2)}) collective-permute-start(f32[2,16,512]{2,1,0:T(8,128)S(1)} %get-tuple-element.57), channel_id=1, source_target_pairs={{0,2},{2,0},{4,6},{6,4},{8,10},{10,8},{12,14},{14,12},{16,18},{18,... | collective-permute-start | bytes 196616 | tf_op jit(solution)/shard_map/ppermute | solution.py:363
  6.8 0.1 collective-permute-start
  6.8 0.9 %collective-permute-done.4.refs_1_ = f32[2,16,512]{2,1,0:T(8,128)S(1)} collective-permute-done((f32[2,16,512]{2,1,0:T(8,128)S(1)}, f32[2,16,512]{2,1,0:T(8,128)S(1)}, u32[]{:S(2)}, u32[]{:S(2)}) %collective-permute-start.4) | collective-permute-done | bytes 65568 | tf_op jit(solution)/shard_map/ppermute | solution.py:363
  7.7 0.3 %collective-permute-start.1 = (f32[2,16,512]{2,1,0:T(8,128)S(1)}, f32[2,16,512]{2,1,0:T(8,128)S(1)}, u32[]{:S(2)}, u32[]{:S(2)}) collective-permute-start(f32[2,16,512]{2,1,0:T(8,128)S(1)} %get-tuple-element.52), channel_id=1, source_target_pairs={{0,2},{2,0},{4,6},{6,4},{8,10},{10,8},{12,14},{14,12},{16,18},{18,... | collective-permute-start | bytes 196616 | tf_op jit(solution)/shard_map/ppermute | solution.py:363
  8.0 0.0 collective-permute-done.3.refs_0_
  8.0 0.0 copy-done
  8.0 0.0 copy-done.1
  8.1 0.8 %collective-permute-start.6 = (f32[2,48,512]{2,1,0:T(8,128)S(1)}, f32[2,48,512]{2,1,0:T(8,128)S(1)}, u32[]{:S(2)}, u32[]{:S(2)}) collective-permute-start(f32[2,48,512]{2,1,0:T(8,128)S(1)} %get-tuple-element.62), channel_id=1, source_target_pairs={{0,2},{2,4},{4,0},{6,8},{8,10},{10,12},{12,6},{14,16},{16,18},{18,... | collective-permute-start | bytes 589832 | tf_op jit(solution)/shard_map/ppermute | solution.py:366
  8.8 0.0 collective-permute-done.2.refs_0_
  8.8 0.6 %step_1_0_0.1 = (f32[2,32,512]{2,1,0:T(8,128)S(1)}, f32[2,16,512]{2,1,0:T(8,128)S(1)}, f32[8,512]{1,0:T(8,128)S(1)}) custom-call(f32[2,48,512]{2,1,0:T(8,128)S(1)} %collective-permute-done.2.refs_0_, f32[1,1,5,2,96,512]{5,4,3,2,1,0:T(8,128)S(1)} %copy-done, f32[1,512]{1,0:T(1,128)S(1)} %copy-done.1, ...), custom_call_target="tpu_custom_call", output_to_operand_aliasing={{2}: (7, {})} | custom-call | flops 30000000 | bytes 1 | tf_op jit(solution)/shard_map/step_1_0_0/pallas_call | solution.py:248
  9.4 0.4 %collective-permute-start.11 = (f32[2,16,512]{2,1,0:T(8,128)S(1)}, f32[2,16,512]{2,1,0:T(8,128)S(1)}, u32[]{:S(2)}, u32[]{:S(2)}) collective-permute-start(f32[2,16,512]{2,1,0:T(8,128)S(1)} %get-tuple-element.68), channel_id=1, source_target_pairs={{0,2},{2,0},{4,6},{6,4},{8,10},{10,8},{12,14},{14,12},{16,18},{18,... | collective-permute-start | bytes 196616 | tf_op jit(solution)/shard_map/ppermute | solution.py:363
  9.9 0.0 collective-permute-done.1.refs_1_
  9.9 0.1 collective-permute-start.10
  10.0 0.0 collective-permute-done.refs_0_
  10.0 1.0 %collective-permute-start.5 = (f32[2,48,512]{2,1,0:T(8,128)S(1)}, f32[2,48,512]{2,1,0:T(8,128)S(1)}, u32[]{:S(2)}, u32[]{:S(2)}) collective-permute-start(f32[2,48,512]{2,1,0:T(8,128)S(1)} %get-tuple-element.61), channel_id=1, source_target_pairs={{0,2},{2,4},{4,0},{6,8},{8,10},{10,12},{12,6},{14,16},{16,18},{18,... | collective-permute-start | bytes 589832 | tf_op jit(solution)/shard_map/ppermute | solution.py:366
  11.0 0.0 collective-permute-done.7.refs_0_
  11.0 0.6 %step_1_1_0.1 = (f32[2,32,512]{2,1,0:T(8,128)S(1)}, f32[2,16,512]{2,1,0:T(8,128)S(1)}, f32[8,512]{1,0:T(8,128)S(1)}) custom-call(f32[2,48,512]{2,1,0:T(8,128)S(1)} %collective-permute-done.7.refs_0_, f32[1,1,5,2,96,512]{5,4,3,2,1,0:T(8,128)S(1)} %copy-done, f32[1,512]{1,0:T(1,128)S(1)} %copy-done.1, ...), custom_call_target="tpu_custom_call", output_to_operand_aliasing={{2}: (7, {})} | custom-call | flops 1000000000 | bytes 1 | tf_op jit(solution)/shard_map/step_1_1_0/pallas_call | solution.py:248
  11.6 0.2 collective-permute-start.8
  11.8 0.0 collective-permute-done.11.refs_1_
  11.8 0.4 %collective-permute-start.9 = (f32[2,16,512]{2,1,0:T(8,128)S(1)}, f32[2,16,512]{2,1,0:T(8,128)S(1)}, u32[]{:S(2)}, u32[]{:S(2)}) collective-permute-start(f32[2,16,512]{2,1,0:T(8,128)S(1)} %get-tuple-element.66), channel_id=1, source_target_pairs={{0,2},{2,0},{4,6},{6,4},{8,10},{10,8},{12,14},{14,12},{16,18},{18,... | collective-permute-start | bytes 196616 | tf_op jit(solution)/shard_map/ppermute | solution.py:363
  12.2 0.0 collective-permute-done.10.refs_0_
  12.2 0.7 %collective-permute-start.18 = (f32[2,48,512]{2,1,0:T(8,128)S(1)}, f32[2,48,512]{2,1,0:T(8,128)S(1)}, u32[]{:S(2)}, u32[]{:S(2)}) collective-permute-start(f32[2,48,512]{2,1,0:T(8,128)S(1)} %get-tuple-element.81), channel_id=1, source_target_pairs={{0,2},{2,4},{4,0},{6,8},{8,10},{10,12},{12,6},{14,16},{16,18},{18,... | collective-permute-start | bytes 589832 | tf_op jit(solution)/shard_map/ppermute | solution.py:366
  12.9 0.2 collective-permute-done.9.refs_1_
  13.1 0.0 collective-permute-done.8.refs_0_
  13.1 1.1 %collective-permute-start.17 = (f32[2,48,512]{2,1,0:T(8,128)S(1)}, f32[2,48,512]{2,1,0:T(8,128)S(1)}, u32[]{:S(2)}, u32[]{:S(2)}) collective-permute-start(f32[2,48,512]{2,1,0:T(8,128)S(1)} %get-tuple-element.80), channel_id=1, source_target_pairs={{0,2},{2,4},{4,0},{6,8},{8,10},{10,12},{12,6},{14,16},{16,18},{18,... | collective-permute-start | bytes 589832 | tf_op jit(solution)/shard_map/ppermute | solution.py:366
  14.2 0.0 collective-permute-done.6.refs_0_
  14.2 0.6 %step_2_0_0.1 = (f32[2,32,512]{2,1,0:T(8,128)S(1)}, f32[2,16,512]{2,1,0:T(8,128)S(1)}, f32[8,512]{1,0:T(8,128)S(1)}) custom-call(f32[2,48,512]{2,1,0:T(8,128)S(1)} %collective-permute-done.6.refs_0_, f32[1,1,5,2,96,512]{5,4,3,2,1,0:T(8,128)S(1)} %copy-done, f32[1,512]{1,0:T(1,128)S(1)} %copy-done.1, ...), custom_call_target="tpu_custom_call", output_to_operand_aliasing={{2}: (7, {})} | custom-call | flops 10000000 | bytes 1 | tf_op jit(solution)/shard_map/step_2_0_0/pallas_call | solution.py:248
  14.8 0.1 collective-permute-start.14
  14.9 0.5 %collective-permute-start.15 = (f32[2,16,512]{2,1,0:T(8,128)S(1)}, f32[2,16,512]{2,1,0:T(8,128)S(1)}, u32[]{:S(2)}, u32[]{:S(2)}) collective-permute-start(f32[2,16,512]{2,1,0:T(8,128)S(1)} %get-tuple-element.76), channel_id=1, source_target_pairs={{0,2},{2,0},{4,6},{6,4},{8,10},{10,8},{12,14},{14,12},{16,18},{18,... | collective-permute-start | bytes 196616 | tf_op jit(solution)/shard_map/ppermute | solution.py:363
  15.4 0.9 %collective-permute-done.5.refs_0_ = f32[2,48,512]{2,1,0:T(8,128)S(1)} collective-permute-done((f32[2,48,512]{2,1,0:T(8,128)S(1)}, f32[2,48,512]{2,1,0:T(8,128)S(1)}, u32[]{:S(2)}, u32[]{:S(2)}) %collective-permute-start.5) | collective-permute-done | bytes 196640 | tf_op jit(solution)/shard_map/ppermute | solution.py:366
  16.2 0.6 %step_2_1_0.1 = (f32[2,32,512]{2,1,0:T(8,128)S(1)}, f32[2,16,512]{2,1,0:T(8,128)S(1)}, f32[8,512]{1,0:T(8,128)S(1)}) custom-call(f32[2,48,512]{2,1,0:T(8,128)S(1)} %collective-permute-done.5.refs_0_, f32[1,1,5,2,96,512]{5,4,3,2,1,0:T(8,128)S(1)} %copy-done, f32[1,512]{1,0:T(1,128)S(1)} %copy-done.1, ...), custom_call_target="tpu_custom_call", output_to_operand_aliasing={{2}: (7, {})} | custom-call | flops 30000000 | bytes 1 | tf_op jit(solution)/shard_map/step_2_1_0/pallas_call | solution.py:248
  16.8 0.1 collective-permute-start.12
  16.9 0.0 collective-permute-done.15.refs_1_
  16.9 0.5 %collective-permute-start.13 = (f32[2,16,512]{2,1,0:T(8,128)S(1)}, f32[2,16,512]{2,1,0:T(8,128)S(1)}, u32[]{:S(2)}, u32[]{:S(2)}) collective-permute-start(f32[2,16,512]{2,1,0:T(8,128)S(1)} %get-tuple-element.74), channel_id=1, source_target_pairs={{0,2},{2,0},{4,6},{6,4},{8,10},{10,8},{12,14},{14,12},{16,18},{18,... | collective-permute-start | bytes 196616 | tf_op jit(solution)/shard_map/ppermute | solution.py:363
  17.4 0.0 collective-permute-done.14.refs_0_
  17.4 0.7 %collective-permute-start.21 = (f32[2,48,512]{2,1,0:T(8,128)S(1)}, f32[2,48,512]{2,1,0:T(8,128)S(1)}, u32[]{:S(2)}, u32[]{:S(2)}) collective-permute-start(f32[2,48,512]{2,1,0:T(8,128)S(1)} %get-tuple-element.86), channel_id=1, source_target_pairs={{0,2},{2,4},{4,0},{6,8},{8,10},{10,12},{12,6},{14,16},{16,18},{18,... | collective-permute-start | bytes 589832 | tf_op jit(solution)/shard_map/ppermute | solution.py:366
  18.1 0.2 collective-permute-done.13.refs_1_
  18.3 0.0 collective-permute-done.12.refs_0_
  18.3 1.3 %collective-permute-start.16 = (f32[2,48,512]{2,1,0:T(8,128)S(1)}, f32[2,48,512]{2,1,0:T(8,128)S(1)}, u32[]{:S(2)}, u32[]{:S(2)}) collective-permute-start(f32[2,48,512]{2,1,0:T(8,128)S(1)} %get-tuple-element.79), channel_id=1, source_target_pairs={{2,4},{6,8},{10,12},{14,16},{18,20},{22,24},{26,28},{3,5},{7,9},{1... | collective-permute-start | bytes 589832 | tf_op jit(solution)/shard_map/ppermute | solution.py:366
  19.6 0.0 collective-permute-done.18.refs_0_
  19.6 0.6 %step_3_0_0.1 = (f32[2,32,512]{2,1,0:T(8,128)S(1)}, f32[2,16,512]{2,1,0:T(8,128)S(1)}, f32[8,512]{1,0:T(8,128)S(1)}) custom-call(f32[2,48,512]{2,1,0:T(8,128)S(1)} %collective-permute-done.18.refs_0_, f32[1,1,5,2,96,512]{5,4,3,2,1,0:T(8,128)S(1)} %copy-done, f32[1,512]{1,0:T(1,128)S(1)} %copy-done.1, ...), custom_call_target="tpu_custom_call", output_to_operand_aliasing={{2}: (7, {})} | custom-call | flops 10000000 | bytes 1 | tf_op jit(solution)/shard_map/step_3_0_0/pallas_call | solution.py:248
  20.2 0.9 %collective-permute-start.23 = (f32[2,16,512]{2,1,0:T(8,128)S(1)}, f32[2,16,512]{2,1,0:T(8,128)S(1)}, u32[]{:S(2)}, u32[]{:S(2)}) collective-permute-start(f32[2,16,512]{2,1,0:T(8,128)S(1)} %get-tuple-element.88), channel_id=1, source_target_pairs={{0,2},{2,0},{4,6},{6,4},{8,10},{10,8},{12,14},{14,12},{16,18},{18,... | collective-permute-start | bytes 196616 | tf_op jit(solution)/shard_map/ppermute | solution.py:363
  21.2 0.1 collective-permute-start.22
  21.3 0.0 collective-permute-done.17.refs_0_
  21.3 0.6 %step_3_1_0.1 = (f32[2,32,512]{2,1,0:T(8,128)S(1)}, f32[2,16,512]{2,1,0:T(8,128)S(1)}, f32[8,512]{1,0:T(8,128)S(1)}) custom-call(f32[2,48,512]{2,1,0:T(8,128)S(1)} %collective-permute-done.17.refs_0_, f32[1,1,5,2,96,512]{5,4,3,2,1,0:T(8,128)S(1)} %copy-done, f32[1,512]{1,0:T(1,128)S(1)} %copy-done.1, ...), custom_call_target="tpu_custom_call", output_to_operand_aliasing={{2}: (7, {})} | custom-call | flops 200000000 | bytes 1 | tf_op jit(solution)/shard_map/step_3_1_0/pallas_call | solution.py:248
  21.8 0.1 collective-permute-start.19
  21.9 0.2 collective-permute-done.23.mate_tail
  22.1 0.4 %collective-permute-start.20 = (f32[2,16,512]{2,1,0:T(8,128)S(1)}, f32[2,16,512]{2,1,0:T(8,128)S(1)}, u32[]{:S(2)}, u32[]{:S(2)}) collective-permute-start(f32[2,16,512]{2,1,0:T(8,128)S(1)} %get-tuple-element.85), channel_id=1, source_target_pairs={{0,2},{2,0},{4,6},{6,4},{8,10},{10,8},{12,14},{14,12},{16,18},{18,... | collective-permute-start | bytes 196616 | tf_op jit(solution)/shard_map/ppermute | solution.py:363
  22.4 0.1 collective-permute-done.22.mate
  22.5 0.9 %collective-permute-done.21.above = f32[2,48,512]{2,1,0:T(8,128)S(1)} collective-permute-done((f32[2,48,512]{2,1,0:T(8,128)S(1)}, f32[2,48,512]{2,1,0:T(8,128)S(1)}, u32[]{:S(2)}, u32[]{:S(2)}) %collective-permute-start.21) | collective-permute-done | bytes 196640 | tf_op jit(solution)/shard_map/ppermute | solution.py:366
  23.4 0.6 %last_0.1 = (f32[2,48,512]{2,1,0:T(8,128)S(1)}, f32[8,512]{1,0:T(8,128)S(1)}) custom-call(f32[2,48,512]{2,1,0:T(8,128)S(1)} %collective-permute-done.21.above, f32[2,32,512]{2,1,0:T(8,128)S(1)} %collective-permute-done.22.mate, f32[2,16,512]{2,1,0:T(8,128)S(1)} %collective-permute-done.23.mate_tail, ...), custom_call_target="tpu_custom_call", output_to_operand_aliasing={{1}: (9, {})} | custom-call | flops 100000000 | bytes 1 | tf_op jit(solution)/shard_map/last_0/pallas_call | solution.py:323
  24.0 0.0 collective-permute-done.20.mate_tail
  24.0 0.0 collective-permute-done.19.mate
  24.0 2.2 %collective-permute-done.16.above = f32[2,48,512]{2,1,0:T(8,128)S(1)} collective-permute-done((f32[2,48,512]{2,1,0:T(8,128)S(1)}, f32[2,48,512]{2,1,0:T(8,128)S(1)}, u32[]{:S(2)}, u32[]{:S(2)}) %collective-permute-start.16) | collective-permute-done | bytes 196640 | tf_op jit(solution)/shard_map/ppermute | solution.py:366
  26.2 0.1 gradient.1
  26.3 1.6 %collective-permute-start.24 = (f32[1,256]{1,0:T(1,128)S(1)}, f32[1,256]{1,0:T(1,128)S(1)}, u32[]{:S(2)}, u32[]{:S(2)}) collective-permute-start(f32[1,256]{1,0:T(1,128)S(1)} %get-tuple-element.93), channel_id=1, source_target_pairs={{0,1},{1,0},{2,3},{3,2},{4,5},{5,4},{6,7},{7,6},{8,9},{9,8},{10,11... | collective-permute-start | bytes 3080 | tf_op jit(solution)/shard_map/ppermute | solution.py:402
  27.8 1.3 %last_1.1 = f32[2,96,512]{2,1,0:T(8,128)} custom-call(f32[2,48,512]{2,1,0:T(8,128)S(1)} %collective-permute-done.16.above, f32[2,32,512]{2,1,0:T(8,128)S(1)} %collective-permute-done.19.mate, f32[2,16,512]{2,1,0:T(8,128)S(1)} %collective-permute-done.20.mate_tail, f32[1,1,5,2,96,512]{5,4,3,2,1,0:T(8,128)S(1)} %copy-done, f32[1,512]{1,0:T(1,128)S(1)} %copy-done.1, ...), custom_call_target="tpu_custom_call" | custom-call | flops 1 | bytes 1 | tf_op jit(solution)/shard_map/last_1/pallas_call | solution.py:323
  29.1 0.8 %collective-permute-done.24 = f32[1,256]{1,0:T(1,128)S(1)} collective-permute-done((f32[1,256]{1,0:T(1,128)S(1)}, f32[1,256]{1,0:T(1,128)S(1)}, u32[]{:S(2)}, u32[]{:S(2)}) %collective-permute-start.24) | collective-permute-done | bytes 1056 | tf_op jit(solution)/shard_map/ppermute | solution.py:402
  29.9 0.6 %add.3 = f32[1,256]{1,0:T(1,128)} add(f32[1,256]{1,0:T(1,128)S(1)} %get-tuple-element.92, f32[1,256]{1,0:T(1,128)S(1)} %collective-permute-done.24) | non-fusion elementwise | flops 256 | bytes 3072 | tf_op jit(solution)/shard_map/add | solution.py:402
  (12 shorter events, 0.0 us)
Async XLA Ops:
  0.8 8.0 %collective-permute-start.2 = (f32[2,48,512]{2,1,0:T(8,128)S(1)}, f32[2,48,512]{2,1,0:T(8,128)S(1)}, u32[]{:S(2)}, u32[]{:S(2)}) collective-permute-start(f32[2,48,512]{2,1,0:T(8,128)S(1)} %get-tuple-element.55), channel_id=1, source_target_pairs={{0,2},{2,4},{4,0},{6,8},{8,10},{10,12},{12,6},{14,16},{16,18},{18,... | collective-permute-start | bytes 589832 | tf_op jit(solution)/shard_map/ppermute | solution.py:366
  3.2 7.7 %collective-permute-start.7 = (f32[2,48,512]{2,1,0:T(8,128)S(1)}, f32[2,48,512]{2,1,0:T(8,128)S(1)}, u32[]{:S(2)}, u32[]{:S(2)}) collective-permute-start(f32[2,48,512]{2,1,0:T(8,128)S(1)} %get-tuple-element.63), channel_id=1, source_target_pairs={{0,2},{2,4},{4,0},{6,8},{8,10},{10,12},{12,6},{14,16},{16,18},{18,... | collective-permute-start | bytes 589832 | tf_op jit(solution)/shard_map/ppermute | solution.py:366
  3.3 4.7 %copy-start = (f32[1,1,5,2,96,512]{5,4,3,2,1,0:T(8,128)S(1)}, f32[1,1,5,2,96,512]{5,4,3,2,1,0:T(8,128)}, u32[]{:S(2)}) copy-start(f32[1,1,5,2,96,512]{5,4,3,2,1,0:T(8,128)} %residual.1) | copy-start | bytes 5898244
  3.3 4.7 %copy-start.1 = (f32[1,512]{1,0:T(1,128)S(1)}, f32[1,512]{1,0:T(1,128)}, u32[]{:S(2)}) copy-start(f32[1,512]{1,0:T(1,128)} %contrast.1) | copy-start | bytes 6148
  3.3 4.7 %copy-start.2 = (s32[4,96]{1,0:T(4,128)S(1)}, s32[4,96]{1,0:T(4,128)}, u32[]{:S(2)}) copy-start(s32[4,96]{1,0:T(4,128)} %sites.1) | copy-start | bytes 4612
  3.3 4.7 %copy-start.3 = (f32[1,4,2]{1,2,0:T(2,128)S(1)}, f32[1,4,2]{1,2,0:T(2,128)}, u32[]{:S(2)}) copy-start(f32[1,4,2]{1,2,0:T(2,128)} %param.11) | copy-start | bytes 100
  6.2 1.8 %collective-permute-start.3 = (f32[2,32,512]{2,1,0:T(8,128)S(1)}, f32[2,32,512]{2,1,0:T(8,128)S(1)}, u32[]{:S(2)}, u32[]{:S(2)}) collective-permute-start(f32[2,32,512]{2,1,0:T(8,128)S(1)} %get-tuple-element.56), channel_id=1, source_target_pairs={{0,2},{2,0},{4,6},{6,4},{8,10},{10,8},{12,14},{14,12},{16,18},{18,... | collective-permute-start | bytes 393224 | tf_op jit(solution)/shard_map/ppermute | solution.py:363
  6.3 1.4 %collective-permute-start.4 = (f32[2,16,512]{2,1,0:T(8,128)S(1)}, f32[2,16,512]{2,1,0:T(8,128)S(1)}, u32[]{:S(2)}, u32[]{:S(2)}) collective-permute-start(f32[2,16,512]{2,1,0:T(8,128)S(1)} %get-tuple-element.57), channel_id=1, source_target_pairs={{0,2},{2,0},{4,6},{6,4},{8,10},{10,8},{12,14},{14,12},{16,18},{18,... | collective-permute-start | bytes 196616 | tf_op jit(solution)/shard_map/ppermute | solution.py:363
  6.8 3.3 %collective-permute-start = (f32[2,32,512]{2,1,0:T(8,128)S(1)}, f32[2,32,512]{2,1,0:T(8,128)S(1)}, u32[]{:S(2)}, u32[]{:S(2)}) collective-permute-start(f32[2,32,512]{2,1,0:T(8,128)S(1)} %get-tuple-element.51), channel_id=1, source_target_pairs={{0,2},{2,0},{4,6},{6,4},{8,10},{10,8},{12,14},{14,12},{16,18},{18,... | collective-permute-start | bytes 393224 | tf_op jit(solution)/shard_map/ppermute | solution.py:363
  7.7 2.2 %collective-permute-start.1 = (f32[2,16,512]{2,1,0:T(8,128)S(1)}, f32[2,16,512]{2,1,0:T(8,128)S(1)}, u32[]{:S(2)}, u32[]{:S(2)}) collective-permute-start(f32[2,16,512]{2,1,0:T(8,128)S(1)} %get-tuple-element.52), channel_id=1, source_target_pairs={{0,2},{2,0},{4,6},{6,4},{8,10},{10,8},{12,14},{14,12},{16,18},{18,... | collective-permute-start | bytes 196616 | tf_op jit(solution)/shard_map/ppermute | solution.py:363
  8.1 6.1 %collective-permute-start.6 = (f32[2,48,512]{2,1,0:T(8,128)S(1)}, f32[2,48,512]{2,1,0:T(8,128)S(1)}, u32[]{:S(2)}, u32[]{:S(2)}) collective-permute-start(f32[2,48,512]{2,1,0:T(8,128)S(1)} %get-tuple-element.62), channel_id=1, source_target_pairs={{0,2},{2,4},{4,0},{6,8},{8,10},{10,12},{12,6},{14,16},{16,18},{18,... | collective-permute-start | bytes 589832 | tf_op jit(solution)/shard_map/ppermute | solution.py:366
  9.4 2.3 %collective-permute-start.11 = (f32[2,16,512]{2,1,0:T(8,128)S(1)}, f32[2,16,512]{2,1,0:T(8,128)S(1)}, u32[]{:S(2)}, u32[]{:S(2)}) collective-permute-start(f32[2,16,512]{2,1,0:T(8,128)S(1)} %get-tuple-element.68), channel_id=1, source_target_pairs={{0,2},{2,0},{4,6},{6,4},{8,10},{10,8},{12,14},{14,12},{16,18},{18,... | collective-permute-start | bytes 196616 | tf_op jit(solution)/shard_map/ppermute | solution.py:363
  9.9 2.3 %collective-permute-start.10 = (f32[2,32,512]{2,1,0:T(8,128)S(1)}, f32[2,32,512]{2,1,0:T(8,128)S(1)}, u32[]{:S(2)}, u32[]{:S(2)}) collective-permute-start(f32[2,32,512]{2,1,0:T(8,128)S(1)} %get-tuple-element.67), channel_id=1, source_target_pairs={{0,2},{2,0},{4,6},{6,4},{8,10},{10,8},{12,14},{14,12},{16,18},{18,... | collective-permute-start | bytes 393224 | tf_op jit(solution)/shard_map/ppermute | solution.py:363
  10.0 6.2 %collective-permute-start.5 = (f32[2,48,512]{2,1,0:T(8,128)S(1)}, f32[2,48,512]{2,1,0:T(8,128)S(1)}, u32[]{:S(2)}, u32[]{:S(2)}) collective-permute-start(f32[2,48,512]{2,1,0:T(8,128)S(1)} %get-tuple-element.61), channel_id=1, source_target_pairs={{0,2},{2,4},{4,0},{6,8},{8,10},{10,12},{12,6},{14,16},{16,18},{18,... | collective-permute-start | bytes 589832 | tf_op jit(solution)/shard_map/ppermute | solution.py:366
  11.6 1.5 %collective-permute-start.8 = (f32[2,32,512]{2,1,0:T(8,128)S(1)}, f32[2,32,512]{2,1,0:T(8,128)S(1)}, u32[]{:S(2)}, u32[]{:S(2)}) collective-permute-start(f32[2,32,512]{2,1,0:T(8,128)S(1)} %get-tuple-element.65), channel_id=1, source_target_pairs={{0,2},{2,0},{4,6},{6,4},{8,10},{10,8},{12,14},{14,12},{16,18},{18,... | collective-permute-start | bytes 393224 | tf_op jit(solution)/shard_map/ppermute | solution.py:363
  11.8 1.3 %collective-permute-start.9 = (f32[2,16,512]{2,1,0:T(8,128)S(1)}, f32[2,16,512]{2,1,0:T(8,128)S(1)}, u32[]{:S(2)}, u32[]{:S(2)}) collective-permute-start(f32[2,16,512]{2,1,0:T(8,128)S(1)} %get-tuple-element.66), channel_id=1, source_target_pairs={{0,2},{2,0},{4,6},{6,4},{8,10},{10,8},{12,14},{14,12},{16,18},{18,... | collective-permute-start | bytes 196616 | tf_op jit(solution)/shard_map/ppermute | solution.py:363
  12.2 7.5 %collective-permute-start.18 = (f32[2,48,512]{2,1,0:T(8,128)S(1)}, f32[2,48,512]{2,1,0:T(8,128)S(1)}, u32[]{:S(2)}, u32[]{:S(2)}) collective-permute-start(f32[2,48,512]{2,1,0:T(8,128)S(1)} %get-tuple-element.81), channel_id=1, source_target_pairs={{0,2},{2,4},{4,0},{6,8},{8,10},{10,12},{12,6},{14,16},{16,18},{18,... | collective-permute-start | bytes 589832 | tf_op jit(solution)/shard_map/ppermute | solution.py:366
  13.1 8.2 %collective-permute-start.17 = (f32[2,48,512]{2,1,0:T(8,128)S(1)}, f32[2,48,512]{2,1,0:T(8,128)S(1)}, u32[]{:S(2)}, u32[]{:S(2)}) collective-permute-start(f32[2,48,512]{2,1,0:T(8,128)S(1)} %get-tuple-element.80), channel_id=1, source_target_pairs={{0,2},{2,4},{4,0},{6,8},{8,10},{10,12},{12,6},{14,16},{16,18},{18,... | collective-permute-start | bytes 589832 | tf_op jit(solution)/shard_map/ppermute | solution.py:366
  14.8 2.6 %collective-permute-start.14 = (f32[2,32,512]{2,1,0:T(8,128)S(1)}, f32[2,32,512]{2,1,0:T(8,128)S(1)}, u32[]{:S(2)}, u32[]{:S(2)}) collective-permute-start(f32[2,32,512]{2,1,0:T(8,128)S(1)} %get-tuple-element.75), channel_id=1, source_target_pairs={{0,2},{2,0},{4,6},{6,4},{8,10},{10,8},{12,14},{14,12},{16,18},{18,... | collective-permute-start | bytes 393224 | tf_op jit(solution)/shard_map/ppermute | solution.py:363
  14.9 2.0 %collective-permute-start.15 = (f32[2,16,512]{2,1,0:T(8,128)S(1)}, f32[2,16,512]{2,1,0:T(8,128)S(1)}, u32[]{:S(2)}, u32[]{:S(2)}) collective-permute-start(f32[2,16,512]{2,1,0:T(8,128)S(1)} %get-tuple-element.76), channel_id=1, source_target_pairs={{0,2},{2,0},{4,6},{6,4},{8,10},{10,8},{12,14},{14,12},{16,18},{18,... | collective-permute-start | bytes 196616 | tf_op jit(solution)/shard_map/ppermute | solution.py:363
  16.8 1.5 %collective-permute-start.12 = (f32[2,32,512]{2,1,0:T(8,128)S(1)}, f32[2,32,512]{2,1,0:T(8,128)S(1)}, u32[]{:S(2)}, u32[]{:S(2)}) collective-permute-start(f32[2,32,512]{2,1,0:T(8,128)S(1)} %get-tuple-element.73), channel_id=1, source_target_pairs={{0,2},{2,0},{4,6},{6,4},{8,10},{10,8},{12,14},{14,12},{16,18},{18,... | collective-permute-start | bytes 393224 | tf_op jit(solution)/shard_map/ppermute | solution.py:363
  16.9 1.4 %collective-permute-start.13 = (f32[2,16,512]{2,1,0:T(8,128)S(1)}, f32[2,16,512]{2,1,0:T(8,128)S(1)}, u32[]{:S(2)}, u32[]{:S(2)}) collective-permute-start(f32[2,16,512]{2,1,0:T(8,128)S(1)} %get-tuple-element.74), channel_id=1, source_target_pairs={{0,2},{2,0},{4,6},{6,4},{8,10},{10,8},{12,14},{14,12},{16,18},{18,... | collective-permute-start | bytes 196616 | tf_op jit(solution)/shard_map/ppermute | solution.py:363
  17.4 6.0 %collective-permute-start.21 = (f32[2,48,512]{2,1,0:T(8,128)S(1)}, f32[2,48,512]{2,1,0:T(8,128)S(1)}, u32[]{:S(2)}, u32[]{:S(2)}) collective-permute-start(f32[2,48,512]{2,1,0:T(8,128)S(1)} %get-tuple-element.86), channel_id=1, source_target_pairs={{0,2},{2,4},{4,0},{6,8},{8,10},{10,12},{12,6},{14,16},{16,18},{18,... | collective-permute-start | bytes 589832 | tf_op jit(solution)/shard_map/ppermute | solution.py:366
  18.3 7.9 %collective-permute-start.16 = (f32[2,48,512]{2,1,0:T(8,128)S(1)}, f32[2,48,512]{2,1,0:T(8,128)S(1)}, u32[]{:S(2)}, u32[]{:S(2)}) collective-permute-start(f32[2,48,512]{2,1,0:T(8,128)S(1)} %get-tuple-element.79), channel_id=1, source_target_pairs={{2,4},{6,8},{10,12},{14,16},{18,20},{22,24},{26,28},{3,5},{7,9},{1... | collective-permute-start | bytes 589832 | tf_op jit(solution)/shard_map/ppermute | solution.py:366
  20.2 1.8 %collective-permute-start.23 = (f32[2,16,512]{2,1,0:T(8,128)S(1)}, f32[2,16,512]{2,1,0:T(8,128)S(1)}, u32[]{:S(2)}, u32[]{:S(2)}) collective-permute-start(f32[2,16,512]{2,1,0:T(8,128)S(1)} %get-tuple-element.88), channel_id=1, source_target_pairs={{0,2},{2,0},{4,6},{6,4},{8,10},{10,8},{12,14},{14,12},{16,18},{18,... | collective-permute-start | bytes 196616 | tf_op jit(solution)/shard_map/ppermute | solution.py:363
  21.2 1.3 %collective-permute-start.22 = (f32[2,32,512]{2,1,0:T(8,128)S(1)}, f32[2,32,512]{2,1,0:T(8,128)S(1)}, u32[]{:S(2)}, u32[]{:S(2)}) collective-permute-start(f32[2,32,512]{2,1,0:T(8,128)S(1)} %get-tuple-element.87), channel_id=1, source_target_pairs={{0,2},{2,0},{4,6},{6,4},{8,10},{10,8},{12,14},{14,12},{16,18},{18,... | collective-permute-start | bytes 393224 | tf_op jit(solution)/shard_map/ppermute | solution.py:363
  21.8 2.1 %collective-permute-start.19 = (f32[2,32,512]{2,1,0:T(8,128)S(1)}, f32[2,32,512]{2,1,0:T(8,128)S(1)}, u32[]{:S(2)}, u32[]{:S(2)}) collective-permute-start(f32[2,32,512]{2,1,0:T(8,128)S(1)} %get-tuple-element.84), channel_id=1, source_target_pairs={{0,2},{2,0},{4,6},{6,4},{8,10},{10,8},{12,14},{14,12},{16,18},{18,... | collective-permute-start | bytes 393224 | tf_op jit(solution)/shard_map/ppermute | solution.py:363
  22.1 1.9 %collective-permute-start.20 = (f32[2,16,512]{2,1,0:T(8,128)S(1)}, f32[2,16,512]{2,1,0:T(8,128)S(1)}, u32[]{:S(2)}, u32[]{:S(2)}) collective-permute-start(f32[2,16,512]{2,1,0:T(8,128)S(1)} %get-tuple-element.85), channel_id=1, source_target_pairs={{0,2},{2,0},{4,6},{6,4},{8,10},{10,8},{12,14},{14,12},{16,18},{18,... | collective-permute-start | bytes 196616 | tf_op jit(solution)/shard_map/ppermute | solution.py:363
  26.3 3.6 %collective-permute-start.24 = (f32[1,256]{1,0:T(1,128)S(1)}, f32[1,256]{1,0:T(1,128)S(1)}, u32[]{:S(2)}, u32[]{:S(2)}) collective-permute-start(f32[1,256]{1,0:T(1,128)S(1)} %get-tuple-element.93), channel_id=1, source_target_pairs={{0,1},{1,0},{2,3},{3,2},{4,5},{5,4},{6,7},{7,6},{8,9},{9,8},{10,11... | collective-permute-start | bytes 3080 | tf_op jit(solution)/shard_map/ppermute | solution.py:402

commit v13 on v11

--- a/solution.py
+++ b/solution.py
@@ -339,6 +339,11 @@
     return sorted(route.items())
 
 
+def surface_alone(route):
+    old = dict(route)[0]
+    return [(source, 0 if source == 0 else old if target == 0 else target) for source, target in route]
+
+
 def local(
     extrapolation_operator,
     impedance_contrast,
@@ -352,14 +357,14 @@
     shots = arriving_downward_matrices.shape[3]
     mate_route = [(level, level ^ 1) for level in range(levels)]
     down_route = cross_route(levels)
-    open_route = [(level, level + 1) for level in range(1, levels - 1, 2)]
+    final_route = surface_alone(down_route)
     shared = (ascending_residual, impedance_contrast, shot_node_indices, emitted_pulse[0].T)
 
     def mate(pieces):
         return [lax.ppermute(piece, "depth", mate_route) for piece in pieces]
 
-    def down(piece, closed=True):
-        return lax.ppermute(piece, "depth", down_route if closed else open_route)
+    def down(piece, final=False):
+        return lax.ppermute(piece, "depth", final_route if final else down_route)
 
     rows = shots // HALVES
     start = (extrapolation_operator, impedance_contrast, ascending_residual, arriving_downward_matrices)
@@ -369,9 +374,9 @@
     beside = [mate(even[2 * half : 2 * half + 2]) for half in range(HALVES)]
     grads = [grad]
 
-    def odd_step(tick, start, pieces, closed=True):
+    def odd_step(tick, start, pieces, final=False):
         odd, grads[0] = step(tick, start, 1, pieces, shared, high, low, grads[0], rows)
-        return down(odd, closed)
+        return down(odd, final)
 
     def even_step(tick, start, pieces):
         *even, grads[0] = step(tick, start, 0, pieces, shared, high, low, grads[0], rows)
@@ -384,7 +389,7 @@
     above, beside = later, latest
     for tick in range(2, TICKS - 1):
         later = [
-            odd_step(tick, half * rows, beside[half], tick < TICKS - 2 or half < HALVES - 1) for half in range(HALVES)
+            odd_step(tick, half * rows, beside[half], tick == TICKS - 2 and half == HALVES - 1) for half in range(HALVES)
         ]
         beside = [even_step(tick, half * rows, [above[half]]) for half in range(HALVES)]
         above = later

time: 30.2 us -> 30.2 us (level)
  waiting for transfers between devices: 5.92 us -> 5.05 us
  starting transfers between devices: 14.6 us -> 15.4 us
    ppermute x8, starting transfers between devices: 8.1 us -> 9.58 us  [down(): return lax.ppermute(piece, 'depth', final_route if final else down_route)]
    ppermute x8, waiting for transfers between devices: 3.58 us -> 2.54 us  [down(): return lax.ppermute(piece, 'depth', final_route if final else down_route)]
    ppermute x16, starting transfers between devices: 4.92 us -> 4.31 us  [mate(): return [lax.ppermute(piece, 'depth', mate_route) for piece in pieces]]
  transfers between devices with their start and end apart: 25 -> 25, of which waited for: 9 -> 8; matrix products, arithmetic and copies ran while one was open for 0% -> 0% of each run, Pallas kernels for 27% -> 27%
where the time goes in v13:
time: 30.2 us; the launch traced here: 30 us
  starting transfers between devices  15.4 us (51%)
  Pallas kernels  8.12 us (27%)
  waiting for transfers between devices  5.05 us (17%)
  between operations  0.82 us (3%)
  other arithmetic  0.56 us (2%)
    ppermute x8, starting transfers between devices, down(): return lax.ppermute(piece, 'depth', final_route if final else down_route)  9.58 us
    ppermute x16, starting transfers between devices, mate(): return [lax.ppermute(piece, 'depth', mate_route) for piece in pieces]  4.31 us
    pallas_call x12, Pallas kernels, step(): pl.pallas_call(functools.partial(step_kernel, tick, start, parity, len(pi...  3.51 us
    pallas_call x2, Pallas kernels, first(): pl.pallas_call(functools.partial(first_kernel, parity, bool(carried)), ou...  2.71 us
    ppermute x8, waiting for transfers between devices, down(): return lax.ppermute(piece, 'depth', final_route if final else down_route)  2.54 us
    pallas_call x2, Pallas kernels, last(): pl.pallas_call(functools.partial(last_kernel, half), out_shape=out_shape,...  1.84 us
    ppermute x16, waiting for transfers between devices, mate(): return [lax.ppermute(piece, 'depth', mate_route) for piece in pieces]  1.7 us
    ppermute x1, starting transfers between devices, local(): gradient = gradient + lax.ppermute(chunks[distance], 'freq', route)  1.55 us
  transfers between devices with their start and end apart: 25, of which 8 were waited for; matrix products, arithmetic and copies ran while one was open for 0% of the time, Pallas kernels for 27%

profile of v13, /device:TPU:16, one launch (start us, length us, event | category | flops | bytes accessed | tf_op | source)
XLA Modules:
  0.0 30.0 jit_solution(8047509036811996301)
XLA Ops:
  0.6 0.1 first_1.1
  0.7 2.3 %collective-permute-start.2 = (f32[2,48,512]{2,1,0:T(8,128)S(1)}, f32[2,48,512]{2,1,0:T(8,128)S(1)}, u32[]{:S(2)}, u32[]{:S(2)}) collective-permute-start(f32[2,48,512]{2,1,0:T(8,128)S(1)} %get-tuple-element.55), channel_id=1, source_target_pairs={{0,2},{2,4},{4,0},{6,8},{8,10},{10,12},{12,6},{14,16},{16,18},{18,... | collective-permute-start | bytes 589832 | tf_op jit(solution)/shard_map/ppermute | solution.py:367
  3.0 0.1 collective-permute-start.7
  3.1 2.6 %first_0.1 = (f32[2,32,512]{2,1,0:T(8,128)S(1)}, f32[2,16,512]{2,1,0:T(8,128)S(1)}, f32[2,32,512]{2,1,0:T(8,128)S(1)}, f32[2,16,512]{2,1,0:T(8,128)S(1)}, bf16[2...) custom-call(f32[1,1,2,512,512]{4,3,2,1,0:T(8,128)} %refs_0_.5, ...), custom_call_target="tpu_custom_call", output_to_operand_aliasing={{4}: (4, {}), {5}: (5, {}), {6}: (6, {})} | custom-call | flops 500000000 | bytes 1 | tf_op jit(solution)/shard_map/first_0/pallas_call | solution.py:173
  5.7 0.1 collective-permute-start.3
  5.8 0.5 %collective-permute-start.4 = (f32[2,16,512]{2,1,0:T(8,128)S(1)}, f32[2,16,512]{2,1,0:T(8,128)S(1)}, u32[]{:S(2)}, u32[]{:S(2)}) collective-permute-start(f32[2,16,512]{2,1,0:T(8,128)S(1)} %get-tuple-element.57), channel_id=1, source_target_pairs={{0,2},{2,0},{4,6},{6,4},{8,10},{10,8},{12,14},{14,12},{16,18},{18,... | collective-permute-start | bytes 196616 | tf_op jit(solution)/shard_map/ppermute | solution.py:364
  6.3 0.1 collective-permute-start
  6.4 0.9 %collective-permute-done.4.refs_1_ = f32[2,16,512]{2,1,0:T(8,128)S(1)} collective-permute-done((f32[2,16,512]{2,1,0:T(8,128)S(1)}, f32[2,16,512]{2,1,0:T(8,128)S(1)}, u32[]{:S(2)}, u32[]{:S(2)}) %collective-permute-start.4) | collective-permute-done | bytes 65568 | tf_op jit(solution)/shard_map/ppermute | solution.py:364
  7.2 0.3 %collective-permute-start.1 = (f32[2,16,512]{2,1,0:T(8,128)S(1)}, f32[2,16,512]{2,1,0:T(8,128)S(1)}, u32[]{:S(2)}, u32[]{:S(2)}) collective-permute-start(f32[2,16,512]{2,1,0:T(8,128)S(1)} %get-tuple-element.52), channel_id=1, source_target_pairs={{0,2},{2,0},{4,6},{6,4},{8,10},{10,8},{12,14},{14,12},{16,18},{18,... | collective-permute-start | bytes 196616 | tf_op jit(solution)/shard_map/ppermute | solution.py:364
  7.6 0.0 collective-permute-done.3.refs_0_
  7.6 0.0 copy-done
  7.6 0.0 copy-done.1
  7.6 0.8 %collective-permute-start.6 = (f32[2,48,512]{2,1,0:T(8,128)S(1)}, f32[2,48,512]{2,1,0:T(8,128)S(1)}, u32[]{:S(2)}, u32[]{:S(2)}) collective-permute-start(f32[2,48,512]{2,1,0:T(8,128)S(1)} %get-tuple-element.62), channel_id=1, source_target_pairs={{0,2},{2,4},{4,0},{6,8},{8,10},{10,12},{12,6},{14,16},{16,18},{18,... | collective-permute-start | bytes 589832 | tf_op jit(solution)/shard_map/ppermute | solution.py:367
  8.4 0.0 collective-permute-done.2.refs_0_
  8.4 0.6 %step_1_0_0.1 = (f32[2,32,512]{2,1,0:T(8,128)S(1)}, f32[2,16,512]{2,1,0:T(8,128)S(1)}, f32[8,512]{1,0:T(8,128)S(1)}) custom-call(f32[2,48,512]{2,1,0:T(8,128)S(1)} %collective-permute-done.2.refs_0_, f32[1,1,5,2,96,512]{5,4,3,2,1,0:T(8,128)S(1)} %copy-done, f32[1,512]{1,0:T(1,128)S(1)} %copy-done.1, ...), custom_call_target="tpu_custom_call", output_to_operand_aliasing={{2}: (7, {})} | custom-call | flops 30000000 | bytes 1 | tf_op jit(solution)/shard_map/step_1_0_0/pallas_call | solution.py:244
  9.0 0.4 %collective-permute-start.11 = (f32[2,16,512]{2,1,0:T(8,128)S(1)}, f32[2,16,512]{2,1,0:T(8,128)S(1)}, u32[]{:S(2)}, u32[]{:S(2)}) collective-permute-start(f32[2,16,512]{2,1,0:T(8,128)S(1)} %get-tuple-element.68), channel_id=1, source_target_pairs={{0,2},{2,0},{4,6},{6,4},{8,10},{10,8},{12,14},{14,12},{16,18},{18,... | collective-permute-start | bytes 196616 | tf_op jit(solution)/shard_map/ppermute | solution.py:364
  9.4 0.0 collective-permute-done.1.refs_1_
  9.4 0.2 collective-permute-start.10
  9.6 0.0 collective-permute-done.refs_0_
  9.6 0.9 %collective-permute-start.5 = (f32[2,48,512]{2,1,0:T(8,128)S(1)}, f32[2,48,512]{2,1,0:T(8,128)S(1)}, u32[]{:S(2)}, u32[]{:S(2)}) collective-permute-start(f32[2,48,512]{2,1,0:T(8,128)S(1)} %get-tuple-element.61), channel_id=1, source_target_pairs={{0,2},{2,4},{4,0},{6,8},{8,10},{10,12},{12,6},{14,16},{16,18},{18,... | collective-permute-start | bytes 589832 | tf_op jit(solution)/shard_map/ppermute | solution.py:367
  10.5 0.0 collective-permute-done.7.refs_0_
  10.5 0.6 %step_1_1_0.1 = (f32[2,32,512]{2,1,0:T(8,128)S(1)}, f32[2,16,512]{2,1,0:T(8,128)S(1)}, f32[8,512]{1,0:T(8,128)S(1)}) custom-call(f32[2,48,512]{2,1,0:T(8,128)S(1)} %collective-permute-done.7.refs_0_, f32[1,1,5,2,96,512]{5,4,3,2,1,0:T(8,128)S(1)} %copy-done, f32[1,512]{1,0:T(1,128)S(1)} %copy-done.1, ...), custom_call_target="tpu_custom_call", output_to_operand_aliasing={{2}: (7, {})} | custom-call | flops 1000000000 | bytes 1 | tf_op jit(solution)/shard_map/step_1_1_0/pallas_call | solution.py:244
  11.1 0.2 collective-permute-start.8
  11.3 0.0 collective-permute-done.11.refs_1_
  11.3 0.3 %collective-permute-start.9 = (f32[2,16,512]{2,1,0:T(8,128)S(1)}, f32[2,16,512]{2,1,0:T(8,128)S(1)}, u32[]{:S(2)}, u32[]{:S(2)}) collective-permute-start(f32[2,16,512]{2,1,0:T(8,128)S(1)} %get-tuple-element.66), channel_id=1, source_target_pairs={{0,2},{2,0},{4,6},{6,4},{8,10},{10,8},{12,14},{14,12},{16,18},{18,... | collective-permute-start | bytes 196616 | tf_op jit(solution)/shard_map/ppermute | solution.py:364
  11.7 0.0 collective-permute-done.10.refs_0_
  11.7 0.8 %collective-permute-start.18 = (f32[2,48,512]{2,1,0:T(8,128)S(1)}, f32[2,48,512]{2,1,0:T(8,128)S(1)}, u32[]{:S(2)}, u32[]{:S(2)}) collective-permute-start(f32[2,48,512]{2,1,0:T(8,128)S(1)} %get-tuple-element.81), channel_id=1, source_target_pairs={{0,2},{2,4},{4,0},{6,8},{8,10},{10,12},{12,6},{14,16},{16,18},{18,... | collective-permute-start | bytes 589832 | tf_op jit(solution)/shard_map/ppermute | solution.py:367
  12.4 0.2 collective-permute-done.9.refs_1_
  12.6 0.0 collective-permute-done.8.refs_0_
  12.6 1.3 %collective-permute-start.17 = (f32[2,48,512]{2,1,0:T(8,128)S(1)}, f32[2,48,512]{2,1,0:T(8,128)S(1)}, u32[]{:S(2)}, u32[]{:S(2)}) collective-permute-start(f32[2,48,512]{2,1,0:T(8,128)S(1)} %get-tuple-element.80), channel_id=1, source_target_pairs={{0,2},{2,4},{4,0},{6,8},{8,10},{10,12},{12,6},{14,16},{16,18},{18,... | collective-permute-start | bytes 589832 | tf_op jit(solution)/shard_map/ppermute | solution.py:367
  13.9 0.0 collective-permute-done.6.refs_0_
  13.9 0.6 %step_2_0_0.1 = (f32[2,32,512]{2,1,0:T(8,128)S(1)}, f32[2,16,512]{2,1,0:T(8,128)S(1)}, f32[8,512]{1,0:T(8,128)S(1)}) custom-call(f32[2,48,512]{2,1,0:T(8,128)S(1)} %collective-permute-done.6.refs_0_, f32[1,1,5,2,96,512]{5,4,3,2,1,0:T(8,128)S(1)} %copy-done, f32[1,512]{1,0:T(1,128)S(1)} %copy-done.1, ...), custom_call_target="tpu_custom_call", output_to_operand_aliasing={{2}: (7, {})} | custom-call | flops 10000000 | bytes 1 | tf_op jit(solution)/shard_map/step_2_0_0/pallas_call | solution.py:244
  14.5 0.1 collective-permute-start.14
  14.6 0.5 %collective-permute-start.15 = (f32[2,16,512]{2,1,0:T(8,128)S(1)}, f32[2,16,512]{2,1,0:T(8,128)S(1)}, u32[]{:S(2)}, u32[]{:S(2)}) collective-permute-start(f32[2,16,512]{2,1,0:T(8,128)S(1)} %get-tuple-element.76), channel_id=1, source_target_pairs={{0,2},{2,0},{4,6},{6,4},{8,10},{10,8},{12,14},{14,12},{16,18},{18,... | collective-permute-start | bytes 196616 | tf_op jit(solution)/shard_map/ppermute | solution.py:364
  15.1 0.7 %collective-permute-done.5.refs_0_ = f32[2,48,512]{2,1,0:T(8,128)S(1)} collective-permute-done((f32[2,48,512]{2,1,0:T(8,128)S(1)}, f32[2,48,512]{2,1,0:T(8,128)S(1)}, u32[]{:S(2)}, u32[]{:S(2)}) %collective-permute-start.5) | collective-permute-done | bytes 196640 | tf_op jit(solution)/shard_map/ppermute | solution.py:367
  15.8 0.6 %step_2_1_0.1 = (f32[2,32,512]{2,1,0:T(8,128)S(1)}, f32[2,16,512]{2,1,0:T(8,128)S(1)}, f32[8,512]{1,0:T(8,128)S(1)}) custom-call(f32[2,48,512]{2,1,0:T(8,128)S(1)} %collective-permute-done.5.refs_0_, f32[1,1,5,2,96,512]{5,4,3,2,1,0:T(8,128)S(1)} %copy-done, f32[1,512]{1,0:T(1,128)S(1)} %copy-done.1, ...), custom_call_target="tpu_custom_call", output_to_operand_aliasing={{2}: (7, {})} | custom-call | flops 30000000 | bytes 1 | tf_op jit(solution)/shard_map/step_2_1_0/pallas_call | solution.py:244
  16.4 0.1 collective-permute-start.12
  16.4 0.0 collective-permute-done.15.refs_1_
  16.5 0.5 %collective-permute-start.13 = (f32[2,16,512]{2,1,0:T(8,128)S(1)}, f32[2,16,512]{2,1,0:T(8,128)S(1)}, u32[]{:S(2)}, u32[]{:S(2)}) collective-permute-start(f32[2,16,512]{2,1,0:T(8,128)S(1)} %get-tuple-element.74), channel_id=1, source_target_pairs={{0,2},{2,0},{4,6},{6,4},{8,10},{10,8},{12,14},{14,12},{16,18},{18,... | collective-permute-start | bytes 196616 | tf_op jit(solution)/shard_map/ppermute | solution.py:364
  16.9 0.0 collective-permute-done.14.refs_0_
  17.0 0.7 %collective-permute-start.21 = (f32[2,48,512]{2,1,0:T(8,128)S(1)}, f32[2,48,512]{2,1,0:T(8,128)S(1)}, u32[]{:S(2)}, u32[]{:S(2)}) collective-permute-start(f32[2,48,512]{2,1,0:T(8,128)S(1)} %get-tuple-element.86), channel_id=1, source_target_pairs={{0,2},{2,4},{4,0},{6,8},{8,10},{10,12},{12,6},{14,16},{16,18},{18,... | collective-permute-start | bytes 589832 | tf_op jit(solution)/shard_map/ppermute | solution.py:367
  17.6 0.2 collective-permute-done.13.refs_1_
  17.9 0.0 collective-permute-done.12.refs_0_
  17.9 2.8 %collective-permute-start.16 = (f32[2,48,512]{2,1,0:T(8,128)S(1)}, f32[2,48,512]{2,1,0:T(8,128)S(1)}, u32[]{:S(2)}, u32[]{:S(2)}) collective-permute-start(f32[2,48,512]{2,1,0:T(8,128)S(1)} %get-tuple-element.79), channel_id=1, source_target_pairs={{0,0},{2,4},{4,2},{6,8},{8,10},{10,12},{12,6},{14,16},{16,18},{18,... | collective-permute-start | bytes 589832 | tf_op jit(solution)/shard_map/ppermute | solution.py:367
  20.7 0.0 collective-permute-done.18.refs_0_
  20.7 0.6 %step_3_0_0.1 = (f32[2,32,512]{2,1,0:T(8,128)S(1)}, f32[2,16,512]{2,1,0:T(8,128)S(1)}, f32[8,512]{1,0:T(8,128)S(1)}) custom-call(f32[2,48,512]{2,1,0:T(8,128)S(1)} %collective-permute-done.18.refs_0_, f32[1,1,5,2,96,512]{5,4,3,2,1,0:T(8,128)S(1)} %copy-done, f32[1,512]{1,0:T(1,128)S(1)} %copy-done.1, ...), custom_call_target="tpu_custom_call", output_to_operand_aliasing={{2}: (7, {})} | custom-call | flops 10000000 | bytes 1 | tf_op jit(solution)/shard_map/step_3_0_0/pallas_call | solution.py:244
  21.3 0.1 collective-permute-start.23
  21.4 0.5 %collective-permute-start.22 = (f32[2,32,512]{2,1,0:T(8,128)S(1)}, f32[2,32,512]{2,1,0:T(8,128)S(1)}, u32[]{:S(2)}, u32[]{:S(2)}) collective-permute-start(f32[2,32,512]{2,1,0:T(8,128)S(1)} %get-tuple-element.87), channel_id=1, source_target_pairs={{0,2},{2,0},{4,6},{6,4},{8,10},{10,8},{12,14},{14,12},{16,18},{18,... | collective-permute-start | bytes 393224 | tf_op jit(solution)/shard_map/ppermute | solution.py:364
  21.9 0.0 collective-permute-done.17.refs_0_
  21.9 0.6 %step_3_1_0.1 = (f32[2,32,512]{2,1,0:T(8,128)S(1)}, f32[2,16,512]{2,1,0:T(8,128)S(1)}, f32[8,512]{1,0:T(8,128)S(1)}) custom-call(f32[2,48,512]{2,1,0:T(8,128)S(1)} %collective-permute-done.17.refs_0_, f32[1,1,5,2,96,512]{5,4,3,2,1,0:T(8,128)S(1)} %copy-done, f32[1,512]{1,0:T(1,128)S(1)} %copy-done.1, ...), custom_call_target="tpu_custom_call", output_to_operand_aliasing={{2}: (7, {})} | custom-call | flops 200000000 | bytes 1 | tf_op jit(solution)/shard_map/step_3_1_0/pallas_call | solution.py:244
  22.4 0.1 collective-permute-start.19
  22.5 0.1 collective-permute-done.23.mate_tail
  22.6 0.4 %collective-permute-start.20 = (f32[2,16,512]{2,1,0:T(8,128)S(1)}, f32[2,16,512]{2,1,0:T(8,128)S(1)}, u32[]{:S(2)}, u32[]{:S(2)}) collective-permute-start(f32[2,16,512]{2,1,0:T(8,128)S(1)} %get-tuple-element.85), channel_id=1, source_target_pairs={{0,2},{2,0},{4,6},{6,4},{8,10},{10,8},{12,14},{14,12},{16,18},{18,... | collective-permute-start | bytes 196616 | tf_op jit(solution)/shard_map/ppermute | solution.py:364
  23.0 0.0 collective-permute-done.22.mate
  23.0 0.0 collective-permute-done.21.above
  23.0 0.6 %last_0.1 = (f32[2,48,512]{2,1,0:T(8,128)S(1)}, f32[8,512]{1,0:T(8,128)S(1)}) custom-call(f32[2,48,512]{2,1,0:T(8,128)S(1)} %collective-permute-done.21.above, f32[2,32,512]{2,1,0:T(8,128)S(1)} %collective-permute-done.22.mate, f32[2,16,512]{2,1,0:T(8,128)S(1)} %collective-permute-done.23.mate_tail, ...), custom_call_target="tpu_custom_call", output_to_operand_aliasing={{1}: (9, {})} | custom-call | flops 100000000 | bytes 1 | tf_op jit(solution)/shard_map/last_0/pallas_call | solution.py:319
  23.6 0.3 %collective-permute-done.20.mate_tail = f32[2,16,512]{2,1,0:T(8,128)S(1)} collective-permute-done((f32[2,16,512]{2,1,0:T(8,128)S(1)}, f32[2,16,512]{2,1,0:T(8,128)S(1)}, u32[]{:S(2)}, u32[]{:S(2)}) %collective-permute-start.20) | collective-permute-done | bytes 65568 | tf_op jit(solution)/shard_map/ppermute | solution.py:364
  23.9 0.0 collective-permute-done.19.mate
  24.0 1.8 %collective-permute-done.16.above = f32[2,48,512]{2,1,0:T(8,128)S(1)} collective-permute-done((f32[2,48,512]{2,1,0:T(8,128)S(1)}, f32[2,48,512]{2,1,0:T(8,128)S(1)}, u32[]{:S(2)}, u32[]{:S(2)}) %collective-permute-start.16) | collective-permute-done | bytes 196640 | tf_op jit(solution)/shard_map/ppermute | solution.py:367
  25.8 0.1 gradient.1
  25.8 1.6 %collective-permute-start.24 = (f32[1,256]{1,0:T(1,128)S(1)}, f32[1,256]{1,0:T(1,128)S(1)}, u32[]{:S(2)}, u32[]{:S(2)}) collective-permute-start(f32[1,256]{1,0:T(1,128)S(1)} %get-tuple-element.93), channel_id=1, source_target_pairs={{0,1},{1,0},{2,3},{3,2},{4,5},{5,4},{6,7},{7,6},{8,9},{9,8},{10,11... | collective-permute-start | bytes 3080 | tf_op jit(solution)/shard_map/ppermute | solution.py:403
  27.4 1.3 %last_1.1 = f32[2,96,512]{2,1,0:T(8,128)} custom-call(f32[2,48,512]{2,1,0:T(8,128)S(1)} %collective-permute-done.16.above, f32[2,32,512]{2,1,0:T(8,128)S(1)} %collective-permute-done.19.mate, f32[2,16,512]{2,1,0:T(8,128)S(1)} %collective-permute-done.20.mate_tail, f32[1,1,5,2,96,512]{5,4,3,2,1,0:T(8,128)S(1)} %copy-done, f32[1,512]{1,0:T(1,128)S(1)} %copy-done.1, ...), custom_call_target="tpu_custom_call" | custom-call | flops 1 | bytes 1 | tf_op jit(solution)/shard_map/last_1/pallas_call | solution.py:319
  28.6 0.8 %collective-permute-done.24 = f32[1,256]{1,0:T(1,128)S(1)} collective-permute-done((f32[1,256]{1,0:T(1,128)S(1)}, f32[1,256]{1,0:T(1,128)S(1)}, u32[]{:S(2)}, u32[]{:S(2)}) %collective-permute-start.24) | collective-permute-done | bytes 1056 | tf_op jit(solution)/shard_map/ppermute | solution.py:403
  29.4 0.6 %add.3 = f32[1,256]{1,0:T(1,128)} add(f32[1,256]{1,0:T(1,128)S(1)} %get-tuple-element.92, f32[1,256]{1,0:T(1,128)S(1)} %collective-permute-done.24) | non-fusion elementwise | flops 256 | bytes 3072 | tf_op jit(solution)/shard_map/add | solution.py:403
  (12 shorter events, 0.0 us)
Async XLA Ops:
  0.7 7.7 %collective-permute-start.2 = (f32[2,48,512]{2,1,0:T(8,128)S(1)}, f32[2,48,512]{2,1,0:T(8,128)S(1)}, u32[]{:S(2)}, u32[]{:S(2)}) collective-permute-start(f32[2,48,512]{2,1,0:T(8,128)S(1)} %get-tuple-element.55), channel_id=1, source_target_pairs={{0,2},{2,4},{4,0},{6,8},{8,10},{10,12},{12,6},{14,16},{16,18},{18,... | collective-permute-start | bytes 589832 | tf_op jit(solution)/shard_map/ppermute | solution.py:367
  3.0 7.5 %collective-permute-start.7 = (f32[2,48,512]{2,1,0:T(8,128)S(1)}, f32[2,48,512]{2,1,0:T(8,128)S(1)}, u32[]{:S(2)}, u32[]{:S(2)}) collective-permute-start(f32[2,48,512]{2,1,0:T(8,128)S(1)} %get-tuple-element.63), channel_id=1, source_target_pairs={{0,2},{2,4},{4,0},{6,8},{8,10},{10,12},{12,6},{14,16},{16,18},{18,... | collective-permute-start | bytes 589832 | tf_op jit(solution)/shard_map/ppermute | solution.py:367
  3.1 4.5 %copy-start = (f32[1,1,5,2,96,512]{5,4,3,2,1,0:T(8,128)S(1)}, f32[1,1,5,2,96,512]{5,4,3,2,1,0:T(8,128)}, u32[]{:S(2)}) copy-start(f32[1,1,5,2,96,512]{5,4,3,2,1,0:T(8,128)} %residual.1) | copy-start | bytes 5898244
  3.1 4.5 %copy-start.1 = (f32[1,512]{1,0:T(1,128)S(1)}, f32[1,512]{1,0:T(1,128)}, u32[]{:S(2)}) copy-start(f32[1,512]{1,0:T(1,128)} %contrast.1) | copy-start | bytes 6148
  3.1 4.5 %copy-start.2 = (s32[4,96]{1,0:T(4,128)S(1)}, s32[4,96]{1,0:T(4,128)}, u32[]{:S(2)}) copy-start(s32[4,96]{1,0:T(4,128)} %sites.1) | copy-start | bytes 4612
  3.1 4.5 %copy-start.3 = (f32[1,4,2]{1,2,0:T(2,128)S(1)}, f32[1,4,2]{1,2,0:T(2,128)}, u32[]{:S(2)}) copy-start(f32[1,4,2]{1,2,0:T(2,128)} %param.11) | copy-start | bytes 100
  5.7 1.8 %collective-permute-start.3 = (f32[2,32,512]{2,1,0:T(8,128)S(1)}, f32[2,32,512]{2,1,0:T(8,128)S(1)}, u32[]{:S(2)}, u32[]{:S(2)}) collective-permute-start(f32[2,32,512]{2,1,0:T(8,128)S(1)} %get-tuple-element.56), channel_id=1, source_target_pairs={{0,2},{2,0},{4,6},{6,4},{8,10},{10,8},{12,14},{14,12},{16,18},{18,... | collective-permute-start | bytes 393224 | tf_op jit(solution)/shard_map/ppermute | solution.py:364
  5.8 1.4 %collective-permute-start.4 = (f32[2,16,512]{2,1,0:T(8,128)S(1)}, f32[2,16,512]{2,1,0:T(8,128)S(1)}, u32[]{:S(2)}, u32[]{:S(2)}) collective-permute-start(f32[2,16,512]{2,1,0:T(8,128)S(1)} %get-tuple-element.57), channel_id=1, source_target_pairs={{0,2},{2,0},{4,6},{6,4},{8,10},{10,8},{12,14},{14,12},{16,18},{18,... | collective-permute-start | bytes 196616 | tf_op jit(solution)/shard_map/ppermute | solution.py:364
  6.3 3.3 %collective-permute-start = (f32[2,32,512]{2,1,0:T(8,128)S(1)}, f32[2,32,512]{2,1,0:T(8,128)S(1)}, u32[]{:S(2)}, u32[]{:S(2)}) collective-permute-start(f32[2,32,512]{2,1,0:T(8,128)S(1)} %get-tuple-element.51), channel_id=1, source_target_pairs={{0,2},{2,0},{4,6},{6,4},{8,10},{10,8},{12,14},{14,12},{16,18},{18,... | collective-permute-start | bytes 393224 | tf_op jit(solution)/shard_map/ppermute | solution.py:364
  7.2 2.1 %collective-permute-start.1 = (f32[2,16,512]{2,1,0:T(8,128)S(1)}, f32[2,16,512]{2,1,0:T(8,128)S(1)}, u32[]{:S(2)}, u32[]{:S(2)}) collective-permute-start(f32[2,16,512]{2,1,0:T(8,128)S(1)} %get-tuple-element.52), channel_id=1, source_target_pairs={{0,2},{2,0},{4,6},{6,4},{8,10},{10,8},{12,14},{14,12},{16,18},{18,... | collective-permute-start | bytes 196616 | tf_op jit(solution)/shard_map/ppermute | solution.py:364
  7.6 6.3 %collective-permute-start.6 = (f32[2,48,512]{2,1,0:T(8,128)S(1)}, f32[2,48,512]{2,1,0:T(8,128)S(1)}, u32[]{:S(2)}, u32[]{:S(2)}) collective-permute-start(f32[2,48,512]{2,1,0:T(8,128)S(1)} %get-tuple-element.62), channel_id=1, source_target_pairs={{0,2},{2,4},{4,0},{6,8},{8,10},{10,12},{12,6},{14,16},{16,18},{18,... | collective-permute-start | bytes 589832 | tf_op jit(solution)/shard_map/ppermute | solution.py:367
  9.0 2.3 %collective-permute-start.11 = (f32[2,16,512]{2,1,0:T(8,128)S(1)}, f32[2,16,512]{2,1,0:T(8,128)S(1)}, u32[]{:S(2)}, u32[]{:S(2)}) collective-permute-start(f32[2,16,512]{2,1,0:T(8,128)S(1)} %get-tuple-element.68), channel_id=1, source_target_pairs={{0,2},{2,0},{4,6},{6,4},{8,10},{10,8},{12,14},{14,12},{16,18},{18,... | collective-permute-start | bytes 196616 | tf_op jit(solution)/shard_map/ppermute | solution.py:364
  9.4 2.3 %collective-permute-start.10 = (f32[2,32,512]{2,1,0:T(8,128)S(1)}, f32[2,32,512]{2,1,0:T(8,128)S(1)}, u32[]{:S(2)}, u32[]{:S(2)}) collective-permute-start(f32[2,32,512]{2,1,0:T(8,128)S(1)} %get-tuple-element.67), channel_id=1, source_target_pairs={{0,2},{2,0},{4,6},{6,4},{8,10},{10,8},{12,14},{14,12},{16,18},{18,... | collective-permute-start | bytes 393224 | tf_op jit(solution)/shard_map/ppermute | solution.py:364
  9.6 6.2 %collective-permute-start.5 = (f32[2,48,512]{2,1,0:T(8,128)S(1)}, f32[2,48,512]{2,1,0:T(8,128)S(1)}, u32[]{:S(2)}, u32[]{:S(2)}) collective-permute-start(f32[2,48,512]{2,1,0:T(8,128)S(1)} %get-tuple-element.61), channel_id=1, source_target_pairs={{0,2},{2,4},{4,0},{6,8},{8,10},{10,12},{12,6},{14,16},{16,18},{18,... | collective-permute-start | bytes 589832 | tf_op jit(solution)/shard_map/ppermute | solution.py:367
  11.1 1.5 %collective-permute-start.8 = (f32[2,32,512]{2,1,0:T(8,128)S(1)}, f32[2,32,512]{2,1,0:T(8,128)S(1)}, u32[]{:S(2)}, u32[]{:S(2)}) collective-permute-start(f32[2,32,512]{2,1,0:T(8,128)S(1)} %get-tuple-element.65), channel_id=1, source_target_pairs={{0,2},{2,0},{4,6},{6,4},{8,10},{10,8},{12,14},{14,12},{16,18},{18,... | collective-permute-start | bytes 393224 | tf_op jit(solution)/shard_map/ppermute | solution.py:364
  11.3 1.3 %collective-permute-start.9 = (f32[2,16,512]{2,1,0:T(8,128)S(1)}, f32[2,16,512]{2,1,0:T(8,128)S(1)}, u32[]{:S(2)}, u32[]{:S(2)}) collective-permute-start(f32[2,16,512]{2,1,0:T(8,128)S(1)} %get-tuple-element.66), channel_id=1, source_target_pairs={{0,2},{2,0},{4,6},{6,4},{8,10},{10,8},{12,14},{14,12},{16,18},{18,... | collective-permute-start | bytes 196616 | tf_op jit(solution)/shard_map/ppermute | solution.py:364
  11.7 9.0 %collective-permute-start.18 = (f32[2,48,512]{2,1,0:T(8,128)S(1)}, f32[2,48,512]{2,1,0:T(8,128)S(1)}, u32[]{:S(2)}, u32[]{:S(2)}) collective-permute-start(f32[2,48,512]{2,1,0:T(8,128)S(1)} %get-tuple-element.81), channel_id=1, source_target_pairs={{0,2},{2,4},{4,0},{6,8},{8,10},{10,12},{12,6},{14,16},{16,18},{18,... | collective-permute-start | bytes 589832 | tf_op jit(solution)/shard_map/ppermute | solution.py:367
  12.6 9.3 %collective-permute-start.17 = (f32[2,48,512]{2,1,0:T(8,128)S(1)}, f32[2,48,512]{2,1,0:T(8,128)S(1)}, u32[]{:S(2)}, u32[]{:S(2)}) collective-permute-start(f32[2,48,512]{2,1,0:T(8,128)S(1)} %get-tuple-element.80), channel_id=1, source_target_pairs={{0,2},{2,4},{4,0},{6,8},{8,10},{10,12},{12,6},{14,16},{16,18},{18,... | collective-permute-start | bytes 589832 | tf_op jit(solution)/shard_map/ppermute | solution.py:367
  14.5 2.5 %collective-permute-start.14 = (f32[2,32,512]{2,1,0:T(8,128)S(1)}, f32[2,32,512]{2,1,0:T(8,128)S(1)}, u32[]{:S(2)}, u32[]{:S(2)}) collective-permute-start(f32[2,32,512]{2,1,0:T(8,128)S(1)} %get-tuple-element.75), channel_id=1, source_target_pairs={{0,2},{2,0},{4,6},{6,4},{8,10},{10,8},{12,14},{14,12},{16,18},{18,... | collective-permute-start | bytes 393224 | tf_op jit(solution)/shard_map/ppermute | solution.py:364
  14.6 1.9 %collective-permute-start.15 = (f32[2,16,512]{2,1,0:T(8,128)S(1)}, f32[2,16,512]{2,1,0:T(8,128)S(1)}, u32[]{:S(2)}, u32[]{:S(2)}) collective-permute-start(f32[2,16,512]{2,1,0:T(8,128)S(1)} %get-tuple-element.76), channel_id=1, source_target_pairs={{0,2},{2,0},{4,6},{6,4},{8,10},{10,8},{12,14},{14,12},{16,18},{18,... | collective-permute-start | bytes 196616 | tf_op jit(solution)/shard_map/ppermute | solution.py:364
  16.4 1.5 %collective-permute-start.12 = (f32[2,32,512]{2,1,0:T(8,128)S(1)}, f32[2,32,512]{2,1,0:T(8,128)S(1)}, u32[]{:S(2)}, u32[]{:S(2)}) collective-permute-start(f32[2,32,512]{2,1,0:T(8,128)S(1)} %get-tuple-element.73), channel_id=1, source_target_pairs={{0,2},{2,0},{4,6},{6,4},{8,10},{10,8},{12,14},{14,12},{16,18},{18,... | collective-permute-start | bytes 393224 | tf_op jit(solution)/shard_map/ppermute | solution.py:364
  16.5 1.4 %collective-permute-start.13 = (f32[2,16,512]{2,1,0:T(8,128)S(1)}, f32[2,16,512]{2,1,0:T(8,128)S(1)}, u32[]{:S(2)}, u32[]{:S(2)}) collective-permute-start(f32[2,16,512]{2,1,0:T(8,128)S(1)} %get-tuple-element.74), channel_id=1, source_target_pairs={{0,2},{2,0},{4,6},{6,4},{8,10},{10,8},{12,14},{14,12},{16,18},{18,... | collective-permute-start | bytes 196616 | tf_op jit(solution)/shard_map/ppermute | solution.py:364
  17.0 6.1 %collective-permute-start.21 = (f32[2,48,512]{2,1,0:T(8,128)S(1)}, f32[2,48,512]{2,1,0:T(8,128)S(1)}, u32[]{:S(2)}, u32[]{:S(2)}) collective-permute-start(f32[2,48,512]{2,1,0:T(8,128)S(1)} %get-tuple-element.86), channel_id=1, source_target_pairs={{0,2},{2,4},{4,0},{6,8},{8,10},{10,12},{12,6},{14,16},{16,18},{18,... | collective-permute-start | bytes 589832 | tf_op jit(solution)/shard_map/ppermute | solution.py:367
  17.9 7.9 %collective-permute-start.16 = (f32[2,48,512]{2,1,0:T(8,128)S(1)}, f32[2,48,512]{2,1,0:T(8,128)S(1)}, u32[]{:S(2)}, u32[]{:S(2)}) collective-permute-start(f32[2,48,512]{2,1,0:T(8,128)S(1)} %get-tuple-element.79), channel_id=1, source_target_pairs={{0,0},{2,4},{4,2},{6,8},{8,10},{10,12},{12,6},{14,16},{16,18},{18,... | collective-permute-start | bytes 589832 | tf_op jit(solution)/shard_map/ppermute | solution.py:367
  21.3 1.3 %collective-permute-start.23 = (f32[2,16,512]{2,1,0:T(8,128)S(1)}, f32[2,16,512]{2,1,0:T(8,128)S(1)}, u32[]{:S(2)}, u32[]{:S(2)}) collective-permute-start(f32[2,16,512]{2,1,0:T(8,128)S(1)} %get-tuple-element.88), channel_id=1, source_target_pairs={{0,2},{2,0},{4,6},{6,4},{8,10},{10,8},{12,14},{14,12},{16,18},{18,... | collective-permute-start | bytes 196616 | tf_op jit(solution)/shard_map/ppermute | solution.py:364
  21.4 1.7 %collective-permute-start.22 = (f32[2,32,512]{2,1,0:T(8,128)S(1)}, f32[2,32,512]{2,1,0:T(8,128)S(1)}, u32[]{:S(2)}, u32[]{:S(2)}) collective-permute-start(f32[2,32,512]{2,1,0:T(8,128)S(1)} %get-tuple-element.87), channel_id=1, source_target_pairs={{0,2},{2,0},{4,6},{6,4},{8,10},{10,8},{12,14},{14,12},{16,18},{18,... | collective-permute-start | bytes 393224 | tf_op jit(solution)/shard_map/ppermute | solution.py:364
  22.4 1.5 %collective-permute-start.19 = (f32[2,32,512]{2,1,0:T(8,128)S(1)}, f32[2,32,512]{2,1,0:T(8,128)S(1)}, u32[]{:S(2)}, u32[]{:S(2)}) collective-permute-start(f32[2,32,512]{2,1,0:T(8,128)S(1)} %get-tuple-element.84), channel_id=1, source_target_pairs={{0,2},{2,0},{4,6},{6,4},{8,10},{10,8},{12,14},{14,12},{16,18},{18,... | collective-permute-start | bytes 393224 | tf_op jit(solution)/shard_map/ppermute | solution.py:364
  22.6 1.4 %collective-permute-start.20 = (f32[2,16,512]{2,1,0:T(8,128)S(1)}, f32[2,16,512]{2,1,0:T(8,128)S(1)}, u32[]{:S(2)}, u32[]{:S(2)}) collective-permute-start(f32[2,16,512]{2,1,0:T(8,128)S(1)} %get-tuple-element.85), channel_id=1, source_target_pairs={{0,2},{2,0},{4,6},{6,4},{8,10},{10,8},{12,14},{14,12},{16,18},{18,... | collective-permute-start | bytes 196616 | tf_op jit(solution)/shard_map/ppermute | solution.py:364
  25.8 3.6 %collective-permute-start.24 = (f32[1,256]{1,0:T(1,128)S(1)}, f32[1,256]{1,0:T(1,128)S(1)}, u32[]{:S(2)}, u32[]{:S(2)}) collective-permute-start(f32[1,256]{1,0:T(1,128)S(1)} %get-tuple-element.93), channel_id=1, source_target_pairs={{0,1},{1,0},{2,3},{3,2},{4,5},{5,4},{6,7},{7,6},{8,9},{9,8},{10,11... | collective-permute-start | bytes 3080 | tf_op jit(solution)/shard_map/ppermute | solution.py:403

commit v14 on v11

--- a/solution.py
+++ b/solution.py
@@ -329,13 +329,20 @@
     )(*operands)
 
 
-def cross_route(levels):
+def cross_route(levels, upper=True):
     route = {level: (level + 1) % levels for level in range(levels)}
     chips = levels // 2
-    if chips % 2 == 0:
+    if chips % 2 or chips < 4:
+        return sorted(route.items())
+    if upper:
         for chip in range(chips - 1, 1, -2):
             route[levels - 1 if chip == chips - 1 else 2 * chip] = 2 * (chip - 2) + 1
-        route[2 if chips > 2 else levels - 1] = 0
+        route[2] = 0
+    else:
+        route[levels - 1] = levels - 3
+        for chip in range(chips - 2, 2, -2):
+            route[2 * chip] = 2 * (chip - 2) + 1
+        route[4] = 0
     return sorted(route.items())
 
 
@@ -352,14 +359,14 @@
     shots = arriving_downward_matrices.shape[3]
     mate_route = [(level, level ^ 1) for level in range(levels)]
     down_route = cross_route(levels)
-    open_route = [(level, level + 1) for level in range(1, levels - 1, 2)]
+    other_route = cross_route(levels, False)
     shared = (ascending_residual, impedance_contrast, shot_node_indices, emitted_pulse[0].T)
 
     def mate(pieces):
         return [lax.ppermute(piece, "depth", mate_route) for piece in pieces]
 
-    def down(piece, closed=True):
-        return lax.ppermute(piece, "depth", down_route if closed else open_route)
+    def down(piece, other=False):
+        return lax.ppermute(piece, "depth", other_route if other else down_route)
 
     rows = shots // HALVES
     start = (extrapolation_operator, impedance_contrast, ascending_residual, arriving_downward_matrices)
@@ -369,9 +376,9 @@
     beside = [mate(even[2 * half : 2 * half + 2]) for half in range(HALVES)]
     grads = [grad]
 
-    def odd_step(tick, start, pieces, closed=True):
+    def odd_step(tick, start, pieces, other=False):
         odd, grads[0] = step(tick, start, 1, pieces, shared, high, low, grads[0], rows)
-        return down(odd, closed)
+        return down(odd, other)
 
     def even_step(tick, start, pieces):
         *even, grads[0] = step(tick, start, 0, pieces, shared, high, low, grads[0], rows)
@@ -384,7 +391,7 @@
     above, beside = later, latest
     for tick in range(2, TICKS - 1):
         later = [
-            odd_step(tick, half * rows, beside[half], tick < TICKS - 2 or half < HALVES - 1) for half in range(HALVES)
+            odd_step(tick, half * rows, beside[half], tick == TICKS - 2 and half == 0) for half in range(HALVES)
         ]
         beside = [even_step(tick, half * rows, [above[half]]) for half in range(HALVES)]
         above = later

time: 30.2 us -> 30.5 us (level)
  the two profiles are of different devices: /device:TPU:16 before, /device:TPU:25 now
where the time goes in v14:
time: 30.5 us; the launch traced here: 30.3 us
  starting transfers between devices  14.9 us (49%)
  Pallas kernels  7.71 us (25%)
  waiting for transfers between devices  6.32 us (21%)
  between operations  0.82 us (3%)
  other arithmetic  0.57 us (2%)
    ppermute x16, starting transfers between devices, mate(): return [lax.ppermute(piece, 'depth', mate_route) for piece in pieces]  8.6 us
    ppermute x8, waiting for transfers between devices, down(): return lax.ppermute(piece, 'depth', other_route if other else down_route)  5.07 us
    ppermute x8, starting transfers between devices, down(): return lax.ppermute(piece, 'depth', other_route if other else down_route)  5.03 us
    pallas_call x12, Pallas kernels, step(): pl.pallas_call(functools.partial(step_kernel, tick, start, parity, len(pi...  3.22 us
    pallas_call x2, Pallas kernels, first(): pl.pallas_call(functools.partial(first_kernel, parity, bool(carried)), ou...  2.57 us
    pallas_call x2, Pallas kernels, last(): pl.pallas_call(functools.partial(last_kernel, half), out_shape=out_shape,...  1.85 us
    ppermute x1, starting transfers between devices, local(): gradient = gradient + lax.ppermute(chunks[distance], 'freq', route)  1.28 us
    ppermute x16, waiting for transfers between devices, mate(): return [lax.ppermute(piece, 'depth', mate_route) for piece in pieces]  1.25 us
  transfers between devices with their start and end apart: 25, of which 4 were waited for; matrix products, arithmetic and copies ran while one was open for 0% of the time, Pallas kernels for 17%

profile of v14, /device:TPU:25, one launch (start us, length us, event | category | flops | bytes accessed | tf_op | source)
XLA Modules:
  0.0 30.3 jit_solution(2534365783801876992)
XLA Ops:
  0.6 2.5 %first_1.1 = (f32[2,48,512]{2,1,0:T(8,128)S(1)}, f32[2,48,512]{2,1,0:T(8,128)S(1)}, bf16[2,512,512]{2,1,0:T(8,128)(2,1)S(1)}, bf16[2,512,512]{2,1,0:T(8,128)(2,1)S(1)}, f32[8,512]{1,0:T(8,128)S(1)}) custom-call(f32[1,1,2,512,512]{4,3,2,1,0:T(8,128)} %refs_0_.5, f32[1,512]{1,0:T(1,128)} %contrast.1, f32[1,1,5,2,96,512]{5,4,3,2,1,0:T(8,128)} %residual.1, ...), custom_call_target="tpu_custom_call" | custom-call | flops 1000000000 | bytes 1 | tf_op jit(solution)/shard_map/first_1/pallas_call | solution.py:173
  3.1 0.1 collective-permute-start.2
  3.2 1.6 %collective-permute-start.7 = (f32[2,48,512]{2,1,0:T(8,128)S(1)}, f32[2,48,512]{2,1,0:T(8,128)S(1)}, u32[]{:S(2)}, u32[]{:S(2)}) collective-permute-start(f32[2,48,512]{2,1,0:T(8,128)S(1)} %get-tuple-element.63), channel_id=1, source_target_pairs={{0,2},{2,4},{4,0},{6,8},{8,10},{10,12},{12,6},{14,16},{16,18},{18,... | collective-permute-start | bytes 589832 | tf_op jit(solution)/shard_map/ppermute | solution.py:369
  4.8 0.1 first_0.1
  4.9 1.5 %collective-permute-start.3 = (f32[2,32,512]{2,1,0:T(8,128)S(1)}, f32[2,32,512]{2,1,0:T(8,128)S(1)}, u32[]{:S(2)}, u32[]{:S(2)}) collective-permute-start(f32[2,32,512]{2,1,0:T(8,128)S(1)} %get-tuple-element.56), channel_id=1, source_target_pairs={{0,2},{2,0},{4,6},{6,4},{8,10},{10,8},{12,14},{14,12},{16,18},{18,... | collective-permute-start | bytes 393224 | tf_op jit(solution)/shard_map/ppermute | solution.py:366
  6.5 0.1 collective-permute-start.4
  6.5 0.4 %collective-permute-start = (f32[2,32,512]{2,1,0:T(8,128)S(1)}, f32[2,32,512]{2,1,0:T(8,128)S(1)}, u32[]{:S(2)}, u32[]{:S(2)}) collective-permute-start(f32[2,32,512]{2,1,0:T(8,128)S(1)} %get-tuple-element.51), channel_id=1, source_target_pairs={{0,2},{2,0},{4,6},{6,4},{8,10},{10,8},{12,14},{14,12},{16,18},{18,... | collective-permute-start | bytes 393224 | tf_op jit(solution)/shard_map/ppermute | solution.py:366
  7.0 0.7 %collective-permute-done.4.refs_1_ = f32[2,16,512]{2,1,0:T(8,128)S(1)} collective-permute-done((f32[2,16,512]{2,1,0:T(8,128)S(1)}, f32[2,16,512]{2,1,0:T(8,128)S(1)}, u32[]{:S(2)}, u32[]{:S(2)}) %collective-permute-start.4) | collective-permute-done | bytes 65568 | tf_op jit(solution)/shard_map/ppermute | solution.py:366
  7.7 0.2 collective-permute-start.1
  7.9 0.0 collective-permute-done.3.refs_0_
  7.9 0.0 copy-done.2
  7.9 0.0 copy-done.3
  7.9 0.5 %step_1_0_1.1 = (f32[2,48,512]{2,1,0:T(8,128)S(1)}, f32[8,512]{1,0:T(8,128)S(1)}) custom-call(f32[2,32,512]{2,1,0:T(8,128)S(1)} %collective-permute-done.3.refs_0_, f32[2,16,512]{2,1,0:T(8,128)S(1)} %collective-permute-done.4.refs_1_, f32[1,1,5,2,96,512]{5,4,3,2,1,0:T(8,128)S(1)} %copy-done, ...), custom_call_target="tpu_custom_call", output_to_operand_aliasing={{1}: (8, {})} | custom-call | flops 10000000 | bytes 1 | tf_op jit(solution)/shard_map/step_1_0_1/pallas_call | solution.py:244
  8.5 1.1 %collective-permute-start.6 = (f32[2,48,512]{2,1,0:T(8,128)S(1)}, f32[2,48,512]{2,1,0:T(8,128)S(1)}, u32[]{:S(2)}, u32[]{:S(2)}) collective-permute-start(f32[2,48,512]{2,1,0:T(8,128)S(1)} %get-tuple-element.62), channel_id=1, source_target_pairs={{0,2},{2,4},{4,0},{6,8},{8,10},{10,12},{12,6},{14,16},{16,18},{18,... | collective-permute-start | bytes 589832 | tf_op jit(solution)/shard_map/ppermute | solution.py:369
  9.6 0.0 collective-permute-done.2.refs_0_
  9.6 0.1 collective-permute-start.11
  9.7 0.0 collective-permute-done.1.refs_1_
  9.7 0.4 %collective-permute-start.10 = (f32[2,32,512]{2,1,0:T(8,128)S(1)}, f32[2,32,512]{2,1,0:T(8,128)S(1)}, u32[]{:S(2)}, u32[]{:S(2)}) collective-permute-start(f32[2,32,512]{2,1,0:T(8,128)S(1)} %get-tuple-element.67), channel_id=1, source_target_pairs={{0,2},{2,0},{4,6},{6,4},{8,10},{10,8},{12,14},{14,12},{16,18},{18,... | collective-permute-start | bytes 393224 | tf_op jit(solution)/shard_map/ppermute | solution.py:366
  10.1 0.0 collective-permute-done.refs_0_
  10.1 0.5 %step_1_1_1.1 = (f32[2,48,512]{2,1,0:T(8,128)S(1)}, f32[8,512]{1,0:T(8,128)S(1)}) custom-call(f32[2,32,512]{2,1,0:T(8,128)S(1)} %collective-permute-done.refs_0_, f32[2,16,512]{2,1,0:T(8,128)S(1)} %collective-permute-done.1.refs_1_, f32[1,1,5,2,96,512]{5,4,3,2,1,0:T(8,128)S(1)} %copy-done, f32[1,512]{1,0:T(1,128)S(1)} %copy-done.1, ...), custom_call_target="tpu_custom_call", output_to_operand_aliasing={{1}: (8, {})} | custom-call | flops 30000000 | bytes 1 | tf_op jit(solution)/shard_map/step_1_1_1/pallas_call | solution.py:244
  10.6 0.8 %collective-permute-start.5 = (f32[2,48,512]{2,1,0:T(8,128)S(1)}, f32[2,48,512]{2,1,0:T(8,128)S(1)}, u32[]{:S(2)}, u32[]{:S(2)}) collective-permute-start(f32[2,48,512]{2,1,0:T(8,128)S(1)} %get-tuple-element.61), channel_id=1, source_target_pairs={{0,2},{2,4},{4,0},{6,8},{8,10},{10,12},{12,6},{14,16},{16,18},{18,... | collective-permute-start | bytes 589832 | tf_op jit(solution)/shard_map/ppermute | solution.py:369
  11.5 0.0 collective-permute-done.7.refs_0_
  11.5 0.4 %collective-permute-start.8 = (f32[2,32,512]{2,1,0:T(8,128)S(1)}, f32[2,32,512]{2,1,0:T(8,128)S(1)}, u32[]{:S(2)}, u32[]{:S(2)}) collective-permute-start(f32[2,32,512]{2,1,0:T(8,128)S(1)} %get-tuple-element.65), channel_id=1, source_target_pairs={{0,2},{2,0},{4,6},{6,4},{8,10},{10,8},{12,14},{14,12},{16,18},{18,... | collective-permute-start | bytes 393224 | tf_op jit(solution)/shard_map/ppermute | solution.py:366
  11.9 0.0 collective-permute-done.11.refs_1_
  11.9 0.1 collective-permute-start.9
  12.0 0.0 collective-permute-done.10.refs_0_
  12.0 0.5 %step_2_0_1.1 = (f32[2,48,512]{2,1,0:T(8,128)S(1)}, f32[8,512]{1,0:T(8,128)S(1)}) custom-call(f32[2,32,512]{2,1,0:T(8,128)S(1)} %collective-permute-done.10.refs_0_, f32[2,16,512]{2,1,0:T(8,128)S(1)} %collective-permute-done.11.refs_1_, f32[1,1,5,2,96,512]{5,4,3,2,1,0:T(8,128)S(1)} %copy-done, ...), custom_call_target="tpu_custom_call", output_to_operand_aliasing={{1}: (8, {})} | custom-call | flops 1000000 | bytes 1 | tf_op jit(solution)/shard_map/step_2_0_1/pallas_call | solution.py:244
  12.5 0.8 %collective-permute-start.18 = (f32[2,48,512]{2,1,0:T(8,128)S(1)}, f32[2,48,512]{2,1,0:T(8,128)S(1)}, u32[]{:S(2)}, u32[]{:S(2)}) collective-permute-start(f32[2,48,512]{2,1,0:T(8,128)S(1)} %get-tuple-element.81), channel_id=1, source_target_pairs={{0,2},{2,4},{4,0},{6,8},{8,10},{10,12},{12,6},{14,16},{16,18},{18,... | collective-permute-start | bytes 589832 | tf_op jit(solution)/shard_map/ppermute | solution.py:369
  13.3 0.0 collective-permute-done.9.refs_1_
  13.3 0.0 collective-permute-done.8.refs_0_
  13.3 0.5 %step_2_1_1.1 = (f32[2,48,512]{2,1,0:T(8,128)S(1)}, f32[8,512]{1,0:T(8,128)S(1)}) custom-call(f32[2,32,512]{2,1,0:T(8,128)S(1)} %collective-permute-done.8.refs_0_, f32[2,16,512]{2,1,0:T(8,128)S(1)} %collective-permute-done.9.refs_1_, f32[1,1,5,2,96,512]{5,4,3,2,1,0:T(8,128)S(1)} %copy-done, ...), custom_call_target="tpu_custom_call", output_to_operand_aliasing={{1}: (8, {})} | custom-call | flops 30000000 | bytes 1 | tf_op jit(solution)/shard_map/step_2_1_1/pallas_call | solution.py:244
  13.9 0.4 %collective-permute-start.17 = (f32[2,48,512]{2,1,0:T(8,128)S(1)}, f32[2,48,512]{2,1,0:T(8,128)S(1)}, u32[]{:S(2)}, u32[]{:S(2)}) collective-permute-start(f32[2,48,512]{2,1,0:T(8,128)S(1)} %get-tuple-element.80), channel_id=1, source_target_pairs={{0,2},{2,4},{4,0},{6,8},{8,10},{10,12},{12,6},{14,16},{16,18},{18,... | collective-permute-start | bytes 589832 | tf_op jit(solution)/shard_map/ppermute | solution.py:369
  14.2 0.0 collective-permute-done.6.refs_0_
  14.2 0.8 %collective-permute-start.14 = (f32[2,32,512]{2,1,0:T(8,128)S(1)}, f32[2,32,512]{2,1,0:T(8,128)S(1)}, u32[]{:S(2)}, u32[]{:S(2)}) collective-permute-start(f32[2,32,512]{2,1,0:T(8,128)S(1)} %get-tuple-element.75), channel_id=1, source_target_pairs={{0,2},{2,0},{4,6},{6,4},{8,10},{10,8},{12,14},{14,12},{16,18},{18,... | collective-permute-start | bytes 393224 | tf_op jit(solution)/shard_map/ppermute | solution.py:366
  15.1 0.1 collective-permute-start.15
  15.1 0.0 collective-permute-done.5.refs_0_
  15.1 2.0 %collective-permute-start.12 = (f32[2,32,512]{2,1,0:T(8,128)S(1)}, f32[2,32,512]{2,1,0:T(8,128)S(1)}, u32[]{:S(2)}, u32[]{:S(2)}) collective-permute-start(f32[2,32,512]{2,1,0:T(8,128)S(1)} %get-tuple-element.73), channel_id=1, source_target_pairs={{0,2},{2,0},{4,6},{6,4},{8,10},{10,8},{12,14},{14,12},{16,18},{18,... | collective-permute-start | bytes 393224 | tf_op jit(solution)/shard_map/ppermute | solution.py:366
  17.1 0.0 collective-permute-done.15.refs_1_
  17.1 0.1 collective-permute-start.13
  17.2 0.0 collective-permute-done.14.refs_0_
  17.2 0.5 %step_3_0_1.1 = (f32[2,48,512]{2,1,0:T(8,128)S(1)}, f32[8,512]{1,0:T(8,128)S(1)}) custom-call(f32[2,32,512]{2,1,0:T(8,128)S(1)} %collective-permute-done.14.refs_0_, f32[2,16,512]{2,1,0:T(8,128)S(1)} %collective-permute-done.15.refs_1_, f32[1,1,5,2,96,512]{5,4,3,2,1,0:T(8,128)S(1)} %copy-done, ...), custom_call_target="tpu_custom_call", output_to_operand_aliasing={{1}: (8, {})} | custom-call | flops 30000000 | bytes 1 | tf_op jit(solution)/shard_map/step_3_0_1/pallas_call | solution.py:244
  17.7 0.2 collective-permute-start.21
  18.0 0.4 %collective-permute-done.13.refs_1_ = f32[2,16,512]{2,1,0:T(8,128)S(1)} collective-permute-done((f32[2,16,512]{2,1,0:T(8,128)S(1)}, f32[2,16,512]{2,1,0:T(8,128)S(1)}, u32[]{:S(2)}, u32[]{:S(2)}) %collective-permute-start.13) | collective-permute-done | bytes 65568 | tf_op jit(solution)/shard_map/ppermute | solution.py:366
  18.4 0.0 collective-permute-done.12.refs_0_
  18.4 0.5 %step_3_1_1.1 = (f32[2,48,512]{2,1,0:T(8,128)S(1)}, f32[8,512]{1,0:T(8,128)S(1)}) custom-call(f32[2,32,512]{2,1,0:T(8,128)S(1)} %collective-permute-done.12.refs_0_, f32[2,16,512]{2,1,0:T(8,128)S(1)} %collective-permute-done.13.refs_1_, f32[1,1,5,2,96,512]{5,4,3,2,1,0:T(8,128)S(1)} %copy-done, ...), custom_call_target="tpu_custom_call", output_to_operand_aliasing={{1}: (8, {})} | custom-call | flops 30000000 | bytes 1 | tf_op jit(solution)/shard_map/step_3_1_1/pallas_call | solution.py:244
  18.9 0.1 collective-permute-start.16
  19.0 0.0 collective-permute-done.18.refs_0_
  19.0 1.1 %collective-permute-start.23 = (f32[2,16,512]{2,1,0:T(8,128)S(1)}, f32[2,16,512]{2,1,0:T(8,128)S(1)}, u32[]{:S(2)}, u32[]{:S(2)}) collective-permute-start(f32[2,16,512]{2,1,0:T(8,128)S(1)} %get-tuple-element.88), channel_id=1, source_target_pairs={{0,2},{2,0},{4,6},{6,4},{8,10},{10,8},{12,14},{14,12},{16,18},{18,... | collective-permute-start | bytes 196616 | tf_op jit(solution)/shard_map/ppermute | solution.py:366
  20.1 0.1 collective-permute-start.22
  20.2 0.0 collective-permute-done.17.refs_0_
  20.2 1.1 %collective-permute-start.19 = (f32[2,32,512]{2,1,0:T(8,128)S(1)}, f32[2,32,512]{2,1,0:T(8,128)S(1)}, u32[]{:S(2)}, u32[]{:S(2)}) collective-permute-start(f32[2,32,512]{2,1,0:T(8,128)S(1)} %get-tuple-element.84), channel_id=1, source_target_pairs={{0,2},{2,0},{4,6},{6,4},{8,10},{10,8},{12,14},{14,12},{16,18},{18,... | collective-permute-start | bytes 393224 | tf_op jit(solution)/shard_map/ppermute | solution.py:366
  21.3 0.0 collective-permute-done.23.mate_tail
  21.3 0.1 collective-permute-start.20
  21.4 0.1 collective-permute-done.22.mate
  21.5 5.1 %collective-permute-done.21.above = f32[2,48,512]{2,1,0:T(8,128)S(1)} collective-permute-done((f32[2,48,512]{2,1,0:T(8,128)S(1)}, f32[2,48,512]{2,1,0:T(8,128)S(1)}, u32[]{:S(2)}, u32[]{:S(2)}) %collective-permute-start.21) | collective-permute-done | bytes 196640 | tf_op jit(solution)/shard_map/ppermute | solution.py:369
  26.5 0.6 %last_0.1 = (f32[2,48,512]{2,1,0:T(8,128)S(1)}, f32[8,512]{1,0:T(8,128)S(1)}) custom-call(f32[2,48,512]{2,1,0:T(8,128)S(1)} %collective-permute-done.21.above, f32[2,32,512]{2,1,0:T(8,128)S(1)} %collective-permute-done.22.mate, f32[2,16,512]{2,1,0:T(8,128)S(1)} %collective-permute-done.23.mate_tail, ...), custom_call_target="tpu_custom_call", output_to_operand_aliasing={{1}: (9, {})} | custom-call | flops 100000000 | bytes 1 | tf_op jit(solution)/shard_map/last_0/pallas_call | solution.py:319
  27.1 0.0 collective-permute-done.20.mate_tail
  27.1 0.0 collective-permute-done.19.mate
  27.1 0.0 collective-permute-done.16.above
  27.1 0.1 gradient.1
  27.2 1.3 %collective-permute-start.24 = (f32[1,256]{1,0:T(1,128)S(1)}, f32[1,256]{1,0:T(1,128)S(1)}, u32[]{:S(2)}, u32[]{:S(2)}) collective-permute-start(f32[1,256]{1,0:T(1,128)S(1)} %get-tuple-element.93), channel_id=1, source_target_pairs={{0,1},{1,0},{2,3},{3,2},{4,5},{5,4},{6,7},{7,6},{8,9},{9,8},{10,11... | collective-permute-start | bytes 3080 | tf_op jit(solution)/shard_map/ppermute | solution.py:405
  28.5 1.3 %last_1.1 = f32[2,96,512]{2,1,0:T(8,128)} custom-call(f32[2,48,512]{2,1,0:T(8,128)S(1)} %collective-permute-done.16.above, f32[2,32,512]{2,1,0:T(8,128)S(1)} %collective-permute-done.19.mate, f32[2,16,512]{2,1,0:T(8,128)S(1)} %collective-permute-done.20.mate_tail, f32[1,1,5,2,96,512]{5,4,3,2,1,0:T(8,128)S(1)} %copy-done, f32[1,512]{1,0:T(1,128)S(1)} %copy-done.1, ...), custom_call_target="tpu_custom_call" | custom-call | flops 1 | bytes 1 | tf_op jit(solution)/shard_map/last_1/pallas_call | solution.py:319
  29.8 0.0 collective-permute-done.24
  29.8 0.6 %add.3 = f32[1,256]{1,0:T(1,128)} add(f32[1,256]{1,0:T(1,128)S(1)} %get-tuple-element.92, f32[1,256]{1,0:T(1,128)S(1)} %collective-permute-done.24) | non-fusion elementwise | flops 256 | bytes 3072 | tf_op jit(solution)/shard_map/add | solution.py:405
  (12 shorter events, 0.0 us)
Async XLA Ops:
  3.1 6.5 %collective-permute-start.2 = (f32[2,48,512]{2,1,0:T(8,128)S(1)}, f32[2,48,512]{2,1,0:T(8,128)S(1)}, u32[]{:S(2)}, u32[]{:S(2)}) collective-permute-start(f32[2,48,512]{2,1,0:T(8,128)S(1)} %get-tuple-element.55), channel_id=1, source_target_pairs={{0,2},{2,4},{4,0},{6,8},{8,10},{10,12},{12,6},{14,16},{16,18},{18,... | collective-permute-start | bytes 589832 | tf_op jit(solution)/shard_map/ppermute | solution.py:369
  3.2 8.3 %collective-permute-start.7 = (f32[2,48,512]{2,1,0:T(8,128)S(1)}, f32[2,48,512]{2,1,0:T(8,128)S(1)}, u32[]{:S(2)}, u32[]{:S(2)}) collective-permute-start(f32[2,48,512]{2,1,0:T(8,128)S(1)} %get-tuple-element.63), channel_id=1, source_target_pairs={{0,2},{2,4},{4,0},{6,8},{8,10},{10,12},{12,6},{14,16},{16,18},{18,... | collective-permute-start | bytes 589832 | tf_op jit(solution)/shard_map/ppermute | solution.py:369
  4.8 3.1 %copy-start = (f32[1,1,5,2,96,512]{5,4,3,2,1,0:T(8,128)S(1)}, f32[1,1,5,2,96,512]{5,4,3,2,1,0:T(8,128)}, u32[]{:S(2)}) copy-start(f32[1,1,5,2,96,512]{5,4,3,2,1,0:T(8,128)} %residual.1) | copy-start | bytes 5898244
  4.8 3.1 %copy-start.1 = (f32[1,512]{1,0:T(1,128)S(1)}, f32[1,512]{1,0:T(1,128)}, u32[]{:S(2)}) copy-start(f32[1,512]{1,0:T(1,128)} %contrast.1) | copy-start | bytes 6148
  4.8 3.1 %copy-start.2 = (s32[4,96]{1,0:T(4,128)S(1)}, s32[4,96]{1,0:T(4,128)}, u32[]{:S(2)}) copy-start(s32[4,96]{1,0:T(4,128)} %sites.1) | copy-start | bytes 4612
  4.8 3.1 %copy-start.3 = (f32[1,4,2]{1,2,0:T(2,128)S(1)}, f32[1,4,2]{1,2,0:T(2,128)}, u32[]{:S(2)}) copy-start(f32[1,4,2]{1,2,0:T(2,128)} %param.11) | copy-start | bytes 100
  4.9 3.0 %collective-permute-start.3 = (f32[2,32,512]{2,1,0:T(8,128)S(1)}, f32[2,32,512]{2,1,0:T(8,128)S(1)}, u32[]{:S(2)}, u32[]{:S(2)}) collective-permute-start(f32[2,32,512]{2,1,0:T(8,128)S(1)} %get-tuple-element.56), channel_id=1, source_target_pairs={{0,2},{2,0},{4,6},{6,4},{8,10},{10,8},{12,14},{14,12},{16,18},{18,... | collective-permute-start | bytes 393224 | tf_op jit(solution)/shard_map/ppermute | solution.py:366
  6.5 1.3 %collective-permute-start.4 = (f32[2,16,512]{2,1,0:T(8,128)S(1)}, f32[2,16,512]{2,1,0:T(8,128)S(1)}, u32[]{:S(2)}, u32[]{:S(2)}) collective-permute-start(f32[2,16,512]{2,1,0:T(8,128)S(1)} %get-tuple-element.57), channel_id=1, source_target_pairs={{0,2},{2,0},{4,6},{6,4},{8,10},{10,8},{12,14},{14,12},{16,18},{18,... | collective-permute-start | bytes 196616 | tf_op jit(solution)/shard_map/ppermute | solution.py:366
  6.5 3.6 %collective-permute-start = (f32[2,32,512]{2,1,0:T(8,128)S(1)}, f32[2,32,512]{2,1,0:T(8,128)S(1)}, u32[]{:S(2)}, u32[]{:S(2)}) collective-permute-start(f32[2,32,512]{2,1,0:T(8,128)S(1)} %get-tuple-element.51), channel_id=1, source_target_pairs={{0,2},{2,0},{4,6},{6,4},{8,10},{10,8},{12,14},{14,12},{16,18},{18,... | collective-permute-start | bytes 393224 | tf_op jit(solution)/shard_map/ppermute | solution.py:366
  7.7 2.0 %collective-permute-start.1 = (f32[2,16,512]{2,1,0:T(8,128)S(1)}, f32[2,16,512]{2,1,0:T(8,128)S(1)}, u32[]{:S(2)}, u32[]{:S(2)}) collective-permute-start(f32[2,16,512]{2,1,0:T(8,128)S(1)} %get-tuple-element.52), channel_id=1, source_target_pairs={{0,2},{2,0},{4,6},{6,4},{8,10},{10,8},{12,14},{14,12},{16,18},{18,... | collective-permute-start | bytes 196616 | tf_op jit(solution)/shard_map/ppermute | solution.py:366
  8.5 5.7 %collective-permute-start.6 = (f32[2,48,512]{2,1,0:T(8,128)S(1)}, f32[2,48,512]{2,1,0:T(8,128)S(1)}, u32[]{:S(2)}, u32[]{:S(2)}) collective-permute-start(f32[2,48,512]{2,1,0:T(8,128)S(1)} %get-tuple-element.62), channel_id=1, source_target_pairs={{0,2},{2,4},{4,0},{6,8},{8,10},{10,12},{12,6},{14,16},{16,18},{18,... | collective-permute-start | bytes 589832 | tf_op jit(solution)/shard_map/ppermute | solution.py:369
  9.6 2.3 %collective-permute-start.11 = (f32[2,16,512]{2,1,0:T(8,128)S(1)}, f32[2,16,512]{2,1,0:T(8,128)S(1)}, u32[]{:S(2)}, u32[]{:S(2)}) collective-permute-start(f32[2,16,512]{2,1,0:T(8,128)S(1)} %get-tuple-element.68), channel_id=1, source_target_pairs={{0,2},{2,0},{4,6},{6,4},{8,10},{10,8},{12,14},{14,12},{16,18},{18,... | collective-permute-start | bytes 196616 | tf_op jit(solution)/shard_map/ppermute | solution.py:366
  9.7 2.3 %collective-permute-start.10 = (f32[2,32,512]{2,1,0:T(8,128)S(1)}, f32[2,32,512]{2,1,0:T(8,128)S(1)}, u32[]{:S(2)}, u32[]{:S(2)}) collective-permute-start(f32[2,32,512]{2,1,0:T(8,128)S(1)} %get-tuple-element.67), channel_id=1, source_target_pairs={{0,2},{2,0},{4,6},{6,4},{8,10},{10,8},{12,14},{14,12},{16,18},{18,... | collective-permute-start | bytes 393224 | tf_op jit(solution)/shard_map/ppermute | solution.py:366
  10.6 4.5 %collective-permute-start.5 = (f32[2,48,512]{2,1,0:T(8,128)S(1)}, f32[2,48,512]{2,1,0:T(8,128)S(1)}, u32[]{:S(2)}, u32[]{:S(2)}) collective-permute-start(f32[2,48,512]{2,1,0:T(8,128)S(1)} %get-tuple-element.61), channel_id=1, source_target_pairs={{0,2},{2,4},{4,0},{6,8},{8,10},{10,12},{12,6},{14,16},{16,18},{18,... | collective-permute-start | bytes 589832 | tf_op jit(solution)/shard_map/ppermute | solution.py:369
  11.5 1.8 %collective-permute-start.8 = (f32[2,32,512]{2,1,0:T(8,128)S(1)}, f32[2,32,512]{2,1,0:T(8,128)S(1)}, u32[]{:S(2)}, u32[]{:S(2)}) collective-permute-start(f32[2,32,512]{2,1,0:T(8,128)S(1)} %get-tuple-element.65), channel_id=1, source_target_pairs={{0,2},{2,0},{4,6},{6,4},{8,10},{10,8},{12,14},{14,12},{16,18},{18,... | collective-permute-start | bytes 393224 | tf_op jit(solution)/shard_map/ppermute | solution.py:366
  11.9 1.4 %collective-permute-start.9 = (f32[2,16,512]{2,1,0:T(8,128)S(1)}, f32[2,16,512]{2,1,0:T(8,128)S(1)}, u32[]{:S(2)}, u32[]{:S(2)}) collective-permute-start(f32[2,16,512]{2,1,0:T(8,128)S(1)} %get-tuple-element.66), channel_id=1, source_target_pairs={{0,2},{2,0},{4,6},{6,4},{8,10},{10,8},{12,14},{14,12},{16,18},{18,... | collective-permute-start | bytes 196616 | tf_op jit(solution)/shard_map/ppermute | solution.py:366
  12.5 6.4 %collective-permute-start.18 = (f32[2,48,512]{2,1,0:T(8,128)S(1)}, f32[2,48,512]{2,1,0:T(8,128)S(1)}, u32[]{:S(2)}, u32[]{:S(2)}) collective-permute-start(f32[2,48,512]{2,1,0:T(8,128)S(1)} %get-tuple-element.81), channel_id=1, source_target_pairs={{0,2},{2,4},{4,0},{6,8},{8,10},{10,12},{12,6},{14,16},{16,18},{18,... | collective-permute-start | bytes 589832 | tf_op jit(solution)/shard_map/ppermute | solution.py:369
  13.9 6.3 %collective-permute-start.17 = (f32[2,48,512]{2,1,0:T(8,128)S(1)}, f32[2,48,512]{2,1,0:T(8,128)S(1)}, u32[]{:S(2)}, u32[]{:S(2)}) collective-permute-start(f32[2,48,512]{2,1,0:T(8,128)S(1)} %get-tuple-element.80), channel_id=1, source_target_pairs={{0,2},{2,4},{4,0},{6,8},{8,10},{10,12},{12,6},{14,16},{16,18},{18,... | collective-permute-start | bytes 589832 | tf_op jit(solution)/shard_map/ppermute | solution.py:369
  14.2 3.0 %collective-permute-start.14 = (f32[2,32,512]{2,1,0:T(8,128)S(1)}, f32[2,32,512]{2,1,0:T(8,128)S(1)}, u32[]{:S(2)}, u32[]{:S(2)}) collective-permute-start(f32[2,32,512]{2,1,0:T(8,128)S(1)} %get-tuple-element.75), channel_id=1, source_target_pairs={{0,2},{2,0},{4,6},{6,4},{8,10},{10,8},{12,14},{14,12},{16,18},{18,... | collective-permute-start | bytes 393224 | tf_op jit(solution)/shard_map/ppermute | solution.py:366
  15.1 2.0 %collective-permute-start.15 = (f32[2,16,512]{2,1,0:T(8,128)S(1)}, f32[2,16,512]{2,1,0:T(8,128)S(1)}, u32[]{:S(2)}, u32[]{:S(2)}) collective-permute-start(f32[2,16,512]{2,1,0:T(8,128)S(1)} %get-tuple-element.76), channel_id=1, source_target_pairs={{0,2},{2,0},{4,6},{6,4},{8,10},{10,8},{12,14},{14,12},{16,18},{18,... | collective-permute-start | bytes 196616 | tf_op jit(solution)/shard_map/ppermute | solution.py:366
  15.1 3.2 %collective-permute-start.12 = (f32[2,32,512]{2,1,0:T(8,128)S(1)}, f32[2,32,512]{2,1,0:T(8,128)S(1)}, u32[]{:S(2)}, u32[]{:S(2)}) collective-permute-start(f32[2,32,512]{2,1,0:T(8,128)S(1)} %get-tuple-element.73), channel_id=1, source_target_pairs={{0,2},{2,0},{4,6},{6,4},{8,10},{10,8},{12,14},{14,12},{16,18},{18,... | collective-permute-start | bytes 393224 | tf_op jit(solution)/shard_map/ppermute | solution.py:366
  17.1 1.3 %collective-permute-start.13 = (f32[2,16,512]{2,1,0:T(8,128)S(1)}, f32[2,16,512]{2,1,0:T(8,128)S(1)}, u32[]{:S(2)}, u32[]{:S(2)}) collective-permute-start(f32[2,16,512]{2,1,0:T(8,128)S(1)} %get-tuple-element.74), channel_id=1, source_target_pairs={{0,2},{2,0},{4,6},{6,4},{8,10},{10,8},{12,14},{14,12},{16,18},{18,... | collective-permute-start | bytes 196616 | tf_op jit(solution)/shard_map/ppermute | solution.py:366
  17.7 8.8 %collective-permute-start.21 = (f32[2,48,512]{2,1,0:T(8,128)S(1)}, f32[2,48,512]{2,1,0:T(8,128)S(1)}, u32[]{:S(2)}, u32[]{:S(2)}) collective-permute-start(f32[2,48,512]{2,1,0:T(8,128)S(1)} %get-tuple-element.86), channel_id=1, source_target_pairs={{0,2},{2,4},{4,6},{6,8},{8,0},{10,12},{12,14},{14,16},{16,10},{18,... | collective-permute-start | bytes 589832 | tf_op jit(solution)/shard_map/ppermute | solution.py:369
  18.9 8.2 %collective-permute-start.16 = (f32[2,48,512]{2,1,0:T(8,128)S(1)}, f32[2,48,512]{2,1,0:T(8,128)S(1)}, u32[]{:S(2)}, u32[]{:S(2)}) collective-permute-start(f32[2,48,512]{2,1,0:T(8,128)S(1)} %get-tuple-element.79), channel_id=1, source_target_pairs={{0,2},{2,4},{4,0},{6,8},{8,10},{10,12},{12,6},{14,16},{16,18},{18,... | collective-permute-start | bytes 589832 | tf_op jit(solution)/shard_map/ppermute | solution.py:369
  19.0 2.3 %collective-permute-start.23 = (f32[2,16,512]{2,1,0:T(8,128)S(1)}, f32[2,16,512]{2,1,0:T(8,128)S(1)}, u32[]{:S(2)}, u32[]{:S(2)}) collective-permute-start(f32[2,16,512]{2,1,0:T(8,128)S(1)} %get-tuple-element.88), channel_id=1, source_target_pairs={{0,2},{2,0},{4,6},{6,4},{8,10},{10,8},{12,14},{14,12},{16,18},{18,... | collective-permute-start | bytes 196616 | tf_op jit(solution)/shard_map/ppermute | solution.py:366
  20.1 1.3 %collective-permute-start.22 = (f32[2,32,512]{2,1,0:T(8,128)S(1)}, f32[2,32,512]{2,1,0:T(8,128)S(1)}, u32[]{:S(2)}, u32[]{:S(2)}) collective-permute-start(f32[2,32,512]{2,1,0:T(8,128)S(1)} %get-tuple-element.87), channel_id=1, source_target_pairs={{0,2},{2,0},{4,6},{6,4},{8,10},{10,8},{12,14},{14,12},{16,18},{18,... | collective-permute-start | bytes 393224 | tf_op jit(solution)/shard_map/ppermute | solution.py:366
  20.2 6.9 %collective-permute-start.19 = (f32[2,32,512]{2,1,0:T(8,128)S(1)}, f32[2,32,512]{2,1,0:T(8,128)S(1)}, u32[]{:S(2)}, u32[]{:S(2)}) collective-permute-start(f32[2,32,512]{2,1,0:T(8,128)S(1)} %get-tuple-element.84), channel_id=1, source_target_pairs={{0,2},{2,0},{4,6},{6,4},{8,10},{10,8},{12,14},{14,12},{16,18},{18,... | collective-permute-start | bytes 393224 | tf_op jit(solution)/shard_map/ppermute | solution.py:366
  21.3 5.8 %collective-permute-start.20 = (f32[2,16,512]{2,1,0:T(8,128)S(1)}, f32[2,16,512]{2,1,0:T(8,128)S(1)}, u32[]{:S(2)}, u32[]{:S(2)}) collective-permute-start(f32[2,16,512]{2,1,0:T(8,128)S(1)} %get-tuple-element.85), channel_id=1, source_target_pairs={{0,2},{2,0},{4,6},{6,4},{8,10},{10,8},{12,14},{14,12},{16,18},{18,... | collective-permute-start | bytes 196616 | tf_op jit(solution)/shard_map/ppermute | solution.py:366
  27.2 2.6 %collective-permute-start.24 = (f32[1,256]{1,0:T(1,128)S(1)}, f32[1,256]{1,0:T(1,128)S(1)}, u32[]{:S(2)}, u32[]{:S(2)}) collective-permute-start(f32[1,256]{1,0:T(1,128)S(1)} %get-tuple-element.93), channel_id=1, source_target_pairs={{0,1},{1,0},{2,3},{3,2},{4,5},{5,4},{6,7},{7,6},{8,9},{9,8},{10,11... | collective-permute-start | bytes 3080 | tf_op jit(solution)/shard_map/ppermute | solution.py:405

commit v15 on v14

--- a/solution.py
+++ b/solution.py
@@ -334,15 +334,11 @@
     chips = levels // 2
     if chips % 2 or chips < 4:
         return sorted(route.items())
-    if upper:
-        for chip in range(chips - 1, 1, -2):
-            route[levels - 1 if chip == chips - 1 else 2 * chip] = 2 * (chip - 2) + 1
-        route[2] = 0
-    else:
-        route[levels - 1] = levels - 3
-        for chip in range(chips - 2, 2, -2):
-            route[2 * chip] = 2 * (chip - 2) + 1
-        route[4] = 0
+    for chip in range(chips - 1, 1, -2):
+        route[levels - 1 if chip == chips - 1 else 2 * chip] = 2 * (chip - 2) + 1
+    route[2] = 0
+    if not upper:
+        route[0], route[2], route[4] = route[4], route[0], 0
     return sorted(route.items())
 
 
@@ -391,7 +387,7 @@
     above, beside = later, latest
     for tick in range(2, TICKS - 1):
         later = [
-            odd_step(tick, half * rows, beside[half], tick == TICKS - 2 and half == 0) for half in range(HALVES)
+            odd_step(tick, half * rows, beside[half], tick == TICKS - 2 and half == HALVES - 1) for half in range(HALVES)
         ]
         beside = [even_step(tick, half * rows, [above[half]]) for half in range(HALVES)]
         above = later

time: 30.5 us -> 29.5 us (0.967)
  the two profiles are of different devices: /device:TPU:25 before, /device:TPU:0 now
where the time goes in v15:
time: 29.5 us; the launch traced here: 29.2 us
  starting transfers between devices  16.6 us (56%)
  Pallas kernels  8.96 us (30%)
  waiting for transfers between devices  2.31 us (8%)
  between operations  0.82 us (3%)
  other arithmetic  0.56 us (2%)
    ppermute x8, starting transfers between devices, down(): return lax.ppermute(piece, 'depth', other_route if other else down_route)  10.8 us
    ppermute x16, starting transfers between devices, mate(): return [lax.ppermute(piece, 'depth', mate_route) for piece in pieces]  4.27 us
    pallas_call x12, Pallas kernels, step(): pl.pallas_call(functools.partial(step_kernel, tick, start, parity, len(pi...  4.05 us
    pallas_call x2, Pallas kernels, first(): pl.pallas_call(functools.partial(first_kernel, parity, bool(carried)), ou...  2.71 us
    pallas_call x2, Pallas kernels, last(): pl.pallas_call(functools.partial(last_kernel, half), out_shape=out_shape,...  2.05 us
    ppermute x16, waiting for transfers between devices, mate(): return [lax.ppermute(piece, 'depth', mate_route) for piece in pieces]  1.59 us
    ppermute x1, starting transfers between devices, local(): gradient = gradient + lax.ppermute(chunks[distance], 'freq', route)  1.55 us
    ppermute x1, waiting for transfers between devices, local(): gradient = gradient + lax.ppermute(chunks[distance], 'freq', route)  0.7 us
  transfers between devices with their start and end apart: 25, of which 6 were waited for; matrix products, arithmetic and copies ran while one was open for 0% of the time, Pallas kernels for 30%

profile of v15, /device:TPU:0, one launch (start us, length us, event | category | flops | bytes accessed | tf_op | source)
XLA Modules:
  0.0 29.2 jit_solution(1110551012034550133)
XLA Ops:
  0.6 0.1 first_1.1
  0.7 2.9 %collective-permute-start.2 = (f32[2,48,512]{2,1,0:T(8,128)S(1)}, f32[2,48,512]{2,1,0:T(8,128)S(1)}, u32[]{:S(2)}, u32[]{:S(2)}) collective-permute-start(f32[2,48,512]{2,1,0:T(8,128)S(1)} %get-tuple-element.55), channel_id=1, source_target_pairs={{0,2},{2,4},{4,0},{6,8},{8,10},{10,12},{12,6},{14,16},{16,18},{18,... | collective-permute-start | bytes 589832 | tf_op jit(solution)/shard_map/ppermute | solution.py:365
  3.6 0.2 collective-permute-start.7
  3.9 2.6 %first_0.1 = (f32[2,32,512]{2,1,0:T(8,128)S(1)}, f32[2,16,512]{2,1,0:T(8,128)S(1)}, f32[2,32,512]{2,1,0:T(8,128)S(1)}, f32[2,16,512]{2,1,0:T(8,128)S(1)}, bf16[2...) custom-call(f32[1,1,2,512,512]{4,3,2,1,0:T(8,128)} %refs_0_.5, ...), custom_call_target="tpu_custom_call", output_to_operand_aliasing={{4}: (4, {}), {5}: (5, {}), {6}: (6, {})} | custom-call | flops 500000000 | bytes 1 | tf_op jit(solution)/shard_map/first_0/pallas_call | solution.py:173
  6.5 0.1 collective-permute-start.3
  6.6 0.5 %collective-permute-start.4 = (f32[2,16,512]{2,1,0:T(8,128)S(1)}, f32[2,16,512]{2,1,0:T(8,128)S(1)}, u32[]{:S(2)}, u32[]{:S(2)}) collective-permute-start(f32[2,16,512]{2,1,0:T(8,128)S(1)} %get-tuple-element.57), channel_id=1, source_target_pairs={{0,2},{2,0},{4,6},{6,4},{8,10},{10,8},{12,14},{14,12},{16,18},{18,... | collective-permute-start | bytes 196616 | tf_op jit(solution)/shard_map/ppermute | solution.py:362
  7.1 0.1 collective-permute-start
  7.2 0.9 %collective-permute-done.4.refs_1_ = f32[2,16,512]{2,1,0:T(8,128)S(1)} collective-permute-done((f32[2,16,512]{2,1,0:T(8,128)S(1)}, f32[2,16,512]{2,1,0:T(8,128)S(1)}, u32[]{:S(2)}, u32[]{:S(2)}) %collective-permute-start.4) | collective-permute-done | bytes 65568 | tf_op jit(solution)/shard_map/ppermute | solution.py:362
  8.0 0.3 %collective-permute-start.1 = (f32[2,16,512]{2,1,0:T(8,128)S(1)}, f32[2,16,512]{2,1,0:T(8,128)S(1)}, u32[]{:S(2)}, u32[]{:S(2)}) collective-permute-start(f32[2,16,512]{2,1,0:T(8,128)S(1)} %get-tuple-element.52), channel_id=1, source_target_pairs={{0,2},{2,0},{4,6},{6,4},{8,10},{10,8},{12,14},{14,12},{16,18},{18,... | collective-permute-start | bytes 196616 | tf_op jit(solution)/shard_map/ppermute | solution.py:362
  8.3 0.0 collective-permute-done.3.refs_0_
  8.3 0.0 copy-done.2
  8.4 0.0 copy-done.3
  8.4 0.8 %collective-permute-start.6 = (f32[2,48,512]{2,1,0:T(8,128)S(1)}, f32[2,48,512]{2,1,0:T(8,128)S(1)}, u32[]{:S(2)}, u32[]{:S(2)}) collective-permute-start(f32[2,48,512]{2,1,0:T(8,128)S(1)} %get-tuple-element.62), channel_id=1, source_target_pairs={{0,2},{2,4},{4,0},{6,8},{8,10},{10,12},{12,6},{14,16},{16,18},{18,... | collective-permute-start | bytes 589832 | tf_op jit(solution)/shard_map/ppermute | solution.py:365
  9.2 0.0 collective-permute-done.2.refs_0_
  9.2 0.7 %step_1_0_0.1 = (f32[2,32,512]{2,1,0:T(8,128)S(1)}, f32[2,16,512]{2,1,0:T(8,128)S(1)}, f32[8,512]{1,0:T(8,128)S(1)}) custom-call(f32[2,48,512]{2,1,0:T(8,128)S(1)} %collective-permute-done.2.refs_0_, f32[1,1,5,2,96,512]{5,4,3,2,1,0:T(8,128)S(1)} %copy-done, f32[1,512]{1,0:T(1,128)S(1)} %copy-done.1, ...), custom_call_target="tpu_custom_call", output_to_operand_aliasing={{2}: (7, {})} | custom-call | flops 30000000 | bytes 1 | tf_op jit(solution)/shard_map/step_1_0_0/pallas_call | solution.py:244
  9.8 0.5 %collective-permute-start.11 = (f32[2,16,512]{2,1,0:T(8,128)S(1)}, f32[2,16,512]{2,1,0:T(8,128)S(1)}, u32[]{:S(2)}, u32[]{:S(2)}) collective-permute-start(f32[2,16,512]{2,1,0:T(8,128)S(1)} %get-tuple-element.68), channel_id=1, source_target_pairs={{0,2},{2,0},{4,6},{6,4},{8,10},{10,8},{12,14},{14,12},{16,18},{18,... | collective-permute-start | bytes 196616 | tf_op jit(solution)/shard_map/ppermute | solution.py:362
  10.4 0.0 collective-permute-done.1.refs_1_
  10.4 0.1 collective-permute-start.10
  10.4 0.0 collective-permute-done.refs_0_
  10.5 1.0 %collective-permute-start.5 = (f32[2,48,512]{2,1,0:T(8,128)S(1)}, f32[2,48,512]{2,1,0:T(8,128)S(1)}, u32[]{:S(2)}, u32[]{:S(2)}) collective-permute-start(f32[2,48,512]{2,1,0:T(8,128)S(1)} %get-tuple-element.61), channel_id=1, source_target_pairs={{0,2},{2,4},{4,0},{6,8},{8,10},{10,12},{12,6},{14,16},{16,18},{18,... | collective-permute-start | bytes 589832 | tf_op jit(solution)/shard_map/ppermute | solution.py:365
  11.5 0.0 collective-permute-done.7.refs_0_
  11.5 0.7 %step_1_1_0.1 = (f32[2,32,512]{2,1,0:T(8,128)S(1)}, f32[2,16,512]{2,1,0:T(8,128)S(1)}, f32[8,512]{1,0:T(8,128)S(1)}) custom-call(f32[2,48,512]{2,1,0:T(8,128)S(1)} %collective-permute-done.7.refs_0_, f32[1,1,5,2,96,512]{5,4,3,2,1,0:T(8,128)S(1)} %copy-done, f32[1,512]{1,0:T(1,128)S(1)} %copy-done.1, ...), custom_call_target="tpu_custom_call", output_to_operand_aliasing={{2}: (7, {})} | custom-call | flops 1000000000 | bytes 1 | tf_op jit(solution)/shard_map/step_1_1_0/pallas_call | solution.py:244
  12.2 0.4 %collective-permute-start.8 = (f32[2,32,512]{2,1,0:T(8,128)S(1)}, f32[2,32,512]{2,1,0:T(8,128)S(1)}, u32[]{:S(2)}, u32[]{:S(2)}) collective-permute-start(f32[2,32,512]{2,1,0:T(8,128)S(1)} %get-tuple-element.65), channel_id=1, source_target_pairs={{0,2},{2,0},{4,6},{6,4},{8,10},{10,8},{12,14},{14,12},{16,18},{18,... | collective-permute-start | bytes 393224 | tf_op jit(solution)/shard_map/ppermute | solution.py:362
  12.5 0.0 collective-permute-done.11.refs_1_
  12.5 0.2 collective-permute-start.9
  12.7 0.0 collective-permute-done.10.refs_0_
  12.7 0.9 %collective-permute-start.18 = (f32[2,48,512]{2,1,0:T(8,128)S(1)}, f32[2,48,512]{2,1,0:T(8,128)S(1)}, u32[]{:S(2)}, u32[]{:S(2)}) collective-permute-start(f32[2,48,512]{2,1,0:T(8,128)S(1)} %get-tuple-element.81), channel_id=1, source_target_pairs={{0,2},{2,4},{4,0},{6,8},{8,10},{10,12},{12,6},{14,16},{16,18},{18,... | collective-permute-start | bytes 589832 | tf_op jit(solution)/shard_map/ppermute | solution.py:365
  13.6 0.2 collective-permute-done.9.refs_1_
  13.8 0.0 collective-permute-done.8.refs_0_
  13.8 1.2 %collective-permute-start.17 = (f32[2,48,512]{2,1,0:T(8,128)S(1)}, f32[2,48,512]{2,1,0:T(8,128)S(1)}, u32[]{:S(2)}, u32[]{:S(2)}) collective-permute-start(f32[2,48,512]{2,1,0:T(8,128)S(1)} %get-tuple-element.80), channel_id=1, source_target_pairs={{0,2},{2,4},{4,0},{6,8},{8,10},{10,12},{12,6},{14,16},{16,18},{18,... | collective-permute-start | bytes 589832 | tf_op jit(solution)/shard_map/ppermute | solution.py:365
  15.0 0.0 collective-permute-done.6.refs_0_
  15.0 0.7 %step_2_0_0.1 = (f32[2,32,512]{2,1,0:T(8,128)S(1)}, f32[2,16,512]{2,1,0:T(8,128)S(1)}, f32[8,512]{1,0:T(8,128)S(1)}) custom-call(f32[2,48,512]{2,1,0:T(8,128)S(1)} %collective-permute-done.6.refs_0_, f32[1,1,5,2,96,512]{5,4,3,2,1,0:T(8,128)S(1)} %copy-done, f32[1,512]{1,0:T(1,128)S(1)} %copy-done.1, ...), custom_call_target="tpu_custom_call", output_to_operand_aliasing={{2}: (7, {})} | custom-call | flops 10000000 | bytes 1 | tf_op jit(solution)/shard_map/step_2_0_0/pallas_call | solution.py:244
  15.7 0.1 collective-permute-start.14
  15.8 0.5 %collective-permute-start.15 = (f32[2,16,512]{2,1,0:T(8,128)S(1)}, f32[2,16,512]{2,1,0:T(8,128)S(1)}, u32[]{:S(2)}, u32[]{:S(2)}) collective-permute-start(f32[2,16,512]{2,1,0:T(8,128)S(1)} %get-tuple-element.76), channel_id=1, source_target_pairs={{0,2},{2,0},{4,6},{6,4},{8,10},{10,8},{12,14},{14,12},{16,18},{18,... | collective-permute-start | bytes 196616 | tf_op jit(solution)/shard_map/ppermute | solution.py:362
  16.3 0.0 collective-permute-done.5.refs_0_
  16.3 0.7 %step_2_1_0.1 = (f32[2,32,512]{2,1,0:T(8,128)S(1)}, f32[2,16,512]{2,1,0:T(8,128)S(1)}, f32[8,512]{1,0:T(8,128)S(1)}) custom-call(f32[2,48,512]{2,1,0:T(8,128)S(1)} %collective-permute-done.5.refs_0_, f32[1,1,5,2,96,512]{5,4,3,2,1,0:T(8,128)S(1)} %copy-done, f32[1,512]{1,0:T(1,128)S(1)} %copy-done.1, ...), custom_call_target="tpu_custom_call", output_to_operand_aliasing={{2}: (7, {})} | custom-call | flops 30000000 | bytes 1 | tf_op jit(solution)/shard_map/step_2_1_0/pallas_call | solution.py:244
  17.0 0.1 collective-permute-start.12
  17.0 0.2 collective-permute-done.15.refs_1_
  17.2 0.3 %collective-permute-start.13 = (f32[2,16,512]{2,1,0:T(8,128)S(1)}, f32[2,16,512]{2,1,0:T(8,128)S(1)}, u32[]{:S(2)}, u32[]{:S(2)}) collective-permute-start(f32[2,16,512]{2,1,0:T(8,128)S(1)} %get-tuple-element.74), channel_id=1, source_target_pairs={{0,2},{2,0},{4,6},{6,4},{8,10},{10,8},{12,14},{14,12},{16,18},{18,... | collective-permute-start | bytes 196616 | tf_op jit(solution)/shard_map/ppermute | solution.py:362
  17.5 0.0 collective-permute-done.14.refs_0_
  17.5 0.8 %collective-permute-start.21 = (f32[2,48,512]{2,1,0:T(8,128)S(1)}, f32[2,48,512]{2,1,0:T(8,128)S(1)}, u32[]{:S(2)}, u32[]{:S(2)}) collective-permute-start(f32[2,48,512]{2,1,0:T(8,128)S(1)} %get-tuple-element.86), channel_id=1, source_target_pairs={{0,2},{2,4},{4,0},{6,8},{8,10},{10,12},{12,6},{14,16},{16,18},{18,... | collective-permute-start | bytes 589832 | tf_op jit(solution)/shard_map/ppermute | solution.py:365
  18.3 0.2 collective-permute-done.13.refs_1_
  18.5 0.0 collective-permute-done.12.refs_0_
  18.5 2.9 %collective-permute-start.16 = (f32[2,48,512]{2,1,0:T(8,128)S(1)}, f32[2,48,512]{2,1,0:T(8,128)S(1)}, u32[]{:S(2)}, u32[]{:S(2)}) collective-permute-start(f32[2,48,512]{2,1,0:T(8,128)S(1)} %get-tuple-element.79), channel_id=1, source_target_pairs={{0,10},{2,4},{4,2},{6,8},{8,0},{10,12},{12,6},{14,16},{16,18},{18,... | collective-permute-start | bytes 589832 | tf_op jit(solution)/shard_map/ppermute | solution.py:365
  21.4 0.0 collective-permute-done.18.refs_0_
  21.4 0.7 %step_3_0_0.1 = (f32[2,32,512]{2,1,0:T(8,128)S(1)}, f32[2,16,512]{2,1,0:T(8,128)S(1)}, f32[8,512]{1,0:T(8,128)S(1)}) custom-call(f32[2,48,512]{2,1,0:T(8,128)S(1)} %collective-permute-done.18.refs_0_, f32[1,1,5,2,96,512]{5,4,3,2,1,0:T(8,128)S(1)} %copy-done, f32[1,512]{1,0:T(1,128)S(1)} %copy-done.1, ...), custom_call_target="tpu_custom_call", output_to_operand_aliasing={{2}: (7, {})} | custom-call | flops 10000000 | bytes 1 | tf_op jit(solution)/shard_map/step_3_0_0/pallas_call | solution.py:244
  22.1 0.1 collective-permute-start.23
  22.2 0.5 %collective-permute-start.22 = (f32[2,32,512]{2,1,0:T(8,128)S(1)}, f32[2,32,512]{2,1,0:T(8,128)S(1)}, u32[]{:S(2)}, u32[]{:S(2)}) collective-permute-start(f32[2,32,512]{2,1,0:T(8,128)S(1)} %get-tuple-element.87), channel_id=1, source_target_pairs={{0,2},{2,0},{4,6},{6,4},{8,10},{10,8},{12,14},{14,12},{16,18},{18,... | collective-permute-start | bytes 393224 | tf_op jit(solution)/shard_map/ppermute | solution.py:362
  22.7 0.0 collective-permute-done.17.refs_0_
  22.7 0.7 %step_3_1_0.1 = (f32[2,32,512]{2,1,0:T(8,128)S(1)}, f32[2,16,512]{2,1,0:T(8,128)S(1)}, f32[8,512]{1,0:T(8,128)S(1)}) custom-call(f32[2,48,512]{2,1,0:T(8,128)S(1)} %collective-permute-done.17.refs_0_, f32[1,1,5,2,96,512]{5,4,3,2,1,0:T(8,128)S(1)} %copy-done, f32[1,512]{1,0:T(1,128)S(1)} %copy-done.1, ...), custom_call_target="tpu_custom_call", output_to_operand_aliasing={{2}: (7, {})} | custom-call | flops 200000000 | bytes 1 | tf_op jit(solution)/shard_map/step_3_1_0/pallas_call | solution.py:244
  23.4 0.1 collective-permute-start.19
  23.5 0.0 collective-permute-done.23.mate_tail
  23.5 0.5 %collective-permute-start.20 = (f32[2,16,512]{2,1,0:T(8,128)S(1)}, f32[2,16,512]{2,1,0:T(8,128)S(1)}, u32[]{:S(2)}, u32[]{:S(2)}) collective-permute-start(f32[2,16,512]{2,1,0:T(8,128)S(1)} %get-tuple-element.85), channel_id=1, source_target_pairs={{0,2},{2,0},{4,6},{6,4},{8,10},{10,8},{12,14},{14,12},{16,18},{18,... | collective-permute-start | bytes 196616 | tf_op jit(solution)/shard_map/ppermute | solution.py:362
  24.0 0.0 collective-permute-done.22.mate
  24.0 0.0 collective-permute-done.21.above
  24.0 0.7 %last_0.1 = (f32[2,48,512]{2,1,0:T(8,128)S(1)}, f32[8,512]{1,0:T(8,128)S(1)}) custom-call(f32[2,48,512]{2,1,0:T(8,128)S(1)} %collective-permute-done.21.above, f32[2,32,512]{2,1,0:T(8,128)S(1)} %collective-permute-done.22.mate, f32[2,16,512]{2,1,0:T(8,128)S(1)} %collective-permute-done.23.mate_tail, ...), custom_call_target="tpu_custom_call", output_to_operand_aliasing={{1}: (9, {})} | custom-call | flops 100000000 | bytes 1 | tf_op jit(solution)/shard_map/last_0/pallas_call | solution.py:319
  24.7 0.2 collective-permute-done.20.mate_tail
  24.9 0.0 collective-permute-done.19.mate
  24.9 0.0 collective-permute-done.16.above
  24.9 0.1 gradient.1
  25.0 1.6 %collective-permute-start.24 = (f32[1,256]{1,0:T(1,128)S(1)}, f32[1,256]{1,0:T(1,128)S(1)}, u32[]{:S(2)}, u32[]{:S(2)}) collective-permute-start(f32[1,256]{1,0:T(1,128)S(1)} %get-tuple-element.93), channel_id=1, source_target_pairs={{0,1},{1,0},{2,3},{3,2},{4,5},{5,4},{6,7},{7,6},{8,9},{9,8},{10,11... | collective-permute-start | bytes 3080 | tf_op jit(solution)/shard_map/ppermute | solution.py:401
  26.6 1.4 %last_1.1 = f32[2,96,512]{2,1,0:T(8,128)} custom-call(f32[2,48,512]{2,1,0:T(8,128)S(1)} %collective-permute-done.16.above, f32[2,32,512]{2,1,0:T(8,128)S(1)} %collective-permute-done.19.mate, f32[2,16,512]{2,1,0:T(8,128)S(1)} %collective-permute-done.20.mate_tail, f32[1,1,5,2,96,512]{5,4,3,2,1,0:T(8,128)S(1)} %copy-done, f32[1,512]{1,0:T(1,128)S(1)} %copy-done.1, ...), custom_call_target="tpu_custom_call" | custom-call | flops 1 | bytes 1 | tf_op jit(solution)/shard_map/last_1/pallas_call | solution.py:319
  28.0 0.7 %collective-permute-done.24 = f32[1,256]{1,0:T(1,128)S(1)} collective-permute-done((f32[1,256]{1,0:T(1,128)S(1)}, f32[1,256]{1,0:T(1,128)S(1)}, u32[]{:S(2)}, u32[]{:S(2)}) %collective-permute-start.24) | collective-permute-done | bytes 1056 | tf_op jit(solution)/shard_map/ppermute | solution.py:401
  28.7 0.6 %add.3 = f32[1,256]{1,0:T(1,128)} add(f32[1,256]{1,0:T(1,128)S(1)} %get-tuple-element.92, f32[1,256]{1,0:T(1,128)S(1)} %collective-permute-done.24) | non-fusion elementwise | flops 256 | bytes 3072 | tf_op jit(solution)/shard_map/add | solution.py:401
  (12 shorter events, 0.0 us)
Async XLA Ops:
  0.7 8.5 %collective-permute-start.2 = (f32[2,48,512]{2,1,0:T(8,128)S(1)}, f32[2,48,512]{2,1,0:T(8,128)S(1)}, u32[]{:S(2)}, u32[]{:S(2)}) collective-permute-start(f32[2,48,512]{2,1,0:T(8,128)S(1)} %get-tuple-element.55), channel_id=1, source_target_pairs={{0,2},{2,4},{4,0},{6,8},{8,10},{10,12},{12,6},{14,16},{16,18},{18,... | collective-permute-start | bytes 589832 | tf_op jit(solution)/shard_map/ppermute | solution.py:365
  3.6 7.9 %collective-permute-start.7 = (f32[2,48,512]{2,1,0:T(8,128)S(1)}, f32[2,48,512]{2,1,0:T(8,128)S(1)}, u32[]{:S(2)}, u32[]{:S(2)}) collective-permute-start(f32[2,48,512]{2,1,0:T(8,128)S(1)} %get-tuple-element.63), channel_id=1, source_target_pairs={{0,2},{2,4},{4,0},{6,8},{8,10},{10,12},{12,6},{14,16},{16,18},{18,... | collective-permute-start | bytes 589832 | tf_op jit(solution)/shard_map/ppermute | solution.py:365
  3.9 4.5 %copy-start = (f32[1,1,5,2,96,512]{5,4,3,2,1,0:T(8,128)S(1)}, f32[1,1,5,2,96,512]{5,4,3,2,1,0:T(8,128)}, u32[]{:S(2)}) copy-start(f32[1,1,5,2,96,512]{5,4,3,2,1,0:T(8,128)} %residual.1) | copy-start | bytes 5898244
  3.9 4.5 %copy-start.1 = (f32[1,512]{1,0:T(1,128)S(1)}, f32[1,512]{1,0:T(1,128)}, u32[]{:S(2)}) copy-start(f32[1,512]{1,0:T(1,128)} %contrast.1) | copy-start | bytes 6148
  3.9 4.5 %copy-start.2 = (s32[4,96]{1,0:T(4,128)S(1)}, s32[4,96]{1,0:T(4,128)}, u32[]{:S(2)}) copy-start(s32[4,96]{1,0:T(4,128)} %sites.1) | copy-start | bytes 4612
  3.9 4.5 %copy-start.3 = (f32[1,4,2]{1,2,0:T(2,128)S(1)}, f32[1,4,2]{1,2,0:T(2,128)}, u32[]{:S(2)}) copy-start(f32[1,4,2]{1,2,0:T(2,128)} %param.11) | copy-start | bytes 100
  6.5 1.8 %collective-permute-start.3 = (f32[2,32,512]{2,1,0:T(8,128)S(1)}, f32[2,32,512]{2,1,0:T(8,128)S(1)}, u32[]{:S(2)}, u32[]{:S(2)}) collective-permute-start(f32[2,32,512]{2,1,0:T(8,128)S(1)} %get-tuple-element.56), channel_id=1, source_target_pairs={{0,2},{2,0},{4,6},{6,4},{8,10},{10,8},{12,14},{14,12},{16,18},{18,... | collective-permute-start | bytes 393224 | tf_op jit(solution)/shard_map/ppermute | solution.py:362
  6.6 1.4 %collective-permute-start.4 = (f32[2,16,512]{2,1,0:T(8,128)S(1)}, f32[2,16,512]{2,1,0:T(8,128)S(1)}, u32[]{:S(2)}, u32[]{:S(2)}) collective-permute-start(f32[2,16,512]{2,1,0:T(8,128)S(1)} %get-tuple-element.57), channel_id=1, source_target_pairs={{0,2},{2,0},{4,6},{6,4},{8,10},{10,8},{12,14},{14,12},{16,18},{18,... | collective-permute-start | bytes 196616 | tf_op jit(solution)/shard_map/ppermute | solution.py:362
  7.1 3.4 %collective-permute-start = (f32[2,32,512]{2,1,0:T(8,128)S(1)}, f32[2,32,512]{2,1,0:T(8,128)S(1)}, u32[]{:S(2)}, u32[]{:S(2)}) collective-permute-start(f32[2,32,512]{2,1,0:T(8,128)S(1)} %get-tuple-element.51), channel_id=1, source_target_pairs={{0,2},{2,0},{4,6},{6,4},{8,10},{10,8},{12,14},{14,12},{16,18},{18,... | collective-permute-start | bytes 393224 | tf_op jit(solution)/shard_map/ppermute | solution.py:362
  8.0 2.4 %collective-permute-start.1 = (f32[2,16,512]{2,1,0:T(8,128)S(1)}, f32[2,16,512]{2,1,0:T(8,128)S(1)}, u32[]{:S(2)}, u32[]{:S(2)}) collective-permute-start(f32[2,16,512]{2,1,0:T(8,128)S(1)} %get-tuple-element.52), channel_id=1, source_target_pairs={{0,2},{2,0},{4,6},{6,4},{8,10},{10,8},{12,14},{14,12},{16,18},{18,... | collective-permute-start | bytes 196616 | tf_op jit(solution)/shard_map/ppermute | solution.py:362
  8.4 6.6 %collective-permute-start.6 = (f32[2,48,512]{2,1,0:T(8,128)S(1)}, f32[2,48,512]{2,1,0:T(8,128)S(1)}, u32[]{:S(2)}, u32[]{:S(2)}) collective-permute-start(f32[2,48,512]{2,1,0:T(8,128)S(1)} %get-tuple-element.62), channel_id=1, source_target_pairs={{0,2},{2,4},{4,0},{6,8},{8,10},{10,12},{12,6},{14,16},{16,18},{18,... | collective-permute-start | bytes 589832 | tf_op jit(solution)/shard_map/ppermute | solution.py:365
  9.8 2.7 %collective-permute-start.11 = (f32[2,16,512]{2,1,0:T(8,128)S(1)}, f32[2,16,512]{2,1,0:T(8,128)S(1)}, u32[]{:S(2)}, u32[]{:S(2)}) collective-permute-start(f32[2,16,512]{2,1,0:T(8,128)S(1)} %get-tuple-element.68), channel_id=1, source_target_pairs={{0,2},{2,0},{4,6},{6,4},{8,10},{10,8},{12,14},{14,12},{16,18},{18,... | collective-permute-start | bytes 196616 | tf_op jit(solution)/shard_map/ppermute | solution.py:362
  10.4 2.4 %collective-permute-start.10 = (f32[2,32,512]{2,1,0:T(8,128)S(1)}, f32[2,32,512]{2,1,0:T(8,128)S(1)}, u32[]{:S(2)}, u32[]{:S(2)}) collective-permute-start(f32[2,32,512]{2,1,0:T(8,128)S(1)} %get-tuple-element.67), channel_id=1, source_target_pairs={{0,2},{2,0},{4,6},{6,4},{8,10},{10,8},{12,14},{14,12},{16,18},{18,... | collective-permute-start | bytes 393224 | tf_op jit(solution)/shard_map/ppermute | solution.py:362
  10.5 5.8 %collective-permute-start.5 = (f32[2,48,512]{2,1,0:T(8,128)S(1)}, f32[2,48,512]{2,1,0:T(8,128)S(1)}, u32[]{:S(2)}, u32[]{:S(2)}) collective-permute-start(f32[2,48,512]{2,1,0:T(8,128)S(1)} %get-tuple-element.61), channel_id=1, source_target_pairs={{0,2},{2,4},{4,0},{6,8},{8,10},{10,12},{12,6},{14,16},{16,18},{18,... | collective-permute-start | bytes 589832 | tf_op jit(solution)/shard_map/ppermute | solution.py:365
  12.2 1.6 %collective-permute-start.8 = (f32[2,32,512]{2,1,0:T(8,128)S(1)}, f32[2,32,512]{2,1,0:T(8,128)S(1)}, u32[]{:S(2)}, u32[]{:S(2)}) collective-permute-start(f32[2,32,512]{2,1,0:T(8,128)S(1)} %get-tuple-element.65), channel_id=1, source_target_pairs={{0,2},{2,0},{4,6},{6,4},{8,10},{10,8},{12,14},{14,12},{16,18},{18,... | collective-permute-start | bytes 393224 | tf_op jit(solution)/shard_map/ppermute | solution.py:362
  12.5 1.3 %collective-permute-start.9 = (f32[2,16,512]{2,1,0:T(8,128)S(1)}, f32[2,16,512]{2,1,0:T(8,128)S(1)}, u32[]{:S(2)}, u32[]{:S(2)}) collective-permute-start(f32[2,16,512]{2,1,0:T(8,128)S(1)} %get-tuple-element.66), channel_id=1, source_target_pairs={{0,2},{2,0},{4,6},{6,4},{8,10},{10,8},{12,14},{14,12},{16,18},{18,... | collective-permute-start | bytes 196616 | tf_op jit(solution)/shard_map/ppermute | solution.py:362
  12.7 8.7 %collective-permute-start.18 = (f32[2,48,512]{2,1,0:T(8,128)S(1)}, f32[2,48,512]{2,1,0:T(8,128)S(1)}, u32[]{:S(2)}, u32[]{:S(2)}) collective-permute-start(f32[2,48,512]{2,1,0:T(8,128)S(1)} %get-tuple-element.81), channel_id=1, source_target_pairs={{0,2},{2,4},{4,0},{6,8},{8,10},{10,12},{12,6},{14,16},{16,18},{18,... | collective-permute-start | bytes 589832 | tf_op jit(solution)/shard_map/ppermute | solution.py:365
  13.8 8.9 %collective-permute-start.17 = (f32[2,48,512]{2,1,0:T(8,128)S(1)}, f32[2,48,512]{2,1,0:T(8,128)S(1)}, u32[]{:S(2)}, u32[]{:S(2)}) collective-permute-start(f32[2,48,512]{2,1,0:T(8,128)S(1)} %get-tuple-element.80), channel_id=1, source_target_pairs={{0,2},{2,4},{4,0},{6,8},{8,10},{10,12},{12,6},{14,16},{16,18},{18,... | collective-permute-start | bytes 589832 | tf_op jit(solution)/shard_map/ppermute | solution.py:365
  15.7 1.9 %collective-permute-start.14 = (f32[2,32,512]{2,1,0:T(8,128)S(1)}, f32[2,32,512]{2,1,0:T(8,128)S(1)}, u32[]{:S(2)}, u32[]{:S(2)}) collective-permute-start(f32[2,32,512]{2,1,0:T(8,128)S(1)} %get-tuple-element.75), channel_id=1, source_target_pairs={{0,2},{2,0},{4,6},{6,4},{8,10},{10,8},{12,14},{14,12},{16,18},{18,... | collective-permute-start | bytes 393224 | tf_op jit(solution)/shard_map/ppermute | solution.py:362
  15.8 1.4 %collective-permute-start.15 = (f32[2,16,512]{2,1,0:T(8,128)S(1)}, f32[2,16,512]{2,1,0:T(8,128)S(1)}, u32[]{:S(2)}, u32[]{:S(2)}) collective-permute-start(f32[2,16,512]{2,1,0:T(8,128)S(1)} %get-tuple-element.76), channel_id=1, source_target_pairs={{0,2},{2,0},{4,6},{6,4},{8,10},{10,8},{12,14},{14,12},{16,18},{18,... | collective-permute-start | bytes 196616 | tf_op jit(solution)/shard_map/ppermute | solution.py:362
  17.0 1.5 %collective-permute-start.12 = (f32[2,32,512]{2,1,0:T(8,128)S(1)}, f32[2,32,512]{2,1,0:T(8,128)S(1)}, u32[]{:S(2)}, u32[]{:S(2)}) collective-permute-start(f32[2,32,512]{2,1,0:T(8,128)S(1)} %get-tuple-element.73), channel_id=1, source_target_pairs={{0,2},{2,0},{4,6},{6,4},{8,10},{10,8},{12,14},{14,12},{16,18},{18,... | collective-permute-start | bytes 393224 | tf_op jit(solution)/shard_map/ppermute | solution.py:362
  17.2 1.3 %collective-permute-start.13 = (f32[2,16,512]{2,1,0:T(8,128)S(1)}, f32[2,16,512]{2,1,0:T(8,128)S(1)}, u32[]{:S(2)}, u32[]{:S(2)}) collective-permute-start(f32[2,16,512]{2,1,0:T(8,128)S(1)} %get-tuple-element.74), channel_id=1, source_target_pairs={{0,2},{2,0},{4,6},{6,4},{8,10},{10,8},{12,14},{14,12},{16,18},{18,... | collective-permute-start | bytes 196616 | tf_op jit(solution)/shard_map/ppermute | solution.py:362
  17.5 6.4 %collective-permute-start.21 = (f32[2,48,512]{2,1,0:T(8,128)S(1)}, f32[2,48,512]{2,1,0:T(8,128)S(1)}, u32[]{:S(2)}, u32[]{:S(2)}) collective-permute-start(f32[2,48,512]{2,1,0:T(8,128)S(1)} %get-tuple-element.86), channel_id=1, source_target_pairs={{0,2},{2,4},{4,0},{6,8},{8,10},{10,12},{12,6},{14,16},{16,18},{18,... | collective-permute-start | bytes 589832 | tf_op jit(solution)/shard_map/ppermute | solution.py:365
  18.5 6.4 %collective-permute-start.16 = (f32[2,48,512]{2,1,0:T(8,128)S(1)}, f32[2,48,512]{2,1,0:T(8,128)S(1)}, u32[]{:S(2)}, u32[]{:S(2)}) collective-permute-start(f32[2,48,512]{2,1,0:T(8,128)S(1)} %get-tuple-element.79), channel_id=1, source_target_pairs={{0,10},{2,4},{4,2},{6,8},{8,0},{10,12},{12,6},{14,16},{16,18},{18,... | collective-permute-start | bytes 589832 | tf_op jit(solution)/shard_map/ppermute | solution.py:365
  22.1 1.4 %collective-permute-start.23 = (f32[2,16,512]{2,1,0:T(8,128)S(1)}, f32[2,16,512]{2,1,0:T(8,128)S(1)}, u32[]{:S(2)}, u32[]{:S(2)}) collective-permute-start(f32[2,16,512]{2,1,0:T(8,128)S(1)} %get-tuple-element.88), channel_id=1, source_target_pairs={{0,2},{2,0},{4,6},{6,4},{8,10},{10,8},{12,14},{14,12},{16,18},{18,... | collective-permute-start | bytes 196616 | tf_op jit(solution)/shard_map/ppermute | solution.py:362
  22.2 1.8 %collective-permute-start.22 = (f32[2,32,512]{2,1,0:T(8,128)S(1)}, f32[2,32,512]{2,1,0:T(8,128)S(1)}, u32[]{:S(2)}, u32[]{:S(2)}) collective-permute-start(f32[2,32,512]{2,1,0:T(8,128)S(1)} %get-tuple-element.87), channel_id=1, source_target_pairs={{0,2},{2,0},{4,6},{6,4},{8,10},{10,8},{12,14},{14,12},{16,18},{18,... | collective-permute-start | bytes 393224 | tf_op jit(solution)/shard_map/ppermute | solution.py:362
  23.4 1.5 %collective-permute-start.19 = (f32[2,32,512]{2,1,0:T(8,128)S(1)}, f32[2,32,512]{2,1,0:T(8,128)S(1)}, u32[]{:S(2)}, u32[]{:S(2)}) collective-permute-start(f32[2,32,512]{2,1,0:T(8,128)S(1)} %get-tuple-element.84), channel_id=1, source_target_pairs={{0,2},{2,0},{4,6},{6,4},{8,10},{10,8},{12,14},{14,12},{16,18},{18,... | collective-permute-start | bytes 393224 | tf_op jit(solution)/shard_map/ppermute | solution.py:362
  23.5 1.4 %collective-permute-start.20 = (f32[2,16,512]{2,1,0:T(8,128)S(1)}, f32[2,16,512]{2,1,0:T(8,128)S(1)}, u32[]{:S(2)}, u32[]{:S(2)}) collective-permute-start(f32[2,16,512]{2,1,0:T(8,128)S(1)} %get-tuple-element.85), channel_id=1, source_target_pairs={{0,2},{2,0},{4,6},{6,4},{8,10},{10,8},{12,14},{14,12},{16,18},{18,... | collective-permute-start | bytes 196616 | tf_op jit(solution)/shard_map/ppermute | solution.py:362
  25.0 3.6 %collective-permute-start.24 = (f32[1,256]{1,0:T(1,128)S(1)}, f32[1,256]{1,0:T(1,128)S(1)}, u32[]{:S(2)}, u32[]{:S(2)}) collective-permute-start(f32[1,256]{1,0:T(1,128)S(1)} %get-tuple-element.93), channel_id=1, source_target_pairs={{0,1},{1,0},{2,3},{3,2},{4,5},{5,4},{6,7},{7,6},{8,9},{9,8},{10,11... | collective-permute-start | bytes 3080 | tf_op jit(solution)/shard_map/ppermute | solution.py:401
